TPU v7x, 32 devices: a whole 2x2x4 slice. The times are simulated.
32 devices in a mesh: ens: 2 (over y), tile: 4 (over z), lev: 2 (over x), sub: 2 (over core).
Axes of the slice: x: 2, y: 2, z: 4, core: 2. Of those that a mesh axis runs over, the one named last changes fastest.
Arguments:
- marine_layered_warmth: float32 [8, 128, 512], P(('ens', 'lev'), 'sub', 'tile'), parts along dimension 0, may hold values from -6 to 6
- bottom_sky_warmth: float32 [8192], P(('ens', 'tile', 'lev', 'sub')), parts along dimension 0, may hold values from -6 to 6
- bottom_breeze_magnitude: float32 [8192], P(('ens', 'tile', 'lev', 'sub')), parts along dimension 0, may hold values from 0.3 to 3
- depth_shares: float32 [4], P('lev'), may hold values from 0.05 to 0.25
- piece_sky_box: int32 [16, 8, 256], P(('tile', 'lev', 'sub')), may hold values from 0 to 255, as said below
- sky_share_fraction: float32 [16, 8, 256], P(('tile', 'lev', 'sub')), as said below
- piece_marine_box: int32 [16, 8, 256], P(('tile', 'lev', 'sub')), may hold values from 0 to 8191, as said below
- marine_share_fraction: float32 [16, 8, 256], P(('tile', 'lev', 'sub')), as said below
- marine_indicator: int32 [128, 512], P('sub', 'tile'), may hold values from 0 to 1
- marine_result_adjoint: float32 [8, 128, 512], P(('ens', 'lev'), 'sub', 'tile'), parts along dimension 0, may hold values from -6 to 6
- energy_transport_adjoint: float32 [8192], P(('ens', 'tile', 'lev', 'sub')), parts along dimension 0, may hold values from -6 to 6
Outputs:
- state_gradient: float32 [8, 128, 512], P(('ens', 'lev'), 'sub', 'tile'), parts along dimension 0
- air_gradient: float32 [8192], P(('ens', 'tile', 'lev', 'sub')), parts along dimension 0
- wind_gradient: float32 [8192], P(('ens', 'tile', 'lev', 'sub')), parts along dimension 0
There are 2 independent parts, one for each index of `ens`. A program takes and returns all parts, laid end to end along the dimension named above; an argument that names none is the same for every part. Nothing has to cross between parts.
Inputs may be any that keep to these rules, and one draw needn't show every extreme that they name: `piece_sky_box`: indices into the device's own 256 atmosphere cells. `piece_marine_box`: slot j of block r = a * 2 + s on ocean device e = (o * 2 + l) * 2 + u is the same exchange-grid cell as slot j of block o * 2 + u on atmosphere device (a * 2 + l) * 2 + s; entries index the device's own 64 x 128 ocean cells row by row. `sky_share_fraction`: in each block the live slots come first, the rest carry weight zero; a live slot also has weight zero where its ocean cell is land; the blocks to 2 ocean owners of every lev index are full from every source. `marine_share_fraction`: zero at the same slots as sky_share_fraction.
All inputs are finite; a program needn't handle non-finite values.
Results may differ from a plain program's by a relative error of at most 0.0003.
Values sent between devices are 32-bit elements; how exact they have to be, the bound alone decides.
No kernel may reach another device: no remote copies, remote signals or barrier semaphores. Data moves between devices by JAX's collectives and lax.ppermute only.
A program may use at most 64 MiB of HBM per device.

v0:
```python
import jax
import jax.numpy as jnp
from jax import lax
from jax.sharding import PartitionSpec as P

BULK_ITERS = 3
STEPS = 3


MIXING = 0.2
TRANSFER = 1.0
STABILITY = 0.5


def extended(block, sides, width):
    for axis, dim in sides:
        count = lax.axis_size(axis)
        forward = [(i, i + 1) for i in range(count - 1)]
        backward = [(target, source) for source, target in forward]
        low = lax.ppermute(
            lax.slice_in_dim(block, block.shape[dim] - width, None, axis=dim), axis, forward
        )
        high = lax.ppermute(lax.slice_in_dim(block, 0, width, axis=dim), axis, backward)
        block = jnp.concatenate([low, block, high], axis=dim)
    return block


def diffuse(tracer_pad, wet_pad):
    center = tracer_pad[:, 1:-1, 1:-1]
    wet_center = wet_pad[1:-1, 1:-1]
    wet_above = wet_pad[:-2, 1:-1]
    wet_below = wet_pad[2:, 1:-1]
    wet_left = wet_pad[1:-1, :-2]
    wet_right = wet_pad[1:-1, 2:]
    beside = (
        wet_above * tracer_pad[:, :-2, 1:-1]
        + wet_below * tracer_pad[:, 2:, 1:-1]
        + wet_left * tracer_pad[:, 1:-1, :-2]
        + wet_right * tracer_pad[:, 1:-1, 2:]
    )
    wet_count = wet_above + wet_below + wet_left + wet_right
    return wet_center * (center + MIXING * (beside - wet_count * center))


def adjoint_diffusion(cotangent, wet):
    tracer = cotangent
    for sweep_index in range(STEPS):
        padded = extended(
            jnp.concatenate([tracer, wet[None]], axis=0), (("tile", 2), ("sub", 1)), 1
        )
        tracer = diffuse(padded[:-1], padded[-1])
    return tracer


def ocean_adjoint(cotangent, wet, depth_shares, weight_rows, ocean_index):
    adjoint = adjoint_diffusion(cotangent, wet)
    partial_heat = jnp.einsum("j,jck->ck", depth_shares, adjoint, precision=lax.Precision.HIGHEST)
    heat_sens = wet * lax.psum(partial_heat, "lev")
    return (adjoint, weight_rows * heat_sens.reshape(-1)[ocean_index])


def ocean_to_air(blocks):
    moved = lax.all_to_all(blocks, ("tile", "sub"), split_axis=1, concat_axis=1, tiled=True)
    return moved


def air_to_ocean(blocks):
    moved = lax.all_to_all(blocks, ("tile", "sub"), split_axis=1, concat_axis=1, tiled=True)
    return moved


def bulk_adjoint(warmth_gap, flux_sens):
    transfer_rate = jnp.full_like(warmth_gap, TRANSFER)
    rates = [transfer_rate]
    slopes = []
    for sweep_index in range(BULK_ITERS):
        bent = jnp.tanh(transfer_rate * warmth_gap)
        slopes.append(TRANSFER * STABILITY * (1.0 - bent * bent))
        transfer_rate = TRANSFER * (1.0 + STABILITY * bent)
        rates.append(transfer_rate)
    contrast_sens = transfer_rate * flux_sens
    rate_sens = warmth_gap * flux_sens
    for sweep_index in reversed(range(BULK_ITERS)):
        inner_sens = rate_sens * slopes[sweep_index]
        contrast_sens = contrast_sens + inner_sens * rates[sweep_index]
        rate_sens = inner_sens * warmth_gap
    return contrast_sens


def owner_stride():
    return 4


def onehot_cells(rows, cell_count):
    return (rows[:, None] == jnp.arange(cell_count, dtype=jnp.int32)[None, :]).astype(jnp.float32)


def pick_cells(lookups, air_index):
    owner_count, slot_count = air_index.shape
    cell_count = lookups.shape[1]
    stride = owner_stride()
    grouped = air_index.reshape(owner_count // stride, stride * slot_count)

    def lookup_block(rows):
        onehot = onehot_cells(rows, cell_count)
        return jnp.einsum("kc,rc->kr", lookups, onehot, precision=lax.Precision.HIGHEST)

    picked = lax.map(lookup_block, grouped)
    return picked.transpose(1, 0, 2).reshape(lookups.shape[0], owner_count, slot_count)


def gather_cells(values, air_index, cell_count):
    owner_count, slot_count = air_index.shape
    stride = owner_stride()
    grouped = air_index.reshape(owner_count // stride, stride * slot_count)
    grouped_values = values.reshape(
        values.shape[0], owner_count // stride, stride * slot_count
    ).transpose(1, 0, 2)

    def add_block(totals, inputs):
        rows, block_values = inputs
        onehot = onehot_cells(rows, cell_count)
        return (
            totals + jnp.einsum("kr,rc->kc", block_values, onehot, precision=lax.Precision.HIGHEST),
            None,
        )

    start = jnp.zeros((values.shape[0], cell_count), jnp.float32)
    totals, unused = lax.scan(add_block, start, (grouped, grouped_values))
    return totals


def per_device(
    marine_layered_warmth,
    bottom_sky_warmth,
    bottom_breeze_magnitude,
    depth_shares,
    piece_sky_box,
    sky_share_fraction,
    piece_marine_box,
    marine_share_fraction,
    marine_indicator,
    marine_result_adjoint,
    energy_transport_adjoint,
):
    wet = marine_indicator.astype(jnp.float32)
    ocean_index = piece_marine_box[0]
    partial_surface = jnp.einsum(
        "j,jck->ck", depth_shares, marine_layered_warmth, precision=lax.Precision.HIGHEST
    )
    surface = lax.psum(partial_surface, "lev")
    surface_lookup = surface.reshape(-1)[ocean_index]
    adjoint, weighted_heat = ocean_adjoint(
        marine_result_adjoint, wet, depth_shares, marine_share_fraction[0], ocean_index
    )
    arrived = ocean_to_air(jnp.stack([surface_lookup, weighted_heat]))
    shared_interface_pieces = arrived[0]
    heat_slots = arrived[1]
    air_index = piece_sky_box[0]
    interface_lookups = jnp.stack(
        [bottom_sky_warmth, bottom_breeze_magnitude, energy_transport_adjoint]
    )
    picked = pick_cells(interface_lookups, air_index)
    difference = shared_interface_pieces - picked[0]
    warmth_gap = picked[1] * difference
    flux_sens = heat_slots + sky_share_fraction[0] * picked[2]
    contrast_sens = bulk_adjoint(warmth_gap, flux_sens)
    surface_sens = contrast_sens * picked[1]
    cell_totals = gather_cells(
        jnp.stack([surface_sens, contrast_sens * difference]), air_index, bottom_sky_warmth.shape[0]
    )
    air_gradient = -cell_totals[0]
    wind_gradient = cell_totals[1]
    returned = air_to_ocean(surface_sens[None])[0]
    partial_slots = jax.ops.segment_sum(
        returned.reshape(-1), ocean_index.reshape(-1), num_segments=wet.size
    ).reshape(wet.shape)
    surface_gradient = lax.psum(partial_slots, "lev")
    state_gradient = wet * adjoint + depth_shares[:, None, None] * surface_gradient
    return (state_gradient, air_gradient, wind_gradient)


def solution(mesh):
    return jax.shard_map(
        per_device,
        mesh=mesh,
        in_specs=(
            P(("ens", "lev"), "sub", "tile"),
            P(("ens", "tile", "lev", "sub")),
            P(("ens", "tile", "lev", "sub")),
            P("lev"),
            P(("tile", "lev", "sub"), None, None),
            P(("tile", "lev", "sub"), None, None),
            P(("tile", "lev", "sub"), None, None),
            P(("tile", "lev", "sub"), None, None),
            P("sub", "tile"),
            P(("ens", "lev"), "sub", "tile"),
            P(("ens", "tile", "lev", "sub")),
        ),
        out_specs=(
            P(("ens", "lev"), "sub", "tile"),
            P(("ens", "tile", "lev", "sub")),
            P(("ens", "tile", "lev", "sub")),
        ),
        check_vma=False,
    )
```

profile of v0, /device:TPU:0, one launch (start us, length us, event | category | flops | bytes accessed | tf_op | source)
XLA Modules:
  0.0 148.5 jit_solution(11885958351341896080)
XLA Ops:
  7.2 0.0 all-reduce.3.cloned.1.call-start
  7.2 0.8 fusion.97
  8.0 0.0 copy-done.2
  8.1 0.1 slice_maximum_fusion.2
  8.1 4.9 %collective-permute-start = (f32[3,64,1]{2,1,0:T(8,128)S(1)}, f32[3,64,1]{2,1,0:T(8,128)S(1)}, u32[]{:S(2)}, u32[]{:S(2)}) collective-permute-start(f32[3,64,1]{2,1,0:T(8,128)S(1)} %get-tuple-element.109), channel_id=1, source_target_pairs={{0,4},{4,8},{8,12},{1,5},{5,9},{9,13},{2,6},{6,10},{10,14},{3,7},{... | collective-permute-start | bytes 2312 | tf_op jit(solution)/shard_map/ppermute | solution.py:20
  13.1 1.3 collective-permute-start.1
  14.4 0.9 collective-permute-done
  15.3 4.3 %collective-permute-done.1 = f32[3,64,1]{2,1,0:T(8,128)S(1)} collective-permute-done((f32[3,64,1]{2,1,0:T(8,128)S(1)}, f32[3,64,1]{2,1,0:T(8,128)S(1)}, u32[]{:S(2)}, u32[]{:S(2)}) %collective-permute-start.1) | collective-permute-done | bytes 800 | tf_op jit(solution)/shard_map/ppermute | solution.py:23
  19.6 0.1 fusion.4
  19.8 1.3 collective-permute-start.2
  21.1 1.3 collective-permute-start.3
  22.4 1.7 %collective-permute-done.3 = f32[3,1,130]{2,1,0:T(1,128)S(1)} collective-permute-done((f32[3,1,130]{2,1,0:T(1,128)S(1)}, f32[3,1,130]{2,1,0:T(1,128)S(1)}, u32[]{:S(2)}, u32[]{:S(2)}) %collective-permute-start.3) | collective-permute-done | bytes 1592 | tf_op jit(solution)/shard_map/ppermute | solution.py:23
  24.1 0.1 fusion.13
  24.2 0.1 fusion.96
  24.3 0.2 fusion.34
  24.5 0.1 slice_maximum_fusion.1
  24.6 3.5 %collective-permute-start.4 = (f32[3,64,1]{2,1,0:T(8,128)S(1)}, f32[3,64,1]{2,1,0:T(8,128)S(1)}, u32[]{:S(2)}, u32[]{:S(2)}) collective-permute-start(f32[3,64,1]{2,1,0:T(8,128)S(1)} %get-tuple-element.107), channel_id=1, source_target_pairs={{0,4},{4,8},{8,12},{1,5},{5,9},{9,13},{2,6},{6,10},{10,14},{3,7},{... | collective-permute-start | bytes 2312 | tf_op jit(solution)/shard_map/ppermute | solution.py:20
  28.1 1.3 collective-permute-start.5
  29.5 1.0 collective-permute-done.4
  30.5 4.1 %collective-permute-done.5 = f32[3,64,1]{2,1,0:T(8,128)S(1)} collective-permute-done((f32[3,64,1]{2,1,0:T(8,128)S(1)}, f32[3,64,1]{2,1,0:T(8,128)S(1)}, u32[]{:S(2)}, u32[]{:S(2)}) %collective-permute-start.5) | collective-permute-done | bytes 800 | tf_op jit(solution)/shard_map/ppermute | solution.py:23
  34.6 0.1 fusion.6
  34.8 1.3 collective-permute-start.6
  36.1 1.3 collective-permute-start.7
  37.4 1.3 while.21
  37.4 0.6 fusion.104
  38.1 0.6 fusion.104
  38.7 0.4 collective-permute-done.7
  39.1 0.1 fusion.18
  39.2 0.1 fusion.95
  39.3 0.2 fusion.45
  39.5 0.1 slice_maximum_fusion
  39.6 3.5 %collective-permute-start.8 = (f32[3,64,1]{2,1,0:T(8,128)S(1)}, f32[3,64,1]{2,1,0:T(8,128)S(1)}, u32[]{:S(2)}, u32[]{:S(2)}) collective-permute-start(f32[3,64,1]{2,1,0:T(8,128)S(1)} %get-tuple-element.105), channel_id=1, source_target_pairs={{0,4},{4,8},{8,12},{1,5},{5,9},{9,13},{2,6},{6,10},{10,14},{3,7},{... | collective-permute-start | bytes 2312 | tf_op jit(solution)/shard_map/ppermute | solution.py:20
  43.1 1.3 collective-permute-start.9
  44.4 1.0 fusion.83
  45.4 0.6 collective-permute-done.8
  46.0 4.1 %collective-permute-done.9 = f32[3,64,1]{2,1,0:T(8,128)S(1)} collective-permute-done((f32[3,64,1]{2,1,0:T(8,128)S(1)}, f32[3,64,1]{2,1,0:T(8,128)S(1)}, u32[]{:S(2)}, u32[]{:S(2)}) %collective-permute-start.9) | collective-permute-done | bytes 800 | tf_op jit(solution)/shard_map/ppermute | solution.py:23
  50.1 0.1 fusion.8
  50.3 1.5 %collective-permute-start.10 = (f32[3,1,130]{2,1,0:T(1,128)S(1)}, f32[3,1,130]{2,1,0:T(1,128)S(1)}, u32[]{:S(2)}, u32[]{:S(2)}) collective-permute-start(f32[3,1,130]{2,1,0:T(1,128)S(1)} %get-tuple-element.99), channel_id=1, source_target_pairs={{0,1},{2,3},{4,5},{6,7},{8,9},{10,11},{12,13},{14,15},{16,17},{18,... | collective-permute-start | bytes 4688 | tf_op jit(solution)/shard_map/ppermute | solution.py:20
  51.9 1.3 collective-permute-start.11
  53.2 1.7 %collective-permute-done.11 = f32[3,1,130]{2,1,0:T(1,128)S(1)} collective-permute-done((f32[3,1,130]{2,1,0:T(1,128)S(1)}, f32[3,1,130]{2,1,0:T(1,128)S(1)}, u32[]{:S(2)}, u32[]{:S(2)}) %collective-permute-start.11) | collective-permute-done | bytes 1592 | tf_op jit(solution)/shard_map/ppermute | solution.py:23
  54.9 0.1 fusion.23
  55.0 0.1 fusion.94
  55.1 0.2 fusion.56
  55.3 1.0 fusion.81
  56.3 0.0 all-reduce.3.cloned.1.call-update
  56.3 19.2 %all-reduce.3.cloned.1.call-done = (f32[64,128]{1,0:T(8,128)}, f32[8192]{0:T(1024)}) async-done(((f32[64,128]{1,0:T(8,128)}, f32[8192]{0:T(1024)}), (f32[64,128]{1,0:T(8,128)}, f32[8192]{0:T(1024)})) %all-reduce.3.cloned.1.call-update) | async-done | bytes 65552 | tf_op jit(solution)/shard_map/psum | solution.py:58
  75.5 0.8 multiply_bitcast_fusion
  76.3 11.8 %gather_fusion.1 = f32[2048]{0:T(1024)S(1)} fusion(f32[8192]{0:T(1024)S(1)} %multiply_bitcast_fusion, s32[2048]{0:T(1024)S(1)} %broadcast_clamp_fusion), kind=kCustom, calls=%fused_computation.1 | custom fusion | bytes 24576 | tf_op jit(solution)/shard_map/gather | solution.py:59
  88.1 11.8 %gather_fusion = f32[2048]{0:T(1024)S(1)} fusion(f32[8192]{0:T(1024)S(1)} %copy-done.1, s32[2048]{0:T(1024)S(1)} %broadcast_clamp_fusion), kind=kCustom, calls=%fused_computation | custom fusion | bytes 24576 | tf_op jit(solution)/shard_map/gather | solution.py:152
  99.9 0.7 copy-done.5
  100.6 0.6 copy.24
  101.2 4.6 %all-to-all-start = ((f32[2,8,256]{2,0,1:T(2,128)}), f32[2,8,256]{2,0,1:T(2,128)S(1)}, u32[]{:S(2)}, u32[]{:S(2)}) async-start(f32[2,8,256]{2,0,1:T(2,128)} %copy.24), calls=%async_computation | async-start | bytes 32768 | tf_op jit(solution)/shard_map/all_to_all | solution.py:63
  105.8 0.1 slice_reduce_fusion.1
  106.0 5.5 %all-to-all-done = f32[2,8,256]{2,0,1:T(2,128)S(1)} async-done(((f32[2,8,256]{2,0,1:T(2,128)}), f32[2,8,256]{2,0,1:T(2,128)S(1)}, u32[]{:S(2)}, u32[]{:S(2)}) %all-to-all-start) | async-done | bytes 16416 | tf_op jit(solution)/shard_map/all_to_all | solution.py:63
  111.6 0.6 copy.27
  112.2 1.1 while.22
  112.3 0.5 convolution_add_fusion.2
  112.8 0.5 convolution_add_fusion.2
  113.3 3.3 %all-to-all-start.1 = ((f32[1,8,256]{2,0,1:T(1,128)}), f32[1,8,256]{2,0,1:T(1,128)S(1)}, u32[]{:S(2)}, u32[]{:S(2)}) async-start(f32[1,8,256]{2,0,1:T(1,128)} %copy.27), calls=%async_computation.1 | async-start | bytes 16384 | tf_op jit(solution)/shard_map/all_to_all | solution.py:68
  116.6 0.6 fusion.99
  117.2 5.0 %all-to-all-done.1 = f32[1,8,256]{2,0,1:T(1,128)S(1)} async-done(((f32[1,8,256]{2,0,1:T(1,128)}), f32[1,8,256]{2,0,1:T(1,128)S(1)}, u32[]{:S(2)}, u32[]{:S(2)}) %all-to-all-start.1) | async-done | bytes 8224 | tf_op jit(solution)/shard_map/all_to_all | solution.py:68
  122.2 11.3 %scatter_custom_fusion = f32[8192]{0:T(1024)S(1)} fusion(s32[2048]{0:T(1024)S(1)} %bitcast.70, f32[2048]{0:T(1024)S(1)} %bitcast.71, f32[]{:T(128)} %constant.7.clone.1), kind=kCustom, calls=%fused_computation.129 | custom fusion | flops 2048 | bytes 32772 | tf_op jit(solution)/shard_map/scatter-add | solution.py:175
  133.4 7.4 %psum.23 = f32[64,128]{1,0:T(8,128)S(1)} all-reduce(f32[64,128]{1,0:T(8,128)S(1)} %bitcast.62), channel_id=1, replica_groups=mesh['ens'=2,'tile'=4,'lev'=2,'sub'=2] {'lev'}, use_global_device_ids=true, to_apply=%region_5.6 | all-reduce | flops 8192 | bytes 65536 | tf_op jit(solution)/shard_map/psum | solution.py:178
  140.9 0.8 multiply_add_fusion
  (55 shorter events, 0.4 us)
Async XLA Ops:
  7.2 37.3 %copy-start = (f32[2,64,128]{2,1,0:T(8,128)S(1)}, f32[2,64,128]{2,1,0:T(8,128)}, u32[]{:S(2)}) copy-start(f32[2,64,128]{2,1,0:T(8,128)} %param.15) | copy-start | bytes 196612
  7.2 0.9 copy-start.2
  7.2 68.3 %all-reduce.3.cloned.1.call-start = ((), (), s32[]{:S(2)}) async-start(), calls=%async_computation.2 | async-start | bytes 131072 | tf_op jit(solution)/shard_map/psum | solution.py:58
  8.1 7.1 %collective-permute-start = (f32[3,64,1]{2,1,0:T(8,128)S(1)}, f32[3,64,1]{2,1,0:T(8,128)S(1)}, u32[]{:S(2)}, u32[]{:S(2)}) collective-permute-start(f32[3,64,1]{2,1,0:T(8,128)S(1)} %get-tuple-element.109), channel_id=1, source_target_pairs={{0,4},{4,8},{8,12},{1,5},{5,9},{9,13},{2,6},{6,10},{10,14},{3,7},{... | collective-permute-start | bytes 2312 | tf_op jit(solution)/shard_map/ppermute | solution.py:20
  13.1 6.5 %collective-permute-start.1 = (f32[3,64,1]{2,1,0:T(8,128)S(1)}, f32[3,64,1]{2,1,0:T(8,128)S(1)}, u32[]{:S(2)}, u32[]{:S(2)}) collective-permute-start(f32[3,64,1]{2,1,0:T(8,128)S(1)} %get-tuple-element.110), channel_id=1, source_target_pairs={{4,0},{8,4},{12,8},{5,1},{9,5},{13,9},{6,2},{10,6},{14,10},{7,3},{... | collective-permute-start | bytes 2312 | tf_op jit(solution)/shard_map/ppermute | solution.py:23
  19.8 2.6 %collective-permute-start.2 = (f32[3,1,130]{2,1,0:T(1,128)S(1)}, f32[3,1,130]{2,1,0:T(1,128)S(1)}, u32[]{:S(2)}, u32[]{:S(2)}) collective-permute-start(f32[3,1,130]{2,1,0:T(1,128)S(1)} %get-tuple-element.103), channel_id=1, source_target_pairs={{0,1},{2,3},{4,5},{6,7},{8,9},{10,11},{12,13},{14,15},{16,17},{18,... | collective-permute-start | bytes 4688 | tf_op jit(solution)/shard_map/ppermute | solution.py:20
  21.1 3.1 %collective-permute-start.3 = (f32[3,1,130]{2,1,0:T(1,128)S(1)}, f32[3,1,130]{2,1,0:T(1,128)S(1)}, u32[]{:S(2)}, u32[]{:S(2)}) collective-permute-start(f32[3,1,130]{2,1,0:T(1,128)S(1)} %get-tuple-element.104), channel_id=1, source_target_pairs={{1,0},{3,2},{5,4},{7,6},{9,8},{11,10},{13,12},{15,14},{17,16},{19,... | collective-permute-start | bytes 4688 | tf_op jit(solution)/shard_map/ppermute | solution.py:23
  24.5 4.9 %copy-start.8 = (f32[256]{0:T(256)S(1)}, f32[256]{0:T(256)}, u32[]{:S(2)}) copy-start(f32[256]{0:T(256)} %param.25) | copy-start | bytes 3076
  24.5 4.9 %copy-start.9 = (f32[256]{0:T(256)S(1)}, f32[256]{0:T(256)}, u32[]{:S(2)}) copy-start(f32[256]{0:T(256)} %param.17) | copy-start | bytes 3076
  24.5 4.9 %copy-start.10 = (f32[256]{0:T(256)S(1)}, f32[256]{0:T(256)}, u32[]{:S(2)}) copy-start(f32[256]{0:T(256)} %param.16) | copy-start | bytes 3076
  24.6 4.9 %copy-start.6 = (s32[1,8,256]{2,1,0:T(8,128)S(1)}, s32[1,8,256]{2,1,0:T(8,128)}, u32[]{:S(2)}) copy-start(s32[1,8,256]{2,1,0:T(8,128)} %param.19) | copy-start | bytes 24580
  24.6 5.9 %collective-permute-start.4 = (f32[3,64,1]{2,1,0:T(8,128)S(1)}, f32[3,64,1]{2,1,0:T(8,128)S(1)}, u32[]{:S(2)}, u32[]{:S(2)}) collective-permute-start(f32[3,64,1]{2,1,0:T(8,128)S(1)} %get-tuple-element.107), channel_id=1, source_target_pairs={{0,4},{4,8},{8,12},{1,5},{5,9},{9,13},{2,6},{6,10},{10,14},{3,7},{... | collective-permute-start | bytes 2312 | tf_op jit(solution)/shard_map/ppermute | solution.py:20
  28.1 6.5 %collective-permute-start.5 = (f32[3,64,1]{2,1,0:T(8,128)S(1)}, f32[3,64,1]{2,1,0:T(8,128)S(1)}, u32[]{:S(2)}, u32[]{:S(2)}) collective-permute-start(f32[3,64,1]{2,1,0:T(8,128)S(1)} %get-tuple-element.108), channel_id=1, source_target_pairs={{4,0},{8,4},{12,8},{5,1},{9,5},{13,9},{6,2},{10,6},{14,10},{7,3},{... | collective-permute-start | bytes 2312 | tf_op jit(solution)/shard_map/ppermute | solution.py:23
  34.8 3.9 %collective-permute-start.6 = (f32[3,1,130]{2,1,0:T(1,128)S(1)}, f32[3,1,130]{2,1,0:T(1,128)S(1)}, u32[]{:S(2)}, u32[]{:S(2)}) collective-permute-start(f32[3,1,130]{2,1,0:T(1,128)S(1)} %get-tuple-element.101), channel_id=1, source_target_pairs={{0,1},{2,3},{4,5},{6,7},{8,9},{10,11},{12,13},{14,15},{16,17},{18,... | collective-permute-start | bytes 4688 | tf_op jit(solution)/shard_map/ppermute | solution.py:20
  36.1 3.1 %collective-permute-start.7 = (f32[3,1,130]{2,1,0:T(1,128)S(1)}, f32[3,1,130]{2,1,0:T(1,128)S(1)}, u32[]{:S(2)}, u32[]{:S(2)}) collective-permute-start(f32[3,1,130]{2,1,0:T(1,128)S(1)} %get-tuple-element.102), channel_id=1, source_target_pairs={{1,0},{3,2},{5,4},{7,6},{9,8},{11,10},{13,12},{15,14},{17,16},{19,... | collective-permute-start | bytes 4688 | tf_op jit(solution)/shard_map/ppermute | solution.py:23
  39.6 4.8 %copy-start.11 = (f32[2]{0:T(128)S(1)}, f32[2]{0:T(128)}, u32[]{:S(2)}) copy-start(f32[2]{0:T(128)} %param.18) | copy-start | bytes 28
  39.6 6.4 %collective-permute-start.8 = (f32[3,64,1]{2,1,0:T(8,128)S(1)}, f32[3,64,1]{2,1,0:T(8,128)S(1)}, u32[]{:S(2)}, u32[]{:S(2)}) collective-permute-start(f32[3,64,1]{2,1,0:T(8,128)S(1)} %get-tuple-element.105), channel_id=1, source_target_pairs={{0,4},{4,8},{8,12},{1,5},{5,9},{9,13},{2,6},{6,10},{10,14},{3,7},{... | collective-permute-start | bytes 2312 | tf_op jit(solution)/shard_map/ppermute | solution.py:20
  43.1 7.0 %collective-permute-start.9 = (f32[3,64,1]{2,1,0:T(8,128)S(1)}, f32[3,64,1]{2,1,0:T(8,128)S(1)}, u32[]{:S(2)}, u32[]{:S(2)}) collective-permute-start(f32[3,64,1]{2,1,0:T(8,128)S(1)} %get-tuple-element.106), channel_id=1, source_target_pairs={{4,0},{8,4},{12,8},{5,1},{9,5},{13,9},{6,2},{10,6},{14,10},{7,3},{... | collective-permute-start | bytes 2312 | tf_op jit(solution)/shard_map/ppermute | solution.py:23
  50.3 2.9 %copy-start.4 = (s32[1,8,256]{2,1,0:T(8,128)S(1)}, s32[1,8,256]{2,1,0:T(8,128)}, u32[]{:S(2)}) copy-start(s32[1,8,256]{2,1,0:T(8,128)} %param.21) | copy-start | bytes 24580
  50.3 2.9 %collective-permute-start.10 = (f32[3,1,130]{2,1,0:T(1,128)S(1)}, f32[3,1,130]{2,1,0:T(1,128)S(1)}, u32[]{:S(2)}, u32[]{:S(2)}) collective-permute-start(f32[3,1,130]{2,1,0:T(1,128)S(1)} %get-tuple-element.99), channel_id=1, source_target_pairs={{0,1},{2,3},{4,5},{6,7},{8,9},{10,11},{12,13},{14,15},{16,17},{18,... | collective-permute-start | bytes 4688 | tf_op jit(solution)/shard_map/ppermute | solution.py:20
  51.9 3.1 %collective-permute-start.11 = (f32[3,1,130]{2,1,0:T(1,128)S(1)}, f32[3,1,130]{2,1,0:T(1,128)S(1)}, u32[]{:S(2)}, u32[]{:S(2)}) collective-permute-start(f32[3,1,130]{2,1,0:T(1,128)S(1)} %get-tuple-element.100), channel_id=1, source_target_pairs={{1,0},{3,2},{5,4},{7,6},{9,8},{11,10},{13,12},{15,14},{17,16},{19,... | collective-permute-start | bytes 4688 | tf_op jit(solution)/shard_map/ppermute | solution.py:23
  56.3 19.2 %copy-start.3 = (s32[64,128]{1,0:T(8,128)S(1)}, s32[64,128]{1,0:T(8,128)}, u32[]{:S(2)}) copy-start(s32[64,128]{1,0:T(8,128)} %param.23) | copy-start | bytes 98308
  76.3 11.8 %copy-start.1 = (f32[8192]{0:T(1024)S(1)}, f32[8192]{0:T(1024)}, u32[]{:S(2)}) copy-start(f32[8192]{0:T(1024)} %get-tuple-element.96) | copy-start | bytes 98308
  99.9 0.7 copy-start.5
  100.6 10.9 %copy-start.7 = (f32[1,8,256]{2,1,0:T(8,128)S(1)}, f32[1,8,256]{2,1,0:T(8,128)}, u32[]{:S(2)}) copy-start(f32[1,8,256]{2,1,0:T(8,128)} %param.20) | copy-start | bytes 24580
  101.2 10.3 %all-to-all-start = ((f32[2,8,256]{2,0,1:T(2,128)}), f32[2,8,256]{2,0,1:T(2,128)S(1)}, u32[]{:S(2)}, u32[]{:S(2)}) async-start(f32[2,8,256]{2,0,1:T(2,128)} %copy.24), calls=%async_computation | async-start | bytes 32768 | tf_op jit(solution)/shard_map/all_to_all | solution.py:63
  113.3 8.9 %all-to-all-start.1 = ((f32[1,8,256]{2,0,1:T(1,128)}), f32[1,8,256]{2,0,1:T(1,128)S(1)}, u32[]{:S(2)}, u32[]{:S(2)}) async-start(f32[1,8,256]{2,0,1:T(1,128)} %copy.27), calls=%async_computation.1 | async-start | bytes 16384 | tf_op jit(solution)/shard_map/all_to_all | solution.py:68
Sparse Core Ops, SparseCore 0:
  56.4 19.0 all-reduce.2
where the time goes:
time: 149 us
  waiting for transfers between devices  48.7 us (33%)
  starting transfers between devices  31.8 us (21%)
  local copies, waits for them, and re-layouts  25.8 us (17%)
  other arithmetic  16 us (11%)
  between operations  14.6 us (10%)
  blocking collectives  7.41 us (5%)
  matrix products  4.17 us (3%)
    psum x1, waiting for transfers between devices, ocean_adjoint(): heat_sens = wet * lax.psum(partial_heat, 'lev')  19.2 us
    ppermute x6, waiting for transfers between devices, extended(): lax.ppermute(lax.slice_in_dim(block, 0, width, axis=dim), axis, backward)  16.5 us
    ppermute x6, starting transfers between devices, extended(): lax.ppermute(lax.slice_in_dim(block, block.shape[dim] - width, None, axis...  16 us
    gather x1, local copies, waits for them, and re-layouts, per_device(): surface_lookup = surface.reshape(-1)[ocean_index]  11.8 us
    gather x2, local copies, waits for them, and re-layouts, ocean_adjoint(): return (adjoint, weight_rows * heat_sens.reshape(-1)[ocean_index])  11.8 us
    scatter-add x1, other arithmetic, per_device(): jax.ops.segment_sum(returned.reshape(-1), ocean_index.reshape(-1), num_se...  11.3 us
    ppermute x6, starting transfers between devices, extended(): lax.ppermute(lax.slice_in_dim(block, 0, width, axis=dim), axis, backward)  7.75 us
    psum x1, blocking collectives, per_device(): surface_gradient = lax.psum(partial_slots, 'lev')  7.41 us
  transfers between devices with their start and end apart: 15, of which 12 were waited for; matrix products, arithmetic and copies ran while one was open for 2% of the time, Pallas kernels for 0%

commit v1 on v0

v1 whole, which is shorter than its diff:
```python
import functools

import jax
import jax.numpy as jnp
from jax import lax
from jax.experimental import pallas as pl
from jax.experimental.pallas import tpu as pltpu
from jax.sharding import PartitionSpec as P

BULK_ITERS = 3
STEPS = 3
HALO = STEPS
MIXING = 0.2
TRANSFER = 1.0
STABILITY = 0.5
F32 = jnp.float32
BF16 = jnp.bfloat16
VMEM = pl.BlockSpec(memory_space=pltpu.VMEM)
SMEM = pl.BlockSpec(memory_space=pltpu.SMEM)


def halves(x):
    high = x.astype(BF16)
    low = (x - high.astype(F32)).astype(BF16)
    return high, low


def call(kernel, out_shapes, operands, specs=None, scratch=()):
    return pl.pallas_call(
        kernel,
        out_shape=[jax.ShapeDtypeStruct(s, F32) for s in out_shapes],
        in_specs=specs or [VMEM] * len(operands),
        out_specs=[VMEM] * len(out_shapes),
        scratch_shapes=list(scratch),
        compiler_params=pltpu.CompilerParams(vmem_limit_bytes=24 * 1024 * 1024),
    )(*operands)


def pack_kernel(n, warm, cot, sea, sky, breeze, energy, shares, sky_index, sky_weight, msg, part):
    sub = lax.axis_index("sub")
    rows, cols = sea.shape
    levels = warm.shape[0]
    wet = sea[...].astype(F32)
    surface = shares[0] * warm[0]
    heat = shares[0] * cot[0]
    for z in range(1, levels):
        surface += shares[z] * warm[z]
        heat += shares[z] * cot[z]
    part[0:rows, :] = surface
    part[rows : 2 * rows, :] = heat
    msg[...] = jnp.zeros_like(msg)
    msg[0 : 2 * n, :] = sky_index[...].astype(F32)
    msg[2 * n : 4 * n, :] = sky_weight[...]
    for i, ref in enumerate((sky, breeze, energy)):
        msg[4 * n + i : 4 * n + i + 1, :] = ref[...]

    def outer(x):
        return jnp.where(sub == 0, x[rows - HALO : rows], x[0:HALO])

    fields = [cot[z] for z in range(levels)] + [wet, heat]
    base = 4 * n + 8
    for i, x in enumerate(fields):
        top, left = base + HALO * (i // 2), cols * (i % 2)
        msg[top : top + HALO, left : left + cols] = outer(x)


def halo_rows(n, msg, i, cols):
    top, left = 4 * n + 8 + HALO * (i // 2), cols * (i % 2)
    return msg[top : top + HALO, left : left + cols]


def air_rows(n, msg, other, step, sub, tile):
    row = 2 * lax.rem(tile + step, n) + sub
    first = sub == 0

    def both(index):
        own, far = msg[pl.ds(index, 1), :], other[pl.ds(index, 1), :]
        return [jnp.where(first, own, far), jnp.where(first, far, own)]

    out = both(row) + both(2 * n + row)
    for i in range(3):
        out += both(4 * n + i)
    return out


def send_kernel(n, far_steps, msg, other, part, lev_out, *far_out):
    sub, tile = lax.axis_index("sub"), lax.axis_index("tile")
    full, cols = part.shape
    lev_out[0:full, :] = part[...]
    lev_out[full : full + 8, :] = jnp.zeros((8, cols), F32)
    lev_out[full : full + HALO, :] = halo_rows(n, other, 3, cols)
    for step, out in zip(far_steps, far_out):
        out[...] = jnp.zeros_like(out)
        for i, row in enumerate(air_rows(n, msg, other, step, sub, tile)):
            out[i : i + 1, :] = row


def edge_place(shape):
    lane = lax.broadcasted_iota(jnp.int32, shape, 1)
    return lax.rem(lane + HALO, shape[1])


def edge_kernel(n, count, *refs):
    lev_parts = refs[:count]
    cot, sea, msg, other, surface_out, ext, right_out, left_out = refs[count:]
    sub, tile = lax.axis_index("sub"), lax.axis_index("tile")
    rows, cols = sea.shape
    levels = cot.shape[0]
    high = rows + 8
    surface_out[...] = sum(ref[0:rows, :] for ref in lev_parts)
    ext[...] = jnp.zeros_like(ext)
    centers = [cot[z] for z in range(levels)] + [sea[...].astype(F32)]
    centers.append(sum(ref[rows : 2 * rows, :] for ref in lev_parts))
    strips = [halo_rows(n, other, i, cols) for i in range(levels + 1)]
    strips.append(sum(ref[2 * rows : 2 * rows + HALO, :] for ref in lev_parts))
    place = edge_place((high, cols))
    edges = jnp.zeros((high, cols), F32)
    for i, (center, strip) in enumerate(zip(centers, strips)):
        base = high * i
        ext[base : base + rows, :] = center
        ext[base + rows : base + rows + HALO, :] = jnp.where(sub == 0, strip, 0.0)
        ext[base + high - HALO : base + high, :] = jnp.where(sub == 0, 0.0, strip)
        field = ext[base : base + high, :]
        moved = pltpu.roll(field, 2 * HALO * i, 1) if i else field
        edges = jnp.where(place // (2 * HALO) == i, moved, edges)
    for step, out in ((1, right_out), (n - 1, left_out)):
        out[0:high, :] = edges
        out[high : out.shape[0], :] = jnp.zeros((out.shape[0] - high, cols), F32)
        for i, row in enumerate(air_rows(n, msg, other, step, sub, tile)):
            out[high + i : high + i + 1, :] = row[:, :cols]
            out[high + 10 + i : high + 11 + i, :] = row[:, cols:]


def diffused(n, ext, from_right, from_left, fields, wet_field, high, tile):
    cols = ext.shape[1]
    place = edge_place((high, cols))
    right = jnp.where(tile < n - 1, from_right[0:high, :], 0.0)
    left = jnp.where(tile > 0, from_left[0:high, :], 0.0)
    edges = jnp.where(lax.rem(place, 2 * HALO) >= HALO, right, left)

    def wide(i):
        moved = pltpu.roll(edges, cols - 2 * HALO * i, 1) if i else edges
        return jnp.concatenate(
            [ext[high * i : high * (i + 1), :], jnp.where(place < 2 * HALO, moved, 0.0)], axis=1
        )

    def around(x):
        return (
            pltpu.roll(x, 1, 0)
            + pltpu.roll(x, high - 1, 0)
            + pltpu.roll(x, 1, 1)
            + pltpu.roll(x, 2 * cols - 1, 1)
        )

    wet = wide(wet_field)
    keep = wet * (1.0 - MIXING * around(wet))
    mix = MIXING * wet
    out = []
    for i in fields:
        v = wet * wide(i)
        for sweep_index in range(STEPS):
            v = keep * v + mix * around(v)
        out.append(v[: high - 8, :cols])
    return wet[: high - 8, :cols], out


def bulk_adjoint(warmth_gap, flux_sens):
    transfer_rate = jnp.full_like(warmth_gap, TRANSFER)
    rates = [transfer_rate]
    slopes = []
    for sweep_index in range(BULK_ITERS):
        bent = jnp.tanh(transfer_rate * warmth_gap)
        slopes.append(TRANSFER * STABILITY * (1.0 - bent * bent))
        transfer_rate = TRANSFER * (1.0 + STABILITY * bent)
        rates.append(transfer_rate)
    contrast_sens = transfer_rate * flux_sens
    rate_sens = warmth_gap * flux_sens
    for sweep_index in reversed(range(BULK_ITERS)):
        inner_sens = rate_sens * slopes[sweep_index]
        contrast_sens = contrast_sens + inner_sens * rates[sweep_index]
        rate_sens = inner_sens * warmth_gap
    return contrast_sens


def onehot(index, count):
    cells = lax.broadcasted_iota(jnp.int32, (count, index.shape[1]), 0)
    return jnp.where(cells == index, 1.0, 0.0).astype(BF16)


def dot(a, b, ca, cb):
    return lax.dot_general(a, b, (((ca,), (cb,)), ((), ())), preferred_element_type=F32)


def slot_kernel(n, far_steps, *refs):
    surface, ext, msg, other, marine, weight, from_right, from_left = refs[:8]
    far_in = dict(zip(far_steps, refs[8 : 8 + len(far_steps)]))
    slots_out = refs[8 + len(far_steps)]
    returns = refs[9 + len(far_steps) : 9 + len(far_steps) + n]
    picks = refs[9 + len(far_steps) + n]
    sub, tile = lax.axis_index("sub"), lax.axis_index("tile")
    rows, cols = surface.shape
    high = rows + 8
    fields = ext.shape[0] // high
    wet, (heat,) = diffused(n, ext, from_right, from_left, [fields - 1], fields - 2, high, tile)
    heat = wet * heat
    table = jnp.concatenate([surface[...], heat], axis=1)
    table = jnp.concatenate(halves(table), axis=0)

    def air_in(step):
        if step == 0:
            return air_rows(n, msg, other, 0, sub, tile)
        if step in far_in:
            return [far_in[step][i : i + 1, :] for i in range(10)]
        ref = from_right if step == 1 else from_left
        return [
            jnp.concatenate(
                [ref[high + i : high + i + 1, :], ref[high + 10 + i : high + 11 + i, :]], axis=1
            )
            for i in range(10)
        ]

    owners = []
    tables = []
    for step in range(n):
        source = lax.rem(tile + step, n)
        air = air_in(step)
        for band in range(2):
            at = 2 * step + band
            cell = marine[pl.ds(2 * source + band, 1), :]
            row, col = cell // cols, lax.rem(cell, cols)
            row_hot = onehot(row, rows)
            spread = dot(table, jnp.concatenate([row_hot, row_hot], axis=0), 0, 0)
            col_mask = lax.broadcasted_iota(jnp.int32, (cols, cell.shape[1]), 0) == col
            for i in range(2):
                piece = jnp.where(col_mask, spread[cols * i : cols * (i + 1)], 0.0)
                picks[i, at : at + 1, :] = jnp.sum(piece, axis=0, keepdims=True)
            sky_hot = onehot(air[band].astype(jnp.int32), air[band].shape[1])
            values = jnp.concatenate([air[4 + band], air[6 + band], air[8 + band]], axis=0)
            found = dot(jnp.concatenate(halves(values), axis=0), sky_hot, 1, 0)
            for i in range(3):
                picks[2 + i, at : at + 1, :] = found[i : i + 1] + found[3 + i : 4 + i]
            picks[5, at : at + 1, :] = air[2 + band]
            picks[6, at : at + 1, :] = weight[pl.ds(2 * source + band, 1), :]
            owners.append((row_hot, col_mask))
            tables.append(sky_hot)

    difference = picks[0] - picks[2]
    wind = picks[3]
    flux_sens = picks[6] * picks[1] + picks[5] * picks[4]
    contrast_sens = bulk_adjoint(wind * difference, flux_sens)
    surface_sens = contrast_sens * wind
    wind_sens = contrast_sens * difference
    total = jnp.zeros((rows, 2 * cols), F32)
    for step in range(n):
        for band in range(2):
            at = 2 * step + band
            row_hot, col_mask = owners[at]
            ocean = surface_sens[at : at + 1]
            spread = jnp.concatenate(
                [jnp.where(col_mask, x.astype(F32), 0.0).astype(BF16) for x in halves(ocean)], axis=0
            )
            total += dot(row_hot, spread, 1, 1)
            values = jnp.concatenate([ocean, wind_sens[at : at + 1]], axis=0)
            sums = dot(jnp.concatenate(halves(values), axis=0), tables[at], 1, 1)
            returns[step][2 * band : 2 * band + 2, :] = sums[0:2] + sums[2:4]
        returns[step][4:8, :] = jnp.zeros((4, returns[step].shape[1]), F32)
    slots_out[...] = total[:, :cols] + total[:, cols:]


def adjoint_kernel(n, ext, from_right, from_left, out):
    tile = lax.axis_index("tile")
    levels = out.shape[0]
    high = out.shape[1] + 8
    wet, adjoint = diffused(
        n, ext, from_right, from_left, list(range(levels)), levels, high, tile
    )
    for z in range(levels):
        out[z] = wet * adjoint[z]


def final_kernel(count, *refs):
    slots = refs[:count]
    adjoint, shares, sums, other, state_out, air_out, wind_out = refs[count:]
    sub = lax.axis_index("sub")
    gradient = sum(ref[...] for ref in slots)
    for z in range(adjoint.shape[0]):
        state_out[z] = adjoint[z] + shares[z] * gradient
    both = sums[...] + other[...]
    own = jnp.where(sub == 0, both[0:2], both[2:4])
    air_out[...] = -own[0:1]
    wind_out[...] = own[1:2]


def shifted(x, axis, step):
    count = lax.axis_size(axis)
    return lax.ppermute(x, axis, [(i, (i + step) % count) for i in range(count)])


def lev_parts(x):
    if lax.axis_size("lev") == 2:
        return [x, shifted(x, "lev", 1)]
    return [lax.psum(x, "lev")]


def per_device(
    marine_layered_warmth,
    bottom_sky_warmth,
    bottom_breeze_magnitude,
    depth_shares,
    piece_sky_box,
    sky_share_fraction,
    piece_marine_box,
    marine_share_fraction,
    marine_indicator,
    marine_result_adjoint,
    energy_transport_adjoint,
):
    n = lax.axis_size("tile")
    levels, rows, cols = marine_layered_warmth.shape
    cells = bottom_sky_warmth.shape[0]
    air = [
        x.reshape(1, cells)
        for x in (bottom_sky_warmth, bottom_breeze_magnitude, energy_transport_adjoint)
    ]
    high = rows + 8
    far_steps = list(range(2, n - 1))
    msg, part = call(
        functools.partial(pack_kernel, n),
        [(4 * n + 16, cells), (2 * rows, cols)],
        [marine_layered_warmth, marine_result_adjoint, marine_indicator, *air, depth_shares]
        + [piece_sky_box[0], sky_share_fraction[0]],
        [VMEM] * 6 + [SMEM] + [VMEM] * 2,
    )
    other = shifted(msg, "sub", 1)
    lev_msg, *far_out = call(
        functools.partial(send_kernel, n, far_steps),
        [(2 * rows + 8, cols)] + [(16, cells)] * len(far_steps),
        [msg, other, part],
    )
    lev_in = lev_parts(lev_msg)
    far_in = [shifted(x, "tile", step) for step, x in zip(far_steps, far_out)]
    far_in = far_in[::-1]
    surface, ext, right_out, left_out = call(
        functools.partial(edge_kernel, n, len(lev_in)),
        [(rows, cols), ((levels + 2) * high, cols)] + [(high + 24, cols)] * 2,
        [*lev_in, marine_result_adjoint, marine_indicator, msg, other],
    )
    from_left = shifted(right_out, "tile", 1)
    from_right = shifted(left_out, "tile", n - 1)
    slots, *returns = call(
        functools.partial(slot_kernel, n, far_steps),
        [(rows, cols)] + [(8, cells)] * n,
        [surface, ext, msg, other, piece_marine_box[0], marine_share_fraction[0]]
        + [from_right, from_left, *far_in],
        scratch=[pltpu.VMEM((7, 2 * n, cells), F32)],
    )
    back = [shifted(returns[step], "tile", step) for step in range(1, n)]
    slot_parts = lev_parts(slots)
    (adjoint,) = call(
        functools.partial(adjoint_kernel, n),
        [(levels, rows, cols)],
        [ext, from_right, from_left],
    )
    sums = returns[0]
    for x in back:
        sums = sums + x
    sums_far = shifted(sums, "sub", 1)
    state, air_gradient, wind_gradient = call(
        functools.partial(final_kernel, len(slot_parts)),
        [(levels, rows, cols), (1, cells), (1, cells)],
        [*slot_parts, adjoint, depth_shares, sums, sums_far],
        [VMEM] * (len(slot_parts) + 1) + [SMEM] + [VMEM] * 2,
    )
    return (state, air_gradient.reshape(cells), wind_gradient.reshape(cells))


def solution(mesh):
    return jax.shard_map(
        per_device,
        mesh=mesh,
        in_specs=(
            P(("ens", "lev"), "sub", "tile"),
            P(("ens", "tile", "lev", "sub")),
            P(("ens", "tile", "lev", "sub")),
            P("lev"),
            P(("tile", "lev", "sub"), None, None),
            P(("tile", "lev", "sub"), None, None),
            P(("tile", "lev", "sub"), None, None),
            P(("tile", "lev", "sub"), None, None),
            P("sub", "tile"),
            P(("ens", "lev"), "sub", "tile"),
            P(("ens", "tile", "lev", "sub")),
        ),
        out_specs=(
            P(("ens", "lev"), "sub", "tile"),
            P(("ens", "tile", "lev", "sub")),
            P(("ens", "tile", "lev", "sub")),
        ),
        check_vma=False,
    )
```

time: 149 us -> 35.5 us (0.24)
  waiting for transfers between devices: 48.7 us -> 10.4 us
  local copies, waits for them, and re-layouts: 25.8 us -> 5.87 us
  starting transfers between devices: 31.8 us -> 13.8 us
  other arithmetic: 16 us -> 0.01 us
  between operations: 14.6 us -> 0.71 us
  blocking collectives: 7.41 us -> 0 us
  Pallas kernels: 0 us -> 4.32 us
  matrix products: 4.17 us -> 0 us
    gather x3 -> x0, local copies, waits for them, and re-layouts: 23.6 us -> none  [the longest x1 11.8 us: per_device(): surface_lookup = surface.reshape(-1)[ocean_index]]
    psum x1 -> x0, waiting for transfers between devices: 19.2 us -> none  [ocean_adjoint(): heat_sens = wet * lax.psum(partial_heat, 'lev')]
    scatter-add x1 -> x0, other arithmetic: 11.3 us -> none  [per_device(): jax.ops.segment_sum(returned.reshape(-1), ocean_index.reshape(-1), num_se...]
    all_to_all x2 -> x0, waiting for transfers between devices: 10.5 us -> none  [the longest x1 5.5 us: ocean_to_air(): lax.all_to_all(blocks, ('tile', 'sub'), split_axis=1, concat_axis=1, tile...]
    ppermute x12 -> x10, starting transfers between devices: 23.8 us -> 13.8 us  [shifted(): lax.ppermute(x, axis, [(i, (i + step) % count) for i in range(count)])]
    ppermute x12 -> x10, waiting for transfers between devices: 19 us -> 10.4 us  [shifted(): lax.ppermute(x, axis, [(i, (i + step) % count) for i in range(count)])]
    all_to_all x2 -> x0, starting transfers between devices: 7.95 us -> none  [the longest x1 4.61 us: ocean_to_air(): lax.all_to_all(blocks, ('tile', 'sub'), split_axis=1, concat_axis=1, tile...]
    psum x1 -> x0, blocking collectives: 7.41 us -> none  [per_device(): surface_gradient = lax.psum(partial_slots, 'lev')]
  transfers between devices with their start and end apart: 15 -> 10, of which waited for: 12 -> 7; matrix products, arithmetic and copies ran while one was open for 2% -> 0% of each run, Pallas kernels for 0% -> 2%
where the time goes in v1:
time: 35.5 us; the launch traced here: 35 us
  starting transfers between devices  13.8 us (39%)
  waiting for transfers between devices  10.4 us (29%)
  local copies, waits for them, and re-layouts  5.87 us (17%)
  Pallas kernels  4.32 us (12%)
  between operations  0.71 us (2%)
    ppermute x10, starting transfers between devices, shifted(): lax.ppermute(x, axis, [(i, (i + step) % count) for i in range(count)])  13.8 us
    ppermute x10, waiting for transfers between devices, shifted(): lax.ppermute(x, axis, [(i, (i + step) % count) for i in range(count)])  10.4 us
    unnamed x26, local copies, waits for them, and re-layouts  5.87 us
    pallas_call x6, Pallas kernels, call(): pl.pallas_call(kernel, out_shape=[jax.ShapeDtypeStruct(s, F32) for s in o...  4.32 us
  transfers between devices with their start and end apart: 10, of which 7 were waited for; matrix products, arithmetic and copies ran while one was open for 0% of the time, Pallas kernels for 2%

profile of v1, /device:TPU:0, one launch (start us, length us, event | category | flops | bytes accessed | tf_op | source)
XLA Modules:
  0.0 35.0 jit_solution(17638974193859116836)
XLA Ops:
  0.6 0.0 copy-start.5
  0.6 0.0 copy-start.9
  0.7 0.7 %copy-done.5 = s32[1,8,256]{2,1,0:T(8,128)S(1)} copy-done((s32[1,8,256]{2,1,0:T(8,128)S(1)}, s32[1,8,256]{2,1,0:T(8,128)}, u32[]{:S(2)}) %copy-start.5) | copy-done | bytes 8216
  1.3 0.0 copy-done.9
  1.3 0.0 copy-start
  1.3 0.8 %copy-done = f32[2,64,128]{2,1,0:T(8,128)S(1)} copy-done((f32[2,64,128]{2,1,0:T(8,128)S(1)}, f32[2,64,128]{2,1,0:T(8,128)}, u32[]{:S(2)}) %copy-start) | copy-done | bytes 65560
  2.2 0.0 copy-start.2
  2.2 0.8 %copy-done.2 = s32[64,128]{1,0:T(8,128)S(1)} copy-done((s32[64,128]{1,0:T(8,128)S(1)}, s32[64,128]{1,0:T(8,128)}, u32[]{:S(2)}) %copy-start.2) | copy-done | bytes 32792
  2.9 0.0 copy-start.4
  2.9 0.8 %copy-done.4 = f32[2,64,128]{2,1,0:T(8,128)S(1)} copy-done((f32[2,64,128]{2,1,0:T(8,128)S(1)}, f32[2,64,128]{2,1,0:T(8,128)}, u32[]{:S(2)}) %copy-start.4) | copy-done | bytes 65560
  3.8 0.0 copy-start.6
  3.8 0.7 %copy-done.6 = f32[1,8,256]{2,1,0:T(8,128)S(1)} copy-done((f32[1,8,256]{2,1,0:T(8,128)S(1)}, f32[1,8,256]{2,1,0:T(8,128)}, u32[]{:S(2)}) %copy-start.6) | copy-done | bytes 8216
  4.5 0.0 copy-start.10
  4.5 0.7 %copy-done.10 = f32[256]{0:T(256)S(1)} copy-done((f32[256]{0:T(256)S(1)}, f32[256]{0:T(256)}, u32[]{:S(2)}) %copy-start.10) | copy-done | bytes 1048
  5.1 0.0 copy-start.11
  5.2 0.7 %copy-done.11 = f32[256]{0:T(256)S(1)} copy-done((f32[256]{0:T(256)S(1)}, f32[256]{0:T(256)}, u32[]{:S(2)}) %copy-start.11) | copy-done | bytes 1048
  5.8 0.0 copy-start.12
  5.8 0.7 %copy-done.12 = f32[256]{0:T(256)S(1)} copy-done((f32[256]{0:T(256)S(1)}, f32[256]{0:T(256)}, u32[]{:S(2)}) %copy-start.12) | copy-done | bytes 1048
  6.5 0.6 %shard_map.130 = (f32[32,256]{1,0:T(8,128)S(1)}, f32[128,128]{1,0:T(8,128)S(1)}) custom-call(f32[2,64,128]{2,1,0:T(8,128)S(1)} %copy-done.4, f32[2,64,128]{2,1,0:T(8,128)S(1)} %copy-done, s32[64,128]{1,0:T(8,128)S(1)} %copy-done.2, f32[1,256]{1,0:T(1,128)S(1)} %bitcast.13, f32[1,256]{1,0:T(1,128)S(1)} %bitcast.14, f32[1,256]{1,0:T(1,128)S(1)} %bitcast.15, ...), custom_call_target="tpu_custom_call" | custom-call | tf_op jit(solution)/shard_map/pallas_call | solution.py:29
  7.1 0.5 %collective-permute-start = (f32[32,256]{1,0:T(8,128)S(1)}, f32[32,256]{1,0:T(8,128)S(1)}, u32[]{:S(2)}, u32[]{:S(2)}) collective-permute-start(f32[32,256]{1,0:T(8,128)S(1)} %get-tuple-element.19.msg.refs_4_.refs_2_), channel_id=1, source_target_pairs={{0,1},{1,0},{2,3},{3,2},{4,5},{5,4},{6,7},{7,6},{8,9},{9,8},{10,11... | collective-permute-start | bytes 98312 | tf_op jit(solution)/shard_map/ppermute | solution.py:296
  7.6 0.9 %collective-permute-done.other.refs_5_.refs_3_ = f32[32,256]{1,0:T(8,128)S(1)} collective-permute-done((f32[32,256]{1,0:T(8,128)S(1)}, f32[32,256]{1,0:T(8,128)S(1)}, u32[]{:S(2)}, u32[]{:S(2)}) %collective-permute-start) | collective-permute-done | bytes 32800 | tf_op jit(solution)/shard_map/ppermute | solution.py:296
  8.4 0.0 copy-start.1
  8.5 0.0 copy-start.3
  8.5 2.9 %collective-permute-start.1 = (f32[136,128]{1,0:T(8,128)S(1)}, f32[136,128]{1,0:T(8,128)S(1)}, u32[]{:S(2)}, u32[]{:S(2)}) collective-permute-start(f32[136,128]{1,0:T(8,128)S(1)} %get-tuple-element.21.refs_0_), channel_id=1, source_target_pairs={{0,2},{2,0},{1,3},{3,1},{4,6},{6,4},{5,7},{7,5},{8,10},{10,8},{9,1... | collective-permute-start | bytes 208904 | tf_op jit(solution)/shard_map/ppermute | solution.py:296
  11.4 2.5 %collective-permute-done.1.refs_1_ = f32[136,128]{1,0:T(8,128)S(1)} collective-permute-done((f32[136,128]{1,0:T(8,128)S(1)}, f32[136,128]{1,0:T(8,128)S(1)}, u32[]{:S(2)}, u32[]{:S(2)}) %collective-permute-start.1) | collective-permute-done | bytes 69664 | tf_op jit(solution)/shard_map/ppermute | solution.py:296
  13.9 0.0 copy-done.1
  13.9 0.0 copy-done.3
  13.9 0.0 copy-start.8
  13.9 0.1 shard_map.132
  14.0 0.0 copy-start.7
  14.0 4.0 %collective-permute-start.2 = (f32[96,128]{1,0:T(8,128)S(1)}, f32[96,128]{1,0:T(8,128)S(1)}, u32[]{:S(2)}, u32[]{:S(2)}) collective-permute-start(f32[96,128]{1,0:T(8,128)S(1)} %get-tuple-element.24), channel_id=1, source_target_pairs={{0,12},{4,0},{8,4},{12,8},{1,13},{5,1},{9,5},{13,9},{2,14},{6,2},{... | collective-permute-start | bytes 147464 | tf_op jit(solution)/shard_map/ppermute | solution.py:296
  18.0 0.0 collective-permute-start.3
  18.0 1.0 %collective-permute-start.4 = (f32[16,256]{1,0:T(8,128)S(1)}, f32[16,256]{1,0:T(8,128)S(1)}, u32[]{:S(2)}, u32[]{:S(2)}) collective-permute-start(f32[16,256]{1,0:T(8,128)S(1)} %get-tuple-element.26), channel_id=1, source_target_pairs={{0,8},{4,12},{8,0},{12,4},{1,9},{5,13},{9,1},{13,5},{2,10},{6,14},... | collective-permute-start | bytes 49160 | tf_op jit(solution)/shard_map/ppermute | solution.py:296
  19.0 3.6 %collective-permute-done.4.refs_8_ = f32[16,256]{1,0:T(8,128)S(1)} collective-permute-done((f32[16,256]{1,0:T(8,128)S(1)}, f32[16,256]{1,0:T(8,128)S(1)}, u32[]{:S(2)}, u32[]{:S(2)}) %collective-permute-start.4) | collective-permute-done | bytes 16416 | tf_op jit(solution)/shard_map/ppermute | solution.py:296
  22.6 0.0 collective-permute-done.2.refs_6_.from_right
  22.6 1.2 %collective-permute-done.3.refs_7_.from_left = f32[96,128]{1,0:T(8,128)S(1)} collective-permute-done((f32[96,128]{1,0:T(8,128)S(1)}, f32[96,128]{1,0:T(8,128)S(1)}, u32[]{:S(2)}, u32[]{:S(2)}) %collective-permute-start.3) | collective-permute-done | bytes 49184 | tf_op jit(solution)/shard_map/ppermute | solution.py:296
  23.9 0.0 copy-done.8
  23.9 0.0 copy-done.7
  23.9 1.9 %shard_map.133 = (f32[64,128]{1,0:T(8,128)S(1)}, f32[8,256]{1,0:T(8,128)S(1)}, f32[8,256]{1,0:T(8,128)S(1)}, f32[8,256]{1,0:T(8,128)S(1)}, f32[8,256]{1,0:T(8,128)S(1)}) custom-call(f32[64,128]{1,0:T(8,128)S(1)} %get-tuple-element.22.refs_0_, f32[288,128]{1,0:T(8,128)S(1)} %get-tuple-element.23.refs_1_.ext, ...), custom_call_target="tpu_custom_call" | custom-call | tf_op jit(solution)/shard_map/pallas_call | solution.py:29
  25.8 0.8 %collective-permute-start.6 = (f32[8,256]{1,0:T(8,128)S(1)}, f32[8,256]{1,0:T(8,128)S(1)}, u32[]{:S(2)}, u32[]{:S(2)}) collective-permute-start(f32[8,256]{1,0:T(8,128)S(1)} %get-tuple-element.29), channel_id=1, source_target_pairs={{0,4},{4,8},{8,12},{12,0},{1,5},{5,9},{9,13},{13,1},{2,6},{6,10},{... | collective-permute-start | bytes 24584 | tf_op jit(solution)/shard_map/ppermute | solution.py:296
  26.6 2.4 %collective-permute-start.7 = (f32[8,256]{1,0:T(8,128)S(1)}, f32[8,256]{1,0:T(8,128)S(1)}, u32[]{:S(2)}, u32[]{:S(2)}) collective-permute-start(f32[8,256]{1,0:T(8,128)S(1)} %get-tuple-element.30), channel_id=1, source_target_pairs={{0,8},{4,12},{8,0},{12,4},{1,9},{5,13},{9,1},{13,5},{2,10},{6,14},... | collective-permute-start | bytes 24584 | tf_op jit(solution)/shard_map/ppermute | solution.py:296
  29.0 0.7 %collective-permute-start.8 = (f32[8,256]{1,0:T(8,128)S(1)}, f32[8,256]{1,0:T(8,128)S(1)}, u32[]{:S(2)}, u32[]{:S(2)}) collective-permute-start(f32[8,256]{1,0:T(8,128)S(1)} %get-tuple-element.31), channel_id=1, source_target_pairs={{0,12},{4,0},{8,4},{12,8},{1,13},{5,1},{9,5},{13,9},{2,14},{6,2},{... | collective-permute-start | bytes 24584 | tf_op jit(solution)/shard_map/ppermute | solution.py:296
  29.7 1.5 %collective-permute-start.5 = (f32[64,128]{1,0:T(8,128)S(1)}, f32[64,128]{1,0:T(8,128)S(1)}, u32[]{:S(2)}, u32[]{:S(2)}) collective-permute-start(f32[64,128]{1,0:T(8,128)S(1)} %get-tuple-element.27.refs_0_), channel_id=1, source_target_pairs={{0,2},{2,0},{1,3},{3,1},{4,6},{6,4},{5,7},{7,5},{8,10},{10,8},{9,1... | collective-permute-start | bytes 98312 | tf_op jit(solution)/shard_map/ppermute | solution.py:296
  31.2 0.1 collective-permute-done.6
  31.3 0.0 collective-permute-done.7
  31.3 1.4 %collective-permute-done.8 = f32[8,256]{1,0:T(8,128)S(1)} collective-permute-done((f32[8,256]{1,0:T(8,128)S(1)}, f32[8,256]{1,0:T(8,128)S(1)}, u32[]{:S(2)}, u32[]{:S(2)}) %collective-permute-start.8) | collective-permute-done | bytes 8224 | tf_op jit(solution)/shard_map/ppermute | solution.py:296
  32.7 0.0 collective-permute-start.9
  32.7 0.5 %shard_map.134.refs_2_ = f32[2,64,128]{2,1,0:T(8,128)S(1)} custom-call(f32[288,128]{1,0:T(8,128)S(1)} %get-tuple-element.23.refs_1_.ext, f32[96,128]{1,0:T(8,128)S(1)} %collective-permute-done.2.refs_6_.from_right, f32[96,128]{1,0:T(8,128)S(1)} %collective-permute-done.3.refs_7_.from_left), custom_call_target="tpu_custom_call" | custom-call | tf_op jit(solution)/shard_map/pallas_call | solution.py:29
  33.2 0.6 %collective-permute-done.9.refs_5_ = f32[8,256]{1,0:T(8,128)S(1)} collective-permute-done((f32[8,256]{1,0:T(8,128)S(1)}, f32[8,256]{1,0:T(8,128)S(1)}, u32[]{:S(2)}, u32[]{:S(2)}) %collective-permute-start.9) | collective-permute-done | bytes 8224 | tf_op jit(solution)/shard_map/ppermute | solution.py:296
  33.9 0.0 collective-permute-done.5.refs_1_
  33.9 1.2 %shard_map.135 = (f32[2,64,128]{2,1,0:T(8,128)}, f32[1,256]{1,0:T(1,128)}, f32[1,256]{1,0:T(1,128)}) custom-call(f32[64,128]{1,0:T(8,128)S(1)} %get-tuple-element.27.refs_0_, f32[64,128]{1,0:T(8,128)S(1)} %collective-permute-done.5.refs_1_, f32[2,64,128]{2,1,0:T(8,128)S(1)} %shard_map.134.refs_2_, f32[2]{0:T(128)S(1)} %copy-done.9, ...), custom_call_target="tpu_custom_call" | custom-call | tf_op jit(solution)/shard_map/pallas_call | solution.py:29
  (2 shorter events, 0.0 us)
Async XLA Ops:
  0.6 0.7 %copy-start.5 = (s32[1,8,256]{2,1,0:T(8,128)S(1)}, s32[1,8,256]{2,1,0:T(8,128)}, u32[]{:S(2)}) copy-start(s32[1,8,256]{2,1,0:T(8,128)} %param.15) | copy-start | bytes 24580
  0.6 0.7 %copy-start.9 = (f32[2]{0:T(128)S(1)}, f32[2]{0:T(128)}, u32[]{:S(2)}) copy-start(f32[2]{0:T(128)} %refs_3_.3) | copy-start | bytes 28
  1.3 0.8 %copy-start = (f32[2,64,128]{2,1,0:T(8,128)S(1)}, f32[2,64,128]{2,1,0:T(8,128)}, u32[]{:S(2)}) copy-start(f32[2,64,128]{2,1,0:T(8,128)} %refs_2_.1) | copy-start | bytes 196612
  2.2 0.8 %copy-start.2 = (s32[64,128]{1,0:T(8,128)S(1)}, s32[64,128]{1,0:T(8,128)}, u32[]{:S(2)}) copy-start(s32[64,128]{1,0:T(8,128)} %refs_3_.2) | copy-start | bytes 98308
  2.9 0.8 %copy-start.4 = (f32[2,64,128]{2,1,0:T(8,128)S(1)}, f32[2,64,128]{2,1,0:T(8,128)}, u32[]{:S(2)}) copy-start(f32[2,64,128]{2,1,0:T(8,128)} %warm.1) | copy-start | bytes 196612
  3.8 0.7 %copy-start.6 = (f32[1,8,256]{2,1,0:T(8,128)S(1)}, f32[1,8,256]{2,1,0:T(8,128)}, u32[]{:S(2)}) copy-start(f32[1,8,256]{2,1,0:T(8,128)} %param.16) | copy-start | bytes 24580
  4.5 0.7 %copy-start.10 = (f32[256]{0:T(256)S(1)}, f32[256]{0:T(256)}, u32[]{:S(2)}) copy-start(f32[256]{0:T(256)} %param.12) | copy-start | bytes 3076
  5.1 0.7 %copy-start.11 = (f32[256]{0:T(256)S(1)}, f32[256]{0:T(256)}, u32[]{:S(2)}) copy-start(f32[256]{0:T(256)} %param.13) | copy-start | bytes 3076
  5.8 0.7 %copy-start.12 = (f32[256]{0:T(256)S(1)}, f32[256]{0:T(256)}, u32[]{:S(2)}) copy-start(f32[256]{0:T(256)} %param.21) | copy-start | bytes 3076
  7.1 1.4 %collective-permute-start = (f32[32,256]{1,0:T(8,128)S(1)}, f32[32,256]{1,0:T(8,128)S(1)}, u32[]{:S(2)}, u32[]{:S(2)}) collective-permute-start(f32[32,256]{1,0:T(8,128)S(1)} %get-tuple-element.19.msg.refs_4_.refs_2_), channel_id=1, source_target_pairs={{0,1},{1,0},{2,3},{3,2},{4,5},{5,4},{6,7},{7,6},{8,9},{9,8},{10,11... | collective-permute-start | bytes 98312 | tf_op jit(solution)/shard_map/ppermute | solution.py:296
  8.4 5.4 %copy-start.1 = (f32[2,64,128]{2,1,0:T(8,128)S(1)}, f32[2,64,128]{2,1,0:T(8,128)}, u32[]{:S(2)}) copy-start(f32[2,64,128]{2,1,0:T(8,128)} %refs_2_.1) | copy-start | bytes 196612
  8.5 5.4 %copy-start.3 = (s32[64,128]{1,0:T(8,128)S(1)}, s32[64,128]{1,0:T(8,128)}, u32[]{:S(2)}) copy-start(s32[64,128]{1,0:T(8,128)} %refs_3_.2) | copy-start | bytes 98308
  8.5 5.4 %collective-permute-start.1 = (f32[136,128]{1,0:T(8,128)S(1)}, f32[136,128]{1,0:T(8,128)S(1)}, u32[]{:S(2)}, u32[]{:S(2)}) collective-permute-start(f32[136,128]{1,0:T(8,128)S(1)} %get-tuple-element.21.refs_0_), channel_id=1, source_target_pairs={{0,2},{2,0},{1,3},{3,1},{4,6},{6,4},{5,7},{7,5},{8,10},{10,8},{9,1... | collective-permute-start | bytes 208904 | tf_op jit(solution)/shard_map/ppermute | solution.py:296
  13.9 10.0 %copy-start.8 = (f32[1,8,256]{2,1,0:T(8,128)S(1)}, f32[1,8,256]{2,1,0:T(8,128)}, u32[]{:S(2)}) copy-start(f32[1,8,256]{2,1,0:T(8,128)} %param.18) | copy-start | bytes 24580
  14.0 9.9 %copy-start.7 = (s32[1,8,256]{2,1,0:T(8,128)S(1)}, s32[1,8,256]{2,1,0:T(8,128)}, u32[]{:S(2)}) copy-start(s32[1,8,256]{2,1,0:T(8,128)} %param.17) | copy-start | bytes 24580
  14.0 8.6 %collective-permute-start.2 = (f32[96,128]{1,0:T(8,128)S(1)}, f32[96,128]{1,0:T(8,128)S(1)}, u32[]{:S(2)}, u32[]{:S(2)}) collective-permute-start(f32[96,128]{1,0:T(8,128)S(1)} %get-tuple-element.24), channel_id=1, source_target_pairs={{0,12},{4,0},{8,4},{12,8},{1,13},{5,1},{9,5},{13,9},{2,14},{6,2},{... | collective-permute-start | bytes 147464 | tf_op jit(solution)/shard_map/ppermute | solution.py:296
  18.0 5.9 %collective-permute-start.3 = (f32[96,128]{1,0:T(8,128)S(1)}, f32[96,128]{1,0:T(8,128)S(1)}, u32[]{:S(2)}, u32[]{:S(2)}) collective-permute-start(f32[96,128]{1,0:T(8,128)S(1)} %get-tuple-element.25), channel_id=1, source_target_pairs={{0,4},{4,8},{8,12},{12,0},{1,5},{5,9},{9,13},{13,1},{2,6},{6,10},{... | collective-permute-start | bytes 147464 | tf_op jit(solution)/shard_map/ppermute | solution.py:296
  18.0 4.6 %collective-permute-start.4 = (f32[16,256]{1,0:T(8,128)S(1)}, f32[16,256]{1,0:T(8,128)S(1)}, u32[]{:S(2)}, u32[]{:S(2)}) collective-permute-start(f32[16,256]{1,0:T(8,128)S(1)} %get-tuple-element.26), channel_id=1, source_target_pairs={{0,8},{4,12},{8,0},{12,4},{1,9},{5,13},{9,1},{13,5},{2,10},{6,14},... | collective-permute-start | bytes 49160 | tf_op jit(solution)/shard_map/ppermute | solution.py:296
  25.8 5.5 %collective-permute-start.6 = (f32[8,256]{1,0:T(8,128)S(1)}, f32[8,256]{1,0:T(8,128)S(1)}, u32[]{:S(2)}, u32[]{:S(2)}) collective-permute-start(f32[8,256]{1,0:T(8,128)S(1)} %get-tuple-element.29), channel_id=1, source_target_pairs={{0,4},{4,8},{8,12},{12,0},{1,5},{5,9},{9,13},{13,1},{2,6},{6,10},{... | collective-permute-start | bytes 24584 | tf_op jit(solution)/shard_map/ppermute | solution.py:296
  26.6 4.7 %collective-permute-start.7 = (f32[8,256]{1,0:T(8,128)S(1)}, f32[8,256]{1,0:T(8,128)S(1)}, u32[]{:S(2)}, u32[]{:S(2)}) collective-permute-start(f32[8,256]{1,0:T(8,128)S(1)} %get-tuple-element.30), channel_id=1, source_target_pairs={{0,8},{4,12},{8,0},{12,4},{1,9},{5,13},{9,1},{13,5},{2,10},{6,14},... | collective-permute-start | bytes 24584 | tf_op jit(solution)/shard_map/ppermute | solution.py:296
  29.0 3.7 %collective-permute-start.8 = (f32[8,256]{1,0:T(8,128)S(1)}, f32[8,256]{1,0:T(8,128)S(1)}, u32[]{:S(2)}, u32[]{:S(2)}) collective-permute-start(f32[8,256]{1,0:T(8,128)S(1)} %get-tuple-element.31), channel_id=1, source_target_pairs={{0,12},{4,0},{8,4},{12,8},{1,13},{5,1},{9,5},{13,9},{2,14},{6,2},{... | collective-permute-start | bytes 24584 | tf_op jit(solution)/shard_map/ppermute | solution.py:296
  29.7 4.2 %collective-permute-start.5 = (f32[64,128]{1,0:T(8,128)S(1)}, f32[64,128]{1,0:T(8,128)S(1)}, u32[]{:S(2)}, u32[]{:S(2)}) collective-permute-start(f32[64,128]{1,0:T(8,128)S(1)} %get-tuple-element.27.refs_0_), channel_id=1, source_target_pairs={{0,2},{2,0},{1,3},{3,1},{4,6},{6,4},{5,7},{7,5},{8,10},{10,8},{9,1... | collective-permute-start | bytes 98312 | tf_op jit(solution)/shard_map/ppermute | solution.py:296
  32.7 1.2 %collective-permute-start.9 = (f32[8,256]{1,0:T(8,128)S(1)}, f32[8,256]{1,0:T(8,128)S(1)}, u32[]{:S(2)}, u32[]{:S(2)}) collective-permute-start(f32[8,256]{1,0:T(8,128)S(1)} %add_add_fusion.refs_4_), channel_id=1, source_target_pairs={{0,1},{1,0},{2,3},{3,2},{4,5},{5,4},{6,7},{7,6},{8,9},{9,8},{10,11... | collective-permute-start | bytes 24584 | tf_op jit(solution)/shard_map/ppermute | solution.py:296

commit v2 on v1

v2 whole, which is shorter than its diff:
```python
import functools

import jax
import jax.numpy as jnp
from jax import lax
from jax.experimental import pallas as pl
from jax.experimental.pallas import tpu as pltpu
from jax.sharding import PartitionSpec as P

BULK_ITERS = 3
STEPS = 3
HALO = STEPS
MIXING = 0.2
TRANSFER = 1.0
STABILITY = 0.5
F32 = jnp.float32
BF16 = jnp.bfloat16
VMEM = pl.BlockSpec(memory_space=pltpu.VMEM)
HBM = pl.BlockSpec(memory_space=pltpu.HBM)


def call(kernel, outs, operands, specs=None, out_specs=None, scratch=(), aliases=None):
    outs = [jax.ShapeDtypeStruct(x, F32) if isinstance(x, tuple) else x for x in outs]
    return pl.pallas_call(
        kernel,
        out_shape=outs,
        in_specs=specs or [VMEM] * len(operands),
        out_specs=out_specs or [VMEM] * len(outs),
        scratch_shapes=list(scratch),
        input_output_aliases=aliases or {},
        compiler_params=pltpu.CompilerParams(vmem_limit_bytes=24 * 1024 * 1024),
    )(*operands)


def halves(x):
    high = x.astype(BF16)
    low = (x - high.astype(F32)).astype(BF16)
    return high, low


def pack_kernel(n, *refs):
    warm, cot, sea, shares, sky, breeze, energy, sky_index, sky_weight = refs[:9]
    msg, ext, surface, share_rows = refs[9:13]
    warm_in, sea_in, shares_in, sky_in, breeze_in, energy_in, index_in, weight_in, sems = refs[13:]
    rows, cols = sea.shape
    levels = warm.shape[0]
    high = rows + 8
    pairs = [(cot.at[z], ext.at[pl.ds(high * z, rows)]) for z in range(levels)]
    pairs += [(sea, sea_in), (sky_index, index_in), (sky_weight, weight_in)]
    pairs += [(sky, sky_in), (breeze, breeze_in), (energy, energy_in)]
    pairs += [(shares, shares_in), (warm, warm_in)]
    copies = [pltpu.make_async_copy(a, b, sems.at[i]) for i, (a, b) in enumerate(pairs)]
    for copy in copies:
        copy.start()
    sub = lax.axis_index("sub")
    msg[...] = jnp.zeros_like(msg)
    for z in range(levels + 1):
        ext[high * z + rows : high * (z + 1), :] = jnp.zeros((8, cols), F32)
    for copy in copies:
        copy.wait()
    ext[high * levels : high * levels + rows, :] = sea_in[...].astype(F32)
    msg[0 : 2 * n, :] = index_in[...].astype(F32)
    msg[2 * n : 4 * n, :] = weight_in[...]
    for i, ref in enumerate((sky_in, breeze_in, energy_in)):
        msg[4 * n + i : 4 * n + i + 1, :] = ref[...]
    base = 4 * n + 8
    for i in range(levels + 1):
        at, top, left = high * i, base + HALO * (i // 2), cols * (i % 2)
        outer = jnp.where(sub == 0, ext[at + rows - HALO : at + rows], ext[at : at + HALO])
        msg[top : top + HALO, left : left + cols] = outer
    surface[...] = sum(shares_in[z] * warm_in[z] for z in range(levels))
    for z in range(levels):
        share_rows[z : z + 1, :] = jnp.full((1, cols), shares_in[z], F32)


def halo_rows(n, msg, i, cols):
    top, left = 4 * n + 8 + HALO * (i // 2), cols * (i % 2)
    return msg[top : top + HALO, left : left + cols]


def both_bands(msg, other, index, sub):
    own, far = msg[pl.ds(index, 1), :], other[pl.ds(index, 1), :]
    return [jnp.where(sub == 0, own, far), jnp.where(sub == 0, far, own)]


def air_rows(n, msg, other, target, band, sub):
    row = 2 * target + band
    places = [row, 2 * n + row] + [4 * n + i for i in range(3)]
    return [x for place in places for x in both_bands(msg, other, place, sub)]


def edge_place(shape):
    lane = lax.broadcasted_iota(jnp.int32, shape, 1)
    return lax.rem(lane + HALO, shape[1])


def send_kernel(n, fields, edge_steps, swap_steps, msg, other, ext_in, ext, *outs):
    sub, tile = lax.axis_index("sub"), lax.axis_index("tile")
    cols = ext.shape[1]
    high = ext.shape[0] // fields
    rows = high - 8
    place = edge_place((high, cols))
    edges = jnp.zeros((high, cols), F32)
    for i in range(fields):
        base = high * i
        strip = halo_rows(n, other, i, cols)
        ext[base : base + rows, :] = ext_in[base : base + rows, :]
        ext[base + rows : base + high, :] = jnp.zeros((8, cols), F32)
        ext[base + rows : base + rows + HALO, :] = jnp.where(sub == 0, strip, 0.0)
        ext[base + high - HALO : base + high, :] = jnp.where(sub == 0, 0.0, strip)
        field = ext[base : base + high, :]
        moved = pltpu.roll(field, 2 * HALO * i, 1) if i else field
        edges = jnp.where(place // (2 * HALO) == i, moved, edges)
    edge_outs, swap_outs = outs[: len(edge_steps)], outs[len(edge_steps) :]
    for step, out in zip(edge_steps, edge_outs):
        out[0:high, :] = edges
        if step:
            for i, row in enumerate(air_rows(n, msg, other, tile ^ step, sub, sub)):
                out[high + i : high + i + 1, :] = row[:, :cols]
                out[high + 10 + i : high + 11 + i, :] = row[:, cols:]
            out[high + 20 : high + 24, :] = jnp.zeros((4, cols), F32)
    for step, out in zip(swap_steps, swap_outs):
        for i, row in enumerate(air_rows(n, msg, other, tile ^ step, 1 - sub, sub)):
            out[i : i + 1, :] = row
        out[10:16, :] = jnp.zeros((6, out.shape[1]), F32)


def diffuse_kernel(n, levels, ext, near_in, edge_in, surface, share_rows, adjoint_out, lev_out):
    tile = lax.axis_index("tile")
    rows, cols = surface.shape
    high = rows + 8
    place = edge_place((high, cols))
    near, beyond = near_in[0:high, :], edge_in[0:high, :]
    even = tile % 2 == 0
    right = jnp.where(tile < n - 1, jnp.where(even, near, beyond), 0.0)
    left = jnp.where(tile > 0, jnp.where(even, beyond, near), 0.0)
    edges = jnp.where(lax.rem(place, 2 * HALO) >= HALO, right, left)

    def wide(i):
        moved = pltpu.roll(edges, cols - 2 * HALO * i, 1) if i else edges
        return jnp.concatenate(
            [ext[high * i : high * (i + 1), :], jnp.where(place < 2 * HALO, moved, 0.0)], axis=1
        )

    def around(x):
        return (
            pltpu.roll(x, 1, 0)
            + pltpu.roll(x, high - 1, 0)
            + pltpu.roll(x, 1, 1)
            + pltpu.roll(x, 2 * cols - 1, 1)
        )

    wet = wide(levels)
    keep = wet * (1.0 - MIXING * around(wet))
    mix = MIXING * wet
    own_wet = wet[:rows, :cols]
    heat = jnp.zeros((rows, cols), F32)
    for z in range(levels):
        v = wet * wide(z)
        for sweep_index in range(STEPS):
            v = keep * v + mix * around(v)
        adjoint = own_wet * v[:rows, :cols]
        adjoint_out[z] = adjoint
        heat += share_rows[z : z + 1, :] * adjoint
    lev_out[0:rows, :] = surface[...]
    lev_out[rows : 2 * rows, :] = own_wet * heat


def bulk_adjoint(warmth_gap, flux_sens):
    transfer_rate = jnp.full_like(warmth_gap, TRANSFER)
    rates = [transfer_rate]
    slopes = []
    for sweep_index in range(BULK_ITERS):
        bent = jnp.tanh(transfer_rate * warmth_gap)
        slopes.append(TRANSFER * STABILITY * (1.0 - bent * bent))
        transfer_rate = TRANSFER * (1.0 + STABILITY * bent)
        rates.append(transfer_rate)
    contrast_sens = transfer_rate * flux_sens
    rate_sens = warmth_gap * flux_sens
    for sweep_index in reversed(range(BULK_ITERS)):
        inner_sens = rate_sens * slopes[sweep_index]
        contrast_sens = contrast_sens + inner_sens * rates[sweep_index]
        rate_sens = inner_sens * warmth_gap
    return contrast_sens


def onehot(index, count):
    cells = lax.broadcasted_iota(jnp.int32, (count, index.shape[1]), 0)
    return jnp.where(cells == index, 1.0, 0.0).astype(BF16)


def dot(a, b, ca, cb):
    return lax.dot_general(a, b, (((ca,), (cb,)), ((), ())), preferred_element_type=F32)


def air_kernel(n, edge_steps, swap_steps, high, msg, other, *refs):
    sub, tile = lax.axis_index("sub"), lax.axis_index("tile")
    edge_in = dict(zip(edge_steps, refs))
    swap_in = dict(zip(swap_steps, refs[len(edge_steps) :]))
    picks, tables = refs[-2:]
    for step in range(n):
        if step == 0:
            air = air_rows(n, msg, other, tile, sub, sub)
        elif step in swap_in:
            air = [swap_in[step][i : i + 1, :] for i in range(10)]
        else:
            ref = edge_in[step]
            air = [
                jnp.concatenate(
                    [ref[high + i : high + i + 1, :], ref[high + 10 + i : high + 11 + i, :]], axis=1
                )
                for i in range(10)
            ]
        for band in range(2):
            at = 2 * step + band
            hot = onehot(air[band].astype(jnp.int32), air[band].shape[1])
            tables[at] = hot
            values = jnp.concatenate([air[4 + band], air[6 + band], air[8 + band]], axis=0)
            found = dot(jnp.concatenate(halves(values), axis=0), hot, 1, 0)
            found = found[0:3] + found[3:6]
            picks[0, at : at + 1, :] = found[0:1]
            picks[1, at : at + 1, :] = found[1:2]
            picks[2, at : at + 1, :] = air[2 + band] * found[2:3]


def slot_kernel(n, count, *refs):
    lev_parts = refs[:count]
    picks, tables, marine, weight, slots_out = refs[count : count + 5]
    returns, held = refs[count + 5 : count + 5 + n], refs[count + 5 + n]
    tile = lax.axis_index("tile")
    rows, cols = slots_out.shape
    table = jnp.concatenate(
        [sum(ref[rows * i : rows * (i + 1), :] for ref in lev_parts) for i in range(2)], axis=1
    )
    table = jnp.concatenate(halves(table), axis=0)
    owners = []
    for step in range(n):
        for band in range(2):
            at, place = 2 * step + band, 2 * (tile ^ step) + band
            cell = marine[pl.ds(place, 1), :]
            row, col = cell // cols, lax.rem(cell, cols)
            row_hot = onehot(row, rows)
            spread = dot(table, jnp.concatenate([row_hot, row_hot], axis=0), 0, 0)
            col_mask = lax.broadcasted_iota(jnp.int32, (cols, cell.shape[1]), 0) == col
            for i in range(2):
                piece = jnp.where(col_mask, spread[cols * i : cols * (i + 1)], 0.0)
                held[i, at : at + 1, :] = jnp.sum(piece, axis=0, keepdims=True)
            held[2, at : at + 1, :] = weight[pl.ds(place, 1), :]
            owners.append((row_hot, col_mask))

    difference = held[0] - picks[0]
    wind = picks[1]
    flux_sens = held[2] * held[1] + picks[2]
    contrast_sens = bulk_adjoint(wind * difference, flux_sens)
    surface_sens = contrast_sens * wind
    wind_sens = contrast_sens * difference
    total = jnp.zeros((rows, 2 * cols), F32)
    for step in range(n):
        for band in range(2):
            at = 2 * step + band
            row_hot, col_mask = owners[at]
            ocean = surface_sens[at : at + 1]
            spread = jnp.concatenate(
                [jnp.where(col_mask, x.astype(F32), 0.0).astype(BF16) for x in halves(ocean)], axis=0
            )
            total += dot(row_hot, spread, 1, 1)
            values = jnp.concatenate([ocean, wind_sens[at : at + 1]], axis=0)
            sums = dot(jnp.concatenate(halves(values), axis=0), tables[at], 1, 1)
            returns[step][2 * band : 2 * band + 2, :] = sums[0:2] + sums[2:4]
        returns[step][4:8, :] = jnp.zeros((4, returns[step].shape[1]), F32)
    slots_out[...] = total[:, :cols] + total[:, cols:]


def final_kernel(count, *refs):
    slots = refs[:count]
    adjoint, share_rows, sums, other, state_out, air_out, wind_out, state, air, wind, sems = refs[count:]
    sub = lax.axis_index("sub")
    gradient = sum(ref[...] for ref in slots)
    for z in range(adjoint.shape[0]):
        state[z] = adjoint[z] + share_rows[z : z + 1, :] * gradient
    copies = [pltpu.make_async_copy(state, state_out, sems.at[0])]
    copies[0].start()
    both = sums[...] + other[...]
    own = jnp.where(sub == 0, both[0:2], both[2:4])
    air[...] = -own[0:1]
    wind[...] = own[1:2]
    for i, (a, b) in enumerate(((air, air_out), (wind, wind_out))):
        copies.append(pltpu.make_async_copy(a, b, sems.at[1 + i]))
        copies[-1].start()
    for copy in copies:
        copy.wait()


def traded(x, step, swap=0):
    n, bands = lax.axis_size("tile"), lax.axis_size("sub")
    pairs = [
        (t * bands + s, (t ^ step) * bands + (s ^ swap)) for t in range(n) for s in range(bands)
    ]
    return lax.ppermute(x, ("tile", "sub"), pairs)


def lev_parts(x):
    if lax.axis_size("lev") == 2:
        return [x, lax.ppermute(x, "lev", [(0, 1), (1, 0)])]
    return [lax.psum(x, "lev")]


def per_device(
    marine_layered_warmth,
    bottom_sky_warmth,
    bottom_breeze_magnitude,
    depth_shares,
    piece_sky_box,
    sky_share_fraction,
    piece_marine_box,
    marine_share_fraction,
    marine_indicator,
    marine_result_adjoint,
    energy_transport_adjoint,
):
    n = lax.axis_size("tile")
    levels, rows, cols = marine_layered_warmth.shape
    cells = bottom_sky_warmth.shape[0]
    high = rows + 8
    if n == 4:
        edge_steps = [1, 3]
    else:
        edge_steps = [1, 0]
    swap_steps = [step for step in range(1, n) if step not in edge_steps]

    raw = [marine_layered_warmth, marine_result_adjoint, marine_indicator, depth_shares]
    raw += [
        x.reshape(1, cells)
        for x in (bottom_sky_warmth, bottom_breeze_magnitude, energy_transport_adjoint)
    ]
    raw += [piece_sky_box[0], sky_share_fraction[0]]
    raw = [pltpu.with_memory_space_constraint(x, pltpu.HBM) for x in raw]
    held = [pltpu.VMEM(x.shape, x.dtype) for x in [raw[0], raw[2]]]
    held += [pltpu.SMEM(depth_shares.shape, F32)]
    held += [pltpu.VMEM(x.shape, x.dtype) for x in raw[4:]]
    msg, ext, surface, share_rows = call(
        functools.partial(pack_kernel, n),
        [(4 * n + 16, cells), ((levels + 1) * high, cols), (rows, cols), (8, cols)],
        raw,
        [HBM] * len(raw),
        scratch=held + [pltpu.SemaphoreType.DMA((8 + levels,))],
    )
    other = traded(msg, 0, 1)
    ext, *sent = call(
        functools.partial(send_kernel, n, levels + 1, edge_steps, swap_steps),
        [ext.shape]
        + [(high + 24 if step else high, cols) for step in edge_steps]
        + [(16, cells)] * len(swap_steps),
        [msg, other, ext],
    )
    near_in = traded(sent[0], 1)
    if n == 4:
        edge_in = traded(sent[1], 3)
    else:
        pairs = [(i, (i + 1) % n) for i in range(1, n, 2)]
        edge_in = lax.ppermute(sent[1], "tile", pairs + [(b, a) for a, b in pairs])
    swapped = [traded(x, step, 1) for step, x in zip(swap_steps, sent[2:])]
    adjoint, lev_msg = call(
        functools.partial(diffuse_kernel, n, levels),
        [(levels, rows, cols), (2 * rows, cols)],
        [ext, near_in, edge_in, surface, share_rows],
    )
    lev_in = lev_parts(lev_msg)
    picks, tables = call(
        functools.partial(air_kernel, n, edge_steps, swap_steps, high),
        [(3, 2 * n, cells), jax.ShapeDtypeStruct((2 * n, cells, cells), BF16)],
        [msg, other, near_in, edge_in, *swapped],
    )
    slots, *returns = call(
        functools.partial(slot_kernel, n, len(lev_in)),
        [(rows, cols)] + [(8, cells)] * n,
        [*lev_in, picks, tables, piece_marine_box[0], marine_share_fraction[0]],
        scratch=[pltpu.VMEM((3, 2 * n, cells), F32)],
    )
    back = [traded(returns[step], step, 1) for step in range(1, n)]
    slot_parts = lev_parts(slots)
    sums = returns[0]
    for x in back:
        sums = sums + x
    sums_far = traded(sums, 0, 1)
    results = [(levels, rows, cols), (1, cells), (1, cells)]
    state, air_gradient, wind_gradient = call(
        functools.partial(final_kernel, len(slot_parts)),
        results,
        [*slot_parts, adjoint, share_rows, sums, sums_far],
        out_specs=[HBM] * 3,
        scratch=[pltpu.VMEM(x, F32) for x in results] + [pltpu.SemaphoreType.DMA((3,))],
    )
    return (state, air_gradient.reshape(cells), wind_gradient.reshape(cells))


def solution(mesh):
    return jax.shard_map(
        per_device,
        mesh=mesh,
        in_specs=(
            P(("ens", "lev"), "sub", "tile"),
            P(("ens", "tile", "lev", "sub")),
            P(("ens", "tile", "lev", "sub")),
            P("lev"),
            P(("tile", "lev", "sub"), None, None),
            P(("tile", "lev", "sub"), None, None),
            P(("tile", "lev", "sub"), None, None),
            P(("tile", "lev", "sub"), None, None),
            P("sub", "tile"),
            P(("ens", "lev"), "sub", "tile"),
            P(("ens", "tile", "lev", "sub")),
        ),
        out_specs=(
            P(("ens", "lev"), "sub", "tile"),
            P(("ens", "tile", "lev", "sub")),
            P(("ens", "tile", "lev", "sub")),
        ),
        check_vma=False,
    )
```

time: 35.5 us -> 30 us (0.85)
  local copies, waits for them, and re-layouts: 5.87 us -> 0.33 us
  waiting for transfers between devices: 10.4 us -> 13.8 us
  starting transfers between devices: 13.8 us -> 10.9 us
    unnamed x26 -> x4, local copies, waits for them, and re-layouts: 5.87 us -> 0.33 us
    ppermute x10, waiting for transfers between devices: 10.4 us -> 13.8 us  [the longest x8 13.8 us: traded(): return lax.ppermute(x, ('tile', 'sub'), pairs)]
    ppermute x10, starting transfers between devices: 13.8 us -> 10.9 us  [the longest x8 8.79 us: traded(): return lax.ppermute(x, ('tile', 'sub'), pairs)]
  transfers between devices with their start and end apart: 10 -> 10, of which waited for: 7 -> 6; matrix products, arithmetic and copies ran while one was open for 0% -> 0% of each run, Pallas kernels for 2% -> 1%
where the time goes in v2:
time: 30 us; the launch traced here: 29.8 us
  waiting for transfers between devices  13.8 us (46%)
  starting transfers between devices  10.9 us (36%)
  Pallas kernels  4.05 us (14%)
  between operations  0.68 us (2%)
  local copies, waits for them, and re-layouts  0.33 us (1%)
    ppermute x8, waiting for transfers between devices, traded(): return lax.ppermute(x, ('tile', 'sub'), pairs)  13.8 us
    ppermute x8, starting transfers between devices, traded(): return lax.ppermute(x, ('tile', 'sub'), pairs)  8.79 us
    pallas_call x6, Pallas kernels, call(): pl.pallas_call(kernel, out_shape=outs, in_specs=specs or [VMEM] * len(ope...  4.05 us
    ppermute x2, starting transfers between devices, lev_parts(): return [x, lax.ppermute(x, 'lev', [(0, 1), (1, 0)])]  2.1 us
  transfers between devices with their start and end apart: 10, of which 6 were waited for; matrix products, arithmetic and copies ran while one was open for 0% of the time, Pallas kernels for 1%

profile of v2, /device:TPU:0, one launch (start us, length us, event | category | flops | bytes accessed | tf_op | source)
XLA Modules:
  0.0 29.8 jit_solution(3900611616485007630)
XLA Ops:
  0.6 1.1 %shard_map.130 = (f32[32,256]{1,0:T(8,128)S(1)}, f32[216,128]{1,0:T(8,128)S(1)}, f32[64,128]{1,0:T(8,128)S(1)}, f32[8,128]{1,0:T(8,128)S(1)}) custom-call(f32[2,64,128]{2,1,0:T(8,128)} %refs_0_.1, f32[2,64,128]{2,1,0:T(8,128)} %refs_1_.1, s32[64,128]{1,0:T(8,128)} %refs_2_.1, f32[2]{0:T(128)} %refs_3_.1, f32[1,256]{1,0:T(1,128)} %bitcast.13, ...), custom_call_target="tpu_custom_call" | custom-call | tf_op jit(solution)/shard_map/pallas_call | solution.py:24
  1.7 0.5 %collective-permute-start = (f32[32,256]{1,0:T(8,128)S(1)}, f32[32,256]{1,0:T(8,128)S(1)}, u32[]{:S(2)}, u32[]{:S(2)}) collective-permute-start(f32[32,256]{1,0:T(8,128)S(1)} %get-tuple-element.23.msg), channel_id=1, source_target_pairs={{0,1},{1,0},{4,5},{5,4},{8,9},{9,8},{12,13},{13,12},{2,3},{3,2},{6... | collective-permute-start | bytes 98312 | tf_op jit(solution)/shard_map/ppermute | solution.py:299
  2.2 0.9 %collective-permute-done.other = f32[32,256]{1,0:T(8,128)S(1)} collective-permute-done((f32[32,256]{1,0:T(8,128)S(1)}, f32[32,256]{1,0:T(8,128)S(1)}, u32[]{:S(2)}, u32[]{:S(2)}) %collective-permute-start) | collective-permute-done | bytes 32800 | tf_op jit(solution)/shard_map/ppermute | solution.py:299
  3.1 0.1 shard_map.131
  3.2 3.0 %collective-permute-start.1 = (f32[96,128]{1,0:T(8,128)S(1)}, f32[96,128]{1,0:T(8,128)S(1)}, u32[]{:S(2)}, u32[]{:S(2)}) collective-permute-start(f32[96,128]{1,0:T(8,128)S(1)} %get-tuple-element.26), channel_id=1, source_target_pairs={{0,4},{1,5},{4,0},{5,1},{8,12},{9,13},{12,8},{13,9},{2,6},{3,7},{6... | collective-permute-start | bytes 147464 | tf_op jit(solution)/shard_map/ppermute | solution.py:299
  6.2 2.5 %collective-permute-start.2 = (f32[96,128]{1,0:T(8,128)S(1)}, f32[96,128]{1,0:T(8,128)S(1)}, u32[]{:S(2)}, u32[]{:S(2)}) collective-permute-start(f32[96,128]{1,0:T(8,128)S(1)} %get-tuple-element.27), channel_id=1, source_target_pairs={{0,12},{1,13},{4,8},{5,9},{8,4},{9,5},{12,0},{13,1},{2,14},{3,15},... | collective-permute-start | bytes 147464 | tf_op jit(solution)/shard_map/ppermute | solution.py:299
  8.7 0.0 collective-permute-done.1.near_in.refs_0_
  8.7 3.4 %collective-permute-done.2.edge_in.refs_1_ = f32[96,128]{1,0:T(8,128)S(1)} collective-permute-done((f32[96,128]{1,0:T(8,128)S(1)}, f32[96,128]{1,0:T(8,128)S(1)}, u32[]{:S(2)}, u32[]{:S(2)}) %collective-permute-start.2) | collective-permute-done | bytes 49184 | tf_op jit(solution)/shard_map/ppermute | solution.py:299
  12.1 0.5 %shard_map.132 = (f32[2,64,128]{2,1,0:T(8,128)S(1)}, f32[128,128]{1,0:T(8,128)S(1)}) custom-call(f32[216,128]{1,0:T(8,128)S(1)} %get-tuple-element.25.ext, f32[96,128]{1,0:T(8,128)S(1)} %collective-permute-done.1.near_in.refs_0_, f32[96,128]{1,0:T(8,128)S(1)} %collective-permute-done.2.edge_in.refs_1_, f32[64,128]{1,0:T(8,128)S(1)} %get-tuple-element.28.surface, ...), custom_call_target="tpu_custom_call" | custom-call | tf_op jit(solution)/shard_map/pallas_call | solution.py:24
  12.6 1.6 %collective-permute-start.3 = (f32[128,128]{1,0:T(8,128)S(1)}, f32[128,128]{1,0:T(8,128)S(1)}, u32[]{:S(2)}, u32[]{:S(2)}) collective-permute-start(f32[128,128]{1,0:T(8,128)S(1)} %get-tuple-element.30.refs_0_), channel_id=1, source_target_pairs={{0,2},{2,0},{1,3},{3,1},{4,6},{6,4},{5,7},{7,5},{8,10},{10,8},{9,1... | collective-permute-start | bytes 196616 | tf_op jit(solution)/shard_map/ppermute | solution.py:304
  14.2 0.0 collective-permute-start.4
  14.2 4.1 %collective-permute-done.4.refs_2_ = f32[16,256]{1,0:T(8,128)S(1)} collective-permute-done((f32[16,256]{1,0:T(8,128)S(1)}, f32[16,256]{1,0:T(8,128)S(1)}, u32[]{:S(2)}, u32[]{:S(2)}) %collective-permute-start.4) | collective-permute-done | bytes 16416 | tf_op jit(solution)/shard_map/ppermute | solution.py:299
  18.2 0.0 copy-start
  18.2 0.0 copy-start.1
  18.2 0.4 %shard_map.133 = (f32[3,8,256]{2,1,0:T(8,128)S(1)}, bf16[8,256,256]{2,1,0:T(8,128)(2,1)S(1)}) custom-call(f32[32,256]{1,0:T(8,128)S(1)} %get-tuple-element.23.msg, f32[32,256]{1,0:T(8,128)S(1)} %collective-permute-done.other, f32[96,128]{1,0:T(8,128)S(1)} %collective-permute-done.1.near_in.refs_0_, f32[96,128]{1,0:T(8,128)S(1)} %collective-permute-done.2.edge_in.refs_1_, ...), custom_call_target="tpu_custom_call" | custom-call | tf_op jit(solution)/shard_map/pallas_call | solution.py:24
  18.6 0.0 collective-permute-done.3.refs_1_
  18.6 0.3 %copy-done = s32[1,8,256]{2,1,0:T(8,128)S(1)} copy-done((s32[1,8,256]{2,1,0:T(8,128)S(1)}, s32[1,8,256]{2,1,0:T(8,128)}, u32[]{:S(2)}) %copy-start) | copy-done | bytes 8216
  18.9 0.0 copy-done.1
  19.0 1.3 %shard_map.134 = (f32[64,128]{1,0:T(8,128)S(1)}, f32[8,256]{1,0:T(8,128)S(1)}, f32[8,256]{1,0:T(8,128)S(1)}, f32[8,256]{1,0:T(8,128)S(1)}, f32[8,256]{1,0:T(8,128)S(1)}) custom-call(f32[128,128]{1,0:T(8,128)S(1)} %get-tuple-element.30.refs_0_, f32[128,128]{1,0:T(8,128)S(1)} %collective-permute-done.3.refs_1_, f32[3,8,256]{2,1,0:T(8,128)S(1)} %get-tuple-element.32.refs_2_, ...), custom_call_target="tpu_custom_call" | custom-call | tf_op jit(solution)/shard_map/pallas_call | solution.py:24
  20.3 0.2 collective-permute-start.6
  20.5 2.6 %collective-permute-start.7 = (f32[8,256]{1,0:T(8,128)S(1)}, f32[8,256]{1,0:T(8,128)S(1)}, u32[]{:S(2)}, u32[]{:S(2)}) collective-permute-start(f32[8,256]{1,0:T(8,128)S(1)} %get-tuple-element.38), channel_id=1, source_target_pairs={{0,9},{1,8},{4,13},{5,12},{8,1},{9,0},{12,5},{13,4},{2,11},{3,10},... | collective-permute-start | bytes 24584 | tf_op jit(solution)/shard_map/ppermute | solution.py:299
  23.1 0.0 collective-permute-start.8
  23.1 0.5 %collective-permute-start.5 = (f32[64,128]{1,0:T(8,128)S(1)}, f32[64,128]{1,0:T(8,128)S(1)}, u32[]{:S(2)}, u32[]{:S(2)}) collective-permute-start(f32[64,128]{1,0:T(8,128)S(1)} %get-tuple-element.34.refs_0_), channel_id=1, source_target_pairs={{0,2},{2,0},{1,3},{3,1},{4,6},{6,4},{5,7},{7,5},{8,10},{10,8},{9,1... | collective-permute-start | bytes 98312 | tf_op jit(solution)/shard_map/ppermute | solution.py:304
  23.6 0.0 collective-permute-done.6
  23.6 0.9 %collective-permute-done.7 = f32[8,256]{1,0:T(8,128)S(1)} collective-permute-done((f32[8,256]{1,0:T(8,128)S(1)}, f32[8,256]{1,0:T(8,128)S(1)}, u32[]{:S(2)}, u32[]{:S(2)}) %collective-permute-start.7) | collective-permute-done | bytes 8224 | tf_op jit(solution)/shard_map/ppermute | solution.py:299
  24.5 3.4 %collective-permute-done.8 = f32[8,256]{1,0:T(8,128)S(1)} collective-permute-done((f32[8,256]{1,0:T(8,128)S(1)}, f32[8,256]{1,0:T(8,128)S(1)}, u32[]{:S(2)}, u32[]{:S(2)}) %collective-permute-start.8) | collective-permute-done | bytes 8224 | tf_op jit(solution)/shard_map/ppermute | solution.py:299
  27.9 0.0 collective-permute-start.9
  28.0 1.2 %collective-permute-done.9.refs_5_ = f32[8,256]{1,0:T(8,128)S(1)} collective-permute-done((f32[8,256]{1,0:T(8,128)S(1)}, f32[8,256]{1,0:T(8,128)S(1)}, u32[]{:S(2)}, u32[]{:S(2)}) %collective-permute-start.9) | collective-permute-done | bytes 8224 | tf_op jit(solution)/shard_map/ppermute | solution.py:299
  29.1 0.0 collective-permute-done.5.refs_1_
  29.1 0.7 %shard_map.135 = (f32[2,64,128]{2,1,0:T(8,128)}, f32[1,256]{1,0:T(1,128)}, f32[1,256]{1,0:T(1,128)}) custom-call(f32[64,128]{1,0:T(8,128)S(1)} %get-tuple-element.34.refs_0_, f32[64,128]{1,0:T(8,128)S(1)} %collective-permute-done.5.refs_1_, f32[2,64,128]{2,1,0:T(8,128)S(1)} %get-tuple-element.35.refs_2_, f32[8,128]{1,0:T(8,128)S(1)} %get-tuple-element.29.share_rows.refs_3_, ...), custom_call_target="tpu_custom_call" | custom-call | tf_op jit(solution)/shard_map/pallas_call | solution.py:24
  (1 shorter events, 0.0 us)
Async XLA Ops:
  1.7 1.4 %collective-permute-start = (f32[32,256]{1,0:T(8,128)S(1)}, f32[32,256]{1,0:T(8,128)S(1)}, u32[]{:S(2)}, u32[]{:S(2)}) collective-permute-start(f32[32,256]{1,0:T(8,128)S(1)} %get-tuple-element.23.msg), channel_id=1, source_target_pairs={{0,1},{1,0},{4,5},{5,4},{8,9},{9,8},{12,13},{13,12},{2,3},{3,2},{6... | collective-permute-start | bytes 98312 | tf_op jit(solution)/shard_map/ppermute | solution.py:299
  3.2 5.5 %collective-permute-start.1 = (f32[96,128]{1,0:T(8,128)S(1)}, f32[96,128]{1,0:T(8,128)S(1)}, u32[]{:S(2)}, u32[]{:S(2)}) collective-permute-start(f32[96,128]{1,0:T(8,128)S(1)} %get-tuple-element.26), channel_id=1, source_target_pairs={{0,4},{1,5},{4,0},{5,1},{8,12},{9,13},{12,8},{13,9},{2,6},{3,7},{6... | collective-permute-start | bytes 147464 | tf_op jit(solution)/shard_map/ppermute | solution.py:299
  6.2 5.9 %collective-permute-start.2 = (f32[96,128]{1,0:T(8,128)S(1)}, f32[96,128]{1,0:T(8,128)S(1)}, u32[]{:S(2)}, u32[]{:S(2)}) collective-permute-start(f32[96,128]{1,0:T(8,128)S(1)} %get-tuple-element.27), channel_id=1, source_target_pairs={{0,12},{1,13},{4,8},{5,9},{8,4},{9,5},{12,0},{13,1},{2,14},{3,15},... | collective-permute-start | bytes 147464 | tf_op jit(solution)/shard_map/ppermute | solution.py:299
  12.6 6.0 %collective-permute-start.3 = (f32[128,128]{1,0:T(8,128)S(1)}, f32[128,128]{1,0:T(8,128)S(1)}, u32[]{:S(2)}, u32[]{:S(2)}) collective-permute-start(f32[128,128]{1,0:T(8,128)S(1)} %get-tuple-element.30.refs_0_), channel_id=1, source_target_pairs={{0,2},{2,0},{1,3},{3,1},{4,6},{6,4},{5,7},{7,5},{8,10},{10,8},{9,1... | collective-permute-start | bytes 196616 | tf_op jit(solution)/shard_map/ppermute | solution.py:304
  14.2 4.1 %collective-permute-start.4 = (f32[16,256]{1,0:T(8,128)S(1)}, f32[16,256]{1,0:T(8,128)S(1)}, u32[]{:S(2)}, u32[]{:S(2)}) collective-permute-start(f32[16,256]{1,0:T(8,128)S(1)} %get-tuple-element.31), channel_id=1, source_target_pairs={{0,9},{1,8},{4,13},{5,12},{8,1},{9,0},{12,5},{13,4},{2,11},{3,10},... | collective-permute-start | bytes 49160 | tf_op jit(solution)/shard_map/ppermute | solution.py:299
  18.2 0.7 %copy-start = (s32[1,8,256]{2,1,0:T(8,128)S(1)}, s32[1,8,256]{2,1,0:T(8,128)}, u32[]{:S(2)}) copy-start(s32[1,8,256]{2,1,0:T(8,128)} %param.17) | copy-start | bytes 24580
  18.2 0.7 %copy-start.1 = (f32[1,8,256]{2,1,0:T(8,128)S(1)}, f32[1,8,256]{2,1,0:T(8,128)}, u32[]{:S(2)}) copy-start(f32[1,8,256]{2,1,0:T(8,128)} %param.18) | copy-start | bytes 24580
  20.3 3.4 %collective-permute-start.6 = (f32[8,256]{1,0:T(8,128)S(1)}, f32[8,256]{1,0:T(8,128)S(1)}, u32[]{:S(2)}, u32[]{:S(2)}) collective-permute-start(f32[8,256]{1,0:T(8,128)S(1)} %get-tuple-element.37), channel_id=1, source_target_pairs={{0,5},{1,4},{4,1},{5,0},{8,13},{9,12},{12,9},{13,8},{2,7},{3,6},{6... | collective-permute-start | bytes 24584 | tf_op jit(solution)/shard_map/ppermute | solution.py:299
  20.5 4.0 %collective-permute-start.7 = (f32[8,256]{1,0:T(8,128)S(1)}, f32[8,256]{1,0:T(8,128)S(1)}, u32[]{:S(2)}, u32[]{:S(2)}) collective-permute-start(f32[8,256]{1,0:T(8,128)S(1)} %get-tuple-element.38), channel_id=1, source_target_pairs={{0,9},{1,8},{4,13},{5,12},{8,1},{9,0},{12,5},{13,4},{2,11},{3,10},... | collective-permute-start | bytes 24584 | tf_op jit(solution)/shard_map/ppermute | solution.py:299
  23.1 4.9 %collective-permute-start.8 = (f32[8,256]{1,0:T(8,128)S(1)}, f32[8,256]{1,0:T(8,128)S(1)}, u32[]{:S(2)}, u32[]{:S(2)}) collective-permute-start(f32[8,256]{1,0:T(8,128)S(1)} %get-tuple-element.39), channel_id=1, source_target_pairs={{0,13},{1,12},{4,9},{5,8},{8,5},{9,4},{12,1},{13,0},{2,15},{3,14},... | collective-permute-start | bytes 24584 | tf_op jit(solution)/shard_map/ppermute | solution.py:299
  23.1 6.1 %collective-permute-start.5 = (f32[64,128]{1,0:T(8,128)S(1)}, f32[64,128]{1,0:T(8,128)S(1)}, u32[]{:S(2)}, u32[]{:S(2)}) collective-permute-start(f32[64,128]{1,0:T(8,128)S(1)} %get-tuple-element.34.refs_0_), channel_id=1, source_target_pairs={{0,2},{2,0},{1,3},{3,1},{4,6},{6,4},{5,7},{7,5},{8,10},{10,8},{9,1... | collective-permute-start | bytes 98312 | tf_op jit(solution)/shard_map/ppermute | solution.py:304
  27.9 1.2 %collective-permute-start.9 = (f32[8,256]{1,0:T(8,128)S(1)}, f32[8,256]{1,0:T(8,128)S(1)}, u32[]{:S(2)}, u32[]{:S(2)}) collective-permute-start(f32[8,256]{1,0:T(8,128)S(1)} %add_add_fusion.refs_4_), channel_id=1, source_target_pairs={{0,1},{1,0},{4,5},{5,4},{8,9},{9,8},{12,13},{13,12},{2,3},{3,2},{6... | collective-permute-start | bytes 24584 | tf_op jit(solution)/shard_map/ppermute | solution.py:299

commit v3 on v2

--- a/solution.py
+++ b/solution.py
@@ -39,9 +39,9 @@
 
 
 def pack_kernel(n, *refs):
-    warm, cot, sea, shares, sky, breeze, energy, sky_index, sky_weight = refs[:9]
-    msg, ext, surface, share_rows = refs[9:13]
-    warm_in, sea_in, shares_in, sky_in, breeze_in, energy_in, index_in, weight_in, sems = refs[13:]
+    warm, cot, sea, shares, sky, breeze, energy, sky_index, sky_weight, marine, marine_weight = refs[:11]
+    msg, ext, surface, share_rows, marine_out, marine_weight_out = refs[11:17]
+    warm_in, sea_in, shares_in, sky_in, breeze_in, energy_in, index_in, weight_in, sems = refs[17:]
     rows, cols = sea.shape
     levels = warm.shape[0]
     high = rows + 8
@@ -49,6 +49,7 @@
     pairs += [(sea, sea_in), (sky_index, index_in), (sky_weight, weight_in)]
     pairs += [(sky, sky_in), (breeze, breeze_in), (energy, energy_in)]
     pairs += [(shares, shares_in), (warm, warm_in)]
+    pairs += [(marine, marine_out), (marine_weight, marine_weight_out)]
     copies = [pltpu.make_async_copy(a, b, sems.at[i]) for i, (a, b) in enumerate(pairs)]
     for copy in copies:
         copy.start()
@@ -83,10 +84,27 @@
     return [jnp.where(sub == 0, own, far), jnp.where(sub == 0, far, own)]
 
 
-def air_rows(n, msg, other, target, band, sub):
+def table_rows(n, msg, other, target, band, sub):
     row = 2 * target + band
-    places = [row, 2 * n + row] + [4 * n + i for i in range(3)]
-    return [x for place in places for x in both_bands(msg, other, place, sub)]
+    return both_bands(msg, other, row, sub) + both_bands(msg, other, 2 * n + row, sub)
+
+
+def value_rows(n, msg, other, sub):
+    return [x for i in range(3) for x in both_bands(msg, other, 4 * n + i, sub)]
+
+
+def write_pairs(out, at, rows):
+    cols = out.shape[1]
+    for i, row in enumerate(rows):
+        out[at + i : at + i + 1, :] = row[:, :cols]
+        out[at + len(rows) + i : at + len(rows) + i + 1, :] = row[:, cols:]
+
+
+def read_pairs(ref, at, count):
+    return [
+        jnp.concatenate([ref[at + i : at + i + 1, :], ref[at + count + i : at + count + i + 1, :]], axis=1)
+        for i in range(count)
+    ]
 
 
 def edge_place(shape):
@@ -94,7 +112,7 @@
     return lax.rem(lane + HALO, shape[1])
 
 
-def send_kernel(n, fields, edge_steps, swap_steps, msg, other, ext_in, ext, *outs):
+def send_kernel(n, fields, msg, other, ext_in, ext, edge_out, near_out):
     sub, tile = lax.axis_index("sub"), lax.axis_index("tile")
     cols = ext.shape[1]
     high = ext.shape[0] // fields
@@ -111,24 +129,31 @@
         field = ext[base : base + high, :]
         moved = pltpu.roll(field, 2 * HALO * i, 1) if i else field
         edges = jnp.where(place // (2 * HALO) == i, moved, edges)
-    edge_outs, swap_outs = outs[: len(edge_steps)], outs[len(edge_steps) :]
-    for step, out in zip(edge_steps, edge_outs):
-        out[0:high, :] = edges
-        if step:
-            for i, row in enumerate(air_rows(n, msg, other, tile ^ step, sub, sub)):
-                out[high + i : high + i + 1, :] = row[:, :cols]
-                out[high + 10 + i : high + 11 + i, :] = row[:, cols:]
-            out[high + 20 : high + 24, :] = jnp.zeros((4, cols), F32)
-    for step, out in zip(swap_steps, swap_outs):
-        for i, row in enumerate(air_rows(n, msg, other, tile ^ step, 1 - sub, sub)):
-            out[i : i + 1, :] = row
-        out[10:16, :] = jnp.zeros((6, out.shape[1]), F32)
-
-
-def diffuse_kernel(n, levels, ext, near_in, edge_in, surface, share_rows, adjoint_out, lev_out):
-    tile = lax.axis_index("tile")
+    edge_out[...] = edges
+    near_out[0:high, :] = edges
+    near = tile ^ 1
+    air = table_rows(n, msg, other, near, sub, sub) + value_rows(n, msg, other, sub)
+    write_pairs(near_out, high, air)
+    at = high + 20
+    for step in range(2, n, 2):
+        write_pairs(near_out, at, table_rows(n, msg, other, near ^ step, 1 - sub, sub))
+        at += 8
+    near_out[at : near_out.shape[0], :] = jnp.zeros((near_out.shape[0] - at, cols), F32)
+
+
+def diffuse_kernel(n, levels, *refs):
+    ext, near_in, edge_in, surface, share_rows, msg, other, adjoint_out, lev_out = refs[:9]
+    sub, tile = lax.axis_index("sub"), lax.axis_index("tile")
     rows, cols = surface.shape
     high = rows + 8
+    own_values = value_rows(n, msg, other, sub)
+    near_values = read_pairs(near_in, high, 10)[4:]
+    for i, out in enumerate(refs[9:]):
+        air = table_rows(n, msg, other, tile ^ (2 * i + 2), 1 - sub, sub) + own_values
+        air += read_pairs(near_in, high + 20 + 8 * i, 4) + near_values
+        for at, row in enumerate(air):
+            out[at : at + 1, :] = row
+        out[20:24, :] = jnp.zeros((4, out.shape[1]), F32)
     place = edge_place((high, cols))
     near, beyond = near_in[0:high, :], edge_in[0:high, :]
     even = tile % 2 == 0
@@ -193,41 +218,36 @@
     return lax.dot_general(a, b, (((ca,), (cb,)), ((), ())), preferred_element_type=F32)
 
 
-def air_kernel(n, edge_steps, swap_steps, high, msg, other, *refs):
+def look_up(air, at, picks, tables):
+    for band in range(2):
+        hot = onehot(air[band].astype(jnp.int32), air[band].shape[1])
+        tables[at + band] = hot
+        values = jnp.concatenate([air[4 + band], air[6 + band], air[8 + band]], axis=0)
+        found = dot(jnp.concatenate(halves(values), axis=0), hot, 1, 0)
+        found = found[0:3] + found[3:6]
+        picks[0, at + band : at + band + 1, :] = found[0:1]
+        picks[1, at + band : at + band + 1, :] = found[1:2]
+        picks[2, at + band : at + band + 1, :] = air[2 + band] * found[2:3]
+
+
+def near_kernel(n, high, msg, other, near_in, picks, tables):
     sub, tile = lax.axis_index("sub"), lax.axis_index("tile")
-    edge_in = dict(zip(edge_steps, refs))
-    swap_in = dict(zip(swap_steps, refs[len(edge_steps) :]))
-    picks, tables = refs[-2:]
-    for step in range(n):
-        if step == 0:
-            air = air_rows(n, msg, other, tile, sub, sub)
-        elif step in swap_in:
-            air = [swap_in[step][i : i + 1, :] for i in range(10)]
-        else:
-            ref = edge_in[step]
-            air = [
-                jnp.concatenate(
-                    [ref[high + i : high + i + 1, :], ref[high + 10 + i : high + 11 + i, :]], axis=1
-                )
-                for i in range(10)
-            ]
-        for band in range(2):
-            at = 2 * step + band
-            hot = onehot(air[band].astype(jnp.int32), air[band].shape[1])
-            tables[at] = hot
-            values = jnp.concatenate([air[4 + band], air[6 + band], air[8 + band]], axis=0)
-            found = dot(jnp.concatenate(halves(values), axis=0), hot, 1, 0)
-            found = found[0:3] + found[3:6]
-            picks[0, at : at + 1, :] = found[0:1]
-            picks[1, at : at + 1, :] = found[1:2]
-            picks[2, at : at + 1, :] = air[2 + band] * found[2:3]
+    own = table_rows(n, msg, other, tile, sub, sub) + value_rows(n, msg, other, sub)
+    look_up(own, 0, picks, tables)
+    look_up(read_pairs(near_in, high, 10), 2, picks, tables)
 
 
 def slot_kernel(n, count, *refs):
-    lev_parts = refs[:count]
-    picks, tables, marine, weight, slots_out = refs[count : count + 5]
-    returns, held = refs[count + 5 : count + 5 + n], refs[count + 5 + n]
+    lev_parts, refs = refs[:count], refs[count:]
+    near_picks, near_tables, marine, weight = refs[:4]
+    far_in, refs = refs[4 : 3 + n // 2], refs[3 + n // 2 :]
+    slots_out, returns, (held, picks, tables) = refs[0], refs[1 : 1 + n], refs[1 + n :]
     tile = lax.axis_index("tile")
+    picks[:, 0:4, :] = near_picks[...]
+    for i, ref in enumerate(far_in):
+        for j in range(2):
+            air = [ref[10 * j + k : 10 * j + k + 1, :] for k in range(10)]
+            look_up(air, 4 * i + 4 + 2 * j, picks, tables)
     rows, cols = slots_out.shape
     table = jnp.concatenate(
         [sum(ref[rows * i : rows * (i + 1), :] for ref in lev_parts) for i in range(2)], axis=1
@@ -264,8 +284,9 @@
                 [jnp.where(col_mask, x.astype(F32), 0.0).astype(BF16) for x in halves(ocean)], axis=0
             )
             total += dot(row_hot, spread, 1, 1)
+            hot = near_tables[at] if at < 4 else tables[at]
             values = jnp.concatenate([ocean, wind_sens[at : at + 1]], axis=0)
-            sums = dot(jnp.concatenate(halves(values), axis=0), tables[at], 1, 1)
+            sums = dot(jnp.concatenate(halves(values), axis=0), hot, 1, 1)
             returns[step][2 * band : 2 * band + 2, :] = sums[0:2] + sums[2:4]
         returns[step][4:8, :] = jnp.zeros((4, returns[step].shape[1]), F32)
     slots_out[...] = total[:, :cols] + total[:, cols:]
@@ -299,6 +320,21 @@
     return lax.ppermute(x, ("tile", "sub"), pairs)
 
 
+def beyond(x):
+    n, levs, bands = (lax.axis_size(axis) for axis in ("tile", "lev", "sub"))
+
+    def place(t, l, s):
+        return (t * levs + l) * bands + s
+
+    pairs = []
+    for l in range(levs):
+        for s in range(bands):
+            for t in range(1, n - 1, 2):
+                pairs += [(place(t, l, s), place(t + 1, l, s)), (place(t + 1, l, s), place(t, l, s))]
+            pairs += [(place(t, l, s), place(t, l ^ 1, s ^ 1)) for t in (0, n - 1)]
+    return lax.ppermute(x, ("tile", "lev", "sub"), pairs)
+
+
 def lev_parts(x):
     if lax.axis_size("lev") == 2:
         return [x, lax.ppermute(x, "lev", [(0, 1), (1, 0)])]
@@ -322,60 +358,50 @@
     levels, rows, cols = marine_layered_warmth.shape
     cells = bottom_sky_warmth.shape[0]
     high = rows + 8
-    if n == 4:
-        edge_steps = [1, 3]
-    else:
-        edge_steps = [1, 0]
-    swap_steps = [step for step in range(1, n) if step not in edge_steps]
-
     raw = [marine_layered_warmth, marine_result_adjoint, marine_indicator, depth_shares]
     raw += [
         x.reshape(1, cells)
         for x in (bottom_sky_warmth, bottom_breeze_magnitude, energy_transport_adjoint)
     ]
-    raw += [piece_sky_box[0], sky_share_fraction[0]]
+    raw += [piece_sky_box[0], sky_share_fraction[0], piece_marine_box[0], marine_share_fraction[0]]
     raw = [pltpu.with_memory_space_constraint(x, pltpu.HBM) for x in raw]
     held = [pltpu.VMEM(x.shape, x.dtype) for x in [raw[0], raw[2]]]
     held += [pltpu.SMEM(depth_shares.shape, F32)]
-    held += [pltpu.VMEM(x.shape, x.dtype) for x in raw[4:]]
-    msg, ext, surface, share_rows = call(
+    held += [pltpu.VMEM(x.shape, x.dtype) for x in raw[4:9]]
+    msg, ext, surface, share_rows, marine, marine_weight = call(
         functools.partial(pack_kernel, n),
-        [(4 * n + 16, cells), ((levels + 1) * high, cols), (rows, cols), (8, cols)],
+        [(4 * n + 16, cells), ((levels + 1) * high, cols), (rows, cols), (8, cols)]
+        + [jax.ShapeDtypeStruct(x.shape, x.dtype) for x in raw[9:]],
         raw,
         [HBM] * len(raw),
-        scratch=held + [pltpu.SemaphoreType.DMA((8 + levels,))],
+        scratch=held + [pltpu.SemaphoreType.DMA((10 + levels,))],
     )
     other = traded(msg, 0, 1)
-    ext, *sent = call(
-        functools.partial(send_kernel, n, levels + 1, edge_steps, swap_steps),
-        [ext.shape]
-        + [(high + 24 if step else high, cols) for step in edge_steps]
-        + [(16, cells)] * len(swap_steps),
+    ext, edge_out, near_out = call(
+        functools.partial(send_kernel, n, levels + 1),
+        [ext.shape, (high, cols), ((high + 20 + 4 * (n - 2) + 7) // 8 * 8, cols)],
         [msg, other, ext],
     )
-    near_in = traded(sent[0], 1)
-    if n == 4:
-        edge_in = traded(sent[1], 3)
-    else:
-        pairs = [(i, (i + 1) % n) for i in range(1, n, 2)]
-        edge_in = lax.ppermute(sent[1], "tile", pairs + [(b, a) for a, b in pairs])
-    swapped = [traded(x, step, 1) for step, x in zip(swap_steps, sent[2:])]
-    adjoint, lev_msg = call(
+    edge_in = beyond(edge_out)
+    near_in = traded(near_out, 1)
+    adjoint, lev_msg, *far_out = call(
         functools.partial(diffuse_kernel, n, levels),
-        [(levels, rows, cols), (2 * rows, cols)],
-        [ext, near_in, edge_in, surface, share_rows],
+        [(levels, rows, cols), (2 * rows, cols)] + [(24, cells)] * (n // 2 - 1),
+        [ext, near_in, edge_in, surface, share_rows, msg, other],
     )
     lev_in = lev_parts(lev_msg)
+    far_in = [traded(x, 2 * i + 2, 1) for i, x in enumerate(far_out)]
     picks, tables = call(
-        functools.partial(air_kernel, n, edge_steps, swap_steps, high),
-        [(3, 2 * n, cells), jax.ShapeDtypeStruct((2 * n, cells, cells), BF16)],
-        [msg, other, near_in, edge_in, *swapped],
+        functools.partial(near_kernel, n, high),
+        [(3, 4, cells), jax.ShapeDtypeStruct((4, cells, cells), BF16)],
+        [msg, other, near_in],
     )
     slots, *returns = call(
         functools.partial(slot_kernel, n, len(lev_in)),
         [(rows, cols)] + [(8, cells)] * n,
-        [*lev_in, picks, tables, piece_marine_box[0], marine_share_fraction[0]],
-        scratch=[pltpu.VMEM((3, 2 * n, cells), F32)],
+        [*lev_in, picks, tables, marine, marine_weight, *far_in],
+        scratch=[pltpu.VMEM((3, 2 * n, cells), F32)] * 2
+        + [pltpu.VMEM((2 * n, cells, cells), BF16)],
     )
     back = [traded(returns[step], step, 1) for step in range(1, n)]
     slot_parts = lev_parts(slots)

time: 30 us -> 27.8 us (0.927)
  waiting for transfers between devices: 13.8 us -> 11.3 us
  starting transfers between devices: 10.9 us -> 11.5 us
  local copies, waits for them, and re-layouts: 0.33 us -> 0 us
    ppermute x8 -> x7, waiting for transfers between devices: 13.8 us -> 8.59 us  [traded(): return lax.ppermute(x, ('tile', 'sub'), pairs)]
    ppermute x0 -> x1, waiting for transfers between devices: none -> 2.73 us  [beyond(): return lax.ppermute(x, ('tile', 'lev', 'sub'), pairs)]
    ppermute x0 -> x1, starting transfers between devices: none -> 0.98 us  [beyond(): return lax.ppermute(x, ('tile', 'lev', 'sub'), pairs)]
    ppermute x8 -> x7, starting transfers between devices: 8.79 us -> 8.39 us  [traded(): return lax.ppermute(x, ('tile', 'sub'), pairs)]
    unnamed x4 -> x0, local copies, waits for them, and re-layouts: 0.33 us -> none
  transfers between devices with their start and end apart: 10 -> 10, of which waited for: 6 -> 5; matrix products, arithmetic and copies ran while one was open for 0% -> 0% of each run, Pallas kernels for 1% -> 1%
where the time goes in v3:
time: 27.8 us; the launch traced here: 27.6 us
  starting transfers between devices  11.5 us (41%)
  waiting for transfers between devices  11.3 us (41%)
  Pallas kernels  4.1 us (15%)
  between operations  0.68 us (2%)
    ppermute x7, waiting for transfers between devices, traded(): return lax.ppermute(x, ('tile', 'sub'), pairs)  8.59 us
    ppermute x7, starting transfers between devices, traded(): return lax.ppermute(x, ('tile', 'sub'), pairs)  8.39 us
    pallas_call x6, Pallas kernels, call(): pl.pallas_call(kernel, out_shape=outs, in_specs=specs or [VMEM] * len(ope...  4.1 us
    ppermute x1, waiting for transfers between devices, beyond(): return lax.ppermute(x, ('tile', 'lev', 'sub'), pairs)  2.73 us
    ppermute x2, starting transfers between devices, lev_parts(): return [x, lax.ppermute(x, 'lev', [(0, 1), (1, 0)])]  2.14 us
    ppermute x1, starting transfers between devices, beyond(): return lax.ppermute(x, ('tile', 'lev', 'sub'), pairs)  0.98 us
  transfers between devices with their start and end apart: 10, of which 5 were waited for; matrix products, arithmetic and copies ran while one was open for 0% of the time, Pallas kernels for 1%

profile of v3, /device:TPU:0, one launch (start us, length us, event | category | flops | bytes accessed | tf_op | source)
XLA Modules:
  0.0 27.6 jit_solution(15291550582514067063)
XLA Ops:
  0.6 1.1 %shard_map.130 = (f32[32,256]{1,0:T(8,128)S(1)}, f32[216,128]{1,0:T(8,128)S(1)}, f32[64,128]{1,0:T(8,128)S(1)}, f32[8,128]{1,0:T(8,128)S(1)}, s32[8,256]{1,0:T(8,128)S(1)}, /*index=5*/f32[8,256]{1,0:T(8,128)S(1)}) custom-call(f32[2,64,128]{2,1,0:T(8,128)} %refs_0_.1, f32[2,64,128]{2,1,0:T(8,128)} %refs_1_.1, s32[64,128]{1,0:T(8,128)} %refs_2_.1, f32[2]{0:T(128)} %refs_3_.1, ...), custom_call_target="tpu_custom_call" | custom-call | tf_op jit(solution)/shard_map/pallas_call | solution.py:24
  1.7 0.5 %collective-permute-start = (f32[32,256]{1,0:T(8,128)S(1)}, f32[32,256]{1,0:T(8,128)S(1)}, u32[]{:S(2)}, u32[]{:S(2)}) collective-permute-start(f32[32,256]{1,0:T(8,128)S(1)} %get-tuple-element.25.msg.refs_5_), channel_id=1, source_target_pairs={{0,1},{1,0},{4,5},{5,4},{8,9},{9,8},{12,13},{13,12},{2,3},{3,2},{6... | collective-permute-start | bytes 98312 | tf_op jit(solution)/shard_map/ppermute | solution.py:320
  2.3 0.9 %collective-permute-done.other.refs_6_ = f32[32,256]{1,0:T(8,128)S(1)} collective-permute-done((f32[32,256]{1,0:T(8,128)S(1)}, f32[32,256]{1,0:T(8,128)S(1)}, u32[]{:S(2)}, u32[]{:S(2)}) %collective-permute-start) | collective-permute-done | bytes 32800 | tf_op jit(solution)/shard_map/ppermute | solution.py:320
  3.1 0.1 shard_map.131
  3.2 3.0 %collective-permute-start.1 = (f32[104,128]{1,0:T(8,128)S(1)}, f32[104,128]{1,0:T(8,128)S(1)}, u32[]{:S(2)}, u32[]{:S(2)}) collective-permute-start(f32[104,128]{1,0:T(8,128)S(1)} %get-tuple-element.28), channel_id=1, source_target_pairs={{0,4},{1,5},{4,0},{5,1},{8,12},{9,13},{12,8},{13,9},{2,6},{3,7},{6... | collective-permute-start | bytes 159752 | tf_op jit(solution)/shard_map/ppermute | solution.py:320
  6.2 1.0 %collective-permute-start.2 = (f32[72,128]{1,0:T(8,128)S(1)}, f32[72,128]{1,0:T(8,128)S(1)}, u32[]{:S(2)}, u32[]{:S(2)}) collective-permute-start(f32[72,128]{1,0:T(8,128)S(1)} %get-tuple-element.29), channel_id=1, source_target_pairs={{4,8},{8,4},{0,3},{12,15},{5,9},{9,5},{1,2},{13,14},{6,10},{10,6},... | collective-permute-start | bytes 110600 | tf_op jit(solution)/shard_map/ppermute | solution.py:335
  7.2 2.7 %collective-permute-done.2.refs_2_ = f32[72,128]{1,0:T(8,128)S(1)} collective-permute-done((f32[72,128]{1,0:T(8,128)S(1)}, f32[72,128]{1,0:T(8,128)S(1)}, u32[]{:S(2)}, u32[]{:S(2)}) %collective-permute-start.2) | collective-permute-done | bytes 36896 | tf_op jit(solution)/shard_map/ppermute | solution.py:335
  9.9 0.0 collective-permute-done.1.refs_1_.near_in
  9.9 0.5 %shard_map.132 = (f32[2,64,128]{2,1,0:T(8,128)S(1)}, f32[128,128]{1,0:T(8,128)S(1)}, f32[24,256]{1,0:T(8,128)S(1)}) custom-call(f32[216,128]{1,0:T(8,128)S(1)} %get-tuple-element.27.refs_0_, f32[104,128]{1,0:T(8,128)S(1)} %collective-permute-done.1.refs_1_.near_in, f32[72,128]{1,0:T(8,128)S(1)} %collective-permute-done.2.refs_2_, ...), custom_call_target="tpu_custom_call" | custom-call | tf_op jit(solution)/shard_map/pallas_call | solution.py:24
  10.5 1.6 %collective-permute-start.3 = (f32[128,128]{1,0:T(8,128)S(1)}, f32[128,128]{1,0:T(8,128)S(1)}, u32[]{:S(2)}, u32[]{:S(2)}) collective-permute-start(f32[128,128]{1,0:T(8,128)S(1)} %get-tuple-element.32.refs_0_), channel_id=1, source_target_pairs={{0,2},{2,0},{1,3},{3,1},{4,6},{6,4},{5,7},{7,5},{8,10},{10,8},{9,1... | collective-permute-start | bytes 196616 | tf_op jit(solution)/shard_map/ppermute | solution.py:340
  12.0 0.9 %collective-permute-start.4 = (f32[24,256]{1,0:T(8,128)S(1)}, f32[24,256]{1,0:T(8,128)S(1)}, u32[]{:S(2)}, u32[]{:S(2)}) collective-permute-start(f32[24,256]{1,0:T(8,128)S(1)} %get-tuple-element.37), channel_id=1, source_target_pairs={{0,9},{1,8},{4,13},{5,12},{8,1},{9,0},{12,5},{13,4},{2,11},{3,10},... | collective-permute-start | bytes 73736 | tf_op jit(solution)/shard_map/ppermute | solution.py:320
  12.9 0.3 shard_map.133
  13.2 3.3 %collective-permute-done.4.refs_6_ = f32[24,256]{1,0:T(8,128)S(1)} collective-permute-done((f32[24,256]{1,0:T(8,128)S(1)}, f32[24,256]{1,0:T(8,128)S(1)}, u32[]{:S(2)}, u32[]{:S(2)}) %collective-permute-start.4) | collective-permute-done | bytes 24608 | tf_op jit(solution)/shard_map/ppermute | solution.py:320
  16.5 0.0 collective-permute-done.3.refs_1_
  16.5 1.4 %shard_map.134 = (f32[64,128]{1,0:T(8,128)S(1)}, f32[8,256]{1,0:T(8,128)S(1)}, f32[8,256]{1,0:T(8,128)S(1)}, f32[8,256]{1,0:T(8,128)S(1)}, f32[8,256]{1,0:T(8,128)S(1)}) custom-call(f32[128,128]{1,0:T(8,128)S(1)} %get-tuple-element.32.refs_0_, f32[128,128]{1,0:T(8,128)S(1)} %collective-permute-done.3.refs_1_, f32[3,4,256]{2,1,0:T(4,128)S(1)} %get-tuple-element.33.refs_2_, ...), custom_call_target="tpu_custom_call" | custom-call | tf_op jit(solution)/shard_map/pallas_call | solution.py:24
  17.9 0.1 collective-permute-start.6
  18.0 2.9 %collective-permute-start.7 = (f32[8,256]{1,0:T(8,128)S(1)}, f32[8,256]{1,0:T(8,128)S(1)}, u32[]{:S(2)}, u32[]{:S(2)}) collective-permute-start(f32[8,256]{1,0:T(8,128)S(1)} %get-tuple-element.42), channel_id=1, source_target_pairs={{0,9},{1,8},{4,13},{5,12},{8,1},{9,0},{12,5},{13,4},{2,11},{3,10},... | collective-permute-start | bytes 24584 | tf_op jit(solution)/shard_map/ppermute | solution.py:320
  20.9 0.9 %collective-permute-start.8 = (f32[8,256]{1,0:T(8,128)S(1)}, f32[8,256]{1,0:T(8,128)S(1)}, u32[]{:S(2)}, u32[]{:S(2)}) collective-permute-start(f32[8,256]{1,0:T(8,128)S(1)} %get-tuple-element.43), channel_id=1, source_target_pairs={{0,13},{1,12},{4,9},{5,8},{8,5},{9,4},{12,1},{13,0},{2,15},{3,14},... | collective-permute-start | bytes 24584 | tf_op jit(solution)/shard_map/ppermute | solution.py:320
  21.8 0.6 %collective-permute-start.5 = (f32[64,128]{1,0:T(8,128)S(1)}, f32[64,128]{1,0:T(8,128)S(1)}, u32[]{:S(2)}, u32[]{:S(2)}) collective-permute-start(f32[64,128]{1,0:T(8,128)S(1)} %get-tuple-element.38.refs_0_), channel_id=1, source_target_pairs={{0,2},{2,0},{1,3},{3,1},{4,6},{6,4},{5,7},{7,5},{8,10},{10,8},{9,1... | collective-permute-start | bytes 98312 | tf_op jit(solution)/shard_map/ppermute | solution.py:340
  22.4 0.0 collective-permute-done.6
  22.4 0.0 collective-permute-done.7
  22.4 3.4 %collective-permute-done.8 = f32[8,256]{1,0:T(8,128)S(1)} collective-permute-done((f32[8,256]{1,0:T(8,128)S(1)}, f32[8,256]{1,0:T(8,128)S(1)}, u32[]{:S(2)}, u32[]{:S(2)}) %collective-permute-start.8) | collective-permute-done | bytes 8224 | tf_op jit(solution)/shard_map/ppermute | solution.py:320
  25.8 0.1 collective-permute-start.9
  25.9 1.1 %collective-permute-done.9.refs_5_ = f32[8,256]{1,0:T(8,128)S(1)} collective-permute-done((f32[8,256]{1,0:T(8,128)S(1)}, f32[8,256]{1,0:T(8,128)S(1)}, u32[]{:S(2)}, u32[]{:S(2)}) %collective-permute-start.9) | collective-permute-done | bytes 8224 | tf_op jit(solution)/shard_map/ppermute | solution.py:320
  26.9 0.0 collective-permute-done.5.refs_1_
  26.9 0.7 %shard_map.135 = (f32[2,64,128]{2,1,0:T(8,128)}, f32[1,256]{1,0:T(1,128)}, f32[1,256]{1,0:T(1,128)}) custom-call(f32[64,128]{1,0:T(8,128)S(1)} %get-tuple-element.38.refs_0_, f32[64,128]{1,0:T(8,128)S(1)} %collective-permute-done.5.refs_1_, f32[2,64,128]{2,1,0:T(8,128)S(1)} %get-tuple-element.39.refs_2_, f32[8,128]{1,0:T(8,128)S(1)} %get-tuple-element.31.refs_4_.refs_3_, ...), custom_call_target="tpu_custom_call" | custom-call | tf_op jit(solution)/shard_map/pallas_call | solution.py:24
  (1 shorter events, 0.0 us)
Async XLA Ops:
  1.7 1.4 %collective-permute-start = (f32[32,256]{1,0:T(8,128)S(1)}, f32[32,256]{1,0:T(8,128)S(1)}, u32[]{:S(2)}, u32[]{:S(2)}) collective-permute-start(f32[32,256]{1,0:T(8,128)S(1)} %get-tuple-element.25.msg.refs_5_), channel_id=1, source_target_pairs={{0,1},{1,0},{4,5},{5,4},{8,9},{9,8},{12,13},{13,12},{2,3},{3,2},{6... | collective-permute-start | bytes 98312 | tf_op jit(solution)/shard_map/ppermute | solution.py:320
  3.2 6.7 %collective-permute-start.1 = (f32[104,128]{1,0:T(8,128)S(1)}, f32[104,128]{1,0:T(8,128)S(1)}, u32[]{:S(2)}, u32[]{:S(2)}) collective-permute-start(f32[104,128]{1,0:T(8,128)S(1)} %get-tuple-element.28), channel_id=1, source_target_pairs={{0,4},{1,5},{4,0},{5,1},{8,12},{9,13},{12,8},{13,9},{2,6},{3,7},{6... | collective-permute-start | bytes 159752 | tf_op jit(solution)/shard_map/ppermute | solution.py:320
  6.2 3.7 %collective-permute-start.2 = (f32[72,128]{1,0:T(8,128)S(1)}, f32[72,128]{1,0:T(8,128)S(1)}, u32[]{:S(2)}, u32[]{:S(2)}) collective-permute-start(f32[72,128]{1,0:T(8,128)S(1)} %get-tuple-element.29), channel_id=1, source_target_pairs={{4,8},{8,4},{0,3},{12,15},{5,9},{9,5},{1,2},{13,14},{6,10},{10,6},... | collective-permute-start | bytes 110600 | tf_op jit(solution)/shard_map/ppermute | solution.py:335
  10.5 6.0 %collective-permute-start.3 = (f32[128,128]{1,0:T(8,128)S(1)}, f32[128,128]{1,0:T(8,128)S(1)}, u32[]{:S(2)}, u32[]{:S(2)}) collective-permute-start(f32[128,128]{1,0:T(8,128)S(1)} %get-tuple-element.32.refs_0_), channel_id=1, source_target_pairs={{0,2},{2,0},{1,3},{3,1},{4,6},{6,4},{5,7},{7,5},{8,10},{10,8},{9,1... | collective-permute-start | bytes 196616 | tf_op jit(solution)/shard_map/ppermute | solution.py:340
  12.0 4.4 %collective-permute-start.4 = (f32[24,256]{1,0:T(8,128)S(1)}, f32[24,256]{1,0:T(8,128)S(1)}, u32[]{:S(2)}, u32[]{:S(2)}) collective-permute-start(f32[24,256]{1,0:T(8,128)S(1)} %get-tuple-element.37), channel_id=1, source_target_pairs={{0,9},{1,8},{4,13},{5,12},{8,1},{9,0},{12,5},{13,4},{2,11},{3,10},... | collective-permute-start | bytes 73736 | tf_op jit(solution)/shard_map/ppermute | solution.py:320
  17.9 4.5 %collective-permute-start.6 = (f32[8,256]{1,0:T(8,128)S(1)}, f32[8,256]{1,0:T(8,128)S(1)}, u32[]{:S(2)}, u32[]{:S(2)}) collective-permute-start(f32[8,256]{1,0:T(8,128)S(1)} %get-tuple-element.41), channel_id=1, source_target_pairs={{0,5},{1,4},{4,1},{5,0},{8,13},{9,12},{12,9},{13,8},{2,7},{3,6},{6... | collective-permute-start | bytes 24584 | tf_op jit(solution)/shard_map/ppermute | solution.py:320
  18.0 4.4 %collective-permute-start.7 = (f32[8,256]{1,0:T(8,128)S(1)}, f32[8,256]{1,0:T(8,128)S(1)}, u32[]{:S(2)}, u32[]{:S(2)}) collective-permute-start(f32[8,256]{1,0:T(8,128)S(1)} %get-tuple-element.42), channel_id=1, source_target_pairs={{0,9},{1,8},{4,13},{5,12},{8,1},{9,0},{12,5},{13,4},{2,11},{3,10},... | collective-permute-start | bytes 24584 | tf_op jit(solution)/shard_map/ppermute | solution.py:320
  20.9 4.9 %collective-permute-start.8 = (f32[8,256]{1,0:T(8,128)S(1)}, f32[8,256]{1,0:T(8,128)S(1)}, u32[]{:S(2)}, u32[]{:S(2)}) collective-permute-start(f32[8,256]{1,0:T(8,128)S(1)} %get-tuple-element.43), channel_id=1, source_target_pairs={{0,13},{1,12},{4,9},{5,8},{8,5},{9,4},{12,1},{13,0},{2,15},{3,14},... | collective-permute-start | bytes 24584 | tf_op jit(solution)/shard_map/ppermute | solution.py:320
  21.8 5.1 %collective-permute-start.5 = (f32[64,128]{1,0:T(8,128)S(1)}, f32[64,128]{1,0:T(8,128)S(1)}, u32[]{:S(2)}, u32[]{:S(2)}) collective-permute-start(f32[64,128]{1,0:T(8,128)S(1)} %get-tuple-element.38.refs_0_), channel_id=1, source_target_pairs={{0,2},{2,0},{1,3},{3,1},{4,6},{6,4},{5,7},{7,5},{8,10},{10,8},{9,1... | collective-permute-start | bytes 98312 | tf_op jit(solution)/shard_map/ppermute | solution.py:340
  25.8 1.2 %collective-permute-start.9 = (f32[8,256]{1,0:T(8,128)S(1)}, f32[8,256]{1,0:T(8,128)S(1)}, u32[]{:S(2)}, u32[]{:S(2)}) collective-permute-start(f32[8,256]{1,0:T(8,128)S(1)} %add_add_fusion.refs_4_), channel_id=1, source_target_pairs={{0,1},{1,0},{4,5},{5,4},{8,9},{9,8},{12,13},{13,12},{2,3},{3,2},{6... | collective-permute-start | bytes 24584 | tf_op jit(solution)/shard_map/ppermute | solution.py:320

commit v4 on v3

--- a/solution.py
+++ b/solution.py
@@ -107,9 +107,40 @@
     ]
 
 
-def edge_place(shape):
-    lane = lax.broadcasted_iota(jnp.int32, shape, 1)
-    return lax.rem(lane + HALO, shape[1])
+def fold_place(cols):
+    lane = lax.broadcasted_iota(jnp.int32, (8, cols), 1)
+    return lax.rem(lane + HALO, cols)
+
+
+def fold_slots(high, cols, fields):
+    each = cols // (2 * HALO * fields)
+    groups = high // 8
+    return [(g // each, g % each) for g in range(groups)], -(-groups // each)
+
+
+def folded(ext, high, fields):
+    cols = ext.shape[1]
+    place = fold_place(cols) // (2 * HALO)
+    slots, tiles = fold_slots(high, cols, fields)
+    out = [jnp.zeros((8, cols), F32)] * tiles
+    for g, (k, at) in enumerate(slots):
+        for i in range(fields):
+            slot = at * fields + i
+            rows = ext[high * i + 8 * g : high * i + 8 * g + 8, :]
+            moved = pltpu.roll(rows, 2 * HALO * slot, 1) if slot else rows
+            out[k] = jnp.where(place == slot, moved, out[k])
+    return jnp.concatenate(out, axis=0)
+
+
+def unfolded(tiles, i, high, fields):
+    cols = tiles[0].shape[1]
+    place = fold_place(cols)
+    out = []
+    for k, at in fold_slots(high, cols, fields)[0]:
+        slot = at * fields + i
+        moved = pltpu.roll(tiles[k], cols - 2 * HALO * slot, 1) if slot else tiles[k]
+        out.append(jnp.where(place < 2 * HALO, moved, 0.0))
+    return jnp.concatenate(out, axis=0)
 
 
 def send_kernel(n, fields, msg, other, ext_in, ext, edge_out, near_out):
@@ -117,8 +148,6 @@
     cols = ext.shape[1]
     high = ext.shape[0] // fields
     rows = high - 8
-    place = edge_place((high, cols))
-    edges = jnp.zeros((high, cols), F32)
     for i in range(fields):
         base = high * i
         strip = halo_rows(n, other, i, cols)
@@ -126,15 +155,14 @@
         ext[base + rows : base + high, :] = jnp.zeros((8, cols), F32)
         ext[base + rows : base + rows + HALO, :] = jnp.where(sub == 0, strip, 0.0)
         ext[base + high - HALO : base + high, :] = jnp.where(sub == 0, 0.0, strip)
-        field = ext[base : base + high, :]
-        moved = pltpu.roll(field, 2 * HALO * i, 1) if i else field
-        edges = jnp.where(place // (2 * HALO) == i, moved, edges)
+    edges = folded(ext, high, fields)
+    fold = edges.shape[0]
     edge_out[...] = edges
-    near_out[0:high, :] = edges
+    near_out[0:fold, :] = edges
     near = tile ^ 1
     air = table_rows(n, msg, other, near, sub, sub) + value_rows(n, msg, other, sub)
-    write_pairs(near_out, high, air)
-    at = high + 20
+    write_pairs(near_out, fold, air)
+    at = fold + 20
     for step in range(2, n, 2):
         write_pairs(near_out, at, table_rows(n, msg, other, near ^ step, 1 - sub, sub))
         at += 8
@@ -146,25 +174,27 @@
     sub, tile = lax.axis_index("sub"), lax.axis_index("tile")
     rows, cols = surface.shape
     high = rows + 8
+    fold = edge_in.shape[0]
     own_values = value_rows(n, msg, other, sub)
-    near_values = read_pairs(near_in, high, 10)[4:]
+    near_values = read_pairs(near_in, fold, 10)[4:]
     for i, out in enumerate(refs[9:]):
         air = table_rows(n, msg, other, tile ^ (2 * i + 2), 1 - sub, sub) + own_values
-        air += read_pairs(near_in, high + 20 + 8 * i, 4) + near_values
+        air += read_pairs(near_in, fold + 20 + 8 * i, 4) + near_values
         for at, row in enumerate(air):
             out[at : at + 1, :] = row
         out[20:24, :] = jnp.zeros((4, out.shape[1]), F32)
-    place = edge_place((high, cols))
-    near, beyond = near_in[0:high, :], edge_in[0:high, :]
     even = tile % 2 == 0
-    right = jnp.where(tile < n - 1, jnp.where(even, near, beyond), 0.0)
-    left = jnp.where(tile > 0, jnp.where(even, beyond, near), 0.0)
-    edges = jnp.where(lax.rem(place, 2 * HALO) >= HALO, right, left)
+    place = fold_place(cols)
+    tiles = []
+    for k in range(0, fold, 8):
+        near, far = near_in[k : k + 8, :], edge_in[k : k + 8, :]
+        right = jnp.where(tile < n - 1, jnp.where(even, near, far), 0.0)
+        left = jnp.where(tile > 0, jnp.where(even, far, near), 0.0)
+        tiles.append(jnp.where(lax.rem(place, 2 * HALO) >= HALO, right, left))
 
     def wide(i):
-        moved = pltpu.roll(edges, cols - 2 * HALO * i, 1) if i else edges
         return jnp.concatenate(
-            [ext[high * i : high * (i + 1), :], jnp.where(place < 2 * HALO, moved, 0.0)], axis=1
+            [ext[high * i : high * (i + 1), :], unfolded(tiles, i, high, levels + 1)], axis=1
         )
 
     def around(x):
@@ -230,11 +260,11 @@
         picks[2, at + band : at + band + 1, :] = air[2 + band] * found[2:3]
 
 
-def near_kernel(n, high, msg, other, near_in, picks, tables):
+def near_kernel(n, fold, msg, other, near_in, picks, tables):
     sub, tile = lax.axis_index("sub"), lax.axis_index("tile")
     own = table_rows(n, msg, other, tile, sub, sub) + value_rows(n, msg, other, sub)
     look_up(own, 0, picks, tables)
-    look_up(read_pairs(near_in, high, 10), 2, picks, tables)
+    look_up(read_pairs(near_in, fold, 10), 2, picks, tables)
 
 
 def slot_kernel(n, count, *refs):
@@ -377,9 +407,10 @@
         scratch=held + [pltpu.SemaphoreType.DMA((10 + levels,))],
     )
     other = traded(msg, 0, 1)
+    fold = 8 * fold_slots(high, cols, levels + 1)[1]
     ext, edge_out, near_out = call(
         functools.partial(send_kernel, n, levels + 1),
-        [ext.shape, (high, cols), ((high + 20 + 4 * (n - 2) + 7) // 8 * 8, cols)],
+        [ext.shape, (fold, cols), ((fold + 20 + 4 * (n - 2) + 7) // 8 * 8, cols)],
         [msg, other, ext],
     )
     edge_in = beyond(edge_out)
@@ -392,7 +423,7 @@
     lev_in = lev_parts(lev_msg)
     far_in = [traded(x, 2 * i + 2, 1) for i, x in enumerate(far_out)]
     picks, tables = call(
-        functools.partial(near_kernel, n, high),
+        functools.partial(near_kernel, n, fold),
         [(3, 4, cells), jax.ShapeDtypeStruct((4, cells, cells), BF16)],
         [msg, other, near_in],
     )

time: 27.8 us -> 27.3 us (0.982)
  waiting for transfers between devices: 11.3 us -> 10.1 us
  starting transfers between devices: 11.5 us -> 12.3 us
    ppermute x7, starting transfers between devices: 8.39 us -> 9.21 us  [traded(): return lax.ppermute(x, ('tile', 'sub'), pairs)]
    ppermute x1, waiting for transfers between devices: 2.73 us -> 2.12 us  [beyond(): return lax.ppermute(x, ('tile', 'lev', 'sub'), pairs)]
    ppermute x7, waiting for transfers between devices: 8.59 us -> 7.99 us  [traded(): return lax.ppermute(x, ('tile', 'sub'), pairs)]
where the time goes in v4:
time: 27.3 us; the launch traced here: 27.2 us
  starting transfers between devices  12.3 us (45%)
  waiting for transfers between devices  10.1 us (37%)
  Pallas kernels  4.1 us (15%)
  between operations  0.67 us (2%)
    ppermute x7, starting transfers between devices, traded(): return lax.ppermute(x, ('tile', 'sub'), pairs)  9.21 us
    ppermute x7, waiting for transfers between devices, traded(): return lax.ppermute(x, ('tile', 'sub'), pairs)  7.99 us
    pallas_call x6, Pallas kernels, call(): pl.pallas_call(kernel, out_shape=outs, in_specs=specs or [VMEM] * len(ope...  4.1 us
    ppermute x1, waiting for transfers between devices, beyond(): return lax.ppermute(x, ('tile', 'lev', 'sub'), pairs)  2.12 us
    ppermute x2, starting transfers between devices, lev_parts(): return [x, lax.ppermute(x, 'lev', [(0, 1), (1, 0)])]  2.09 us
    ppermute x1, starting transfers between devices, beyond(): return lax.ppermute(x, ('tile', 'lev', 'sub'), pairs)  0.98 us
  transfers between devices with their start and end apart: 10, of which 5 were waited for; matrix products, arithmetic and copies ran while one was open for 0% of the time, Pallas kernels for 1%

profile of v4, /device:TPU:0, one launch (start us, length us, event | category | flops | bytes accessed | tf_op | source)
XLA Modules:
  0.0 27.2 jit_solution(5319511112535128960)
XLA Ops:
  0.6 1.1 %shard_map.130 = (f32[32,256]{1,0:T(8,128)S(1)}, f32[216,128]{1,0:T(8,128)S(1)}, f32[64,128]{1,0:T(8,128)S(1)}, f32[8,128]{1,0:T(8,128)S(1)}, s32[8,256]{1,0:T(8,128)S(1)}, /*index=5*/f32[8,256]{1,0:T(8,128)S(1)}) custom-call(f32[2,64,128]{2,1,0:T(8,128)} %refs_0_.1, f32[2,64,128]{2,1,0:T(8,128)} %refs_1_.1, s32[64,128]{1,0:T(8,128)} %refs_2_.1, f32[2]{0:T(128)} %refs_3_.1, ...), custom_call_target="tpu_custom_call" | custom-call | tf_op jit(solution)/shard_map/pallas_call | solution.py:24
  1.7 0.5 %collective-permute-start = (f32[32,256]{1,0:T(8,128)S(1)}, f32[32,256]{1,0:T(8,128)S(1)}, u32[]{:S(2)}, u32[]{:S(2)}) collective-permute-start(f32[32,256]{1,0:T(8,128)S(1)} %get-tuple-element.25.msg.refs_5_), channel_id=1, source_target_pairs={{0,1},{1,0},{4,5},{5,4},{8,9},{9,8},{12,13},{13,12},{2,3},{3,2},{6... | collective-permute-start | bytes 98312 | tf_op jit(solution)/shard_map/ppermute | solution.py:350
  2.3 0.9 %collective-permute-done.other.refs_6_ = f32[32,256]{1,0:T(8,128)S(1)} collective-permute-done((f32[32,256]{1,0:T(8,128)S(1)}, f32[32,256]{1,0:T(8,128)S(1)}, u32[]{:S(2)}, u32[]{:S(2)}) %collective-permute-start) | collective-permute-done | bytes 32800 | tf_op jit(solution)/shard_map/ppermute | solution.py:350
  3.1 0.1 shard_map.131
  3.2 3.0 %collective-permute-start.1 = (f32[48,128]{1,0:T(8,128)S(1)}, f32[48,128]{1,0:T(8,128)S(1)}, u32[]{:S(2)}, u32[]{:S(2)}) collective-permute-start(f32[48,128]{1,0:T(8,128)S(1)} %get-tuple-element.28), channel_id=1, source_target_pairs={{0,4},{1,5},{4,0},{5,1},{8,12},{9,13},{12,8},{13,9},{2,6},{3,7},{6... | collective-permute-start | bytes 73736 | tf_op jit(solution)/shard_map/ppermute | solution.py:350
  6.2 1.0 %collective-permute-start.2 = (f32[16,128]{1,0:T(8,128)S(1)}, f32[16,128]{1,0:T(8,128)S(1)}, u32[]{:S(2)}, u32[]{:S(2)}) collective-permute-start(f32[16,128]{1,0:T(8,128)S(1)} %get-tuple-element.29), channel_id=1, source_target_pairs={{4,8},{8,4},{0,3},{12,15},{5,9},{9,5},{1,2},{13,14},{6,10},{10,6},... | collective-permute-start | bytes 24584 | tf_op jit(solution)/shard_map/ppermute | solution.py:365
  7.2 2.1 %collective-permute-done.2.refs_2_ = f32[16,128]{1,0:T(8,128)S(1)} collective-permute-done((f32[16,128]{1,0:T(8,128)S(1)}, f32[16,128]{1,0:T(8,128)S(1)}, u32[]{:S(2)}, u32[]{:S(2)}) %collective-permute-start.2) | collective-permute-done | bytes 8224 | tf_op jit(solution)/shard_map/ppermute | solution.py:365
  9.3 0.0 collective-permute-done.1.refs_1_.near_in
  9.3 0.5 %shard_map.132 = (f32[2,64,128]{2,1,0:T(8,128)S(1)}, f32[128,128]{1,0:T(8,128)S(1)}, f32[24,256]{1,0:T(8,128)S(1)}) custom-call(f32[216,128]{1,0:T(8,128)S(1)} %get-tuple-element.27.refs_0_, f32[48,128]{1,0:T(8,128)S(1)} %collective-permute-done.1.refs_1_.near_in, f32[16,128]{1,0:T(8,128)S(1)} %collective-permute-done.2.refs_2_, ...), custom_call_target="tpu_custom_call" | custom-call | tf_op jit(solution)/shard_map/pallas_call | solution.py:24
  9.9 1.6 %collective-permute-start.3 = (f32[128,128]{1,0:T(8,128)S(1)}, f32[128,128]{1,0:T(8,128)S(1)}, u32[]{:S(2)}, u32[]{:S(2)}) collective-permute-start(f32[128,128]{1,0:T(8,128)S(1)} %get-tuple-element.32.refs_0_), channel_id=1, source_target_pairs={{0,2},{2,0},{1,3},{3,1},{4,6},{6,4},{5,7},{7,5},{8,10},{10,8},{9,1... | collective-permute-start | bytes 196616 | tf_op jit(solution)/shard_map/ppermute | solution.py:370
  11.4 1.2 %collective-permute-start.4 = (f32[24,256]{1,0:T(8,128)S(1)}, f32[24,256]{1,0:T(8,128)S(1)}, u32[]{:S(2)}, u32[]{:S(2)}) collective-permute-start(f32[24,256]{1,0:T(8,128)S(1)} %get-tuple-element.37), channel_id=1, source_target_pairs={{0,9},{1,8},{4,13},{5,12},{8,1},{9,0},{12,5},{13,4},{2,11},{3,10},... | collective-permute-start | bytes 73736 | tf_op jit(solution)/shard_map/ppermute | solution.py:350
  12.6 0.3 shard_map.133
  12.9 2.7 %collective-permute-done.4.refs_6_ = f32[24,256]{1,0:T(8,128)S(1)} collective-permute-done((f32[24,256]{1,0:T(8,128)S(1)}, f32[24,256]{1,0:T(8,128)S(1)}, u32[]{:S(2)}, u32[]{:S(2)}) %collective-permute-start.4) | collective-permute-done | bytes 24608 | tf_op jit(solution)/shard_map/ppermute | solution.py:350
  15.6 0.0 collective-permute-done.3.refs_1_
  15.6 1.4 %shard_map.134 = (f32[64,128]{1,0:T(8,128)S(1)}, f32[8,256]{1,0:T(8,128)S(1)}, f32[8,256]{1,0:T(8,128)S(1)}, f32[8,256]{1,0:T(8,128)S(1)}, f32[8,256]{1,0:T(8,128)S(1)}) custom-call(f32[128,128]{1,0:T(8,128)S(1)} %get-tuple-element.32.refs_0_, f32[128,128]{1,0:T(8,128)S(1)} %collective-permute-done.3.refs_1_, f32[3,4,256]{2,1,0:T(4,128)S(1)} %get-tuple-element.33.refs_2_, ...), custom_call_target="tpu_custom_call" | custom-call | tf_op jit(solution)/shard_map/pallas_call | solution.py:24
  17.0 0.5 %collective-permute-start.6 = (f32[8,256]{1,0:T(8,128)S(1)}, f32[8,256]{1,0:T(8,128)S(1)}, u32[]{:S(2)}, u32[]{:S(2)}) collective-permute-start(f32[8,256]{1,0:T(8,128)S(1)} %get-tuple-element.41), channel_id=1, source_target_pairs={{0,5},{1,4},{4,1},{5,0},{8,13},{9,12},{12,9},{13,8},{2,7},{3,6},{6... | collective-permute-start | bytes 24584 | tf_op jit(solution)/shard_map/ppermute | solution.py:350
  17.5 3.0 %collective-permute-start.7 = (f32[8,256]{1,0:T(8,128)S(1)}, f32[8,256]{1,0:T(8,128)S(1)}, u32[]{:S(2)}, u32[]{:S(2)}) collective-permute-start(f32[8,256]{1,0:T(8,128)S(1)} %get-tuple-element.42), channel_id=1, source_target_pairs={{0,9},{1,8},{4,13},{5,12},{8,1},{9,0},{12,5},{13,4},{2,11},{3,10},... | collective-permute-start | bytes 24584 | tf_op jit(solution)/shard_map/ppermute | solution.py:350
  20.4 1.0 %collective-permute-start.8 = (f32[8,256]{1,0:T(8,128)S(1)}, f32[8,256]{1,0:T(8,128)S(1)}, u32[]{:S(2)}, u32[]{:S(2)}) collective-permute-start(f32[8,256]{1,0:T(8,128)S(1)} %get-tuple-element.43), channel_id=1, source_target_pairs={{0,13},{1,12},{4,9},{5,8},{8,5},{9,4},{12,1},{13,0},{2,15},{3,14},... | collective-permute-start | bytes 24584 | tf_op jit(solution)/shard_map/ppermute | solution.py:350
  21.4 0.5 %collective-permute-start.5 = (f32[64,128]{1,0:T(8,128)S(1)}, f32[64,128]{1,0:T(8,128)S(1)}, u32[]{:S(2)}, u32[]{:S(2)}) collective-permute-start(f32[64,128]{1,0:T(8,128)S(1)} %get-tuple-element.38.refs_0_), channel_id=1, source_target_pairs={{0,2},{2,0},{1,3},{3,1},{4,6},{6,4},{5,7},{7,5},{8,10},{10,8},{9,1... | collective-permute-start | bytes 98312 | tf_op jit(solution)/shard_map/ppermute | solution.py:370
  21.9 0.0 collective-permute-done.6
  21.9 0.0 collective-permute-done.7
  21.9 3.4 %collective-permute-done.8 = f32[8,256]{1,0:T(8,128)S(1)} collective-permute-done((f32[8,256]{1,0:T(8,128)S(1)}, f32[8,256]{1,0:T(8,128)S(1)}, u32[]{:S(2)}, u32[]{:S(2)}) %collective-permute-start.8) | collective-permute-done | bytes 8224 | tf_op jit(solution)/shard_map/ppermute | solution.py:350
  25.3 0.1 collective-permute-start.9
  25.4 1.1 %collective-permute-done.9.refs_5_ = f32[8,256]{1,0:T(8,128)S(1)} collective-permute-done((f32[8,256]{1,0:T(8,128)S(1)}, f32[8,256]{1,0:T(8,128)S(1)}, u32[]{:S(2)}, u32[]{:S(2)}) %collective-permute-start.9) | collective-permute-done | bytes 8224 | tf_op jit(solution)/shard_map/ppermute | solution.py:350
  26.5 0.0 collective-permute-done.5.refs_1_
  26.5 0.7 %shard_map.135 = (f32[2,64,128]{2,1,0:T(8,128)}, f32[1,256]{1,0:T(1,128)}, f32[1,256]{1,0:T(1,128)}) custom-call(f32[64,128]{1,0:T(8,128)S(1)} %get-tuple-element.38.refs_0_, f32[64,128]{1,0:T(8,128)S(1)} %collective-permute-done.5.refs_1_, f32[2,64,128]{2,1,0:T(8,128)S(1)} %get-tuple-element.39.refs_2_, f32[8,128]{1,0:T(8,128)S(1)} %get-tuple-element.31.refs_4_.refs_3_, ...), custom_call_target="tpu_custom_call" | custom-call | tf_op jit(solution)/shard_map/pallas_call | solution.py:24
  (1 shorter events, 0.0 us)
Async XLA Ops:
  1.7 1.4 %collective-permute-start = (f32[32,256]{1,0:T(8,128)S(1)}, f32[32,256]{1,0:T(8,128)S(1)}, u32[]{:S(2)}, u32[]{:S(2)}) collective-permute-start(f32[32,256]{1,0:T(8,128)S(1)} %get-tuple-element.25.msg.refs_5_), channel_id=1, source_target_pairs={{0,1},{1,0},{4,5},{5,4},{8,9},{9,8},{12,13},{13,12},{2,3},{3,2},{6... | collective-permute-start | bytes 98312 | tf_op jit(solution)/shard_map/ppermute | solution.py:350
  3.2 6.1 %collective-permute-start.1 = (f32[48,128]{1,0:T(8,128)S(1)}, f32[48,128]{1,0:T(8,128)S(1)}, u32[]{:S(2)}, u32[]{:S(2)}) collective-permute-start(f32[48,128]{1,0:T(8,128)S(1)} %get-tuple-element.28), channel_id=1, source_target_pairs={{0,4},{1,5},{4,0},{5,1},{8,12},{9,13},{12,8},{13,9},{2,6},{3,7},{6... | collective-permute-start | bytes 73736 | tf_op jit(solution)/shard_map/ppermute | solution.py:350
  6.2 3.1 %collective-permute-start.2 = (f32[16,128]{1,0:T(8,128)S(1)}, f32[16,128]{1,0:T(8,128)S(1)}, u32[]{:S(2)}, u32[]{:S(2)}) collective-permute-start(f32[16,128]{1,0:T(8,128)S(1)} %get-tuple-element.29), channel_id=1, source_target_pairs={{4,8},{8,4},{0,3},{12,15},{5,9},{9,5},{1,2},{13,14},{6,10},{10,6},... | collective-permute-start | bytes 24584 | tf_op jit(solution)/shard_map/ppermute | solution.py:365
  9.9 5.7 %collective-permute-start.3 = (f32[128,128]{1,0:T(8,128)S(1)}, f32[128,128]{1,0:T(8,128)S(1)}, u32[]{:S(2)}, u32[]{:S(2)}) collective-permute-start(f32[128,128]{1,0:T(8,128)S(1)} %get-tuple-element.32.refs_0_), channel_id=1, source_target_pairs={{0,2},{2,0},{1,3},{3,1},{4,6},{6,4},{5,7},{7,5},{8,10},{10,8},{9,1... | collective-permute-start | bytes 196616 | tf_op jit(solution)/shard_map/ppermute | solution.py:370
  11.4 4.2 %collective-permute-start.4 = (f32[24,256]{1,0:T(8,128)S(1)}, f32[24,256]{1,0:T(8,128)S(1)}, u32[]{:S(2)}, u32[]{:S(2)}) collective-permute-start(f32[24,256]{1,0:T(8,128)S(1)} %get-tuple-element.37), channel_id=1, source_target_pairs={{0,9},{1,8},{4,13},{5,12},{8,1},{9,0},{12,5},{13,4},{2,11},{3,10},... | collective-permute-start | bytes 73736 | tf_op jit(solution)/shard_map/ppermute | solution.py:350
  17.0 4.9 %collective-permute-start.6 = (f32[8,256]{1,0:T(8,128)S(1)}, f32[8,256]{1,0:T(8,128)S(1)}, u32[]{:S(2)}, u32[]{:S(2)}) collective-permute-start(f32[8,256]{1,0:T(8,128)S(1)} %get-tuple-element.41), channel_id=1, source_target_pairs={{0,5},{1,4},{4,1},{5,0},{8,13},{9,12},{12,9},{13,8},{2,7},{3,6},{6... | collective-permute-start | bytes 24584 | tf_op jit(solution)/shard_map/ppermute | solution.py:350
  17.5 4.5 %collective-permute-start.7 = (f32[8,256]{1,0:T(8,128)S(1)}, f32[8,256]{1,0:T(8,128)S(1)}, u32[]{:S(2)}, u32[]{:S(2)}) collective-permute-start(f32[8,256]{1,0:T(8,128)S(1)} %get-tuple-element.42), channel_id=1, source_target_pairs={{0,9},{1,8},{4,13},{5,12},{8,1},{9,0},{12,5},{13,4},{2,11},{3,10},... | collective-permute-start | bytes 24584 | tf_op jit(solution)/shard_map/ppermute | solution.py:350
  20.4 4.9 %collective-permute-start.8 = (f32[8,256]{1,0:T(8,128)S(1)}, f32[8,256]{1,0:T(8,128)S(1)}, u32[]{:S(2)}, u32[]{:S(2)}) collective-permute-start(f32[8,256]{1,0:T(8,128)S(1)} %get-tuple-element.43), channel_id=1, source_target_pairs={{0,13},{1,12},{4,9},{5,8},{8,5},{9,4},{12,1},{13,0},{2,15},{3,14},... | collective-permute-start | bytes 24584 | tf_op jit(solution)/shard_map/ppermute | solution.py:350
  21.4 5.1 %collective-permute-start.5 = (f32[64,128]{1,0:T(8,128)S(1)}, f32[64,128]{1,0:T(8,128)S(1)}, u32[]{:S(2)}, u32[]{:S(2)}) collective-permute-start(f32[64,128]{1,0:T(8,128)S(1)} %get-tuple-element.38.refs_0_), channel_id=1, source_target_pairs={{0,2},{2,0},{1,3},{3,1},{4,6},{6,4},{5,7},{7,5},{8,10},{10,8},{9,1... | collective-permute-start | bytes 98312 | tf_op jit(solution)/shard_map/ppermute | solution.py:370
  25.3 1.2 %collective-permute-start.9 = (f32[8,256]{1,0:T(8,128)S(1)}, f32[8,256]{1,0:T(8,128)S(1)}, u32[]{:S(2)}, u32[]{:S(2)}) collective-permute-start(f32[8,256]{1,0:T(8,128)S(1)} %add_add_fusion.refs_4_), channel_id=1, source_target_pairs={{0,1},{1,0},{4,5},{5,4},{8,9},{9,8},{12,13},{13,12},{2,3},{3,2},{6... | collective-permute-start | bytes 24584 | tf_op jit(solution)/shard_map/ppermute | solution.py:350

commit v5 on v4

--- a/solution.py
+++ b/solution.py
@@ -100,6 +100,16 @@
         out[at + len(rows) + i : at + len(rows) + i + 1, :] = row[:, cols:]
 
 
+def write_halves(out, at, x):
+    count, cols = x.shape[0], out.shape[1]
+    out[at : at + count, :] = x[:, :cols]
+    out[at + count : at + 2 * count, :] = x[:, cols:]
+
+
+def read_halves(ref, at, count):
+    return jnp.concatenate([ref[at : at + count, :], ref[at + count : at + 2 * count, :]], axis=1)
+
+
 def read_pairs(ref, at, count):
     return [
         jnp.concatenate([ref[at + i : at + i + 1, :], ref[at + count + i : at + count + i + 1, :]], axis=1)
@@ -170,14 +180,14 @@
 
 
 def diffuse_kernel(n, levels, *refs):
-    ext, near_in, edge_in, surface, share_rows, msg, other, adjoint_out, lev_out = refs[:9]
+    ext, near_in, edge_in, surface, share_rows, msg, other, marine, adjoint_out, lev_out = refs[:10]
     sub, tile = lax.axis_index("sub"), lax.axis_index("tile")
     rows, cols = surface.shape
     high = rows + 8
     fold = edge_in.shape[0]
     own_values = value_rows(n, msg, other, sub)
     near_values = read_pairs(near_in, fold, 10)[4:]
-    for i, out in enumerate(refs[9:]):
+    for i, out in enumerate(refs[10:]):
         air = table_rows(n, msg, other, tile ^ (2 * i + 2), 1 - sub, sub) + own_values
         air += read_pairs(near_in, fold + 20 + 8 * i, 4) + near_values
         for at, row in enumerate(air):
@@ -219,6 +229,8 @@
         heat += share_rows[z : z + 1, :] * adjoint
     lev_out[0:rows, :] = surface[...]
     lev_out[rows : 2 * rows, :] = own_wet * heat
+    if lev_out.shape[0] > 2 * rows:
+        write_halves(lev_out, 2 * rows, marine[...].astype(F32))
 
 
 def bulk_adjoint(warmth_gap, flux_sens):
@@ -267,23 +279,23 @@
     look_up(read_pairs(near_in, fold, 10), 2, picks, tables)
 
 
-def slot_kernel(n, count, *refs):
+def slot_kernel(n, count, rows, *refs):
     lev_parts, refs = refs[:count], refs[count:]
     near_picks, near_tables, marine, weight = refs[:4]
     far_in, refs = refs[4 : 3 + n // 2], refs[3 + n // 2 :]
-    slots_out, returns, (held, picks, tables) = refs[0], refs[1 : 1 + n], refs[1 + n :]
-    tile = lax.axis_index("tile")
+    values_out, chip_out, returns = refs[0], refs[1], refs[2 : 2 + n]
+    held, picks, tables = refs[2 + n :]
+    sub, tile = lax.axis_index("sub"), lax.axis_index("tile")
+    cols = chip_out.shape[1]
     picks[:, 0:4, :] = near_picks[...]
     for i, ref in enumerate(far_in):
         for j in range(2):
             air = [ref[10 * j + k : 10 * j + k + 1, :] for k in range(10)]
             look_up(air, 4 * i + 4 + 2 * j, picks, tables)
-    rows, cols = slots_out.shape
     table = jnp.concatenate(
         [sum(ref[rows * i : rows * (i + 1), :] for ref in lev_parts) for i in range(2)], axis=1
     )
     table = jnp.concatenate(halves(table), axis=0)
-    owners = []
     for step in range(n):
         for band in range(2):
             at, place = 2 * step + band, 2 * (tile ^ step) + band
@@ -296,7 +308,6 @@
                 piece = jnp.where(col_mask, spread[cols * i : cols * (i + 1)], 0.0)
                 held[i, at : at + 1, :] = jnp.sum(piece, axis=0, keepdims=True)
             held[2, at : at + 1, :] = weight[pl.ds(place, 1), :]
-            owners.append((row_hot, col_mask))
 
     difference = held[0] - picks[0]
     wind = picks[1]
@@ -304,35 +315,93 @@
     contrast_sens = bulk_adjoint(wind * difference, flux_sens)
     surface_sens = contrast_sens * wind
     wind_sens = contrast_sens * difference
+    values_out[...] = surface_sens
+    for step in range(n):
+        for band in range(2):
+            at = 2 * step + band
+            hot = near_tables[at] if at < 4 else tables[at]
+            values = jnp.concatenate([surface_sens[at : at + 1], wind_sens[at : at + 1]], axis=0)
+            sums = dot(jnp.concatenate(halves(values), axis=0), hot, 1, 1)
+            sums = sums[0:2] + sums[2:4]
+            returns[step][2 * band : 2 * band + 2, :] = sums[:, :cols]
+            returns[step][2 * band + 4 : 2 * band + 6, :] = sums[:, cols:]
+    if n == 4:
+        chip_out[0:8, :] = jnp.where(sub == 0, returns[2][...], returns[1][...])
+        write_halves(chip_out, 8, surface_sens)
+        chip_out[8:16, :] = jnp.where(sub == 0, returns[3][...], chip_out[8:16, :])
+        chip_out[24:40, :] = lev_parts[-1][2 * rows : 2 * rows + 16, :]
+
+
+def scatter(n, rows, cols, tile, cell_of, value_of):
     total = jnp.zeros((rows, 2 * cols), F32)
     for step in range(n):
         for band in range(2):
-            at = 2 * step + band
-            row_hot, col_mask = owners[at]
-            ocean = surface_sens[at : at + 1]
+            cell = cell_of(2 * (tile ^ step) + band)
+            row, col = cell // cols, lax.rem(cell, cols)
+            col_mask = lax.broadcasted_iota(jnp.int32, (cols, cell.shape[1]), 0) == col
+            value = value_of(2 * step + band)
             spread = jnp.concatenate(
-                [jnp.where(col_mask, x.astype(F32), 0.0).astype(BF16) for x in halves(ocean)], axis=0
+                [jnp.where(col_mask, x.astype(F32), 0.0).astype(BF16) for x in halves(value)], axis=0
             )
-            total += dot(row_hot, spread, 1, 1)
-            hot = near_tables[at] if at < 4 else tables[at]
-            values = jnp.concatenate([ocean, wind_sens[at : at + 1]], axis=0)
-            sums = dot(jnp.concatenate(halves(values), axis=0), hot, 1, 1)
-            returns[step][2 * band : 2 * band + 2, :] = sums[0:2] + sums[2:4]
-        returns[step][4:8, :] = jnp.zeros((4, returns[step].shape[1]), F32)
-    slots_out[...] = total[:, :cols] + total[:, cols:]
-
-
-def final_kernel(count, *refs):
-    slots = refs[:count]
-    adjoint, share_rows, sums, other, state_out, air_out, wind_out, state, air, wind, sems = refs[count:]
+            total += dot(onehot(row, rows), spread, 1, 1)
+    return total[:, :cols] + total[:, cols:]
+
+
+def own_kernel(n, marine, values, out):
+    tile = lax.axis_index("tile")
+    rows, cols = out.shape
+    out[...] = scatter(
+        n, rows, cols, tile, lambda i: marine[pl.ds(i, 1), :], lambda i: values[i : i + 1, :]
+    )
+
+
+def post_kernel(n, first, second, own, slots, lev_in, theirs, gradient, out, cells, values):
+    even = lax.axis_index("sub") == 0
+    tile = lax.axis_index("tile")
+    rows, cols = gradient.shape
+    out[0:8, :] = first[0:8, :] + own[...] + jnp.where(even, 0.0, second[0:8, :])
+
+    @pl.when(even)
+    def _():
+        for band, (ref, at) in enumerate(((lev_in, 2 * rows), (theirs, 24))):
+            cells[...] = read_halves(ref, at, 2 * n).astype(jnp.int32)
+            values[...] = read_halves(second, 4 * n * band, 2 * n)
+            total = scatter(
+                n, rows, cols, tile, lambda i: cells[pl.ds(i, 1), :], lambda i: values[i : i + 1, :]
+            )
+            if band == 0:
+                gradient[...] = slots[...] + total
+            else:
+                out[8 : rows + 8, :] = total
+
+    @pl.when(jnp.logical_not(even))
+    def _():
+        gradient[...] = slots[...]
+        out[8 : rows + 8, :] = jnp.zeros_like(slots)
+
+
+def merge_kernel(values, near, two, three, theirs, first, second):
+    even = lax.axis_index("sub") == 0
+    first[...] = jnp.zeros_like(first)
+    first[0:8, :] = jnp.where(even, near[...] + theirs[0:8, :], three[...] + theirs[8:16, :])
+    write_halves(second, 0, values[...])
+    second[0:8, :] = jnp.where(even, second[0:8, :], two[...] + theirs[0:8, :])
+    second[16:32, :] = theirs[8:24, :]
+
+
+def final_kernel(merged, slots, adjoint, share_rows, sums, other, *refs):
+    state_out, air_out, wind_out, state, air, wind, sems = refs
     sub = lax.axis_index("sub")
-    gradient = sum(ref[...] for ref in slots)
+    gradient = slots[...]
+    if merged:
+        gradient += jnp.where(sub == 0, 0.0, other[8 : slots.shape[0] + 8, :])
     for z in range(adjoint.shape[0]):
         state[z] = adjoint[z] + share_rows[z : z + 1, :] * gradient
     copies = [pltpu.make_async_copy(state, state_out, sems.at[0])]
     copies[0].start()
-    both = sums[...] + other[...]
-    own = jnp.where(sub == 0, both[0:2], both[2:4])
+    both = sums[0:8, :] + other[0:8, :]
+    own = [jnp.where(sub == 0, both[i : i + 2], both[i + 2 : i + 4]) for i in (0, 4)]
+    own = jnp.concatenate(own, axis=1)
     air[...] = -own[0:1]
     wind[...] = own[1:2]
     for i, (a, b) in enumerate(((air, air_out), (wind, wind_out))):
@@ -362,6 +431,17 @@
             for t in range(1, n - 1, 2):
                 pairs += [(place(t, l, s), place(t + 1, l, s)), (place(t + 1, l, s), place(t, l, s))]
             pairs += [(place(t, l, s), place(t, l ^ 1, s ^ 1)) for t in (0, n - 1)]
+    return lax.ppermute(x, ("tile", "lev", "sub"), pairs)
+
+
+def by_core(x, even, odd):
+    n, levs, bands = (lax.axis_size(axis) for axis in ("tile", "lev", "sub"))
+    pairs = []
+    for t in range(n):
+        for l in range(levs):
+            for s in range(bands):
+                tx, lx = odd if s else even
+                pairs.append(((t * levs + l) * bands + s, ((t ^ tx) * levs + (l ^ lx)) * bands + s))
     return lax.ppermute(x, ("tile", "lev", "sub"), pairs)
 
 
@@ -384,7 +464,7 @@
     marine_result_adjoint,
     energy_transport_adjoint,
 ):
-    n = lax.axis_size("tile")
+    n, levs = lax.axis_size("tile"), lax.axis_size("lev")
     levels, rows, cols = marine_layered_warmth.shape
     cells = bottom_sky_warmth.shape[0]
     high = rows + 8
@@ -415,10 +495,11 @@
     )
     edge_in = beyond(edge_out)
     near_in = traded(near_out, 1)
+    merged = n == 4 and levs == 2
     adjoint, lev_msg, *far_out = call(
         functools.partial(diffuse_kernel, n, levels),
-        [(levels, rows, cols), (2 * rows, cols)] + [(24, cells)] * (n // 2 - 1),
-        [ext, near_in, edge_in, surface, share_rows, msg, other],
+        [(levels, rows, cols), (2 * rows + (16 if merged else 0), cols)] + [(24, cells)] * (n // 2 - 1),
+        [ext, near_in, edge_in, surface, share_rows, msg, other, marine],
     )
     lev_in = lev_parts(lev_msg)
     far_in = [traded(x, 2 * i + 2, 1) for i, x in enumerate(far_out)]
@@ -427,24 +508,37 @@
         [(3, 4, cells), jax.ShapeDtypeStruct((4, cells, cells), BF16)],
         [msg, other, near_in],
     )
-    slots, *returns = call(
-        functools.partial(slot_kernel, n, len(lev_in)),
-        [(rows, cols)] + [(8, cells)] * n,
+    values, chip, *returns = call(
+        functools.partial(slot_kernel, n, len(lev_in), rows),
+        [(2 * n, cells), (40, cols)] + [(8, cols)] * n,
         [*lev_in, picks, tables, marine, marine_weight, *far_in],
         scratch=[pltpu.VMEM((3, 2 * n, cells), F32)] * 2
         + [pltpu.VMEM((2 * n, cells, cells), BF16)],
     )
-    back = [traded(returns[step], step, 1) for step in range(1, n)]
-    slot_parts = lev_parts(slots)
-    sums = returns[0]
-    for x in back:
-        sums = sums + x
-    sums_far = traded(sums, 0, 1)
+    (slots,) = call(functools.partial(own_kernel, n), [(rows, cols)], [marine, values])
+    if merged:
+        theirs = traded(chip, 0, 1)
+        first, second = call(
+            merge_kernel, [(32, cols), (32, cols)], [values, *returns[1:], theirs]
+        )
+        first = by_core(first, (1, 0), (3, 0))
+        second = by_core(second, (0, 1), (2, 0))
+        gradient, sums = call(
+            functools.partial(post_kernel, n),
+            [(rows, cols), (rows + 8, cols)],
+            [first, second, returns[0], slots, lev_in[1], theirs],
+            scratch=[pltpu.VMEM((2 * n, cells), jnp.int32), pltpu.VMEM((2 * n, cells), F32)],
+        )
+    else:
+        gradient = sum(lev_parts(slots))
+        sums = returns[0]
+        for step in range(1, n):
+            sums = sums + traded(returns[step], step, 1)
     results = [(levels, rows, cols), (1, cells), (1, cells)]
     state, air_gradient, wind_gradient = call(
-        functools.partial(final_kernel, len(slot_parts)),
+        functools.partial(final_kernel, merged),
         results,
-        [*slot_parts, adjoint, share_rows, sums, sums_far],
+        [gradient, adjoint, share_rows, sums, traded(sums, 0, 1)],
         out_specs=[HBM] * 3,
         scratch=[pltpu.VMEM(x, F32) for x in results] + [pltpu.SemaphoreType.DMA((3,))],
     )

time: 27.3 us -> 26.2 us (0.960)
  starting transfers between devices: 12.3 us -> 10.3 us
  Pallas kernels: 4.1 us -> 4.99 us
    ppermute x7 -> x5, starting transfers between devices: 9.21 us -> 5.81 us  [traded(): return lax.ppermute(x, ('tile', 'sub'), pairs)]
    ppermute x0 -> x2, waiting for transfers between devices: none -> 2.73 us  [by_core(): return lax.ppermute(x, ('tile', 'lev', 'sub'), pairs)]
    ppermute x7 -> x5, waiting for transfers between devices: 7.99 us -> 5.27 us  [traded(): return lax.ppermute(x, ('tile', 'sub'), pairs)]
    ppermute x0 -> x2, starting transfers between devices: none -> 1.95 us  [by_core(): return lax.ppermute(x, ('tile', 'lev', 'sub'), pairs)]
    pallas_call x6 -> x9, Pallas kernels: 4.1 us -> 4.99 us  [call(): pl.pallas_call(kernel, out_shape=outs, in_specs=specs or [VMEM] * len(ope...]
    ppermute x2 -> x1, starting transfers between devices: 2.09 us -> 1.56 us  [lev_parts(): return [x, lax.ppermute(x, 'lev', [(0, 1), (1, 0)])]]
  transfers between devices with their start and end apart: 10 -> 9, of which waited for: 5 -> 7; matrix products, arithmetic and copies ran while one was open for 0% -> 0% of each run, Pallas kernels for 1% -> 3%
where the time goes in v5:
time: 26.2 us; the launch traced here: 26.1 us
  starting transfers between devices  10.3 us (39%)
  waiting for transfers between devices  10.1 us (39%)
  Pallas kernels  4.99 us (19%)
  between operations  0.67 us (3%)
    ppermute x5, starting transfers between devices, traded(): return lax.ppermute(x, ('tile', 'sub'), pairs)  5.81 us
    ppermute x5, waiting for transfers between devices, traded(): return lax.ppermute(x, ('tile', 'sub'), pairs)  5.27 us
    pallas_call x9, Pallas kernels, call(): pl.pallas_call(kernel, out_shape=outs, in_specs=specs or [VMEM] * len(ope...  4.99 us
    ppermute x2, waiting for transfers between devices, by_core(): return lax.ppermute(x, ('tile', 'lev', 'sub'), pairs)  2.73 us
    ppermute x1, waiting for transfers between devices, beyond(): return lax.ppermute(x, ('tile', 'lev', 'sub'), pairs)  2.12 us
    ppermute x2, starting transfers between devices, by_core(): return lax.ppermute(x, ('tile', 'lev', 'sub'), pairs)  1.95 us
    ppermute x1, starting transfers between devices, lev_parts(): return [x, lax.ppermute(x, 'lev', [(0, 1), (1, 0)])]  1.56 us
    ppermute x1, starting transfers between devices, beyond(): return lax.ppermute(x, ('tile', 'lev', 'sub'), pairs)  0.98 us
  transfers between devices with their start and end apart: 9, of which 7 were waited for; matrix products, arithmetic and copies ran while one was open for 0% of the time, Pallas kernels for 3%

profile of v5, /device:TPU:0, one launch (start us, length us, event | category | flops | bytes accessed | tf_op | source)
XLA Modules:
  0.0 26.1 jit_solution(6964376725069108352)
XLA Ops:
  0.6 1.1 %shard_map.130 = (f32[32,256]{1,0:T(8,128)S(1)}, f32[216,128]{1,0:T(8,128)S(1)}, f32[64,128]{1,0:T(8,128)S(1)}, f32[8,128]{1,0:T(8,128)S(1)}, s32[8,256]{1,0:T(8,128)S(1)}, /*index=5*/f32[8,256]{1,0:T(8,128)S(1)}) custom-call(f32[2,64,128]{2,1,0:T(8,128)} %refs_0_.1, f32[2,64,128]{2,1,0:T(8,128)} %refs_1_.1, s32[64,128]{1,0:T(8,128)} %refs_2_.1, f32[2]{0:T(128)} %refs_3_.1, ...), custom_call_target="tpu_custom_call" | custom-call | tf_op jit(solution)/shard_map/pallas_call | solution.py:24
  1.7 0.5 %collective-permute-start = (f32[32,256]{1,0:T(8,128)S(1)}, f32[32,256]{1,0:T(8,128)S(1)}, u32[]{:S(2)}, u32[]{:S(2)}) collective-permute-start(f32[32,256]{1,0:T(8,128)S(1)} %get-tuple-element.30.msg.refs_5_), channel_id=1, source_target_pairs={{0,1},{1,0},{4,5},{5,4},{8,9},{9,8},{12,13},{13,12},{2,3},{3,2},{6... | collective-permute-start | bytes 98312 | tf_op jit(solution)/shard_map/ppermute | solution.py:419
  2.3 0.9 %collective-permute-done.other.refs_6_ = f32[32,256]{1,0:T(8,128)S(1)} collective-permute-done((f32[32,256]{1,0:T(8,128)S(1)}, f32[32,256]{1,0:T(8,128)S(1)}, u32[]{:S(2)}, u32[]{:S(2)}) %collective-permute-start) | collective-permute-done | bytes 32800 | tf_op jit(solution)/shard_map/ppermute | solution.py:419
  3.1 0.1 shard_map.131
  3.2 3.0 %collective-permute-start.1 = (f32[48,128]{1,0:T(8,128)S(1)}, f32[48,128]{1,0:T(8,128)S(1)}, u32[]{:S(2)}, u32[]{:S(2)}) collective-permute-start(f32[48,128]{1,0:T(8,128)S(1)} %get-tuple-element.33), channel_id=1, source_target_pairs={{0,4},{1,5},{4,0},{5,1},{8,12},{9,13},{12,8},{13,9},{2,6},{3,7},{6... | collective-permute-start | bytes 73736 | tf_op jit(solution)/shard_map/ppermute | solution.py:419
  6.2 1.0 %collective-permute-start.2 = (f32[16,128]{1,0:T(8,128)S(1)}, f32[16,128]{1,0:T(8,128)S(1)}, u32[]{:S(2)}, u32[]{:S(2)}) collective-permute-start(f32[16,128]{1,0:T(8,128)S(1)} %get-tuple-element.34), channel_id=1, source_target_pairs={{4,8},{8,4},{0,3},{12,15},{5,9},{9,5},{1,2},{13,14},{6,10},{10,6},... | collective-permute-start | bytes 24584 | tf_op jit(solution)/shard_map/ppermute | solution.py:434
  7.2 2.1 %collective-permute-done.2.refs_2_ = f32[16,128]{1,0:T(8,128)S(1)} collective-permute-done((f32[16,128]{1,0:T(8,128)S(1)}, f32[16,128]{1,0:T(8,128)S(1)}, u32[]{:S(2)}, u32[]{:S(2)}) %collective-permute-start.2) | collective-permute-done | bytes 8224 | tf_op jit(solution)/shard_map/ppermute | solution.py:434
  9.3 0.0 collective-permute-done.1.refs_1_.near_in
  9.3 0.5 %shard_map.132 = (f32[2,64,128]{2,1,0:T(8,128)S(1)}, f32[144,128]{1,0:T(8,128)S(1)}, f32[24,256]{1,0:T(8,128)S(1)}) custom-call(f32[216,128]{1,0:T(8,128)S(1)} %get-tuple-element.32.refs_0_, f32[48,128]{1,0:T(8,128)S(1)} %collective-permute-done.1.refs_1_.near_in, f32[16,128]{1,0:T(8,128)S(1)} %collective-permute-done.2.refs_2_, ...), custom_call_target="tpu_custom_call" | custom-call | tf_op jit(solution)/shard_map/pallas_call | solution.py:24
  9.9 1.6 %collective-permute-start.3 = (f32[144,128]{1,0:T(8,128)S(1)}, f32[144,128]{1,0:T(8,128)S(1)}, u32[]{:S(2)}, u32[]{:S(2)}) collective-permute-start(f32[144,128]{1,0:T(8,128)S(1)} %get-tuple-element.38.refs_0_), channel_id=1, source_target_pairs={{0,2},{2,0},{1,3},{3,1},{4,6},{6,4},{5,7},{7,5},{8,10},{10,8},{9,1... | collective-permute-start | bytes 221192 | tf_op jit(solution)/shard_map/ppermute | solution.py:450
  11.4 1.2 %collective-permute-start.4 = (f32[24,256]{1,0:T(8,128)S(1)}, f32[24,256]{1,0:T(8,128)S(1)}, u32[]{:S(2)}, u32[]{:S(2)}) collective-permute-start(f32[24,256]{1,0:T(8,128)S(1)} %get-tuple-element.42), channel_id=1, source_target_pairs={{0,9},{1,8},{4,13},{5,12},{8,1},{9,0},{12,5},{13,4},{2,11},{3,10},... | collective-permute-start | bytes 73736 | tf_op jit(solution)/shard_map/ppermute | solution.py:419
  12.6 0.3 shard_map.133
  12.9 2.7 %collective-permute-done.4.refs_6_ = f32[24,256]{1,0:T(8,128)S(1)} collective-permute-done((f32[24,256]{1,0:T(8,128)S(1)}, f32[24,256]{1,0:T(8,128)S(1)}, u32[]{:S(2)}, u32[]{:S(2)}) %collective-permute-start.4) | collective-permute-done | bytes 24608 | tf_op jit(solution)/shard_map/ppermute | solution.py:419
  15.6 0.0 collective-permute-done.3.refs_1_.lev_in
  15.6 1.0 %shard_map.134 = (f32[8,256]{1,0:T(8,128)S(1)}, f32[40,128]{1,0:T(8,128)S(1)}, f32[8,128]{1,0:T(8,128)S(1)}, f32[8,128]{1,0:T(8,128)S(1)}, f32[8,128]{1,0:T(8,128)S(1)}, /*index=5*/f32[8,128]{1,0:T(8,128)S(1)}) custom-call(f32[144,128]{1,0:T(8,128)S(1)} %get-tuple-element.38.refs_0_, f32[144,128]{1,0:T(8,128)S(1)} %collective-permute-done.3.refs_1_.lev_in, ...), custom_call_target="tpu_custom_call" | custom-call | tf_op jit(solution)/shard_map/pallas_call | solution.py:24
  16.6 0.6 %collective-permute-start.5 = (f32[40,128]{1,0:T(8,128)S(1)}, f32[40,128]{1,0:T(8,128)S(1)}, u32[]{:S(2)}, u32[]{:S(2)}) collective-permute-start(f32[40,128]{1,0:T(8,128)S(1)} %get-tuple-element.47), channel_id=1, source_target_pairs={{0,1},{1,0},{4,5},{5,4},{8,9},{9,8},{12,13},{13,12},{2,3},{3,2},{6... | collective-permute-start | bytes 61448 | tf_op jit(solution)/shard_map/ppermute | solution.py:419
  17.2 0.8 %collective-permute-done.5.theirs = f32[40,128]{1,0:T(8,128)S(1)} collective-permute-done((f32[40,128]{1,0:T(8,128)S(1)}, f32[40,128]{1,0:T(8,128)S(1)}, u32[]{:S(2)}, u32[]{:S(2)}) %collective-permute-start.5) | collective-permute-done | bytes 20512 | tf_op jit(solution)/shard_map/ppermute | solution.py:419
  18.1 1.4 %collective-permute-start.6 = (f32[32,128]{1,0:T(8,128)S(1)}, f32[32,128]{1,0:T(8,128)S(1)}, u32[]{:S(2)}, u32[]{:S(2)}) collective-permute-start(f32[32,128]{1,0:T(8,128)S(1)} %get-tuple-element.48), channel_id=1, source_target_pairs={{0,4},{1,13},{2,6},{3,15},{4,0},{5,9},{6,2},{7,11},{8,12},{9,5},{1... | collective-permute-start | bytes 49160 | tf_op jit(solution)/shard_map/ppermute | solution.py:445
  19.5 0.5 %collective-permute-start.7 = (f32[32,128]{1,0:T(8,128)S(1)}, f32[32,128]{1,0:T(8,128)S(1)}, u32[]{:S(2)}, u32[]{:S(2)}) collective-permute-start(f32[32,128]{1,0:T(8,128)S(1)} %get-tuple-element.49), channel_id=1, source_target_pairs={{0,2},{1,9},{2,0},{3,11},{4,6},{5,13},{6,4},{7,15},{8,10},{9,1},{1... | collective-permute-start | bytes 49160 | tf_op jit(solution)/shard_map/ppermute | solution.py:445
  20.0 0.5 %shard_map.136.slots = f32[64,128]{1,0:T(8,128)S(1)} custom-call(s32[8,256]{1,0:T(8,128)S(1)} %get-tuple-element.37.refs_7_.refs_4_.marine, f32[8,256]{1,0:T(8,128)S(1)} %get-tuple-element.43.values), custom_call_target="tpu_custom_call" | custom-call | tf_op jit(solution)/shard_map/pallas_call | solution.py:24
  20.5 1.3 %collective-permute-done.6.first = f32[32,128]{1,0:T(8,128)S(1)} collective-permute-done((f32[32,128]{1,0:T(8,128)S(1)}, f32[32,128]{1,0:T(8,128)S(1)}, u32[]{:S(2)}, u32[]{:S(2)}) %collective-permute-start.6) | collective-permute-done | bytes 16416 | tf_op jit(solution)/shard_map/ppermute | solution.py:445
  21.8 1.4 %collective-permute-done.7.second = f32[32,128]{1,0:T(8,128)S(1)} collective-permute-done((f32[32,128]{1,0:T(8,128)S(1)}, f32[32,128]{1,0:T(8,128)S(1)}, u32[]{:S(2)}, u32[]{:S(2)}) %collective-permute-start.7) | collective-permute-done | bytes 16416 | tf_op jit(solution)/shard_map/ppermute | solution.py:445
  23.3 0.8 %shard_map.137 = (f32[64,128]{1,0:T(8,128)S(1)}, f32[72,128]{1,0:T(8,128)S(1)}) custom-call(f32[32,128]{1,0:T(8,128)S(1)} %collective-permute-done.6.first, f32[32,128]{1,0:T(8,128)S(1)} %collective-permute-done.7.second, f32[8,128]{1,0:T(8,128)S(1)} %get-tuple-element.50.own, f32[64,128]{1,0:T(8,128)S(1)} %shard_map.136.slots, ...), custom_call_target="tpu_custom_call" | custom-call | tf_op jit(solution)/shard_map/pallas_call | solution.py:24
  24.0 0.5 %collective-permute-start.8 = (f32[72,128]{1,0:T(8,128)S(1)}, f32[72,128]{1,0:T(8,128)S(1)}, u32[]{:S(2)}, u32[]{:S(2)}) collective-permute-start(f32[72,128]{1,0:T(8,128)S(1)} %get-tuple-element.53.sums), channel_id=1, source_target_pairs={{0,1},{1,0},{4,5},{5,4},{8,9},{9,8},{12,13},{13,12},{2,3},{3,2},{6... | collective-permute-start | bytes 110600 | tf_op jit(solution)/shard_map/ppermute | solution.py:419
  24.5 0.9 %collective-permute-done.8.other = f32[72,128]{1,0:T(8,128)S(1)} collective-permute-done((f32[72,128]{1,0:T(8,128)S(1)}, f32[72,128]{1,0:T(8,128)S(1)}, u32[]{:S(2)}, u32[]{:S(2)}) %collective-permute-start.8) | collective-permute-done | bytes 36896 | tf_op jit(solution)/shard_map/ppermute | solution.py:419
  25.4 0.7 %shard_map.138 = (f32[2,64,128]{2,1,0:T(8,128)}, f32[1,256]{1,0:T(1,128)}, f32[1,256]{1,0:T(1,128)}) custom-call(f32[64,128]{1,0:T(8,128)S(1)} %get-tuple-element.51.slots, f32[2,64,128]{2,1,0:T(8,128)S(1)} %get-tuple-element.52.adjoint, f32[8,128]{1,0:T(8,128)S(1)} %get-tuple-element.36.refs_4_.share_rows, f32[72,128]{1,0:T(8,128)S(1)} %get-tuple-element.53.sums, ...), custom_call_target="tpu_custom_call" | custom-call | tf_op jit(solution)/shard_map/pallas_call | solution.py:24
  (1 shorter events, 0.0 us)
Async XLA Ops:
  1.7 1.4 %collective-permute-start = (f32[32,256]{1,0:T(8,128)S(1)}, f32[32,256]{1,0:T(8,128)S(1)}, u32[]{:S(2)}, u32[]{:S(2)}) collective-permute-start(f32[32,256]{1,0:T(8,128)S(1)} %get-tuple-element.30.msg.refs_5_), channel_id=1, source_target_pairs={{0,1},{1,0},{4,5},{5,4},{8,9},{9,8},{12,13},{13,12},{2,3},{3,2},{6... | collective-permute-start | bytes 98312 | tf_op jit(solution)/shard_map/ppermute | solution.py:419
  3.2 6.1 %collective-permute-start.1 = (f32[48,128]{1,0:T(8,128)S(1)}, f32[48,128]{1,0:T(8,128)S(1)}, u32[]{:S(2)}, u32[]{:S(2)}) collective-permute-start(f32[48,128]{1,0:T(8,128)S(1)} %get-tuple-element.33), channel_id=1, source_target_pairs={{0,4},{1,5},{4,0},{5,1},{8,12},{9,13},{12,8},{13,9},{2,6},{3,7},{6... | collective-permute-start | bytes 73736 | tf_op jit(solution)/shard_map/ppermute | solution.py:419
  6.2 3.1 %collective-permute-start.2 = (f32[16,128]{1,0:T(8,128)S(1)}, f32[16,128]{1,0:T(8,128)S(1)}, u32[]{:S(2)}, u32[]{:S(2)}) collective-permute-start(f32[16,128]{1,0:T(8,128)S(1)} %get-tuple-element.34), channel_id=1, source_target_pairs={{4,8},{8,4},{0,3},{12,15},{5,9},{9,5},{1,2},{13,14},{6,10},{10,6},... | collective-permute-start | bytes 24584 | tf_op jit(solution)/shard_map/ppermute | solution.py:434
  9.9 5.7 %collective-permute-start.3 = (f32[144,128]{1,0:T(8,128)S(1)}, f32[144,128]{1,0:T(8,128)S(1)}, u32[]{:S(2)}, u32[]{:S(2)}) collective-permute-start(f32[144,128]{1,0:T(8,128)S(1)} %get-tuple-element.38.refs_0_), channel_id=1, source_target_pairs={{0,2},{2,0},{1,3},{3,1},{4,6},{6,4},{5,7},{7,5},{8,10},{10,8},{9,1... | collective-permute-start | bytes 221192 | tf_op jit(solution)/shard_map/ppermute | solution.py:450
  11.4 4.2 %collective-permute-start.4 = (f32[24,256]{1,0:T(8,128)S(1)}, f32[24,256]{1,0:T(8,128)S(1)}, u32[]{:S(2)}, u32[]{:S(2)}) collective-permute-start(f32[24,256]{1,0:T(8,128)S(1)} %get-tuple-element.42), channel_id=1, source_target_pairs={{0,9},{1,8},{4,13},{5,12},{8,1},{9,0},{12,5},{13,4},{2,11},{3,10},... | collective-permute-start | bytes 73736 | tf_op jit(solution)/shard_map/ppermute | solution.py:419
  16.6 1.5 %collective-permute-start.5 = (f32[40,128]{1,0:T(8,128)S(1)}, f32[40,128]{1,0:T(8,128)S(1)}, u32[]{:S(2)}, u32[]{:S(2)}) collective-permute-start(f32[40,128]{1,0:T(8,128)S(1)} %get-tuple-element.47), channel_id=1, source_target_pairs={{0,1},{1,0},{4,5},{5,4},{8,9},{9,8},{12,13},{13,12},{2,3},{3,2},{6... | collective-permute-start | bytes 61448 | tf_op jit(solution)/shard_map/ppermute | solution.py:419
  18.1 3.7 %collective-permute-start.6 = (f32[32,128]{1,0:T(8,128)S(1)}, f32[32,128]{1,0:T(8,128)S(1)}, u32[]{:S(2)}, u32[]{:S(2)}) collective-permute-start(f32[32,128]{1,0:T(8,128)S(1)} %get-tuple-element.48), channel_id=1, source_target_pairs={{0,4},{1,13},{2,6},{3,15},{4,0},{5,9},{6,2},{7,11},{8,12},{9,5},{1... | collective-permute-start | bytes 49160 | tf_op jit(solution)/shard_map/ppermute | solution.py:445
  19.5 3.7 %collective-permute-start.7 = (f32[32,128]{1,0:T(8,128)S(1)}, f32[32,128]{1,0:T(8,128)S(1)}, u32[]{:S(2)}, u32[]{:S(2)}) collective-permute-start(f32[32,128]{1,0:T(8,128)S(1)} %get-tuple-element.49), channel_id=1, source_target_pairs={{0,2},{1,9},{2,0},{3,11},{4,6},{5,13},{6,4},{7,15},{8,10},{9,1},{1... | collective-permute-start | bytes 49160 | tf_op jit(solution)/shard_map/ppermute | solution.py:445
  24.0 1.4 %collective-permute-start.8 = (f32[72,128]{1,0:T(8,128)S(1)}, f32[72,128]{1,0:T(8,128)S(1)}, u32[]{:S(2)}, u32[]{:S(2)}) collective-permute-start(f32[72,128]{1,0:T(8,128)S(1)} %get-tuple-element.53.sums), channel_id=1, source_target_pairs={{0,1},{1,0},{4,5},{5,4},{8,9},{9,8},{12,13},{13,12},{2,3},{3,2},{6... | collective-permute-start | bytes 110600 | tf_op jit(solution)/shard_map/ppermute | solution.py:419

commit v6 on v5

--- a/solution.py
+++ b/solution.py
@@ -292,20 +292,18 @@
         for j in range(2):
             air = [ref[10 * j + k : 10 * j + k + 1, :] for k in range(10)]
             look_up(air, 4 * i + 4 + 2 * j, picks, tables)
-    table = jnp.concatenate(
-        [sum(ref[rows * i : rows * (i + 1), :] for ref in lev_parts) for i in range(2)], axis=1
-    )
-    table = jnp.concatenate(halves(table), axis=0)
+    table = sum(ref[0 : 2 * rows, :] for ref in lev_parts)
+    table = jnp.concatenate(halves(table), axis=1)
     for step in range(n):
         for band in range(2):
             at, place = 2 * step + band, 2 * (tile ^ step) + band
             cell = marine[pl.ds(place, 1), :]
             row, col = cell // cols, lax.rem(cell, cols)
-            row_hot = onehot(row, rows)
-            spread = dot(table, jnp.concatenate([row_hot, row_hot], axis=0), 0, 0)
-            col_mask = lax.broadcasted_iota(jnp.int32, (cols, cell.shape[1]), 0) == col
+            col_hot = onehot(col, cols)
+            spread = dot(table, jnp.concatenate([col_hot, col_hot], axis=0), 1, 0)
+            row_mask = lax.broadcasted_iota(jnp.int32, (rows, cell.shape[1]), 0) == row
             for i in range(2):
-                piece = jnp.where(col_mask, spread[cols * i : cols * (i + 1)], 0.0)
+                piece = jnp.where(row_mask, spread[rows * i : rows * (i + 1)], 0.0)
                 held[i, at : at + 1, :] = jnp.sum(piece, axis=0, keepdims=True)
             held[2, at : at + 1, :] = weight[pl.ds(place, 1), :]
 
@@ -333,18 +331,21 @@
 
 
 def scatter(n, rows, cols, tile, cell_of, value_of):
-    total = jnp.zeros((rows, 2 * cols), F32)
+    total = jnp.zeros((2 * rows, cols), F32)
     for step in range(n):
         for band in range(2):
             cell = cell_of(2 * (tile ^ step) + band)
             row, col = cell // cols, lax.rem(cell, cols)
-            col_mask = lax.broadcasted_iota(jnp.int32, (cols, cell.shape[1]), 0) == col
-            value = value_of(2 * step + band)
+            row_mask = lax.broadcasted_iota(jnp.int32, (rows, cell.shape[1]), 0) == row
             spread = jnp.concatenate(
-                [jnp.where(col_mask, x.astype(F32), 0.0).astype(BF16) for x in halves(value)], axis=0
+                [
+                    jnp.where(row_mask, x.astype(F32), 0.0).astype(BF16)
+                    for x in halves(value_of(2 * step + band))
+                ],
+                axis=0,
             )
-            total += dot(onehot(row, rows), spread, 1, 1)
-    return total[:, :cols] + total[:, cols:]
+            total += dot(spread, onehot(col, cols), 1, 1)
+    return total[:rows] + total[rows:]
 
 
 def own_kernel(n, marine, values, out):

time: 26.2 us -> 26.1 us (level)
  Pallas kernels: 4.99 us -> 4.52 us
    pallas_call x9, Pallas kernels: 4.99 us -> 4.52 us  [call(): pl.pallas_call(kernel, out_shape=outs, in_specs=specs or [VMEM] * len(ope...]
  transfers between devices with their start and end apart: 9 -> 9, of which waited for: 7 -> 7; matrix products, arithmetic and copies ran while one was open for 0% -> 0% of each run, Pallas kernels for 3% -> 2%
where the time goes in v6:
time: 26.1 us; the launch traced here: 26 us
  starting transfers between devices  10.5 us (40%)
  waiting for transfers between devices  10.2 us (39%)
  Pallas kernels  4.52 us (17%)
  between operations  0.68 us (3%)
    ppermute x5, starting transfers between devices, traded(): return lax.ppermute(x, ('tile', 'sub'), pairs)  6.05 us
    ppermute x5, waiting for transfers between devices, traded(): return lax.ppermute(x, ('tile', 'sub'), pairs)  5.27 us
    pallas_call x9, Pallas kernels, call(): pl.pallas_call(kernel, out_shape=outs, in_specs=specs or [VMEM] * len(ope...  4.52 us
    ppermute x2, waiting for transfers between devices, by_core(): return lax.ppermute(x, ('tile', 'lev', 'sub'), pairs)  2.84 us
    ppermute x1, waiting for transfers between devices, beyond(): return lax.ppermute(x, ('tile', 'lev', 'sub'), pairs)  2.12 us
    ppermute x2, starting transfers between devices, by_core(): return lax.ppermute(x, ('tile', 'lev', 'sub'), pairs)  1.95 us
    ppermute x1, starting transfers between devices, lev_parts(): return [x, lax.ppermute(x, 'lev', [(0, 1), (1, 0)])]  1.56 us
    ppermute x1, starting transfers between devices, beyond(): return lax.ppermute(x, ('tile', 'lev', 'sub'), pairs)  0.98 us
  transfers between devices with their start and end apart: 9, of which 7 were waited for; matrix products, arithmetic and copies ran while one was open for 0% of the time, Pallas kernels for 2%

profile of v6, /device:TPU:0, one launch (start us, length us, event | category | flops | bytes accessed | tf_op | source)
XLA Modules:
  0.0 26.0 jit_solution(13658007198581364482)
XLA Ops:
  0.6 1.1 %shard_map.130 = (f32[32,256]{1,0:T(8,128)S(1)}, f32[216,128]{1,0:T(8,128)S(1)}, f32[64,128]{1,0:T(8,128)S(1)}, f32[8,128]{1,0:T(8,128)S(1)}, s32[8,256]{1,0:T(8,128)S(1)}, /*index=5*/f32[8,256]{1,0:T(8,128)S(1)}) custom-call(f32[2,64,128]{2,1,0:T(8,128)} %refs_0_.1, f32[2,64,128]{2,1,0:T(8,128)} %refs_1_.1, s32[64,128]{1,0:T(8,128)} %refs_2_.1, f32[2]{0:T(128)} %refs_3_.1, ...), custom_call_target="tpu_custom_call" | custom-call | tf_op jit(solution)/shard_map/pallas_call | solution.py:24
  1.7 0.5 %collective-permute-start = (f32[32,256]{1,0:T(8,128)S(1)}, f32[32,256]{1,0:T(8,128)S(1)}, u32[]{:S(2)}, u32[]{:S(2)}) collective-permute-start(f32[32,256]{1,0:T(8,128)S(1)} %get-tuple-element.30.msg.refs_5_), channel_id=1, source_target_pairs={{0,1},{1,0},{4,5},{5,4},{8,9},{9,8},{12,13},{13,12},{2,3},{3,2},{6... | collective-permute-start | bytes 98312 | tf_op jit(solution)/shard_map/ppermute | solution.py:420
  2.3 0.9 %collective-permute-done.other.refs_6_ = f32[32,256]{1,0:T(8,128)S(1)} collective-permute-done((f32[32,256]{1,0:T(8,128)S(1)}, f32[32,256]{1,0:T(8,128)S(1)}, u32[]{:S(2)}, u32[]{:S(2)}) %collective-permute-start) | collective-permute-done | bytes 32800 | tf_op jit(solution)/shard_map/ppermute | solution.py:420
  3.1 0.1 shard_map.131
  3.2 3.0 %collective-permute-start.1 = (f32[48,128]{1,0:T(8,128)S(1)}, f32[48,128]{1,0:T(8,128)S(1)}, u32[]{:S(2)}, u32[]{:S(2)}) collective-permute-start(f32[48,128]{1,0:T(8,128)S(1)} %get-tuple-element.33), channel_id=1, source_target_pairs={{0,4},{1,5},{4,0},{5,1},{8,12},{9,13},{12,8},{13,9},{2,6},{3,7},{6... | collective-permute-start | bytes 73736 | tf_op jit(solution)/shard_map/ppermute | solution.py:420
  6.2 1.0 %collective-permute-start.2 = (f32[16,128]{1,0:T(8,128)S(1)}, f32[16,128]{1,0:T(8,128)S(1)}, u32[]{:S(2)}, u32[]{:S(2)}) collective-permute-start(f32[16,128]{1,0:T(8,128)S(1)} %get-tuple-element.34), channel_id=1, source_target_pairs={{4,8},{8,4},{0,3},{12,15},{5,9},{9,5},{1,2},{13,14},{6,10},{10,6},... | collective-permute-start | bytes 24584 | tf_op jit(solution)/shard_map/ppermute | solution.py:435
  7.2 2.1 %collective-permute-done.2.refs_2_ = f32[16,128]{1,0:T(8,128)S(1)} collective-permute-done((f32[16,128]{1,0:T(8,128)S(1)}, f32[16,128]{1,0:T(8,128)S(1)}, u32[]{:S(2)}, u32[]{:S(2)}) %collective-permute-start.2) | collective-permute-done | bytes 8224 | tf_op jit(solution)/shard_map/ppermute | solution.py:435
  9.3 0.0 collective-permute-done.1.refs_1_.near_in
  9.3 0.5 %shard_map.132 = (f32[2,64,128]{2,1,0:T(8,128)S(1)}, f32[144,128]{1,0:T(8,128)S(1)}, f32[24,256]{1,0:T(8,128)S(1)}) custom-call(f32[216,128]{1,0:T(8,128)S(1)} %get-tuple-element.32.refs_0_, f32[48,128]{1,0:T(8,128)S(1)} %collective-permute-done.1.refs_1_.near_in, f32[16,128]{1,0:T(8,128)S(1)} %collective-permute-done.2.refs_2_, ...), custom_call_target="tpu_custom_call" | custom-call | tf_op jit(solution)/shard_map/pallas_call | solution.py:24
  9.9 1.6 %collective-permute-start.3 = (f32[144,128]{1,0:T(8,128)S(1)}, f32[144,128]{1,0:T(8,128)S(1)}, u32[]{:S(2)}, u32[]{:S(2)}) collective-permute-start(f32[144,128]{1,0:T(8,128)S(1)} %get-tuple-element.38.refs_0_), channel_id=1, source_target_pairs={{0,2},{2,0},{1,3},{3,1},{4,6},{6,4},{5,7},{7,5},{8,10},{10,8},{9,1... | collective-permute-start | bytes 221192 | tf_op jit(solution)/shard_map/ppermute | solution.py:451
  11.4 1.2 %collective-permute-start.4 = (f32[24,256]{1,0:T(8,128)S(1)}, f32[24,256]{1,0:T(8,128)S(1)}, u32[]{:S(2)}, u32[]{:S(2)}) collective-permute-start(f32[24,256]{1,0:T(8,128)S(1)} %get-tuple-element.42), channel_id=1, source_target_pairs={{0,9},{1,8},{4,13},{5,12},{8,1},{9,0},{12,5},{13,4},{2,11},{3,10},... | collective-permute-start | bytes 73736 | tf_op jit(solution)/shard_map/ppermute | solution.py:420
  12.6 0.3 shard_map.133
  12.9 2.7 %collective-permute-done.4.refs_6_ = f32[24,256]{1,0:T(8,128)S(1)} collective-permute-done((f32[24,256]{1,0:T(8,128)S(1)}, f32[24,256]{1,0:T(8,128)S(1)}, u32[]{:S(2)}, u32[]{:S(2)}) %collective-permute-start.4) | collective-permute-done | bytes 24608 | tf_op jit(solution)/shard_map/ppermute | solution.py:420
  15.6 0.0 collective-permute-done.3.refs_1_.lev_in
  15.6 0.9 %shard_map.134 = (f32[8,256]{1,0:T(8,128)S(1)}, f32[40,128]{1,0:T(8,128)S(1)}, f32[8,128]{1,0:T(8,128)S(1)}, f32[8,128]{1,0:T(8,128)S(1)}, f32[8,128]{1,0:T(8,128)S(1)}, /*index=5*/f32[8,128]{1,0:T(8,128)S(1)}) custom-call(f32[144,128]{1,0:T(8,128)S(1)} %get-tuple-element.38.refs_0_, f32[144,128]{1,0:T(8,128)S(1)} %collective-permute-done.3.refs_1_.lev_in, ...), custom_call_target="tpu_custom_call" | custom-call | tf_op jit(solution)/shard_map/pallas_call | solution.py:24
  16.5 0.6 %collective-permute-start.5 = (f32[40,128]{1,0:T(8,128)S(1)}, f32[40,128]{1,0:T(8,128)S(1)}, u32[]{:S(2)}, u32[]{:S(2)}) collective-permute-start(f32[40,128]{1,0:T(8,128)S(1)} %get-tuple-element.47), channel_id=1, source_target_pairs={{0,1},{1,0},{4,5},{5,4},{8,9},{9,8},{12,13},{13,12},{2,3},{3,2},{6... | collective-permute-start | bytes 61448 | tf_op jit(solution)/shard_map/ppermute | solution.py:420
  17.1 0.8 %collective-permute-done.5.theirs = f32[40,128]{1,0:T(8,128)S(1)} collective-permute-done((f32[40,128]{1,0:T(8,128)S(1)}, f32[40,128]{1,0:T(8,128)S(1)}, u32[]{:S(2)}, u32[]{:S(2)}) %collective-permute-start.5) | collective-permute-done | bytes 20512 | tf_op jit(solution)/shard_map/ppermute | solution.py:420
  18.0 1.4 %collective-permute-start.6 = (f32[32,128]{1,0:T(8,128)S(1)}, f32[32,128]{1,0:T(8,128)S(1)}, u32[]{:S(2)}, u32[]{:S(2)}) collective-permute-start(f32[32,128]{1,0:T(8,128)S(1)} %get-tuple-element.48), channel_id=1, source_target_pairs={{0,4},{1,13},{2,6},{3,15},{4,0},{5,9},{6,2},{7,11},{8,12},{9,5},{1... | collective-permute-start | bytes 49160 | tf_op jit(solution)/shard_map/ppermute | solution.py:446
  19.4 0.5 %collective-permute-start.7 = (f32[32,128]{1,0:T(8,128)S(1)}, f32[32,128]{1,0:T(8,128)S(1)}, u32[]{:S(2)}, u32[]{:S(2)}) collective-permute-start(f32[32,128]{1,0:T(8,128)S(1)} %get-tuple-element.49), channel_id=1, source_target_pairs={{0,2},{1,9},{2,0},{3,11},{4,6},{5,13},{6,4},{7,15},{8,10},{9,1},{1... | collective-permute-start | bytes 49160 | tf_op jit(solution)/shard_map/ppermute | solution.py:446
  19.9 0.4 %shard_map.136.slots = f32[64,128]{1,0:T(8,128)S(1)} custom-call(s32[8,256]{1,0:T(8,128)S(1)} %get-tuple-element.37.refs_7_.refs_4_.marine, f32[8,256]{1,0:T(8,128)S(1)} %get-tuple-element.43.values), custom_call_target="tpu_custom_call" | custom-call | tf_op jit(solution)/shard_map/pallas_call | solution.py:24
  20.3 1.4 %collective-permute-done.6.first = f32[32,128]{1,0:T(8,128)S(1)} collective-permute-done((f32[32,128]{1,0:T(8,128)S(1)}, f32[32,128]{1,0:T(8,128)S(1)}, u32[]{:S(2)}, u32[]{:S(2)}) %collective-permute-start.6) | collective-permute-done | bytes 16416 | tf_op jit(solution)/shard_map/ppermute | solution.py:446
  21.7 1.4 %collective-permute-done.7.second = f32[32,128]{1,0:T(8,128)S(1)} collective-permute-done((f32[32,128]{1,0:T(8,128)S(1)}, f32[32,128]{1,0:T(8,128)S(1)}, u32[]{:S(2)}, u32[]{:S(2)}) %collective-permute-start.7) | collective-permute-done | bytes 16416 | tf_op jit(solution)/shard_map/ppermute | solution.py:446
  23.1 0.6 %shard_map.137 = (f32[64,128]{1,0:T(8,128)S(1)}, f32[72,128]{1,0:T(8,128)S(1)}) custom-call(f32[32,128]{1,0:T(8,128)S(1)} %collective-permute-done.6.first, f32[32,128]{1,0:T(8,128)S(1)} %collective-permute-done.7.second, f32[8,128]{1,0:T(8,128)S(1)} %get-tuple-element.50.own, f32[64,128]{1,0:T(8,128)S(1)} %shard_map.136.slots, ...), custom_call_target="tpu_custom_call" | custom-call | tf_op jit(solution)/shard_map/pallas_call | solution.py:24
  23.7 0.7 %collective-permute-start.8 = (f32[72,128]{1,0:T(8,128)S(1)}, f32[72,128]{1,0:T(8,128)S(1)}, u32[]{:S(2)}, u32[]{:S(2)}) collective-permute-start(f32[72,128]{1,0:T(8,128)S(1)} %get-tuple-element.53.sums), channel_id=1, source_target_pairs={{0,1},{1,0},{4,5},{5,4},{8,9},{9,8},{12,13},{13,12},{2,3},{3,2},{6... | collective-permute-start | bytes 110600 | tf_op jit(solution)/shard_map/ppermute | solution.py:420
  24.4 0.9 %collective-permute-done.8.other = f32[72,128]{1,0:T(8,128)S(1)} collective-permute-done((f32[72,128]{1,0:T(8,128)S(1)}, f32[72,128]{1,0:T(8,128)S(1)}, u32[]{:S(2)}, u32[]{:S(2)}) %collective-permute-start.8) | collective-permute-done | bytes 36896 | tf_op jit(solution)/shard_map/ppermute | solution.py:420
  25.3 0.7 %shard_map.138 = (f32[2,64,128]{2,1,0:T(8,128)}, f32[1,256]{1,0:T(1,128)}, f32[1,256]{1,0:T(1,128)}) custom-call(f32[64,128]{1,0:T(8,128)S(1)} %get-tuple-element.51.slots, f32[2,64,128]{2,1,0:T(8,128)S(1)} %get-tuple-element.52.adjoint, f32[8,128]{1,0:T(8,128)S(1)} %get-tuple-element.36.refs_4_.share_rows, f32[72,128]{1,0:T(8,128)S(1)} %get-tuple-element.53.sums, ...), custom_call_target="tpu_custom_call" | custom-call | tf_op jit(solution)/shard_map/pallas_call | solution.py:24
  (1 shorter events, 0.0 us)
Async XLA Ops:
  1.7 1.4 %collective-permute-start = (f32[32,256]{1,0:T(8,128)S(1)}, f32[32,256]{1,0:T(8,128)S(1)}, u32[]{:S(2)}, u32[]{:S(2)}) collective-permute-start(f32[32,256]{1,0:T(8,128)S(1)} %get-tuple-element.30.msg.refs_5_), channel_id=1, source_target_pairs={{0,1},{1,0},{4,5},{5,4},{8,9},{9,8},{12,13},{13,12},{2,3},{3,2},{6... | collective-permute-start | bytes 98312 | tf_op jit(solution)/shard_map/ppermute | solution.py:420
  3.2 6.1 %collective-permute-start.1 = (f32[48,128]{1,0:T(8,128)S(1)}, f32[48,128]{1,0:T(8,128)S(1)}, u32[]{:S(2)}, u32[]{:S(2)}) collective-permute-start(f32[48,128]{1,0:T(8,128)S(1)} %get-tuple-element.33), channel_id=1, source_target_pairs={{0,4},{1,5},{4,0},{5,1},{8,12},{9,13},{12,8},{13,9},{2,6},{3,7},{6... | collective-permute-start | bytes 73736 | tf_op jit(solution)/shard_map/ppermute | solution.py:420
  6.2 3.1 %collective-permute-start.2 = (f32[16,128]{1,0:T(8,128)S(1)}, f32[16,128]{1,0:T(8,128)S(1)}, u32[]{:S(2)}, u32[]{:S(2)}) collective-permute-start(f32[16,128]{1,0:T(8,128)S(1)} %get-tuple-element.34), channel_id=1, source_target_pairs={{4,8},{8,4},{0,3},{12,15},{5,9},{9,5},{1,2},{13,14},{6,10},{10,6},... | collective-permute-start | bytes 24584 | tf_op jit(solution)/shard_map/ppermute | solution.py:435
  9.9 5.7 %collective-permute-start.3 = (f32[144,128]{1,0:T(8,128)S(1)}, f32[144,128]{1,0:T(8,128)S(1)}, u32[]{:S(2)}, u32[]{:S(2)}) collective-permute-start(f32[144,128]{1,0:T(8,128)S(1)} %get-tuple-element.38.refs_0_), channel_id=1, source_target_pairs={{0,2},{2,0},{1,3},{3,1},{4,6},{6,4},{5,7},{7,5},{8,10},{10,8},{9,1... | collective-permute-start | bytes 221192 | tf_op jit(solution)/shard_map/ppermute | solution.py:451
  11.4 4.2 %collective-permute-start.4 = (f32[24,256]{1,0:T(8,128)S(1)}, f32[24,256]{1,0:T(8,128)S(1)}, u32[]{:S(2)}, u32[]{:S(2)}) collective-permute-start(f32[24,256]{1,0:T(8,128)S(1)} %get-tuple-element.42), channel_id=1, source_target_pairs={{0,9},{1,8},{4,13},{5,12},{8,1},{9,0},{12,5},{13,4},{2,11},{3,10},... | collective-permute-start | bytes 73736 | tf_op jit(solution)/shard_map/ppermute | solution.py:420
  16.5 1.5 %collective-permute-start.5 = (f32[40,128]{1,0:T(8,128)S(1)}, f32[40,128]{1,0:T(8,128)S(1)}, u32[]{:S(2)}, u32[]{:S(2)}) collective-permute-start(f32[40,128]{1,0:T(8,128)S(1)} %get-tuple-element.47), channel_id=1, source_target_pairs={{0,1},{1,0},{4,5},{5,4},{8,9},{9,8},{12,13},{13,12},{2,3},{3,2},{6... | collective-permute-start | bytes 61448 | tf_op jit(solution)/shard_map/ppermute | solution.py:420
  18.0 3.7 %collective-permute-start.6 = (f32[32,128]{1,0:T(8,128)S(1)}, f32[32,128]{1,0:T(8,128)S(1)}, u32[]{:S(2)}, u32[]{:S(2)}) collective-permute-start(f32[32,128]{1,0:T(8,128)S(1)} %get-tuple-element.48), channel_id=1, source_target_pairs={{0,4},{1,13},{2,6},{3,15},{4,0},{5,9},{6,2},{7,11},{8,12},{9,5},{1... | collective-permute-start | bytes 49160 | tf_op jit(solution)/shard_map/ppermute | solution.py:446
  19.4 3.7 %collective-permute-start.7 = (f32[32,128]{1,0:T(8,128)S(1)}, f32[32,128]{1,0:T(8,128)S(1)}, u32[]{:S(2)}, u32[]{:S(2)}) collective-permute-start(f32[32,128]{1,0:T(8,128)S(1)} %get-tuple-element.49), channel_id=1, source_target_pairs={{0,2},{1,9},{2,0},{3,11},{4,6},{5,13},{6,4},{7,15},{8,10},{9,1},{1... | collective-permute-start | bytes 49160 | tf_op jit(solution)/shard_map/ppermute | solution.py:446
  23.7 1.6 %collective-permute-start.8 = (f32[72,128]{1,0:T(8,128)S(1)}, f32[72,128]{1,0:T(8,128)S(1)}, u32[]{:S(2)}, u32[]{:S(2)}) collective-permute-start(f32[72,128]{1,0:T(8,128)S(1)} %get-tuple-element.53.sums), channel_id=1, source_target_pairs={{0,1},{1,0},{4,5},{5,4},{8,9},{9,8},{12,13},{13,12},{2,3},{3,2},{6... | collective-permute-start | bytes 110600 | tf_op jit(solution)/shard_map/ppermute | solution.py:420

commit v7 on v6

--- a/solution.py
+++ b/solution.py
@@ -36,6 +36,42 @@
     high = x.astype(BF16)
     low = (x - high.astype(F32)).astype(BF16)
     return high, low
+
+
+def fold_place(cols):
+    lane = lax.broadcasted_iota(jnp.int32, (8, cols), 1)
+    return lax.rem(lane + HALO, cols)
+
+
+def fold_slots(high, cols, fields):
+    each = cols // (2 * HALO * fields)
+    groups = high // 8
+    return [(g // each, g % each) for g in range(groups)], -(-groups // each)
+
+
+def folded(ext, high, fields):
+    cols = ext.shape[1]
+    place = fold_place(cols) // (2 * HALO)
+    slots, tiles = fold_slots(high, cols, fields)
+    out = [jnp.zeros((8, cols), F32)] * tiles
+    for g, (k, at) in enumerate(slots):
+        for i in range(fields):
+            slot = at * fields + i
+            rows = ext[high * i + 8 * g : high * i + 8 * g + 8, :]
+            moved = pltpu.roll(rows, 2 * HALO * slot, 1) if slot else rows
+            out[k] = jnp.where(place == slot, moved, out[k])
+    return jnp.concatenate(out, axis=0)
+
+
+def unfolded(tiles, i, high, fields):
+    cols = tiles[0].shape[1]
+    place = fold_place(cols)
+    out = []
+    for k, at in fold_slots(high, cols, fields)[0]:
+        slot = at * fields + i
+        moved = pltpu.roll(tiles[k], cols - 2 * HALO * slot, 1) if slot else tiles[k]
+        out.append(jnp.where(place < 2 * HALO, moved, 0.0))
+    return jnp.concatenate(out, axis=0)
 
 
 def pack_kernel(n, *refs):
@@ -69,6 +105,9 @@
         at, top, left = high * i, base + HALO * (i // 2), cols * (i % 2)
         outer = jnp.where(sub == 0, ext[at + rows - HALO : at + rows], ext[at : at + HALO])
         msg[top : top + HALO, left : left + cols] = outer
+    edges = folded(ext, high, levels + 1)
+    for k in range(2):
+        msg[4 * n + 16 : 4 * n + 24, cols * k : cols * (k + 1)] = edges[8 * k : 8 * k + 8]
     surface[...] = sum(shares_in[z] * warm_in[z] for z in range(levels))
     for z in range(levels):
         share_rows[z : z + 1, :] = jnp.full((1, cols), shares_in[z], F32)
@@ -115,42 +154,6 @@
         jnp.concatenate([ref[at + i : at + i + 1, :], ref[at + count + i : at + count + i + 1, :]], axis=1)
         for i in range(count)
     ]
-
-
-def fold_place(cols):
-    lane = lax.broadcasted_iota(jnp.int32, (8, cols), 1)
-    return lax.rem(lane + HALO, cols)
-
-
-def fold_slots(high, cols, fields):
-    each = cols // (2 * HALO * fields)
-    groups = high // 8
-    return [(g // each, g % each) for g in range(groups)], -(-groups // each)
-
-
-def folded(ext, high, fields):
-    cols = ext.shape[1]
-    place = fold_place(cols) // (2 * HALO)
-    slots, tiles = fold_slots(high, cols, fields)
-    out = [jnp.zeros((8, cols), F32)] * tiles
-    for g, (k, at) in enumerate(slots):
-        for i in range(fields):
-            slot = at * fields + i
-            rows = ext[high * i + 8 * g : high * i + 8 * g + 8, :]
-            moved = pltpu.roll(rows, 2 * HALO * slot, 1) if slot else rows
-            out[k] = jnp.where(place == slot, moved, out[k])
-    return jnp.concatenate(out, axis=0)
-
-
-def unfolded(tiles, i, high, fields):
-    cols = tiles[0].shape[1]
-    place = fold_place(cols)
-    out = []
-    for k, at in fold_slots(high, cols, fields)[0]:
-        slot = at * fields + i
-        moved = pltpu.roll(tiles[k], cols - 2 * HALO * slot, 1) if slot else tiles[k]
-        out.append(jnp.where(place < 2 * HALO, moved, 0.0))
-    return jnp.concatenate(out, axis=0)
 
 
 def send_kernel(n, fields, msg, other, ext_in, ext, edge_out, near_out):
@@ -165,16 +168,27 @@
         ext[base + rows : base + high, :] = jnp.zeros((8, cols), F32)
         ext[base + rows : base + rows + HALO, :] = jnp.where(sub == 0, strip, 0.0)
         ext[base + high - HALO : base + high, :] = jnp.where(sub == 0, 0.0, strip)
-    edges = folded(ext, high, fields)
+    slots, count = fold_slots(high, cols, fields)
+    tile_at, at = slots[-1]
+    place = fold_place(cols) // (2 * HALO)
+    tiles = [other[4 * n + 16 : 4 * n + 24, cols * k : cols * (k + 1)] for k in range(count)]
+    for i in range(fields):
+        strip = halo_rows(n, msg, i, cols)
+        blank = jnp.zeros((8 - 2 * HALO, cols), F32)
+        rows_beyond = [jnp.where(sub == 1, strip, 0.0), blank, jnp.where(sub == 1, 0.0, strip)]
+        slot = at * fields + i
+        moved = pltpu.roll(jnp.concatenate(rows_beyond, axis=0), 2 * HALO * slot, 1)
+        tiles[tile_at] = jnp.where(place == slot, moved, tiles[tile_at])
+    edges = jnp.concatenate(tiles, axis=0)
     fold = edges.shape[0]
     edge_out[...] = edges
     near_out[0:fold, :] = edges
     near = tile ^ 1
-    air = table_rows(n, msg, other, near, sub, sub) + value_rows(n, msg, other, sub)
+    air = table_rows(n, msg, other, near, 1 - sub, sub) + value_rows(n, msg, other, sub)
     write_pairs(near_out, fold, air)
     at = fold + 20
     for step in range(2, n, 2):
-        write_pairs(near_out, at, table_rows(n, msg, other, near ^ step, 1 - sub, sub))
+        write_pairs(near_out, at, table_rows(n, msg, other, near ^ step, sub, sub))
         at += 8
     near_out[at : near_out.shape[0], :] = jnp.zeros((near_out.shape[0] - at, cols), F32)
 
@@ -190,9 +204,7 @@
     for i, out in enumerate(refs[10:]):
         air = table_rows(n, msg, other, tile ^ (2 * i + 2), 1 - sub, sub) + own_values
         air += read_pairs(near_in, fold + 20 + 8 * i, 4) + near_values
-        for at, row in enumerate(air):
-            out[at : at + 1, :] = row
-        out[20:24, :] = jnp.zeros((4, out.shape[1]), F32)
+        write_pairs(out, 0, air)
     even = tile % 2 == 0
     place = fold_place(cols)
     tiles = []
@@ -289,9 +301,9 @@
     cols = chip_out.shape[1]
     picks[:, 0:4, :] = near_picks[...]
     for i, ref in enumerate(far_in):
+        air = read_pairs(ref, 0, 20)
         for j in range(2):
-            air = [ref[10 * j + k : 10 * j + k + 1, :] for k in range(10)]
-            look_up(air, 4 * i + 4 + 2 * j, picks, tables)
+            look_up(air[10 * j : 10 * j + 10], 4 * i + 4 + 2 * j, picks, tables)
     table = sum(ref[0 : 2 * rows, :] for ref in lev_parts)
     table = jnp.concatenate(halves(table), axis=1)
     for step in range(n):
@@ -421,18 +433,12 @@
 
 
 def beyond(x):
-    n, levs, bands = (lax.axis_size(axis) for axis in ("tile", "lev", "sub"))
-
-    def place(t, l, s):
-        return (t * levs + l) * bands + s
-
+    n, bands = lax.axis_size("tile"), lax.axis_size("sub")
     pairs = []
-    for l in range(levs):
-        for s in range(bands):
-            for t in range(1, n - 1, 2):
-                pairs += [(place(t, l, s), place(t + 1, l, s)), (place(t + 1, l, s), place(t, l, s))]
-            pairs += [(place(t, l, s), place(t, l ^ 1, s ^ 1)) for t in (0, n - 1)]
-    return lax.ppermute(x, ("tile", "lev", "sub"), pairs)
+    for t in range(n):
+        to = t if t in (0, n - 1) else ((t + 1) ^ 1) - 1
+        pairs += [(t * bands + s, to * bands + (s ^ 1)) for s in range(bands)]
+    return lax.ppermute(x, ("tile", "sub"), pairs)
 
 
 def by_core(x, even, odd):
@@ -481,7 +487,7 @@
     held += [pltpu.VMEM(x.shape, x.dtype) for x in raw[4:9]]
     msg, ext, surface, share_rows, marine, marine_weight = call(
         functools.partial(pack_kernel, n),
-        [(4 * n + 16, cells), ((levels + 1) * high, cols), (rows, cols), (8, cols)]
+        [(4 * n + 24, cells), ((levels + 1) * high, cols), (rows, cols), (8, cols)]
         + [jax.ShapeDtypeStruct(x.shape, x.dtype) for x in raw[9:]],
         raw,
         [HBM] * len(raw),
@@ -495,11 +501,11 @@
         [msg, other, ext],
     )
     edge_in = beyond(edge_out)
-    near_in = traded(near_out, 1)
+    near_in = traded(near_out, 1, 1)
     merged = n == 4 and levs == 2
     adjoint, lev_msg, *far_out = call(
         functools.partial(diffuse_kernel, n, levels),
-        [(levels, rows, cols), (2 * rows + (16 if merged else 0), cols)] + [(24, cells)] * (n // 2 - 1),
+        [(levels, rows, cols), (2 * rows + (16 if merged else 0), cols)] + [(40, cols)] * (n // 2 - 1),
         [ext, near_in, edge_in, surface, share_rows, msg, other, marine],
     )
     lev_in = lev_parts(lev_msg)

time: 26.1 us -> 25.5 us (0.977)
  waiting for transfers between devices: 10.2 us -> 7.92 us
  starting transfers between devices: 10.5 us -> 12.1 us
    ppermute x5, starting transfers between devices: 6.05 us -> 7.4 us  [traded(): return lax.ppermute(x, ('tile', 'sub'), pairs)]
    ppermute x1, waiting for transfers between devices: 2.12 us -> 0.83 us  [beyond(): return lax.ppermute(x, ('tile', 'sub'), pairs)]
    ppermute x5, waiting for transfers between devices: 5.27 us -> 4.24 us  [traded(): return lax.ppermute(x, ('tile', 'sub'), pairs)]
    ppermute x1, starting transfers between devices: 0.98 us -> 0.35 us  [beyond(): return lax.ppermute(x, ('tile', 'sub'), pairs)]
    ppermute x2, starting transfers between devices: 1.95 us -> 2.41 us  [by_core(): return lax.ppermute(x, ('tile', 'lev', 'sub'), pairs)]
    ppermute x1, starting transfers between devices: 1.56 us -> 1.95 us  [lev_parts(): return [x, lax.ppermute(x, 'lev', [(0, 1), (1, 0)])]]
  transfers between devices with their start and end apart: 9 -> 9, of which waited for: 7 -> 8; matrix products, arithmetic and copies ran while one was open for 0% -> 0% of each run, Pallas kernels for 2% -> 2%
where the time goes in v7:
time: 25.5 us; the launch traced here: 25.3 us
  starting transfers between devices  12.1 us (47%)
  waiting for transfers between devices  7.92 us (31%)
  Pallas kernels  4.59 us (18%)
  between operations  0.68 us (3%)
    ppermute x5, starting transfers between devices, traded(): return lax.ppermute(x, ('tile', 'sub'), pairs)  7.4 us
    pallas_call x9, Pallas kernels, call(): pl.pallas_call(kernel, out_shape=outs, in_specs=specs or [VMEM] * len(ope...  4.59 us
    ppermute x5, waiting for transfers between devices, traded(): return lax.ppermute(x, ('tile', 'sub'), pairs)  4.24 us
    ppermute x2, waiting for transfers between devices, by_core(): return lax.ppermute(x, ('tile', 'lev', 'sub'), pairs)  2.84 us
    ppermute x2, starting transfers between devices, by_core(): return lax.ppermute(x, ('tile', 'lev', 'sub'), pairs)  2.41 us
    ppermute x1, starting transfers between devices, lev_parts(): return [x, lax.ppermute(x, 'lev', [(0, 1), (1, 0)])]  1.95 us
    ppermute x1, waiting for transfers between devices, beyond(): return lax.ppermute(x, ('tile', 'sub'), pairs)  0.83 us
  transfers between devices with their start and end apart: 9, of which 8 were waited for; matrix products, arithmetic and copies ran while one was open for 0% of the time, Pallas kernels for 2%

profile of v7, /device:TPU:0, one launch (start us, length us, event | category | flops | bytes accessed | tf_op | source)
XLA Modules:
  0.0 25.3 jit_solution(11684692272815253774)
XLA Ops:
  0.6 1.2 %shard_map.130 = (f32[40,256]{1,0:T(8,128)S(1)}, f32[216,128]{1,0:T(8,128)S(1)}, f32[64,128]{1,0:T(8,128)S(1)}, f32[8,128]{1,0:T(8,128)S(1)}, s32[8,256]{1,0:T(8,128)S(1)}, /*index=5*/f32[8,256]{1,0:T(8,128)S(1)}) custom-call(f32[2,64,128]{2,1,0:T(8,128)} %refs_0_.1, f32[2,64,128]{2,1,0:T(8,128)} %refs_1_.1, s32[64,128]{1,0:T(8,128)} %refs_2_.1, f32[2]{0:T(128)} %refs_3_.1, ...), custom_call_target="tpu_custom_call" | custom-call | tf_op jit(solution)/shard_map/pallas_call | solution.py:24
  1.8 0.5 %collective-permute-start = (f32[40,256]{1,0:T(8,128)S(1)}, f32[40,256]{1,0:T(8,128)S(1)}, u32[]{:S(2)}, u32[]{:S(2)}) collective-permute-start(f32[40,256]{1,0:T(8,128)S(1)} %get-tuple-element.30.msg.refs_5_), channel_id=1, source_target_pairs={{0,1},{1,0},{4,5},{5,4},{8,9},{9,8},{12,13},{13,12},{2,3},{3,2},{6... | collective-permute-start | bytes 122888 | tf_op jit(solution)/shard_map/ppermute | solution.py:432
  2.4 0.9 %collective-permute-done.other.refs_6_ = f32[40,256]{1,0:T(8,128)S(1)} collective-permute-done((f32[40,256]{1,0:T(8,128)S(1)}, f32[40,256]{1,0:T(8,128)S(1)}, u32[]{:S(2)}, u32[]{:S(2)}) %collective-permute-start) | collective-permute-done | bytes 40992 | tf_op jit(solution)/shard_map/ppermute | solution.py:432
  3.2 0.1 shard_map.131
  3.3 2.7 %collective-permute-start.1 = (f32[48,128]{1,0:T(8,128)S(1)}, f32[48,128]{1,0:T(8,128)S(1)}, u32[]{:S(2)}, u32[]{:S(2)}) collective-permute-start(f32[48,128]{1,0:T(8,128)S(1)} %get-tuple-element.33), channel_id=1, source_target_pairs={{0,5},{1,4},{4,1},{5,0},{8,13},{9,12},{12,9},{13,8},{2,7},{3,6},{6... | collective-permute-start | bytes 73736 | tf_op jit(solution)/shard_map/ppermute | solution.py:432
  6.0 0.3 %collective-permute-start.2 = (f32[16,128]{1,0:T(8,128)S(1)}, f32[16,128]{1,0:T(8,128)S(1)}, u32[]{:S(2)}, u32[]{:S(2)}) collective-permute-start(f32[16,128]{1,0:T(8,128)S(1)} %get-tuple-element.34), channel_id=1, source_target_pairs={{0,1},{1,0},{4,9},{5,8},{8,5},{9,4},{12,13},{13,12},{2,3},{3,2},{6... | collective-permute-start | bytes 24584 | tf_op jit(solution)/shard_map/ppermute | solution.py:441
  6.4 0.8 %collective-permute-done.2.refs_2_ = f32[16,128]{1,0:T(8,128)S(1)} collective-permute-done((f32[16,128]{1,0:T(8,128)S(1)}, f32[16,128]{1,0:T(8,128)S(1)}, u32[]{:S(2)}, u32[]{:S(2)}) %collective-permute-start.2) | collective-permute-done | bytes 8224 | tf_op jit(solution)/shard_map/ppermute | solution.py:441
  7.2 0.3 %collective-permute-done.1.refs_1_.near_in = f32[48,128]{1,0:T(8,128)S(1)} collective-permute-done((f32[48,128]{1,0:T(8,128)S(1)}, f32[48,128]{1,0:T(8,128)S(1)}, u32[]{:S(2)}, u32[]{:S(2)}) %collective-permute-start.1) | collective-permute-done | bytes 24608 | tf_op jit(solution)/shard_map/ppermute | solution.py:432
  7.5 0.5 %shard_map.132 = (f32[2,64,128]{2,1,0:T(8,128)S(1)}, f32[144,128]{1,0:T(8,128)S(1)}, f32[40,128]{1,0:T(8,128)S(1)}) custom-call(f32[216,128]{1,0:T(8,128)S(1)} %get-tuple-element.32.refs_0_, f32[48,128]{1,0:T(8,128)S(1)} %collective-permute-done.1.refs_1_.near_in, f32[16,128]{1,0:T(8,128)S(1)} %collective-permute-done.2.refs_2_, ...), custom_call_target="tpu_custom_call" | custom-call | tf_op jit(solution)/shard_map/pallas_call | solution.py:24
  8.1 1.9 %collective-permute-start.3 = (f32[144,128]{1,0:T(8,128)S(1)}, f32[144,128]{1,0:T(8,128)S(1)}, u32[]{:S(2)}, u32[]{:S(2)}) collective-permute-start(f32[144,128]{1,0:T(8,128)S(1)} %get-tuple-element.38.refs_0_), channel_id=1, source_target_pairs={{0,2},{2,0},{1,3},{3,1},{4,6},{6,4},{5,7},{7,5},{8,10},{10,8},{9,1... | collective-permute-start | bytes 221192 | tf_op jit(solution)/shard_map/ppermute | solution.py:457
  10.0 3.4 %collective-permute-start.4 = (f32[40,128]{1,0:T(8,128)S(1)}, f32[40,128]{1,0:T(8,128)S(1)}, u32[]{:S(2)}, u32[]{:S(2)}) collective-permute-start(f32[40,128]{1,0:T(8,128)S(1)} %get-tuple-element.42), channel_id=1, source_target_pairs={{0,9},{1,8},{4,13},{5,12},{8,1},{9,0},{12,5},{13,4},{2,11},{3,10},... | collective-permute-start | bytes 61448 | tf_op jit(solution)/shard_map/ppermute | solution.py:432
  13.5 0.3 %shard_map.133 = (f32[3,4,256]{2,1,0:T(4,128)S(1)}, bf16[4,256,256]{2,1,0:T(8,128)(2,1)S(1)}) custom-call(f32[40,256]{1,0:T(8,128)S(1)} %get-tuple-element.30.msg.refs_5_, f32[40,256]{1,0:T(8,128)S(1)} %collective-permute-done.other.refs_6_, f32[48,128]{1,0:T(8,128)S(1)} %collective-permute-done.1.refs_1_.near_in), custom_call_target="tpu_custom_call" | custom-call | tf_op jit(solution)/shard_map/pallas_call | solution.py:24
  13.7 1.2 %collective-permute-done.4.refs_6_ = f32[40,128]{1,0:T(8,128)S(1)} collective-permute-done((f32[40,128]{1,0:T(8,128)S(1)}, f32[40,128]{1,0:T(8,128)S(1)}, u32[]{:S(2)}, u32[]{:S(2)}) %collective-permute-start.4) | collective-permute-done | bytes 20512 | tf_op jit(solution)/shard_map/ppermute | solution.py:432
  15.0 0.0 collective-permute-done.3.refs_1_.lev_in
  15.0 0.9 %shard_map.134 = (f32[8,256]{1,0:T(8,128)S(1)}, f32[40,128]{1,0:T(8,128)S(1)}, f32[8,128]{1,0:T(8,128)S(1)}, f32[8,128]{1,0:T(8,128)S(1)}, f32[8,128]{1,0:T(8,128)S(1)}, /*index=5*/f32[8,128]{1,0:T(8,128)S(1)}) custom-call(f32[144,128]{1,0:T(8,128)S(1)} %get-tuple-element.38.refs_0_, f32[144,128]{1,0:T(8,128)S(1)} %collective-permute-done.3.refs_1_.lev_in, ...), custom_call_target="tpu_custom_call" | custom-call | tf_op jit(solution)/shard_map/pallas_call | solution.py:24
  15.9 0.4 %collective-permute-start.5 = (f32[40,128]{1,0:T(8,128)S(1)}, f32[40,128]{1,0:T(8,128)S(1)}, u32[]{:S(2)}, u32[]{:S(2)}) collective-permute-start(f32[40,128]{1,0:T(8,128)S(1)} %get-tuple-element.47), channel_id=1, source_target_pairs={{0,1},{1,0},{4,5},{5,4},{8,9},{9,8},{12,13},{13,12},{2,3},{3,2},{6... | collective-permute-start | bytes 61448 | tf_op jit(solution)/shard_map/ppermute | solution.py:432
  16.3 0.8 %collective-permute-done.5.theirs = f32[40,128]{1,0:T(8,128)S(1)} collective-permute-done((f32[40,128]{1,0:T(8,128)S(1)}, f32[40,128]{1,0:T(8,128)S(1)}, u32[]{:S(2)}, u32[]{:S(2)}) %collective-permute-start.5) | collective-permute-done | bytes 20512 | tf_op jit(solution)/shard_map/ppermute | solution.py:432
  17.2 1.9 %collective-permute-start.6 = (f32[32,128]{1,0:T(8,128)S(1)}, f32[32,128]{1,0:T(8,128)S(1)}, u32[]{:S(2)}, u32[]{:S(2)}) collective-permute-start(f32[32,128]{1,0:T(8,128)S(1)} %get-tuple-element.48), channel_id=1, source_target_pairs={{0,4},{1,13},{2,6},{3,15},{4,0},{5,9},{6,2},{7,11},{8,12},{9,5},{1... | collective-permute-start | bytes 49160 | tf_op jit(solution)/shard_map/ppermute | solution.py:452
  19.0 0.5 %collective-permute-start.7 = (f32[32,128]{1,0:T(8,128)S(1)}, f32[32,128]{1,0:T(8,128)S(1)}, u32[]{:S(2)}, u32[]{:S(2)}) collective-permute-start(f32[32,128]{1,0:T(8,128)S(1)} %get-tuple-element.49), channel_id=1, source_target_pairs={{0,2},{1,9},{2,0},{3,11},{4,6},{5,13},{6,4},{7,15},{8,10},{9,1},{1... | collective-permute-start | bytes 49160 | tf_op jit(solution)/shard_map/ppermute | solution.py:452
  19.6 0.4 %shard_map.136.slots = f32[64,128]{1,0:T(8,128)S(1)} custom-call(s32[8,256]{1,0:T(8,128)S(1)} %get-tuple-element.37.refs_7_.refs_4_.marine, f32[8,256]{1,0:T(8,128)S(1)} %get-tuple-element.43.values), custom_call_target="tpu_custom_call" | custom-call | tf_op jit(solution)/shard_map/pallas_call | solution.py:24
  19.9 1.0 %collective-permute-done.6.first = f32[32,128]{1,0:T(8,128)S(1)} collective-permute-done((f32[32,128]{1,0:T(8,128)S(1)}, f32[32,128]{1,0:T(8,128)S(1)}, u32[]{:S(2)}, u32[]{:S(2)}) %collective-permute-start.6) | collective-permute-done | bytes 16416 | tf_op jit(solution)/shard_map/ppermute | solution.py:452
  20.9 1.9 %collective-permute-done.7.second = f32[32,128]{1,0:T(8,128)S(1)} collective-permute-done((f32[32,128]{1,0:T(8,128)S(1)}, f32[32,128]{1,0:T(8,128)S(1)}, u32[]{:S(2)}, u32[]{:S(2)}) %collective-permute-start.7) | collective-permute-done | bytes 16416 | tf_op jit(solution)/shard_map/ppermute | solution.py:452
  22.8 0.6 %shard_map.137 = (f32[64,128]{1,0:T(8,128)S(1)}, f32[72,128]{1,0:T(8,128)S(1)}) custom-call(f32[32,128]{1,0:T(8,128)S(1)} %collective-permute-done.6.first, f32[32,128]{1,0:T(8,128)S(1)} %collective-permute-done.7.second, f32[8,128]{1,0:T(8,128)S(1)} %get-tuple-element.50.own, f32[64,128]{1,0:T(8,128)S(1)} %shard_map.136.slots, ...), custom_call_target="tpu_custom_call" | custom-call | tf_op jit(solution)/shard_map/pallas_call | solution.py:24
  23.3 0.3 %collective-permute-start.8 = (f32[72,128]{1,0:T(8,128)S(1)}, f32[72,128]{1,0:T(8,128)S(1)}, u32[]{:S(2)}, u32[]{:S(2)}) collective-permute-start(f32[72,128]{1,0:T(8,128)S(1)} %get-tuple-element.53.sums), channel_id=1, source_target_pairs={{0,1},{1,0},{4,5},{5,4},{8,9},{9,8},{12,13},{13,12},{2,3},{3,2},{6... | collective-permute-start | bytes 110600 | tf_op jit(solution)/shard_map/ppermute | solution.py:432
  23.7 1.0 %collective-permute-done.8.other = f32[72,128]{1,0:T(8,128)S(1)} collective-permute-done((f32[72,128]{1,0:T(8,128)S(1)}, f32[72,128]{1,0:T(8,128)S(1)}, u32[]{:S(2)}, u32[]{:S(2)}) %collective-permute-start.8) | collective-permute-done | bytes 36896 | tf_op jit(solution)/shard_map/ppermute | solution.py:432
  24.6 0.7 %shard_map.138 = (f32[2,64,128]{2,1,0:T(8,128)}, f32[1,256]{1,0:T(1,128)}, f32[1,256]{1,0:T(1,128)}) custom-call(f32[64,128]{1,0:T(8,128)S(1)} %get-tuple-element.51.slots, f32[2,64,128]{2,1,0:T(8,128)S(1)} %get-tuple-element.52.adjoint, f32[8,128]{1,0:T(8,128)S(1)} %get-tuple-element.36.refs_4_.share_rows, f32[72,128]{1,0:T(8,128)S(1)} %get-tuple-element.53.sums, ...), custom_call_target="tpu_custom_call" | custom-call | tf_op jit(solution)/shard_map/pallas_call | solution.py:24
  (1 shorter events, 0.0 us)
Async XLA Ops:
  1.8 1.4 %collective-permute-start = (f32[40,256]{1,0:T(8,128)S(1)}, f32[40,256]{1,0:T(8,128)S(1)}, u32[]{:S(2)}, u32[]{:S(2)}) collective-permute-start(f32[40,256]{1,0:T(8,128)S(1)} %get-tuple-element.30.msg.refs_5_), channel_id=1, source_target_pairs={{0,1},{1,0},{4,5},{5,4},{8,9},{9,8},{12,13},{13,12},{2,3},{3,2},{6... | collective-permute-start | bytes 122888 | tf_op jit(solution)/shard_map/ppermute | solution.py:432
  3.3 4.2 %collective-permute-start.1 = (f32[48,128]{1,0:T(8,128)S(1)}, f32[48,128]{1,0:T(8,128)S(1)}, u32[]{:S(2)}, u32[]{:S(2)}) collective-permute-start(f32[48,128]{1,0:T(8,128)S(1)} %get-tuple-element.33), channel_id=1, source_target_pairs={{0,5},{1,4},{4,1},{5,0},{8,13},{9,12},{12,9},{13,8},{2,7},{3,6},{6... | collective-permute-start | bytes 73736 | tf_op jit(solution)/shard_map/ppermute | solution.py:432
  6.0 1.2 %collective-permute-start.2 = (f32[16,128]{1,0:T(8,128)S(1)}, f32[16,128]{1,0:T(8,128)S(1)}, u32[]{:S(2)}, u32[]{:S(2)}) collective-permute-start(f32[16,128]{1,0:T(8,128)S(1)} %get-tuple-element.34), channel_id=1, source_target_pairs={{0,1},{1,0},{4,9},{5,8},{8,5},{9,4},{12,13},{13,12},{2,3},{3,2},{6... | collective-permute-start | bytes 24584 | tf_op jit(solution)/shard_map/ppermute | solution.py:441
  8.1 6.9 %collective-permute-start.3 = (f32[144,128]{1,0:T(8,128)S(1)}, f32[144,128]{1,0:T(8,128)S(1)}, u32[]{:S(2)}, u32[]{:S(2)}) collective-permute-start(f32[144,128]{1,0:T(8,128)S(1)} %get-tuple-element.38.refs_0_), channel_id=1, source_target_pairs={{0,2},{2,0},{1,3},{3,1},{4,6},{6,4},{5,7},{7,5},{8,10},{10,8},{9,1... | collective-permute-start | bytes 221192 | tf_op jit(solution)/shard_map/ppermute | solution.py:457
  10.0 4.9 %collective-permute-start.4 = (f32[40,128]{1,0:T(8,128)S(1)}, f32[40,128]{1,0:T(8,128)S(1)}, u32[]{:S(2)}, u32[]{:S(2)}) collective-permute-start(f32[40,128]{1,0:T(8,128)S(1)} %get-tuple-element.42), channel_id=1, source_target_pairs={{0,9},{1,8},{4,13},{5,12},{8,1},{9,0},{12,5},{13,4},{2,11},{3,10},... | collective-permute-start | bytes 61448 | tf_op jit(solution)/shard_map/ppermute | solution.py:432
  15.9 1.3 %collective-permute-start.5 = (f32[40,128]{1,0:T(8,128)S(1)}, f32[40,128]{1,0:T(8,128)S(1)}, u32[]{:S(2)}, u32[]{:S(2)}) collective-permute-start(f32[40,128]{1,0:T(8,128)S(1)} %get-tuple-element.47), channel_id=1, source_target_pairs={{0,1},{1,0},{4,5},{5,4},{8,9},{9,8},{12,13},{13,12},{2,3},{3,2},{6... | collective-permute-start | bytes 61448 | tf_op jit(solution)/shard_map/ppermute | solution.py:432
  17.2 3.7 %collective-permute-start.6 = (f32[32,128]{1,0:T(8,128)S(1)}, f32[32,128]{1,0:T(8,128)S(1)}, u32[]{:S(2)}, u32[]{:S(2)}) collective-permute-start(f32[32,128]{1,0:T(8,128)S(1)} %get-tuple-element.48), channel_id=1, source_target_pairs={{0,4},{1,13},{2,6},{3,15},{4,0},{5,9},{6,2},{7,11},{8,12},{9,5},{1... | collective-permute-start | bytes 49160 | tf_op jit(solution)/shard_map/ppermute | solution.py:452
  19.0 3.7 %collective-permute-start.7 = (f32[32,128]{1,0:T(8,128)S(1)}, f32[32,128]{1,0:T(8,128)S(1)}, u32[]{:S(2)}, u32[]{:S(2)}) collective-permute-start(f32[32,128]{1,0:T(8,128)S(1)} %get-tuple-element.49), channel_id=1, source_target_pairs={{0,2},{1,9},{2,0},{3,11},{4,6},{5,13},{6,4},{7,15},{8,10},{9,1},{1... | collective-permute-start | bytes 49160 | tf_op jit(solution)/shard_map/ppermute | solution.py:452
  23.3 1.3 %collective-permute-start.8 = (f32[72,128]{1,0:T(8,128)S(1)}, f32[72,128]{1,0:T(8,128)S(1)}, u32[]{:S(2)}, u32[]{:S(2)}) collective-permute-start(f32[72,128]{1,0:T(8,128)S(1)} %get-tuple-element.53.sums), channel_id=1, source_target_pairs={{0,1},{1,0},{4,5},{5,4},{8,9},{9,8},{12,13},{13,12},{2,3},{3,2},{6... | collective-permute-start | bytes 110600 | tf_op jit(solution)/shard_map/ppermute | solution.py:432

commit v8 on v7

--- a/solution.py
+++ b/solution.py
@@ -63,29 +63,67 @@
     return jnp.concatenate(out, axis=0)
 
 
-def unfolded(tiles, i, high, fields):
-    cols = tiles[0].shape[1]
-    place = fold_place(cols)
+def lanes_from(shape, first, count):
+    lane = lax.broadcasted_iota(jnp.int32, shape, 1)
+    return (lane >= first) & (lane < first + count)
+
+
+def turn_lanes(x, by):
+    by = by % x.shape[1]
+    return pltpu.roll(x, by, 1) if by else x
+
+
+def own_strips(fields):
+    width = 2 * HALO
+    cols = fields[0].shape[1]
+    out = jnp.zeros_like(fields[0])
+    for z, x in enumerate(fields):
+        base = 3 * width * z
+        out = jnp.where(lanes_from(x.shape, base, width), turn_lanes(x, base + width), out)
+        out = jnp.where(lanes_from(x.shape, base + 2 * width, width), turn_lanes(x, base + 2 * width), out)
+    return out
+
+
+def strips_beyond(tiles, own, fields, count):
+    width = 2 * HALO
+    high, cols = own.shape
     out = []
-    for k, at in fold_slots(high, cols, fields)[0]:
-        slot = at * fields + i
-        moved = pltpu.roll(tiles[k], cols - 2 * HALO * slot, 1) if slot else tiles[k]
-        out.append(jnp.where(place < 2 * HALO, moved, 0.0))
+    for g, (k, at) in enumerate(fold_slots(high, cols, count)[0]):
+        x = own[8 * g : 8 * g + 8]
+        for z, i in enumerate(fields):
+            base = width * (3 * z + 1)
+            moved = turn_lanes(tiles[k], base - width * (at * count + i))
+            x = jnp.where(lanes_from(x.shape, base, width), moved, x)
+        out.append(x)
     return jnp.concatenate(out, axis=0)
 
 
+def around(x):
+    high, cols = x.shape
+    return pltpu.roll(x, 1, 0) + pltpu.roll(x, high - 1, 0) + pltpu.roll(x, 1, 1) + pltpu.roll(x, cols - 1, 1)
+
+
+def diffused(wet, fields):
+    keep = wet * (1.0 - MIXING * around(wet))
+    mix = MIXING * wet
+    out = []
+    for v in fields:
+        v = wet * v
+        for sweep_index in range(STEPS):
+            v = keep * v + mix * around(v)
+        out.append(v)
+    return out
+
+
 def pack_kernel(n, *refs):
-    warm, cot, sea, shares, sky, breeze, energy, sky_index, sky_weight, marine, marine_weight = refs[:11]
-    msg, ext, surface, share_rows, marine_out, marine_weight_out = refs[11:17]
-    warm_in, sea_in, shares_in, sky_in, breeze_in, energy_in, index_in, weight_in, sems = refs[17:]
+    cot, sea, sky, breeze, energy, sky_index, sky_weight, msg, ext = refs[:9]
+    sea_in, sky_in, breeze_in, energy_in, index_in, weight_in, sems = refs[9:]
     rows, cols = sea.shape
-    levels = warm.shape[0]
+    levels = cot.shape[0]
     high = rows + 8
     pairs = [(cot.at[z], ext.at[pl.ds(high * z, rows)]) for z in range(levels)]
     pairs += [(sea, sea_in), (sky_index, index_in), (sky_weight, weight_in)]
     pairs += [(sky, sky_in), (breeze, breeze_in), (energy, energy_in)]
-    pairs += [(shares, shares_in), (warm, warm_in)]
-    pairs += [(marine, marine_out), (marine_weight, marine_weight_out)]
     copies = [pltpu.make_async_copy(a, b, sems.at[i]) for i, (a, b) in enumerate(pairs)]
     for copy in copies:
         copy.start()
@@ -108,9 +146,6 @@
     edges = folded(ext, high, levels + 1)
     for k in range(2):
         msg[4 * n + 16 : 4 * n + 24, cols * k : cols * (k + 1)] = edges[8 * k : 8 * k + 8]
-    surface[...] = sum(shares_in[z] * warm_in[z] for z in range(levels))
-    for z in range(levels):
-        share_rows[z : z + 1, :] = jnp.full((1, cols), shares_in[z], F32)
 
 
 def halo_rows(n, msg, i, cols):
@@ -193,50 +228,60 @@
     near_out[at : near_out.shape[0], :] = jnp.zeros((near_out.shape[0] - at, cols), F32)
 
 
+def side_kernel(levels, ext, *refs):
+    warm, shares, marine, marine_weight = refs[:4]
+    block, strips, surface, share_rows, marine_out, marine_weight_out = refs[4:10]
+    warm_in, shares_in, sems = refs[10:]
+    pairs = [(warm, warm_in), (shares, shares_in), (marine, marine_out), (marine_weight, marine_weight_out)]
+    copies = [pltpu.make_async_copy(a, b, sems.at[i]) for i, (a, b) in enumerate(pairs)]
+    for copy in copies:
+        copy.start()
+    rows, cols = surface.shape
+    high = rows + 8
+    fields = [ext[high * i : high * (i + 1), :] for i in range(levels + 1)]
+    for z, x in enumerate(diffused(fields[levels], fields[:levels])):
+        block[z] = x[:rows]
+    strips[0:high, :] = own_strips(fields[:levels])
+    strips[high : 2 * high, :] = own_strips([fields[levels]] * levels)
+    for copy in copies:
+        copy.wait()
+    surface[...] = sum(shares_in[z] * warm_in[z] for z in range(levels))
+    for z in range(levels):
+        share_rows[z : z + 1, :] = jnp.full((1, cols), shares_in[z], F32)
+
+
 def diffuse_kernel(n, levels, *refs):
-    ext, near_in, edge_in, surface, share_rows, msg, other, marine, adjoint_out, lev_out = refs[:10]
+    ext, near_in, edge_in, surface, share_rows, msg, other, marine, block, strips = refs[:10]
+    adjoint_out, lev_out = refs[10:12]
     sub, tile = lax.axis_index("sub"), lax.axis_index("tile")
     rows, cols = surface.shape
     high = rows + 8
     fold = edge_in.shape[0]
     own_values = value_rows(n, msg, other, sub)
     near_values = read_pairs(near_in, fold, 10)[4:]
-    for i, out in enumerate(refs[10:]):
+    for i, out in enumerate(refs[12:]):
         air = table_rows(n, msg, other, tile ^ (2 * i + 2), 1 - sub, sub) + own_values
         air += read_pairs(near_in, fold + 20 + 8 * i, 4) + near_values
         write_pairs(out, 0, air)
     even = tile % 2 == 0
-    place = fold_place(cols)
+    lane = lax.broadcasted_iota(jnp.int32, (8, cols), 1)
     tiles = []
     for k in range(0, fold, 8):
         near, far = near_in[k : k + 8, :], edge_in[k : k + 8, :]
         right = jnp.where(tile < n - 1, jnp.where(even, near, far), 0.0)
         left = jnp.where(tile > 0, jnp.where(even, far, near), 0.0)
-        tiles.append(jnp.where(lax.rem(place, 2 * HALO) >= HALO, right, left))
-
-    def wide(i):
-        return jnp.concatenate(
-            [ext[high * i : high * (i + 1), :], unfolded(tiles, i, high, levels + 1)], axis=1
-        )
-
-    def around(x):
-        return (
-            pltpu.roll(x, 1, 0)
-            + pltpu.roll(x, high - 1, 0)
-            + pltpu.roll(x, 1, 1)
-            + pltpu.roll(x, 2 * cols - 1, 1)
-        )
-
-    wet = wide(levels)
-    keep = wet * (1.0 - MIXING * around(wet))
-    mix = MIXING * wet
-    own_wet = wet[:rows, :cols]
+        tiles.append(jnp.where(lax.rem(lane, 2 * HALO) < HALO, right, turn_lanes(left, 2 * HALO)))
+    wet = strips_beyond(tiles, strips[high : 2 * high, :], [levels] * levels, levels + 1)
+    strip = strips_beyond(tiles, strips[0:high, :], list(range(levels)), levels + 1)
+    strip = diffused(wet, [strip])[0][:rows]
+    own_wet = ext[high * levels : high * levels + rows, :]
     heat = jnp.zeros((rows, cols), F32)
     for z in range(levels):
-        v = wet * wide(z)
-        for sweep_index in range(STEPS):
-            v = keep * v + mix * around(v)
-        adjoint = own_wet * v[:rows, :cols]
+        base = 6 * HALO * z
+        v = jnp.where(lanes_from((rows, cols), 0, HALO), turn_lanes(strip, -base - 4 * HALO), block[z])
+        last = turn_lanes(strip, -base - 2 * HALO)
+        v = jnp.where(lanes_from((rows, cols), cols - HALO, HALO), last, v)
+        adjoint = own_wet * v
         adjoint_out[z] = adjoint
         heat += share_rows[z : z + 1, :] * adjoint
     lev_out[0:rows, :] = surface[...]
@@ -272,38 +317,50 @@
     return lax.dot_general(a, b, (((ca,), (cb,)), ((), ())), preferred_element_type=F32)
 
 
-def look_up(air, at, picks, tables):
+def turned(x):
+    return x.astype(F32).T.astype(BF16)
+
+
+def look_up(air, at, picks, tables, uppers, turn=False):
+    cols = tables.shape[2] if turn else tables.shape[1]
     for band in range(2):
-        hot = onehot(air[band].astype(jnp.int32), air[band].shape[1])
-        tables[at + band] = hot
-        values = jnp.concatenate([air[4 + band], air[6 + band], air[8 + band]], axis=0)
+        cell = air[band].astype(jnp.int32)
+        hot = onehot(lax.rem(cell, cols), cols)
+        tables[at + band] = turned(hot) if turn else hot
+        values = [air[4 + band], air[6 + band], air[8 + band]]
+        values = jnp.concatenate([x[:, :cols] for x in values] + [x[:, cols:] for x in values], axis=0)
         found = dot(jnp.concatenate(halves(values), axis=0), hot, 1, 0)
-        found = found[0:3] + found[3:6]
-        picks[0, at + band : at + band + 1, :] = found[0:1]
-        picks[1, at + band : at + band + 1, :] = found[1:2]
-        picks[2, at + band : at + band + 1, :] = air[2 + band] * found[2:3]
-
-
-def near_kernel(n, fold, msg, other, near_in, picks, tables):
+        found = found[0:6] + found[6:12]
+        upper = cell >= cols
+        found = jnp.where(upper, found[3:6], found[0:3])
+        place = slice(at + band, at + band + 1)
+        picks[0, place, :] = found[0:1]
+        picks[1, place, :] = found[1:2]
+        picks[2, place, :] = air[2 + band] * found[2:3]
+        uppers[place, :] = upper.astype(F32)
+
+
+def near_kernel(n, fold, msg, other, near_in, picks, tables, uppers):
     sub, tile = lax.axis_index("sub"), lax.axis_index("tile")
     own = table_rows(n, msg, other, tile, sub, sub) + value_rows(n, msg, other, sub)
-    look_up(own, 0, picks, tables)
-    look_up(read_pairs(near_in, fold, 10), 2, picks, tables)
+    look_up(own, 0, picks, tables, uppers, True)
+    look_up(read_pairs(near_in, fold, 10), 2, picks, tables, uppers, True)
 
 
 def slot_kernel(n, count, rows, *refs):
     lev_parts, refs = refs[:count], refs[count:]
-    near_picks, near_tables, marine, weight = refs[:4]
-    far_in, refs = refs[4 : 3 + n // 2], refs[3 + n // 2 :]
+    near_picks, near_tables, near_uppers, marine, weight = refs[:5]
+    far_in, refs = refs[5 : 4 + n // 2], refs[4 + n // 2 :]
     values_out, chip_out, returns = refs[0], refs[1], refs[2 : 2 + n]
-    held, picks, tables = refs[2 + n :]
+    held, picks, tables, uppers = refs[2 + n :]
     sub, tile = lax.axis_index("sub"), lax.axis_index("tile")
     cols = chip_out.shape[1]
     picks[:, 0:4, :] = near_picks[...]
+    uppers[0:4, :] = near_uppers[0:4, :]
     for i, ref in enumerate(far_in):
         air = read_pairs(ref, 0, 20)
         for j in range(2):
-            look_up(air[10 * j : 10 * j + 10], 4 * i + 4 + 2 * j, picks, tables)
+            look_up(air[10 * j : 10 * j + 10], 4 * i + 4 + 2 * j, picks, tables, uppers)
     table = sum(ref[0 : 2 * rows, :] for ref in lev_parts)
     table = jnp.concatenate(halves(table), axis=1)
     for step in range(n):
@@ -329,12 +386,15 @@
     for step in range(n):
         for band in range(2):
             at = 2 * step + band
-            hot = near_tables[at] if at < 4 else tables[at]
+            near = at < 4
+            hot = near_tables[at] if near else tables[at]
+            upper = uppers[at : at + 1, :]
             values = jnp.concatenate([surface_sens[at : at + 1], wind_sens[at : at + 1]], axis=0)
-            sums = dot(jnp.concatenate(halves(values), axis=0), hot, 1, 1)
-            sums = sums[0:2] + sums[2:4]
-            returns[step][2 * band : 2 * band + 2, :] = sums[:, :cols]
-            returns[step][2 * band + 4 : 2 * band + 6, :] = sums[:, cols:]
+            values = jnp.concatenate([values * (1.0 - upper), values * upper], axis=0)
+            sums = dot(jnp.concatenate(halves(values), axis=0), hot, 1, 0 if near else 1)
+            sums = sums[0:4] + sums[4:8]
+            returns[step][2 * band : 2 * band + 2, :] = sums[0:2]
+            returns[step][2 * band + 4 : 2 * band + 6, :] = sums[2:4]
     if n == 4:
         chip_out[0:8, :] = jnp.where(sub == 0, returns[2][...], returns[1][...])
         write_halves(chip_out, 8, surface_sens)
@@ -342,33 +402,48 @@
         chip_out[24:40, :] = lev_parts[-1][2 * rows : 2 * rows + 16, :]
 
 
-def scatter(n, rows, cols, tile, cell_of, value_of):
+def scatter(n, rows, cols, tile, cell_of, value_of, col_hot_of=None):
     total = jnp.zeros((2 * rows, cols), F32)
     for step in range(n):
         for band in range(2):
+            at = 2 * step + band
             cell = cell_of(2 * (tile ^ step) + band)
             row, col = cell // cols, lax.rem(cell, cols)
             row_mask = lax.broadcasted_iota(jnp.int32, (rows, cell.shape[1]), 0) == row
             spread = jnp.concatenate(
-                [
-                    jnp.where(row_mask, x.astype(F32), 0.0).astype(BF16)
-                    for x in halves(value_of(2 * step + band))
-                ],
+                [jnp.where(row_mask, x.astype(F32), 0.0).astype(BF16) for x in halves(value_of(at))],
                 axis=0,
             )
-            total += dot(spread, onehot(col, cols), 1, 1)
+            if col_hot_of:
+                total += dot(spread, col_hot_of(at), 1, 0)
+            else:
+                total += dot(spread, onehot(col, cols), 1, 1)
     return total[:rows] + total[rows:]
 
 
-def own_kernel(n, marine, values, out):
+def own_kernel(n, marine, values, *refs):
     tile = lax.axis_index("tile")
+    if len(refs) > 1:
+        lev_in, theirs, out, cells, tables = refs
+        rows, cols = out.shape
+
+        @pl.when(lax.axis_index("sub") == 0)
+        def _():
+            for band, (ref, at) in enumerate(((lev_in, 2 * rows), (theirs, 24))):
+                cells[2 * n * band : 2 * n * (band + 1), :] = read_halves(ref, at, 2 * n).astype(jnp.int32)
+                for i in range(2 * n):
+                    place = 2 * n * band + 2 * (tile ^ (i // 2)) + i % 2
+                    col = lax.rem(cells[pl.ds(place, 1), :], cols)
+                    tables[2 * n * band + i] = turned(onehot(col, cols))
+
+    out = refs[2] if len(refs) > 1 else refs[0]
     rows, cols = out.shape
     out[...] = scatter(
         n, rows, cols, tile, lambda i: marine[pl.ds(i, 1), :], lambda i: values[i : i + 1, :]
     )
 
 
-def post_kernel(n, first, second, own, slots, lev_in, theirs, gradient, out, cells, values):
+def post_kernel(n, first, second, own, slots, cells, tables, gradient, out, values):
     even = lax.axis_index("sub") == 0
     tile = lax.axis_index("tile")
     rows, cols = gradient.shape
@@ -376,11 +451,17 @@
 
     @pl.when(even)
     def _():
-        for band, (ref, at) in enumerate(((lev_in, 2 * rows), (theirs, 24))):
-            cells[...] = read_halves(ref, at, 2 * n).astype(jnp.int32)
+        for band in range(2):
+            base = 2 * n * band
             values[...] = read_halves(second, 4 * n * band, 2 * n)
             total = scatter(
-                n, rows, cols, tile, lambda i: cells[pl.ds(i, 1), :], lambda i: values[i : i + 1, :]
+                n,
+                rows,
+                cols,
+                tile,
+                lambda i: cells[pl.ds(base + i, 1), :],
+                lambda i: values[i : i + 1, :],
+                lambda i: tables[base + i],
             )
             if band == 0:
                 gradient[...] = slots[...] + total
@@ -475,23 +556,28 @@
     levels, rows, cols = marine_layered_warmth.shape
     cells = bottom_sky_warmth.shape[0]
     high = rows + 8
-    raw = [marine_layered_warmth, marine_result_adjoint, marine_indicator, depth_shares]
-    raw += [
+    def pinned(*arrays):
+        return [pltpu.with_memory_space_constraint(x, pltpu.HBM) for x in arrays]
+
+    def like(x):
+        return jax.ShapeDtypeStruct(x.shape, x.dtype)
+
+    def buffers(arrays):
+        return [pltpu.VMEM(x.shape, x.dtype) for x in arrays]
+
+    air = [
         x.reshape(1, cells)
         for x in (bottom_sky_warmth, bottom_breeze_magnitude, energy_transport_adjoint)
     ]
-    raw += [piece_sky_box[0], sky_share_fraction[0], piece_marine_box[0], marine_share_fraction[0]]
-    raw = [pltpu.with_memory_space_constraint(x, pltpu.HBM) for x in raw]
-    held = [pltpu.VMEM(x.shape, x.dtype) for x in [raw[0], raw[2]]]
-    held += [pltpu.SMEM(depth_shares.shape, F32)]
-    held += [pltpu.VMEM(x.shape, x.dtype) for x in raw[4:9]]
-    msg, ext, surface, share_rows, marine, marine_weight = call(
+    raw = pinned(
+        marine_result_adjoint, marine_indicator, *air, piece_sky_box[0], sky_share_fraction[0]
+    )
+    msg, ext = call(
         functools.partial(pack_kernel, n),
-        [(4 * n + 24, cells), ((levels + 1) * high, cols), (rows, cols), (8, cols)]
-        + [jax.ShapeDtypeStruct(x.shape, x.dtype) for x in raw[9:]],
+        [(4 * n + 24, cells), ((levels + 1) * high, cols)],
         raw,
         [HBM] * len(raw),
-        scratch=held + [pltpu.SemaphoreType.DMA((10 + levels,))],
+        scratch=buffers(raw[1:]) + [pltpu.SemaphoreType.DMA((len(raw) - 1 + levels,))],
     )
     other = traded(msg, 0, 1)
     fold = 8 * fold_slots(high, cols, levels + 1)[1]
@@ -502,29 +588,43 @@
     )
     edge_in = beyond(edge_out)
     near_in = traded(near_out, 1, 1)
+    raw = pinned(marine_layered_warmth, depth_shares, piece_marine_box[0], marine_share_fraction[0])
+    block, strips, surface, share_rows, marine, marine_weight = call(
+        functools.partial(side_kernel, levels),
+        [(levels, rows, cols), (2 * high, cols), (rows, cols), (8, cols), like(raw[2]), like(raw[3])],
+        [ext, *raw],
+        [VMEM] + [HBM] * 4,
+        scratch=buffers(raw[:1])
+        + [pltpu.SMEM(depth_shares.shape, F32), pltpu.SemaphoreType.DMA((4,))],
+    )
     merged = n == 4 and levs == 2
     adjoint, lev_msg, *far_out = call(
         functools.partial(diffuse_kernel, n, levels),
         [(levels, rows, cols), (2 * rows + (16 if merged else 0), cols)] + [(40, cols)] * (n // 2 - 1),
-        [ext, near_in, edge_in, surface, share_rows, msg, other, marine],
+        [ext, near_in, edge_in, surface, share_rows, msg, other, marine, block, strips],
     )
     lev_in = lev_parts(lev_msg)
     far_in = [traded(x, 2 * i + 2, 1) for i, x in enumerate(far_out)]
-    picks, tables = call(
+    picks, tables, uppers = call(
         functools.partial(near_kernel, n, fold),
-        [(3, 4, cells), jax.ShapeDtypeStruct((4, cells, cells), BF16)],
+        [(3, 4, cells), jax.ShapeDtypeStruct((4, cells, cols), BF16), (8, cells)],
         [msg, other, near_in],
     )
     values, chip, *returns = call(
         functools.partial(slot_kernel, n, len(lev_in), rows),
         [(2 * n, cells), (40, cols)] + [(8, cols)] * n,
-        [*lev_in, picks, tables, marine, marine_weight, *far_in],
+        [*lev_in, picks, tables, uppers, marine, marine_weight, *far_in],
         scratch=[pltpu.VMEM((3, 2 * n, cells), F32)] * 2
-        + [pltpu.VMEM((2 * n, cells, cells), BF16)],
-    )
-    (slots,) = call(functools.partial(own_kernel, n), [(rows, cols)], [marine, values])
+        + [pltpu.VMEM((2 * n, cols, cells), BF16), pltpu.VMEM((2 * n, cells), F32)],
+    )
     if merged:
         theirs = traded(chip, 0, 1)
+        slots, partner_cells, partner_tables = call(
+            functools.partial(own_kernel, n),
+            [(rows, cols), jax.ShapeDtypeStruct((4 * n, cells), jnp.int32)]
+            + [jax.ShapeDtypeStruct((4 * n, cells, cols), BF16)],
+            [marine, values, lev_in[1], theirs],
+        )
         first, second = call(
             merge_kernel, [(32, cols), (32, cols)], [values, *returns[1:], theirs]
         )
@@ -533,10 +633,11 @@
         gradient, sums = call(
             functools.partial(post_kernel, n),
             [(rows, cols), (rows + 8, cols)],
-            [first, second, returns[0], slots, lev_in[1], theirs],
-            scratch=[pltpu.VMEM((2 * n, cells), jnp.int32), pltpu.VMEM((2 * n, cells), F32)],
+            [first, second, returns[0], slots, partner_cells, partner_tables],
+            scratch=[pltpu.VMEM((2 * n, cells), F32)],
         )
     else:
+        (slots,) = call(functools.partial(own_kernel, n), [(rows, cols)], [marine, values])
         gradient = sum(lev_parts(slots))
         sums = returns[0]
         for step in range(1, n):

time: 25.5 us -> 25.1 us (0.984)
  waiting for transfers between devices: 7.92 us -> 6.43 us
  Pallas kernels: 4.59 us -> 5.43 us
    pallas_call x9 -> x10, Pallas kernels: 4.59 us -> 5.43 us  [call(): pl.pallas_call(kernel, out_shape=outs, in_specs=specs or [VMEM] * len(ope...]
    ppermute x1, waiting for transfers between devices: 0.83 us -> 0.01 us  [beyond(): return lax.ppermute(x, ('tile', 'sub'), pairs)]
    ppermute x2, waiting for transfers between devices: 2.84 us -> 2.46 us  [by_core(): return lax.ppermute(x, ('tile', 'lev', 'sub'), pairs)]
    ppermute x5, waiting for transfers between devices: 4.24 us -> 3.97 us  [traded(): return lax.ppermute(x, ('tile', 'sub'), pairs)]
  transfers between devices with their start and end apart: 9 -> 9, of which waited for: 8 -> 7; matrix products, arithmetic and copies ran while one was open for 0% -> 0% of each run, Pallas kernels for 2% -> 8%
where the time goes in v8:
time: 25.1 us; the launch traced here: 24.8 us
  starting transfers between devices  12.3 us (49%)
  waiting for transfers between devices  6.43 us (26%)
  Pallas kernels  5.43 us (22%)
  between operations  0.7 us (3%)
    ppermute x5, starting transfers between devices, traded(): return lax.ppermute(x, ('tile', 'sub'), pairs)  7.56 us
    pallas_call x10, Pallas kernels, call(): pl.pallas_call(kernel, out_shape=outs, in_specs=specs or [VMEM] * len(ope...  5.43 us
    ppermute x5, waiting for transfers between devices, traded(): return lax.ppermute(x, ('tile', 'sub'), pairs)  3.97 us
    ppermute x2, waiting for transfers between devices, by_core(): return lax.ppermute(x, ('tile', 'lev', 'sub'), pairs)  2.46 us
    ppermute x2, starting transfers between devices, by_core(): return lax.ppermute(x, ('tile', 'lev', 'sub'), pairs)  2.41 us
    ppermute x1, starting transfers between devices, lev_parts(): return [x, lax.ppermute(x, 'lev', [(0, 1), (1, 0)])]  1.95 us
  transfers between devices with their start and end apart: 9, of which 7 were waited for; matrix products, arithmetic and copies ran while one was open for 0% of the time, Pallas kernels for 8%

profile of v8, /device:TPU:0, one launch (start us, length us, event | category | flops | bytes accessed | tf_op | source)
XLA Modules:
  0.0 24.8 jit_solution(11636244137598023582)
XLA Ops:
  0.6 1.0 %shard_map.130 = (f32[40,256]{1,0:T(8,128)S(1)}, f32[216,128]{1,0:T(8,128)S(1)}) custom-call(f32[2,64,128]{2,1,0:T(8,128)} %refs_0_.2, s32[64,128]{1,0:T(8,128)} %refs_1_.2, f32[1,256]{1,0:T(1,128)} %bitcast.13, f32[1,256]{1,0:T(1,128)} %bitcast.14, f32[1,256]{1,0:T(1,128)} %bitcast.15, s32[8,256]{1,0:T(8,128)} %bitcast.9, f32[8,256]{1,0:T(8,128)} %bitcast.10), custom_call_target="tpu_custom_call" | custom-call | tf_op jit(solution)/shard_map/pallas_call | solution.py:24
  1.6 0.5 %collective-permute-start = (f32[40,256]{1,0:T(8,128)S(1)}, f32[40,256]{1,0:T(8,128)S(1)}, u32[]{:S(2)}, u32[]{:S(2)}) collective-permute-start(f32[40,256]{1,0:T(8,128)S(1)} %get-tuple-element.36.msg.refs_5_), channel_id=1, source_target_pairs={{0,1},{1,0},{4,5},{5,4},{8,9},{9,8},{12,13},{13,12},{2,3},{3,2},{6... | collective-permute-start | bytes 122888 | tf_op jit(solution)/shard_map/ppermute | solution.py:513
  2.1 0.9 %collective-permute-done.other.refs_6_ = f32[40,256]{1,0:T(8,128)S(1)} collective-permute-done((f32[40,256]{1,0:T(8,128)S(1)}, f32[40,256]{1,0:T(8,128)S(1)}, u32[]{:S(2)}, u32[]{:S(2)}) %collective-permute-start) | collective-permute-done | bytes 40992 | tf_op jit(solution)/shard_map/ppermute | solution.py:513
  3.0 0.1 shard_map.131
  3.1 2.7 %collective-permute-start.1 = (f32[48,128]{1,0:T(8,128)S(1)}, f32[48,128]{1,0:T(8,128)S(1)}, u32[]{:S(2)}, u32[]{:S(2)}) collective-permute-start(f32[48,128]{1,0:T(8,128)S(1)} %get-tuple-element.39), channel_id=1, source_target_pairs={{0,5},{1,4},{4,1},{5,0},{8,13},{9,12},{12,9},{13,8},{2,7},{3,6},{6... | collective-permute-start | bytes 73736 | tf_op jit(solution)/shard_map/ppermute | solution.py:513
  5.8 0.3 %collective-permute-start.2 = (f32[16,128]{1,0:T(8,128)S(1)}, f32[16,128]{1,0:T(8,128)S(1)}, u32[]{:S(2)}, u32[]{:S(2)}) collective-permute-start(f32[16,128]{1,0:T(8,128)S(1)} %get-tuple-element.40), channel_id=1, source_target_pairs={{0,1},{1,0},{4,9},{5,8},{8,5},{9,4},{12,13},{13,12},{2,3},{3,2},{6... | collective-permute-start | bytes 24584 | tf_op jit(solution)/shard_map/ppermute | solution.py:522
  6.1 1.0 %shard_map.132 = (f32[2,64,128]{2,1,0:T(8,128)S(1)}, f32[144,128]{1,0:T(8,128)S(1)}, f32[64,128]{1,0:T(8,128)S(1)}, f32[8,128]{1,0:T(8,128)S(1)}, s32[8,256]{1,0:T(8,128)S(1)}, /*index=5*/f32[8,256]{1,0:T(8,128)S(1)}) custom-call(f32[216,128]{1,0:T(8,128)S(1)} %get-tuple-element.38.ext.refs_0_, f32[2,64,128]{2,1,0:T(8,128)} %refs_0_.3, f32[2]{0:T(128)} %refs_1_.3, ...), custom_call_target="tpu_custom_call" | custom-call | tf_op jit(solution)/shard_map/pallas_call | solution.py:24
  7.2 0.0 collective-permute-done.2.refs_2_
  7.2 0.1 collective-permute-done.1.refs_1_.near_in
  7.3 0.5 %shard_map.133 = (f32[2,64,128]{2,1,0:T(8,128)S(1)}, f32[144,128]{1,0:T(8,128)S(1)}, f32[40,128]{1,0:T(8,128)S(1)}) custom-call(f32[216,128]{1,0:T(8,128)S(1)} %get-tuple-element.38.ext.refs_0_, f32[48,128]{1,0:T(8,128)S(1)} %collective-permute-done.1.refs_1_.near_in, f32[16,128]{1,0:T(8,128)S(1)} %collective-permute-done.2.refs_2_, ...), custom_call_target="tpu_custom_call" | custom-call | tf_op jit(solution)/shard_map/pallas_call | solution.py:24
  7.8 1.9 %collective-permute-start.3 = (f32[144,128]{1,0:T(8,128)S(1)}, f32[144,128]{1,0:T(8,128)S(1)}, u32[]{:S(2)}, u32[]{:S(2)}) collective-permute-start(f32[144,128]{1,0:T(8,128)S(1)} %get-tuple-element.46.refs_0_), channel_id=1, source_target_pairs={{0,2},{2,0},{1,3},{3,1},{4,6},{6,4},{5,7},{7,5},{8,10},{10,8},{9,1... | collective-permute-start | bytes 221192 | tf_op jit(solution)/shard_map/ppermute | solution.py:538
  9.8 3.4 %collective-permute-start.4 = (f32[40,128]{1,0:T(8,128)S(1)}, f32[40,128]{1,0:T(8,128)S(1)}, u32[]{:S(2)}, u32[]{:S(2)}) collective-permute-start(f32[40,128]{1,0:T(8,128)S(1)} %get-tuple-element.51), channel_id=1, source_target_pairs={{0,9},{1,8},{4,13},{5,12},{8,1},{9,0},{12,5},{13,4},{2,11},{3,10},... | collective-permute-start | bytes 61448 | tf_op jit(solution)/shard_map/ppermute | solution.py:513
  13.2 0.2 shard_map.134
  13.5 1.2 %collective-permute-done.4.refs_7_ = f32[40,128]{1,0:T(8,128)S(1)} collective-permute-done((f32[40,128]{1,0:T(8,128)S(1)}, f32[40,128]{1,0:T(8,128)S(1)}, u32[]{:S(2)}, u32[]{:S(2)}) %collective-permute-start.4) | collective-permute-done | bytes 20512 | tf_op jit(solution)/shard_map/ppermute | solution.py:513
  14.7 0.0 collective-permute-done.3.refs_1_.refs_0_
  14.7 0.8 %shard_map.135 = (f32[8,256]{1,0:T(8,128)S(1)}, f32[40,128]{1,0:T(8,128)S(1)}, f32[8,128]{1,0:T(8,128)S(1)}, f32[8,128]{1,0:T(8,128)S(1)}, f32[8,128]{1,0:T(8,128)S(1)}, /*index=5*/f32[8,128]{1,0:T(8,128)S(1)}) custom-call(f32[144,128]{1,0:T(8,128)S(1)} %get-tuple-element.46.refs_0_, f32[144,128]{1,0:T(8,128)S(1)} %collective-permute-done.3.refs_1_.refs_0_, ...), custom_call_target="tpu_custom_call" | custom-call | tf_op jit(solution)/shard_map/pallas_call | solution.py:24
  15.5 0.5 %collective-permute-start.5 = (f32[40,128]{1,0:T(8,128)S(1)}, f32[40,128]{1,0:T(8,128)S(1)}, u32[]{:S(2)}, u32[]{:S(2)}) collective-permute-start(f32[40,128]{1,0:T(8,128)S(1)} %get-tuple-element.56), channel_id=1, source_target_pairs={{0,1},{1,0},{4,5},{5,4},{8,9},{9,8},{12,13},{13,12},{2,3},{3,2},{6... | collective-permute-start | bytes 61448 | tf_op jit(solution)/shard_map/ppermute | solution.py:513
  15.9 0.8 %collective-permute-done.5.theirs.refs_1_ = f32[40,128]{1,0:T(8,128)S(1)} collective-permute-done((f32[40,128]{1,0:T(8,128)S(1)}, f32[40,128]{1,0:T(8,128)S(1)}, u32[]{:S(2)}, u32[]{:S(2)}) %collective-permute-start.5) | collective-permute-done | bytes 20512 | tf_op jit(solution)/shard_map/ppermute | solution.py:513
  16.8 1.9 %collective-permute-start.6 = (f32[32,128]{1,0:T(8,128)S(1)}, f32[32,128]{1,0:T(8,128)S(1)}, u32[]{:S(2)}, u32[]{:S(2)}) collective-permute-start(f32[32,128]{1,0:T(8,128)S(1)} %get-tuple-element.57), channel_id=1, source_target_pairs={{0,4},{1,13},{2,6},{3,15},{4,0},{5,9},{6,2},{7,11},{8,12},{9,5},{1... | collective-permute-start | bytes 49160 | tf_op jit(solution)/shard_map/ppermute | solution.py:533
  18.7 0.5 %collective-permute-start.7 = (f32[32,128]{1,0:T(8,128)S(1)}, f32[32,128]{1,0:T(8,128)S(1)}, u32[]{:S(2)}, u32[]{:S(2)}) collective-permute-start(f32[32,128]{1,0:T(8,128)S(1)} %get-tuple-element.58), channel_id=1, source_target_pairs={{0,2},{1,9},{2,0},{3,11},{4,6},{5,13},{6,4},{7,15},{8,10},{9,1},{1... | collective-permute-start | bytes 49160 | tf_op jit(solution)/shard_map/ppermute | solution.py:533
  19.2 0.7 %shard_map.137 = (f32[64,128]{1,0:T(8,128)S(1)}, s32[16,256]{1,0:T(8,128)S(1)}, bf16[16,256,128]{2,1,0:T(8,128)(2,1)S(1)}) custom-call(s32[8,256]{1,0:T(8,128)S(1)} %get-tuple-element.43.refs_7_.refs_5_.marine, f32[8,256]{1,0:T(8,128)S(1)} %get-tuple-element.52.values, f32[144,128]{1,0:T(8,128)S(1)} %collective-permute-done.3.refs_1_.refs_0_, ...), custom_call_target="tpu_custom_call" | custom-call | tf_op jit(solution)/shard_map/pallas_call | solution.py:24
  19.9 0.6 %collective-permute-done.6.first = f32[32,128]{1,0:T(8,128)S(1)} collective-permute-done((f32[32,128]{1,0:T(8,128)S(1)}, f32[32,128]{1,0:T(8,128)S(1)}, u32[]{:S(2)}, u32[]{:S(2)}) %collective-permute-start.6) | collective-permute-done | bytes 16416 | tf_op jit(solution)/shard_map/ppermute | solution.py:533
  20.5 1.9 %collective-permute-done.7.second = f32[32,128]{1,0:T(8,128)S(1)} collective-permute-done((f32[32,128]{1,0:T(8,128)S(1)}, f32[32,128]{1,0:T(8,128)S(1)}, u32[]{:S(2)}, u32[]{:S(2)}) %collective-permute-start.7) | collective-permute-done | bytes 16416 | tf_op jit(solution)/shard_map/ppermute | solution.py:533
  22.4 0.4 %shard_map.138 = (f32[64,128]{1,0:T(8,128)S(1)}, f32[72,128]{1,0:T(8,128)S(1)}) custom-call(f32[32,128]{1,0:T(8,128)S(1)} %collective-permute-done.6.first, f32[32,128]{1,0:T(8,128)S(1)} %collective-permute-done.7.second, f32[8,128]{1,0:T(8,128)S(1)} %get-tuple-element.59.own, f32[64,128]{1,0:T(8,128)S(1)} %get-tuple-element.60.slots, ...), custom_call_target="tpu_custom_call" | custom-call | tf_op jit(solution)/shard_map/pallas_call | solution.py:24
  22.8 0.4 %collective-permute-start.8 = (f32[72,128]{1,0:T(8,128)S(1)}, f32[72,128]{1,0:T(8,128)S(1)}, u32[]{:S(2)}, u32[]{:S(2)}) collective-permute-start(f32[72,128]{1,0:T(8,128)S(1)} %get-tuple-element.65.sums), channel_id=1, source_target_pairs={{0,1},{1,0},{4,5},{5,4},{8,9},{9,8},{12,13},{13,12},{2,3},{3,2},{6... | collective-permute-start | bytes 110600 | tf_op jit(solution)/shard_map/ppermute | solution.py:513
  23.3 0.9 %collective-permute-done.8.other = f32[72,128]{1,0:T(8,128)S(1)} collective-permute-done((f32[72,128]{1,0:T(8,128)S(1)}, f32[72,128]{1,0:T(8,128)S(1)}, u32[]{:S(2)}, u32[]{:S(2)}) %collective-permute-start.8) | collective-permute-done | bytes 36896 | tf_op jit(solution)/shard_map/ppermute | solution.py:513
  24.1 0.7 %shard_map.139 = (f32[2,64,128]{2,1,0:T(8,128)}, f32[1,256]{1,0:T(1,128)}, f32[1,256]{1,0:T(1,128)}) custom-call(f32[64,128]{1,0:T(8,128)S(1)} %get-tuple-element.63.slots, f32[2,64,128]{2,1,0:T(8,128)S(1)} %get-tuple-element.64.adjoint, f32[8,128]{1,0:T(8,128)S(1)} %get-tuple-element.42.refs_4_.share_rows, f32[72,128]{1,0:T(8,128)S(1)} %get-tuple-element.65.sums, ...), custom_call_target="tpu_custom_call" | custom-call | tf_op jit(solution)/shard_map/pallas_call | solution.py:24
  (1 shorter events, 0.0 us)
Async XLA Ops:
  1.6 1.4 %collective-permute-start = (f32[40,256]{1,0:T(8,128)S(1)}, f32[40,256]{1,0:T(8,128)S(1)}, u32[]{:S(2)}, u32[]{:S(2)}) collective-permute-start(f32[40,256]{1,0:T(8,128)S(1)} %get-tuple-element.36.msg.refs_5_), channel_id=1, source_target_pairs={{0,1},{1,0},{4,5},{5,4},{8,9},{9,8},{12,13},{13,12},{2,3},{3,2},{6... | collective-permute-start | bytes 122888 | tf_op jit(solution)/shard_map/ppermute | solution.py:513
  3.1 4.2 %collective-permute-start.1 = (f32[48,128]{1,0:T(8,128)S(1)}, f32[48,128]{1,0:T(8,128)S(1)}, u32[]{:S(2)}, u32[]{:S(2)}) collective-permute-start(f32[48,128]{1,0:T(8,128)S(1)} %get-tuple-element.39), channel_id=1, source_target_pairs={{0,5},{1,4},{4,1},{5,0},{8,13},{9,12},{12,9},{13,8},{2,7},{3,6},{6... | collective-permute-start | bytes 73736 | tf_op jit(solution)/shard_map/ppermute | solution.py:513
  5.8 1.4 %collective-permute-start.2 = (f32[16,128]{1,0:T(8,128)S(1)}, f32[16,128]{1,0:T(8,128)S(1)}, u32[]{:S(2)}, u32[]{:S(2)}) collective-permute-start(f32[16,128]{1,0:T(8,128)S(1)} %get-tuple-element.40), channel_id=1, source_target_pairs={{0,1},{1,0},{4,9},{5,8},{8,5},{9,4},{12,13},{13,12},{2,3},{3,2},{6... | collective-permute-start | bytes 24584 | tf_op jit(solution)/shard_map/ppermute | solution.py:522
  7.8 6.9 %collective-permute-start.3 = (f32[144,128]{1,0:T(8,128)S(1)}, f32[144,128]{1,0:T(8,128)S(1)}, u32[]{:S(2)}, u32[]{:S(2)}) collective-permute-start(f32[144,128]{1,0:T(8,128)S(1)} %get-tuple-element.46.refs_0_), channel_id=1, source_target_pairs={{0,2},{2,0},{1,3},{3,1},{4,6},{6,4},{5,7},{7,5},{8,10},{10,8},{9,1... | collective-permute-start | bytes 221192 | tf_op jit(solution)/shard_map/ppermute | solution.py:538
  9.8 4.9 %collective-permute-start.4 = (f32[40,128]{1,0:T(8,128)S(1)}, f32[40,128]{1,0:T(8,128)S(1)}, u32[]{:S(2)}, u32[]{:S(2)}) collective-permute-start(f32[40,128]{1,0:T(8,128)S(1)} %get-tuple-element.51), channel_id=1, source_target_pairs={{0,9},{1,8},{4,13},{5,12},{8,1},{9,0},{12,5},{13,4},{2,11},{3,10},... | collective-permute-start | bytes 61448 | tf_op jit(solution)/shard_map/ppermute | solution.py:513
  15.5 1.3 %collective-permute-start.5 = (f32[40,128]{1,0:T(8,128)S(1)}, f32[40,128]{1,0:T(8,128)S(1)}, u32[]{:S(2)}, u32[]{:S(2)}) collective-permute-start(f32[40,128]{1,0:T(8,128)S(1)} %get-tuple-element.56), channel_id=1, source_target_pairs={{0,1},{1,0},{4,5},{5,4},{8,9},{9,8},{12,13},{13,12},{2,3},{3,2},{6... | collective-permute-start | bytes 61448 | tf_op jit(solution)/shard_map/ppermute | solution.py:513
  16.8 3.7 %collective-permute-start.6 = (f32[32,128]{1,0:T(8,128)S(1)}, f32[32,128]{1,0:T(8,128)S(1)}, u32[]{:S(2)}, u32[]{:S(2)}) collective-permute-start(f32[32,128]{1,0:T(8,128)S(1)} %get-tuple-element.57), channel_id=1, source_target_pairs={{0,4},{1,13},{2,6},{3,15},{4,0},{5,9},{6,2},{7,11},{8,12},{9,5},{1... | collective-permute-start | bytes 49160 | tf_op jit(solution)/shard_map/ppermute | solution.py:533
  18.7 3.7 %collective-permute-start.7 = (f32[32,128]{1,0:T(8,128)S(1)}, f32[32,128]{1,0:T(8,128)S(1)}, u32[]{:S(2)}, u32[]{:S(2)}) collective-permute-start(f32[32,128]{1,0:T(8,128)S(1)} %get-tuple-element.58), channel_id=1, source_target_pairs={{0,2},{1,9},{2,0},{3,11},{4,6},{5,13},{6,4},{7,15},{8,10},{9,1},{1... | collective-permute-start | bytes 49160 | tf_op jit(solution)/shard_map/ppermute | solution.py:533
  22.8 1.3 %collective-permute-start.8 = (f32[72,128]{1,0:T(8,128)S(1)}, f32[72,128]{1,0:T(8,128)S(1)}, u32[]{:S(2)}, u32[]{:S(2)}) collective-permute-start(f32[72,128]{1,0:T(8,128)S(1)} %get-tuple-element.65.sums), channel_id=1, source_target_pairs={{0,1},{1,0},{4,5},{5,4},{8,9},{9,8},{12,13},{13,12},{2,3},{3,2},{6... | collective-permute-start | bytes 110600 | tf_op jit(solution)/shard_map/ppermute | solution.py:513

commit v9 on v8

--- a/solution.py
+++ b/solution.py
@@ -63,9 +63,13 @@
     return jnp.concatenate(out, axis=0)
 
 
+def strip_base(z):
+    return 6 * HALO * z - 4 * HALO
+
+
 def lanes_from(shape, first, count):
     lane = lax.broadcasted_iota(jnp.int32, shape, 1)
-    return (lane >= first) & (lane < first + count)
+    return lax.rem(lane + (-first) % shape[1], shape[1]) < count
 
 
 def turn_lanes(x, by):
@@ -78,7 +82,7 @@
     cols = fields[0].shape[1]
     out = jnp.zeros_like(fields[0])
     for z, x in enumerate(fields):
-        base = 3 * width * z
+        base = strip_base(z)
         out = jnp.where(lanes_from(x.shape, base, width), turn_lanes(x, base + width), out)
         out = jnp.where(lanes_from(x.shape, base + 2 * width, width), turn_lanes(x, base + 2 * width), out)
     return out
@@ -91,11 +95,18 @@
     for g, (k, at) in enumerate(fold_slots(high, cols, count)[0]):
         x = own[8 * g : 8 * g + 8]
         for z, i in enumerate(fields):
-            base = width * (3 * z + 1)
+            base = strip_base(z) + width
             moved = turn_lanes(tiles[k], base - width * (at * count + i))
             x = jnp.where(lanes_from(x.shape, base, width), moved, x)
         out.append(x)
     return jnp.concatenate(out, axis=0)
+
+
+def from_strips(strip, z, block):
+    shape = block.shape
+    first, last = lanes_from(shape, 0, HALO), lanes_from(shape, -HALO, HALO)
+    block = jnp.where(first, turn_lanes(strip, -strip_base(z) - 4 * HALO), block)
+    return jnp.where(last, turn_lanes(strip, -strip_base(z) - 2 * HALO), block)
 
 
 def around(x):
@@ -230,8 +241,8 @@
 
 def side_kernel(levels, ext, *refs):
     warm, shares, marine, marine_weight = refs[:4]
-    block, strips, surface, share_rows, marine_out, marine_weight_out = refs[4:10]
-    warm_in, shares_in, sems = refs[10:]
+    block, strips, surface, block_heat, share_rows, marine_out, marine_weight_out = refs[4:11]
+    warm_in, shares_in, sems = refs[11:]
     pairs = [(warm, warm_in), (shares, shares_in), (marine, marine_out), (marine_weight, marine_weight_out)]
     copies = [pltpu.make_async_copy(a, b, sems.at[i]) for i, (a, b) in enumerate(pairs)]
     for copy in copies:
@@ -246,13 +257,14 @@
     for copy in copies:
         copy.wait()
     surface[...] = sum(shares_in[z] * warm_in[z] for z in range(levels))
+    block_heat[...] = sum(shares_in[z] * block[z] for z in range(levels))
     for z in range(levels):
         share_rows[z : z + 1, :] = jnp.full((1, cols), shares_in[z], F32)
 
 
 def diffuse_kernel(n, levels, *refs):
-    ext, near_in, edge_in, surface, share_rows, msg, other, marine, block, strips = refs[:10]
-    adjoint_out, lev_out = refs[10:12]
+    ext, near_in, edge_in, surface, share_rows, msg, other, marine, block_heat, strips = refs[:10]
+    strip_out, lev_out = refs[10:12]
     sub, tile = lax.axis_index("sub"), lax.axis_index("tile")
     rows, cols = surface.shape
     high = rows + 8
@@ -275,15 +287,11 @@
     strip = strips_beyond(tiles, strips[0:high, :], list(range(levels)), levels + 1)
     strip = diffused(wet, [strip])[0][:rows]
     own_wet = ext[high * levels : high * levels + rows, :]
-    heat = jnp.zeros((rows, cols), F32)
-    for z in range(levels):
-        base = 6 * HALO * z
-        v = jnp.where(lanes_from((rows, cols), 0, HALO), turn_lanes(strip, -base - 4 * HALO), block[z])
-        last = turn_lanes(strip, -base - 2 * HALO)
-        v = jnp.where(lanes_from((rows, cols), cols - HALO, HALO), last, v)
-        adjoint = own_wet * v
-        adjoint_out[z] = adjoint
-        heat += share_rows[z : z + 1, :] * adjoint
+    strip_out[...] = strip
+    heat = share_rows[0:1, :] * strip
+    for z in range(1, levels):
+        heat += share_rows[z : z + 1, :] * turn_lanes(strip, strip_base(0) - strip_base(z))
+    heat = from_strips(heat, 0, block_heat[...])
     lev_out[0:rows, :] = surface[...]
     lev_out[rows : 2 * rows, :] = own_wet * heat
     if lev_out.shape[0] > 2 * rows:
@@ -340,19 +348,22 @@
         uppers[place, :] = upper.astype(F32)
 
 
-def near_kernel(n, fold, msg, other, near_in, picks, tables, uppers):
+def near_kernel(n, fold, msg, other, near_in, ext, block, strip, picks, tables, uppers, adjoint):
     sub, tile = lax.axis_index("sub"), lax.axis_index("tile")
     own = table_rows(n, msg, other, tile, sub, sub) + value_rows(n, msg, other, sub)
     look_up(own, 0, picks, tables, uppers, True)
     look_up(read_pairs(near_in, fold, 10), 2, picks, tables, uppers, True)
+    levels, rows, cols = adjoint.shape
+    own_wet = ext[(rows + 8) * levels : (rows + 8) * levels + rows, :]
+    for z in range(levels):
+        adjoint[z] = own_wet * from_strips(strip[...], z, block[z])
 
 
 def slot_kernel(n, count, rows, *refs):
     lev_parts, refs = refs[:count], refs[count:]
     near_picks, near_tables, near_uppers, marine, weight = refs[:5]
     far_in, refs = refs[5 : 4 + n // 2], refs[4 + n // 2 :]
-    values_out, chip_out, returns = refs[0], refs[1], refs[2 : 2 + n]
-    held, picks, tables, uppers = refs[2 + n :]
+    values_out, wind_out, uppers, tables, chip_out, held, picks = refs
     sub, tile = lax.axis_index("sub"), lax.axis_index("tile")
     cols = chip_out.shape[1]
     picks[:, 0:4, :] = near_picks[...]
@@ -383,23 +394,64 @@
     surface_sens = contrast_sens * wind
     wind_sens = contrast_sens * difference
     values_out[...] = surface_sens
-    for step in range(n):
-        for band in range(2):
-            at = 2 * step + band
-            near = at < 4
-            hot = near_tables[at] if near else tables[at]
-            upper = uppers[at : at + 1, :]
-            values = jnp.concatenate([surface_sens[at : at + 1], wind_sens[at : at + 1]], axis=0)
-            values = jnp.concatenate([values * (1.0 - upper), values * upper], axis=0)
-            sums = dot(jnp.concatenate(halves(values), axis=0), hot, 1, 0 if near else 1)
-            sums = sums[0:4] + sums[4:8]
-            returns[step][2 * band : 2 * band + 2, :] = sums[0:2]
-            returns[step][2 * band + 4 : 2 * band + 6, :] = sums[2:4]
+    wind_out[...] = wind_sens
     if n == 4:
-        chip_out[0:8, :] = jnp.where(sub == 0, returns[2][...], returns[1][...])
+        sums = functools.partial(air_sums, values_out, wind_out, uppers, near_tables, tables)
         write_halves(chip_out, 8, surface_sens)
-        chip_out[8:16, :] = jnp.where(sub == 0, returns[3][...], chip_out[8:16, :])
         chip_out[24:40, :] = lev_parts[-1][2 * rows : 2 * rows + 16, :]
+
+        lead = leads()
+
+        @pl.when(lead)
+        def _():
+            chip_out[0:8, :] = sums(2)
+            chip_out[8:16, :] = sums(1)
+
+        @pl.when(jnp.logical_not(lead))
+        def _():
+            chip_out[0:8, :] = sums(3)
+
+
+def leads():
+    tile = lax.axis_index("tile")
+    return (lax.axis_index("sub") == 1) != ((tile == 1) | (tile == 2))
+
+
+def air_sums(values, winds, uppers, near_tables, tables, step):
+    rows = [None] * 4
+    for band in range(2):
+        at = 2 * step + band
+        near = at < 4
+        hot = near_tables[at] if near else tables[at]
+        place = slice(at, at + 1)
+        upper = uppers[place, :]
+        both = jnp.concatenate([values[place, :], winds[place, :]], axis=0)
+        both = jnp.concatenate([both * (1.0 - upper), both * upper], axis=0)
+        sums = dot(jnp.concatenate(halves(both), axis=0), hot, 1, 0 if near else 1)
+        sums = sums[0:4] + sums[4:8]
+        rows[band], rows[2 + band] = sums[0:2], sums[2:4]
+    return jnp.concatenate(rows, axis=0)
+
+
+def kept_kernel(n, values, winds, uppers, near_tables, tables, *returns):
+    sums = functools.partial(air_sums, values, winds, uppers, near_tables, tables)
+    if n != 4:
+        for step in range(n):
+            returns[step][...] = sums(step)
+        return
+    lead = leads()
+    own, first, second = returns
+    own[...] = sums(0)
+
+    @pl.when(lead)
+    def _():
+        first[...] = sums(3)
+        second[...] = jnp.zeros_like(second)
+
+    @pl.when(jnp.logical_not(lead))
+    def _():
+        first[...] = sums(2)
+        second[...] = sums(1)
 
 
 def scatter(n, rows, cols, tile, cell_of, value_of, col_hot_of=None):
@@ -427,7 +479,7 @@
         lev_in, theirs, out, cells, tables = refs
         rows, cols = out.shape
 
-        @pl.when(lax.axis_index("sub") == 0)
+        @pl.when(leads())
         def _():
             for band, (ref, at) in enumerate(((lev_in, 2 * rows), (theirs, 24))):
                 cells[2 * n * band : 2 * n * (band + 1), :] = read_halves(ref, at, 2 * n).astype(jnp.int32)
@@ -443,43 +495,49 @@
     )
 
 
-def post_kernel(n, first, second, own, slots, cells, tables, gradient, out, values):
-    even = lax.axis_index("sub") == 0
-    tile = lax.axis_index("tile")
-    rows, cols = gradient.shape
-    out[0:8, :] = first[0:8, :] + own[...] + jnp.where(even, 0.0, second[0:8, :])
-
-    @pl.when(even)
+def partner_part(n, band, second, cells, tables, values, shape):
+    rows, cols = shape
+    base = 2 * n * band
+    values[...] = read_halves(second, 4 * n * band, 2 * n)
+    return scatter(
+        n,
+        rows,
+        cols,
+        lax.axis_index("tile"),
+        lambda i: cells[pl.ds(base + i, 1), :],
+        lambda i: values[i : i + 1, :],
+        lambda i: tables[base + i],
+    )
+
+
+def post_kernel(n, first, second, own, cells, tables, out, second_out, values):
+    lead = leads()
+    rows, cols = out.shape[0] - 8, out.shape[1]
+    out[0:8, :] = first[0:8, :] + own[...] + jnp.where(lead, 0.0, second[0:8, :])
+    second_out[...] = second[...]
+
+    @pl.when(lead)
     def _():
-        for band in range(2):
-            base = 2 * n * band
-            values[...] = read_halves(second, 4 * n * band, 2 * n)
-            total = scatter(
-                n,
-                rows,
-                cols,
-                tile,
-                lambda i: cells[pl.ds(base + i, 1), :],
-                lambda i: values[i : i + 1, :],
-                lambda i: tables[base + i],
-            )
-            if band == 0:
-                gradient[...] = slots[...] + total
-            else:
-                out[8 : rows + 8, :] = total
-
-    @pl.when(jnp.logical_not(even))
+        out[8 : rows + 8, :] = partner_part(n, 1, second, cells, tables, values, (rows, cols))
+
+    @pl.when(jnp.logical_not(lead))
     def _():
-        gradient[...] = slots[...]
-        out[8 : rows + 8, :] = jnp.zeros_like(slots)
-
-
-def merge_kernel(values, near, two, three, theirs, first, second):
-    even = lax.axis_index("sub") == 0
+        out[8 : rows + 8, :] = jnp.zeros((rows, cols), F32)
+
+
+def gradient_kernel(n, second, slots, cells, tables, gradient, values):
+    gradient[...] = slots[...]
+
+    @pl.when(leads())
+    def _():
+        gradient[...] += partner_part(n, 0, second, cells, tables, values, gradient.shape)
+
+
+def merge_kernel(values, kept_first, kept_second, theirs, first, second):
     first[...] = jnp.zeros_like(first)
-    first[0:8, :] = jnp.where(even, near[...] + theirs[0:8, :], three[...] + theirs[8:16, :])
+    first[0:8, :] = kept_first[...] + theirs[0:8, :]
     write_halves(second, 0, values[...])
-    second[0:8, :] = jnp.where(even, second[0:8, :], two[...] + theirs[0:8, :])
+    second[0:8, :] = jnp.where(leads(), second[0:8, :], kept_second[...] + theirs[8:16, :])
     second[16:32, :] = theirs[8:24, :]
 
 
@@ -488,7 +546,7 @@
     sub = lax.axis_index("sub")
     gradient = slots[...]
     if merged:
-        gradient += jnp.where(sub == 0, 0.0, other[8 : slots.shape[0] + 8, :])
+        gradient += jnp.where(leads(), 0.0, other[8 : slots.shape[0] + 8, :])
     for z in range(adjoint.shape[0]):
         state[z] = adjoint[z] + share_rows[z : z + 1, :] * gradient
     copies = [pltpu.make_async_copy(state, state_out, sems.at[0])]
@@ -522,14 +580,17 @@
     return lax.ppermute(x, ("tile", "sub"), pairs)
 
 
-def by_core(x, even, odd):
+def by_role(x, lead, rest):
     n, levs, bands = (lax.axis_size(axis) for axis in ("tile", "lev", "sub"))
+
+    def place(t, l, is_lead):
+        return (t * levs + l) * bands + (is_lead if t in (0, n - 1) else 1 - is_lead)
+
     pairs = []
     for t in range(n):
         for l in range(levs):
-            for s in range(bands):
-                tx, lx = odd if s else even
-                pairs.append(((t * levs + l) * bands + s, ((t ^ tx) * levs + (l ^ lx)) * bands + s))
+            for is_lead, (tx, lx) in enumerate((rest, lead)):
+                pairs.append((place(t, l, is_lead), place(t ^ tx, l ^ lx, is_lead)))
     return lax.ppermute(x, ("tile", "lev", "sub"), pairs)
 
 
@@ -589,33 +650,41 @@
     edge_in = beyond(edge_out)
     near_in = traded(near_out, 1, 1)
     raw = pinned(marine_layered_warmth, depth_shares, piece_marine_box[0], marine_share_fraction[0])
-    block, strips, surface, share_rows, marine, marine_weight = call(
+    block, strips, surface, block_heat, share_rows, marine, marine_weight = call(
         functools.partial(side_kernel, levels),
-        [(levels, rows, cols), (2 * high, cols), (rows, cols), (8, cols), like(raw[2]), like(raw[3])],
+        [(levels, rows, cols), (2 * high, cols)]
+        + [(rows, cols)] * 2
+        + [(8, cols), like(raw[2]), like(raw[3])],
         [ext, *raw],
         [VMEM] + [HBM] * 4,
         scratch=buffers(raw[:1])
         + [pltpu.SMEM(depth_shares.shape, F32), pltpu.SemaphoreType.DMA((4,))],
     )
     merged = n == 4 and levs == 2
-    adjoint, lev_msg, *far_out = call(
+    strip, lev_msg, *far_out = call(
         functools.partial(diffuse_kernel, n, levels),
-        [(levels, rows, cols), (2 * rows + (16 if merged else 0), cols)] + [(40, cols)] * (n // 2 - 1),
-        [ext, near_in, edge_in, surface, share_rows, msg, other, marine, block, strips],
+        [(rows, cols), (2 * rows + (16 if merged else 0), cols)] + [(40, cols)] * (n // 2 - 1),
+        [ext, near_in, edge_in, surface, share_rows, msg, other, marine, block_heat, strips],
     )
     lev_in = lev_parts(lev_msg)
     far_in = [traded(x, 2 * i + 2, 1) for i, x in enumerate(far_out)]
-    picks, tables, uppers = call(
+    picks, tables, uppers, adjoint = call(
         functools.partial(near_kernel, n, fold),
-        [(3, 4, cells), jax.ShapeDtypeStruct((4, cells, cols), BF16), (8, cells)],
-        [msg, other, near_in],
-    )
-    values, chip, *returns = call(
+        [(3, 4, cells), jax.ShapeDtypeStruct((4, cells, cols), BF16), (8, cells)]
+        + [(levels, rows, cols)],
+        [msg, other, near_in, ext, block, strip],
+    )
+    values, winds, uppers, far_tables, chip = call(
         functools.partial(slot_kernel, n, len(lev_in), rows),
-        [(2 * n, cells), (40, cols)] + [(8, cols)] * n,
+        [(2 * n, cells)] * 3
+        + [jax.ShapeDtypeStruct((2 * n, cols, cells), BF16), (40, cols)],
         [*lev_in, picks, tables, uppers, marine, marine_weight, *far_in],
-        scratch=[pltpu.VMEM((3, 2 * n, cells), F32)] * 2
-        + [pltpu.VMEM((2 * n, cols, cells), BF16), pltpu.VMEM((2 * n, cells), F32)],
+        scratch=[pltpu.VMEM((3, 2 * n, cells), F32)] * 2,
+    )
+    returns = call(
+        functools.partial(kept_kernel, n),
+        [(8, cols)] * (3 if merged else n),
+        [values, winds, uppers, tables, far_tables],
     )
     if merged:
         theirs = traded(chip, 0, 1)
@@ -628,13 +697,20 @@
         first, second = call(
             merge_kernel, [(32, cols), (32, cols)], [values, *returns[1:], theirs]
         )
-        first = by_core(first, (1, 0), (3, 0))
-        second = by_core(second, (0, 1), (2, 0))
-        gradient, sums = call(
+        first = by_role(first, (3, 0), (2, 0))
+        second = by_role(second, (0, 1), (1, 0))
+        scratch = [pltpu.VMEM((2 * n, cells), F32)]
+        sums, second = call(
             functools.partial(post_kernel, n),
-            [(rows, cols), (rows + 8, cols)],
-            [first, second, returns[0], slots, partner_cells, partner_tables],
-            scratch=[pltpu.VMEM((2 * n, cells), F32)],
+            [(rows + 8, cols), (32, cols)],
+            [first, second, returns[0], partner_cells, partner_tables],
+            scratch=scratch,
+        )
+        (gradient,) = call(
+            functools.partial(gradient_kernel, n),
+            [(rows, cols)],
+            [second, slots, partner_cells, partner_tables],
+            scratch=scratch,
         )
     else:
         (slots,) = call(functools.partial(own_kernel, n), [(rows, cols)], [marine, values])

time: 25.1 us -> 24.8 us (0.988)
  Pallas kernels: 5.43 us -> 4.99 us
  starting transfers between devices: 12.3 us -> 12.6 us
    ppermute x2, starting transfers between devices: 2.41 us -> 3.07 us  [by_role(): return lax.ppermute(x, ('tile', 'lev', 'sub'), pairs)]
    pallas_call x10 -> x12, Pallas kernels: 5.43 us -> 4.99 us  [call(): pl.pallas_call(kernel, out_shape=outs, in_specs=specs or [VMEM] * len(ope...]
    ppermute x5, starting transfers between devices: 7.56 us -> 7.24 us  [traded(): return lax.ppermute(x, ('tile', 'sub'), pairs)]
  transfers between devices with their start and end apart: 9 -> 9, of which waited for: 7 -> 6; matrix products, arithmetic and copies ran while one was open for 0% -> 0% of each run, Pallas kernels for 8% -> 8%
where the time goes in v9:
time: 24.8 us; the launch traced here: 24.5 us
  starting transfers between devices  12.6 us (51%)
  waiting for transfers between devices  6.23 us (25%)
  Pallas kernels  4.99 us (20%)
  between operations  0.71 us (3%)
    ppermute x5, starting transfers between devices, traded(): return lax.ppermute(x, ('tile', 'sub'), pairs)  7.24 us
    pallas_call x12, Pallas kernels, call(): pl.pallas_call(kernel, out_shape=outs, in_specs=specs or [VMEM] * len(ope...  4.99 us
    ppermute x5, waiting for transfers between devices, traded(): return lax.ppermute(x, ('tile', 'sub'), pairs)  3.85 us
    ppermute x2, starting transfers between devices, by_role(): return lax.ppermute(x, ('tile', 'lev', 'sub'), pairs)  3.07 us
    ppermute x2, waiting for transfers between devices, by_role(): return lax.ppermute(x, ('tile', 'lev', 'sub'), pairs)  2.38 us
    ppermute x1, starting transfers between devices, lev_parts(): return [x, lax.ppermute(x, 'lev', [(0, 1), (1, 0)])]  1.95 us
  transfers between devices with their start and end apart: 9, of which 6 were waited for; matrix products, arithmetic and copies ran while one was open for 0% of the time, Pallas kernels for 8%

profile of v9, /device:TPU:0, one launch (start us, length us, event | category | flops | bytes accessed | tf_op | source)
XLA Modules:
  0.0 24.5 jit_solution(13888264476935115313)
XLA Ops:
  0.6 1.0 %shard_map.130 = (f32[40,256]{1,0:T(8,128)S(1)}, f32[216,128]{1,0:T(8,128)S(1)}) custom-call(f32[2,64,128]{2,1,0:T(8,128)} %refs_0_.2, s32[64,128]{1,0:T(8,128)} %refs_1_.2, f32[1,256]{1,0:T(1,128)} %bitcast.13, f32[1,256]{1,0:T(1,128)} %bitcast.14, f32[1,256]{1,0:T(1,128)} %bitcast.15, s32[8,256]{1,0:T(8,128)} %bitcast.9, f32[8,256]{1,0:T(8,128)} %bitcast.10), custom_call_target="tpu_custom_call" | custom-call | tf_op jit(solution)/shard_map/pallas_call | solution.py:24
  1.6 0.5 %collective-permute-start = (f32[40,256]{1,0:T(8,128)S(1)}, f32[40,256]{1,0:T(8,128)S(1)}, u32[]{:S(2)}, u32[]{:S(2)}) collective-permute-start(f32[40,256]{1,0:T(8,128)S(1)} %get-tuple-element.40.msg.refs_5_), channel_id=1, source_target_pairs={{0,1},{1,0},{4,5},{5,4},{8,9},{9,8},{12,13},{13,12},{2,3},{3,2},{6... | collective-permute-start | bytes 122888 | tf_op jit(solution)/shard_map/ppermute | solution.py:571
  2.1 0.9 %collective-permute-done.other.refs_6_ = f32[40,256]{1,0:T(8,128)S(1)} collective-permute-done((f32[40,256]{1,0:T(8,128)S(1)}, f32[40,256]{1,0:T(8,128)S(1)}, u32[]{:S(2)}, u32[]{:S(2)}) %collective-permute-start) | collective-permute-done | bytes 40992 | tf_op jit(solution)/shard_map/ppermute | solution.py:571
  3.0 0.1 shard_map.131
  3.1 2.7 %collective-permute-start.1 = (f32[48,128]{1,0:T(8,128)S(1)}, f32[48,128]{1,0:T(8,128)S(1)}, u32[]{:S(2)}, u32[]{:S(2)}) collective-permute-start(f32[48,128]{1,0:T(8,128)S(1)} %get-tuple-element.43), channel_id=1, source_target_pairs={{0,5},{1,4},{4,1},{5,0},{8,13},{9,12},{12,9},{13,8},{2,7},{3,6},{6... | collective-permute-start | bytes 73736 | tf_op jit(solution)/shard_map/ppermute | solution.py:571
  5.8 0.3 %collective-permute-start.2 = (f32[16,128]{1,0:T(8,128)S(1)}, f32[16,128]{1,0:T(8,128)S(1)}, u32[]{:S(2)}, u32[]{:S(2)}) collective-permute-start(f32[16,128]{1,0:T(8,128)S(1)} %get-tuple-element.44), channel_id=1, source_target_pairs={{0,1},{1,0},{4,9},{5,8},{8,5},{9,4},{12,13},{13,12},{2,3},{3,2},{6... | collective-permute-start | bytes 24584 | tf_op jit(solution)/shard_map/ppermute | solution.py:580
  6.1 1.1 %shard_map.132 = (f32[2,64,128]{2,1,0:T(8,128)S(1)}, f32[144,128]{1,0:T(8,128)S(1)}, f32[64,128]{1,0:T(8,128)S(1)}, f32[64,128]{1,0:T(8,128)S(1)}, f32[8,128]{1,...) custom-call(f32[216,128]{1,0:T(8,128)S(1)} %get-tuple-element.42.ext.refs_0_, f32[2,64,128]{2,1,0:T(8,128)} %refs_0_.3, ...), custom_call_target="tpu_custom_call" | custom-call | tf_op jit(solution)/shard_map/pallas_call | solution.py:24
  7.3 0.0 collective-permute-done.2.refs_2_
  7.3 0.0 collective-permute-done.1.refs_1_.near_in
  7.3 0.6 %shard_map.133 = (f32[64,128]{1,0:T(8,128)S(1)}, f32[144,128]{1,0:T(8,128)S(1)}, f32[40,128]{1,0:T(8,128)S(1)}) custom-call(f32[216,128]{1,0:T(8,128)S(1)} %get-tuple-element.42.ext.refs_0_, f32[48,128]{1,0:T(8,128)S(1)} %collective-permute-done.1.refs_1_.near_in, f32[16,128]{1,0:T(8,128)S(1)} %collective-permute-done.2.refs_2_, ...), custom_call_target="tpu_custom_call" | custom-call | tf_op jit(solution)/shard_map/pallas_call | solution.py:24
  7.9 1.9 %collective-permute-start.3 = (f32[144,128]{1,0:T(8,128)S(1)}, f32[144,128]{1,0:T(8,128)S(1)}, u32[]{:S(2)}, u32[]{:S(2)}) collective-permute-start(f32[144,128]{1,0:T(8,128)S(1)} %get-tuple-element.50.refs_0_), channel_id=1, source_target_pairs={{0,2},{2,0},{1,3},{3,1},{4,6},{6,4},{5,7},{7,5},{8,10},{10,8},{9,1... | collective-permute-start | bytes 221192 | tf_op jit(solution)/shard_map/ppermute | solution.py:599
  9.8 3.4 %collective-permute-start.4 = (f32[40,128]{1,0:T(8,128)S(1)}, f32[40,128]{1,0:T(8,128)S(1)}, u32[]{:S(2)}, u32[]{:S(2)}) collective-permute-start(f32[40,128]{1,0:T(8,128)S(1)} %get-tuple-element.57), channel_id=1, source_target_pairs={{0,9},{1,8},{4,13},{5,12},{8,1},{9,0},{12,5},{13,4},{2,11},{3,10},... | collective-permute-start | bytes 61448 | tf_op jit(solution)/shard_map/ppermute | solution.py:571
  13.3 0.2 shard_map.134
  13.5 1.2 %collective-permute-done.4.refs_7_ = f32[40,128]{1,0:T(8,128)S(1)} collective-permute-done((f32[40,128]{1,0:T(8,128)S(1)}, f32[40,128]{1,0:T(8,128)S(1)}, u32[]{:S(2)}, u32[]{:S(2)}) %collective-permute-start.4) | collective-permute-done | bytes 20512 | tf_op jit(solution)/shard_map/ppermute | solution.py:571
  14.7 0.0 collective-permute-done.3.refs_1_.refs_0_
  14.7 0.7 %shard_map.135 = (f32[8,256]{1,0:T(8,128)S(1)}, f32[8,256]{1,0:T(8,128)S(1)}, f32[8,256]{1,0:T(8,128)S(1)}, bf16[8,128,256]{2,1,0:T(8,128)(2,1)S(1)}, f32[40,128]{1,0:T(8,128)S(1)}) custom-call(f32[144,128]{1,0:T(8,128)S(1)} %get-tuple-element.50.refs_0_, f32[144,128]{1,0:T(8,128)S(1)} %collective-permute-done.3.refs_1_.refs_0_, ...), custom_call_target="tpu_custom_call" | custom-call | tf_op jit(solution)/shard_map/pallas_call | solution.py:24
  15.4 0.5 %collective-permute-start.5 = (f32[40,128]{1,0:T(8,128)S(1)}, f32[40,128]{1,0:T(8,128)S(1)}, u32[]{:S(2)}, u32[]{:S(2)}) collective-permute-start(f32[40,128]{1,0:T(8,128)S(1)} %get-tuple-element.64), channel_id=1, source_target_pairs={{0,1},{1,0},{4,5},{5,4},{8,9},{9,8},{12,13},{13,12},{2,3},{3,2},{6... | collective-permute-start | bytes 61448 | tf_op jit(solution)/shard_map/ppermute | solution.py:571
  15.9 0.3 %shard_map.136 = (f32[8,128]{1,0:T(8,128)S(1)}, f32[8,128]{1,0:T(8,128)S(1)}, f32[8,128]{1,0:T(8,128)S(1)}) custom-call(f32[8,256]{1,0:T(8,128)S(1)} %get-tuple-element.58.values, f32[8,256]{1,0:T(8,128)S(1)} %get-tuple-element.59.winds, f32[8,256]{1,0:T(8,128)S(1)} %get-tuple-element.60.uppers, ...), custom_call_target="tpu_custom_call" | custom-call | tf_op jit(solution)/shard_map/pallas_call | solution.py:24
  16.2 0.5 %collective-permute-done.5.theirs.refs_1_ = f32[40,128]{1,0:T(8,128)S(1)} collective-permute-done((f32[40,128]{1,0:T(8,128)S(1)}, f32[40,128]{1,0:T(8,128)S(1)}, u32[]{:S(2)}, u32[]{:S(2)}) %collective-permute-start.5) | collective-permute-done | bytes 20512 | tf_op jit(solution)/shard_map/ppermute | solution.py:571
  16.8 2.6 %collective-permute-start.6 = (f32[32,128]{1,0:T(8,128)S(1)}, f32[32,128]{1,0:T(8,128)S(1)}, u32[]{:S(2)}, u32[]{:S(2)}) collective-permute-start(f32[32,128]{1,0:T(8,128)S(1)} %get-tuple-element.65), channel_id=1, source_target_pairs={{0,9},{1,13},{2,11},{3,15},{5,12},{4,8},{7,14},{6,10},{9,0},{8,4},... | collective-permute-start | bytes 49160 | tf_op jit(solution)/shard_map/ppermute | solution.py:594
  19.4 0.4 %collective-permute-start.7 = (f32[32,128]{1,0:T(8,128)S(1)}, f32[32,128]{1,0:T(8,128)S(1)}, u32[]{:S(2)}, u32[]{:S(2)}) collective-permute-start(f32[32,128]{1,0:T(8,128)S(1)} %get-tuple-element.66), channel_id=1, source_target_pairs={{0,5},{1,3},{2,7},{3,1},{5,0},{4,6},{7,2},{6,4},{9,12},{8,10},{11,... | collective-permute-start | bytes 49160 | tf_op jit(solution)/shard_map/ppermute | solution.py:594
  19.8 0.3 %shard_map.138 = (f32[64,128]{1,0:T(8,128)S(1)}, s32[16,256]{1,0:T(8,128)S(1)}, bf16[16,256,128]{2,1,0:T(8,128)(2,1)S(1)}) custom-call(s32[8,256]{1,0:T(8,128)S(1)} %get-tuple-element.47.refs_7_.refs_5_.marine, f32[8,256]{1,0:T(8,128)S(1)} %get-tuple-element.58.values, f32[144,128]{1,0:T(8,128)S(1)} %collective-permute-done.3.refs_1_.refs_0_, ...), custom_call_target="tpu_custom_call" | custom-call | tf_op jit(solution)/shard_map/pallas_call | solution.py:24
  20.2 0.7 %collective-permute-done.6.first = f32[32,128]{1,0:T(8,128)S(1)} collective-permute-done((f32[32,128]{1,0:T(8,128)S(1)}, f32[32,128]{1,0:T(8,128)S(1)}, u32[]{:S(2)}, u32[]{:S(2)}) %collective-permute-start.6) | collective-permute-done | bytes 16416 | tf_op jit(solution)/shard_map/ppermute | solution.py:594
  20.8 1.7 %collective-permute-done.7.second = f32[32,128]{1,0:T(8,128)S(1)} collective-permute-done((f32[32,128]{1,0:T(8,128)S(1)}, f32[32,128]{1,0:T(8,128)S(1)}, u32[]{:S(2)}, u32[]{:S(2)}) %collective-permute-start.7) | collective-permute-done | bytes 16416 | tf_op jit(solution)/shard_map/ppermute | solution.py:594
  22.6 0.1 collective-permute-start.8
  22.7 1.2 %collective-permute-done.8.other = f32[72,128]{1,0:T(8,128)S(1)} collective-permute-done((f32[72,128]{1,0:T(8,128)S(1)}, f32[72,128]{1,0:T(8,128)S(1)}, u32[]{:S(2)}, u32[]{:S(2)}) %collective-permute-start.8) | collective-permute-done | bytes 36896 | tf_op jit(solution)/shard_map/ppermute | solution.py:571
  23.9 0.7 %shard_map.141 = (f32[2,64,128]{2,1,0:T(8,128)}, f32[1,256]{1,0:T(1,128)}, f32[1,256]{1,0:T(1,128)}) custom-call(f32[64,128]{1,0:T(8,128)S(1)} %shard_map.140.slots, f32[2,64,128]{2,1,0:T(8,128)S(1)} %get-tuple-element.72.adjoint, f32[8,128]{1,0:T(8,128)S(1)} %get-tuple-element.46.refs_4_.share_rows, f32[72,128]{1,0:T(8,128)S(1)} %get-tuple-element.73.sums, ...), custom_call_target="tpu_custom_call" | custom-call | tf_op jit(solution)/shard_map/pallas_call | solution.py:24
  (3 shorter events, 0.0 us)
Async XLA Ops:
  1.6 1.4 %collective-permute-start = (f32[40,256]{1,0:T(8,128)S(1)}, f32[40,256]{1,0:T(8,128)S(1)}, u32[]{:S(2)}, u32[]{:S(2)}) collective-permute-start(f32[40,256]{1,0:T(8,128)S(1)} %get-tuple-element.40.msg.refs_5_), channel_id=1, source_target_pairs={{0,1},{1,0},{4,5},{5,4},{8,9},{9,8},{12,13},{13,12},{2,3},{3,2},{6... | collective-permute-start | bytes 122888 | tf_op jit(solution)/shard_map/ppermute | solution.py:571
  3.1 4.2 %collective-permute-start.1 = (f32[48,128]{1,0:T(8,128)S(1)}, f32[48,128]{1,0:T(8,128)S(1)}, u32[]{:S(2)}, u32[]{:S(2)}) collective-permute-start(f32[48,128]{1,0:T(8,128)S(1)} %get-tuple-element.43), channel_id=1, source_target_pairs={{0,5},{1,4},{4,1},{5,0},{8,13},{9,12},{12,9},{13,8},{2,7},{3,6},{6... | collective-permute-start | bytes 73736 | tf_op jit(solution)/shard_map/ppermute | solution.py:571
  5.8 1.5 %collective-permute-start.2 = (f32[16,128]{1,0:T(8,128)S(1)}, f32[16,128]{1,0:T(8,128)S(1)}, u32[]{:S(2)}, u32[]{:S(2)}) collective-permute-start(f32[16,128]{1,0:T(8,128)S(1)} %get-tuple-element.44), channel_id=1, source_target_pairs={{0,1},{1,0},{4,9},{5,8},{8,5},{9,4},{12,13},{13,12},{2,3},{3,2},{6... | collective-permute-start | bytes 24584 | tf_op jit(solution)/shard_map/ppermute | solution.py:580
  7.9 6.9 %collective-permute-start.3 = (f32[144,128]{1,0:T(8,128)S(1)}, f32[144,128]{1,0:T(8,128)S(1)}, u32[]{:S(2)}, u32[]{:S(2)}) collective-permute-start(f32[144,128]{1,0:T(8,128)S(1)} %get-tuple-element.50.refs_0_), channel_id=1, source_target_pairs={{0,2},{2,0},{1,3},{3,1},{4,6},{6,4},{5,7},{7,5},{8,10},{10,8},{9,1... | collective-permute-start | bytes 221192 | tf_op jit(solution)/shard_map/ppermute | solution.py:599
  9.8 4.9 %collective-permute-start.4 = (f32[40,128]{1,0:T(8,128)S(1)}, f32[40,128]{1,0:T(8,128)S(1)}, u32[]{:S(2)}, u32[]{:S(2)}) collective-permute-start(f32[40,128]{1,0:T(8,128)S(1)} %get-tuple-element.57), channel_id=1, source_target_pairs={{0,9},{1,8},{4,13},{5,12},{8,1},{9,0},{12,5},{13,4},{2,11},{3,10},... | collective-permute-start | bytes 61448 | tf_op jit(solution)/shard_map/ppermute | solution.py:571
  15.4 1.4 %collective-permute-start.5 = (f32[40,128]{1,0:T(8,128)S(1)}, f32[40,128]{1,0:T(8,128)S(1)}, u32[]{:S(2)}, u32[]{:S(2)}) collective-permute-start(f32[40,128]{1,0:T(8,128)S(1)} %get-tuple-element.64), channel_id=1, source_target_pairs={{0,1},{1,0},{4,5},{5,4},{8,9},{9,8},{12,13},{13,12},{2,3},{3,2},{6... | collective-permute-start | bytes 61448 | tf_op jit(solution)/shard_map/ppermute | solution.py:571
  16.8 4.1 %collective-permute-start.6 = (f32[32,128]{1,0:T(8,128)S(1)}, f32[32,128]{1,0:T(8,128)S(1)}, u32[]{:S(2)}, u32[]{:S(2)}) collective-permute-start(f32[32,128]{1,0:T(8,128)S(1)} %get-tuple-element.65), channel_id=1, source_target_pairs={{0,9},{1,13},{2,11},{3,15},{5,12},{4,8},{7,14},{6,10},{9,0},{8,4},... | collective-permute-start | bytes 49160 | tf_op jit(solution)/shard_map/ppermute | solution.py:594
  19.4 3.2 %collective-permute-start.7 = (f32[32,128]{1,0:T(8,128)S(1)}, f32[32,128]{1,0:T(8,128)S(1)}, u32[]{:S(2)}, u32[]{:S(2)}) collective-permute-start(f32[32,128]{1,0:T(8,128)S(1)} %get-tuple-element.66), channel_id=1, source_target_pairs={{0,5},{1,3},{2,7},{3,1},{5,0},{4,6},{7,2},{6,4},{9,12},{8,10},{11,... | collective-permute-start | bytes 49160 | tf_op jit(solution)/shard_map/ppermute | solution.py:594
  22.6 1.3 %collective-permute-start.8 = (f32[72,128]{1,0:T(8,128)S(1)}, f32[72,128]{1,0:T(8,128)S(1)}, u32[]{:S(2)}, u32[]{:S(2)}) collective-permute-start(f32[72,128]{1,0:T(8,128)S(1)} %get-tuple-element.73.sums), channel_id=1, source_target_pairs={{0,1},{1,0},{4,5},{5,4},{8,9},{9,8},{12,13},{13,12},{2,3},{3,2},{6... | collective-permute-start | bytes 110600 | tf_op jit(solution)/shard_map/ppermute | solution.py:571

commit v10 on v9

--- a/solution.py
+++ b/solution.py
@@ -241,8 +241,8 @@
 
 def side_kernel(levels, ext, *refs):
     warm, shares, marine, marine_weight = refs[:4]
-    block, strips, surface, block_heat, share_rows, marine_out, marine_weight_out = refs[4:11]
-    warm_in, shares_in, sems = refs[11:]
+    block, strips, heat_strips, surface, block_heat, share_rows, marine_out, marine_weight_out = refs[4:12]
+    warm_in, shares_in, sems = refs[12:]
     pairs = [(warm, warm_in), (shares, shares_in), (marine, marine_out), (marine_weight, marine_weight_out)]
     copies = [pltpu.make_async_copy(a, b, sems.at[i]) for i, (a, b) in enumerate(pairs)]
     for copy in copies:
@@ -258,13 +258,16 @@
         copy.wait()
     surface[...] = sum(shares_in[z] * warm_in[z] for z in range(levels))
     block_heat[...] = sum(shares_in[z] * block[z] for z in range(levels))
+    mixed = sum(shares_in[z] * fields[z] for z in range(levels))
+    heat_strips[0:high, :] = own_strips([mixed])
+    heat_strips[high : 2 * high, :] = own_strips(fields[levels:])
     for z in range(levels):
         share_rows[z : z + 1, :] = jnp.full((1, cols), shares_in[z], F32)
 
 
 def diffuse_kernel(n, levels, *refs):
     ext, near_in, edge_in, surface, share_rows, msg, other, marine, block_heat, strips = refs[:10]
-    strip_out, lev_out = refs[10:12]
+    fold_out, lev_out = refs[10:12]
     sub, tile = lax.axis_index("sub"), lax.axis_index("tile")
     rows, cols = surface.shape
     high = rows + 8
@@ -283,15 +286,15 @@
         right = jnp.where(tile < n - 1, jnp.where(even, near, far), 0.0)
         left = jnp.where(tile > 0, jnp.where(even, far, near), 0.0)
         tiles.append(jnp.where(lax.rem(lane, 2 * HALO) < HALO, right, turn_lanes(left, 2 * HALO)))
-    wet = strips_beyond(tiles, strips[high : 2 * high, :], [levels] * levels, levels + 1)
-    strip = strips_beyond(tiles, strips[0:high, :], list(range(levels)), levels + 1)
-    strip = diffused(wet, [strip])[0][:rows]
+    fold_out[...] = jnp.concatenate(tiles, axis=0)
+    mixed = []
+    for x in tiles:
+        shifted = [turn_lanes(x, -2 * HALO * z) for z in range(levels)]
+        mixed.append(sum(share_rows[z : z + 1, :] * y for z, y in enumerate(shifted)))
+    wet = strips_beyond(tiles, strips[high : 2 * high, :], [levels], levels + 1)
+    heat = diffused(wet, [strips_beyond(mixed, strips[0:high, :], [0], levels + 1)])[0]
+    heat = from_strips(heat[:rows], 0, block_heat[...])
     own_wet = ext[high * levels : high * levels + rows, :]
-    strip_out[...] = strip
-    heat = share_rows[0:1, :] * strip
-    for z in range(1, levels):
-        heat += share_rows[z : z + 1, :] * turn_lanes(strip, strip_base(0) - strip_base(z))
-    heat = from_strips(heat, 0, block_heat[...])
     lev_out[0:rows, :] = surface[...]
     lev_out[rows : 2 * rows, :] = own_wet * heat
     if lev_out.shape[0] > 2 * rows:
@@ -317,8 +320,8 @@
 
 
 def onehot(index, count):
-    cells = lax.broadcasted_iota(jnp.int32, (count, index.shape[1]), 0)
-    return jnp.where(cells == index, 1.0, 0.0).astype(BF16)
+    cells = lax.broadcasted_iota(jnp.int32, (count, index.shape[1]), 0).astype(BF16)
+    return jnp.where(cells == index.astype(BF16), jnp.ones((), BF16), jnp.zeros((), BF16))
 
 
 def dot(a, b, ca, cb):
@@ -348,15 +351,20 @@
         uppers[place, :] = upper.astype(F32)
 
 
-def near_kernel(n, fold, msg, other, near_in, ext, block, strip, picks, tables, uppers, adjoint):
+def near_kernel(n, fold, msg, other, near_in, ext, block, strips, folds, picks, tables, uppers, adjoint):
     sub, tile = lax.axis_index("sub"), lax.axis_index("tile")
     own = table_rows(n, msg, other, tile, sub, sub) + value_rows(n, msg, other, sub)
     look_up(own, 0, picks, tables, uppers, True)
     look_up(read_pairs(near_in, fold, 10), 2, picks, tables, uppers, True)
     levels, rows, cols = adjoint.shape
-    own_wet = ext[(rows + 8) * levels : (rows + 8) * levels + rows, :]
+    high = rows + 8
+    tiles = [folds[k : k + 8, :] for k in range(0, fold, 8)]
+    wet = strips_beyond(tiles, strips[high : 2 * high, :], [levels] * levels, levels + 1)
+    strip = strips_beyond(tiles, strips[0:high, :], list(range(levels)), levels + 1)
+    strip = diffused(wet, [strip])[0][:rows]
+    own_wet = ext[high * levels : high * levels + rows, :]
     for z in range(levels):
-        adjoint[z] = own_wet * from_strips(strip[...], z, block[z])
+        adjoint[z] = own_wet * from_strips(strip, z, block[z])
 
 
 def slot_kernel(n, count, rows, *refs):
@@ -650,9 +658,9 @@
     edge_in = beyond(edge_out)
     near_in = traded(near_out, 1, 1)
     raw = pinned(marine_layered_warmth, depth_shares, piece_marine_box[0], marine_share_fraction[0])
-    block, strips, surface, block_heat, share_rows, marine, marine_weight = call(
+    block, strips, heat_strips, surface, block_heat, share_rows, marine, marine_weight = call(
         functools.partial(side_kernel, levels),
-        [(levels, rows, cols), (2 * high, cols)]
+        [(levels, rows, cols), (2 * high, cols), (2 * high, cols)]
         + [(rows, cols)] * 2
         + [(8, cols), like(raw[2]), like(raw[3])],
         [ext, *raw],
@@ -661,10 +669,10 @@
         + [pltpu.SMEM(depth_shares.shape, F32), pltpu.SemaphoreType.DMA((4,))],
     )
     merged = n == 4 and levs == 2
-    strip, lev_msg, *far_out = call(
+    folds, lev_msg, *far_out = call(
         functools.partial(diffuse_kernel, n, levels),
-        [(rows, cols), (2 * rows + (16 if merged else 0), cols)] + [(40, cols)] * (n // 2 - 1),
-        [ext, near_in, edge_in, surface, share_rows, msg, other, marine, block_heat, strips],
+        [(fold, cols), (2 * rows + (16 if merged else 0), cols)] + [(40, cols)] * (n // 2 - 1),
+        [ext, near_in, edge_in, surface, share_rows, msg, other, marine, block_heat, heat_strips],
     )
     lev_in = lev_parts(lev_msg)
     far_in = [traded(x, 2 * i + 2, 1) for i, x in enumerate(far_out)]
@@ -672,7 +680,7 @@
         functools.partial(near_kernel, n, fold),
         [(3, 4, cells), jax.ShapeDtypeStruct((4, cells, cols), BF16), (8, cells)]
         + [(levels, rows, cols)],
-        [msg, other, near_in, ext, block, strip],
+        [msg, other, near_in, ext, block, strips, folds],
     )
     values, winds, uppers, far_tables, chip = call(
         functools.partial(slot_kernel, n, len(lev_in), rows),

time: 24.8 us -> 24.6 us (level)
  waiting for transfers between devices: 6.23 us -> 5.93 us
  Pallas kernels: 4.99 us -> 5.26 us
    ppermute x5, waiting for transfers between devices: 3.85 us -> 3.52 us  [traded(): return lax.ppermute(x, ('tile', 'sub'), pairs)]
    pallas_call x12, Pallas kernels: 4.99 us -> 5.26 us  [call(): pl.pallas_call(kernel, out_shape=outs, in_specs=specs or [VMEM] * len(ope...]
  transfers between devices with their start and end apart: 9 -> 9, of which waited for: 6 -> 6; matrix products, arithmetic and copies ran while one was open for 0% -> 0% of each run, Pallas kernels for 8% -> 10%
where the time goes in v10:
time: 24.6 us; the launch traced here: 24.4 us
  starting transfers between devices  12.5 us (51%)
  waiting for transfers between devices  5.93 us (24%)
  Pallas kernels  5.26 us (21%)
  between operations  0.71 us (3%)
    ppermute x5, starting transfers between devices, traded(): return lax.ppermute(x, ('tile', 'sub'), pairs)  7.24 us
    pallas_call x12, Pallas kernels, call(): pl.pallas_call(kernel, out_shape=outs, in_specs=specs or [VMEM] * len(ope...  5.26 us
    ppermute x5, waiting for transfers between devices, traded(): return lax.ppermute(x, ('tile', 'sub'), pairs)  3.52 us
    ppermute x2, starting transfers between devices, by_role(): return lax.ppermute(x, ('tile', 'lev', 'sub'), pairs)  3.07 us
    ppermute x2, waiting for transfers between devices, by_role(): return lax.ppermute(x, ('tile', 'lev', 'sub'), pairs)  2.41 us
    ppermute x1, starting transfers between devices, lev_parts(): return [x, lax.ppermute(x, 'lev', [(0, 1), (1, 0)])]  1.83 us
  transfers between devices with their start and end apart: 9, of which 6 were waited for; matrix products, arithmetic and copies ran while one was open for 0% of the time, Pallas kernels for 10%

profile of v10, /device:TPU:0, one launch (start us, length us, event | category | flops | bytes accessed | tf_op | source)
XLA Modules:
  0.0 24.4 jit_solution(10570271355790702455)
XLA Ops:
  0.6 1.0 %shard_map.130 = (f32[40,256]{1,0:T(8,128)S(1)}, f32[216,128]{1,0:T(8,128)S(1)}) custom-call(f32[2,64,128]{2,1,0:T(8,128)} %refs_0_.2, s32[64,128]{1,0:T(8,128)} %refs_1_.2, f32[1,256]{1,0:T(1,128)} %bitcast.13, f32[1,256]{1,0:T(1,128)} %bitcast.14, f32[1,256]{1,0:T(1,128)} %bitcast.15, s32[8,256]{1,0:T(8,128)} %bitcast.9, f32[8,256]{1,0:T(8,128)} %bitcast.10), custom_call_target="tpu_custom_call" | custom-call | tf_op jit(solution)/shard_map/pallas_call | solution.py:24
  1.6 0.5 %collective-permute-start = (f32[40,256]{1,0:T(8,128)S(1)}, f32[40,256]{1,0:T(8,128)S(1)}, u32[]{:S(2)}, u32[]{:S(2)}) collective-permute-start(f32[40,256]{1,0:T(8,128)S(1)} %get-tuple-element.41.msg.refs_5_), channel_id=1, source_target_pairs={{0,1},{1,0},{4,5},{5,4},{8,9},{9,8},{12,13},{13,12},{2,3},{3,2},{6... | collective-permute-start | bytes 122888 | tf_op jit(solution)/shard_map/ppermute | solution.py:579
  2.1 0.9 %collective-permute-done.other.refs_6_ = f32[40,256]{1,0:T(8,128)S(1)} collective-permute-done((f32[40,256]{1,0:T(8,128)S(1)}, f32[40,256]{1,0:T(8,128)S(1)}, u32[]{:S(2)}, u32[]{:S(2)}) %collective-permute-start) | collective-permute-done | bytes 40992 | tf_op jit(solution)/shard_map/ppermute | solution.py:579
  3.0 0.1 shard_map.131
  3.1 2.7 %collective-permute-start.1 = (f32[48,128]{1,0:T(8,128)S(1)}, f32[48,128]{1,0:T(8,128)S(1)}, u32[]{:S(2)}, u32[]{:S(2)}) collective-permute-start(f32[48,128]{1,0:T(8,128)S(1)} %get-tuple-element.44), channel_id=1, source_target_pairs={{0,5},{1,4},{4,1},{5,0},{8,13},{9,12},{12,9},{13,8},{2,7},{3,6},{6... | collective-permute-start | bytes 73736 | tf_op jit(solution)/shard_map/ppermute | solution.py:579
  5.8 0.3 %collective-permute-start.2 = (f32[16,128]{1,0:T(8,128)S(1)}, f32[16,128]{1,0:T(8,128)S(1)}, u32[]{:S(2)}, u32[]{:S(2)}) collective-permute-start(f32[16,128]{1,0:T(8,128)S(1)} %get-tuple-element.45), channel_id=1, source_target_pairs={{0,1},{1,0},{4,9},{5,8},{8,5},{9,4},{12,13},{13,12},{2,3},{3,2},{6... | collective-permute-start | bytes 24584 | tf_op jit(solution)/shard_map/ppermute | solution.py:588
  6.1 1.2 %shard_map.132 = (f32[2,64,128]{2,1,0:T(8,128)S(1)}, f32[144,128]{1,0:T(8,128)S(1)}, f32[144,128]{1,0:T(8,128)S(1)}, f32[64,128]{1,0:T(8,128)S(1)}, f32[64,128]{...) custom-call(f32[216,128]{1,0:T(8,128)S(1)} %get-tuple-element.43.ext.refs_0_, ...), custom_call_target="tpu_custom_call" | custom-call | tf_op jit(solution)/shard_map/pallas_call | solution.py:24
  7.3 0.0 collective-permute-done.2.refs_2_
  7.4 0.0 collective-permute-done.1.refs_1_.near_in
  7.4 0.5 %shard_map.133 = (f32[16,128]{1,0:T(8,128)S(1)}, f32[144,128]{1,0:T(8,128)S(1)}, f32[40,128]{1,0:T(8,128)S(1)}) custom-call(f32[216,128]{1,0:T(8,128)S(1)} %get-tuple-element.43.ext.refs_0_, f32[48,128]{1,0:T(8,128)S(1)} %collective-permute-done.1.refs_1_.near_in, f32[16,128]{1,0:T(8,128)S(1)} %collective-permute-done.2.refs_2_, ...), custom_call_target="tpu_custom_call" | custom-call | tf_op jit(solution)/shard_map/pallas_call | solution.py:24
  7.9 1.8 %collective-permute-start.3 = (f32[144,128]{1,0:T(8,128)S(1)}, f32[144,128]{1,0:T(8,128)S(1)}, u32[]{:S(2)}, u32[]{:S(2)}) collective-permute-start(f32[144,128]{1,0:T(8,128)S(1)} %get-tuple-element.51.refs_0_), channel_id=1, source_target_pairs={{0,2},{2,0},{1,3},{3,1},{4,6},{6,4},{5,7},{7,5},{8,10},{10,8},{9,1... | collective-permute-start | bytes 221192 | tf_op jit(solution)/shard_map/ppermute | solution.py:607
  9.7 3.4 %collective-permute-start.4 = (f32[40,128]{1,0:T(8,128)S(1)}, f32[40,128]{1,0:T(8,128)S(1)}, u32[]{:S(2)}, u32[]{:S(2)}) collective-permute-start(f32[40,128]{1,0:T(8,128)S(1)} %get-tuple-element.59), channel_id=1, source_target_pairs={{0,9},{1,8},{4,13},{5,12},{8,1},{9,0},{12,5},{13,4},{2,11},{3,10},... | collective-permute-start | bytes 61448 | tf_op jit(solution)/shard_map/ppermute | solution.py:579
  13.2 0.5 %shard_map.134 = (f32[3,4,256]{2,1,0:T(4,128)S(1)}, bf16[4,256,128]{2,1,0:T(8,128)(2,1)S(1)}, f32[8,256]{1,0:T(8,128)S(1)}, f32[2,64,128]{2,1,0:T(8,128)S(1)}) custom-call(f32[40,256]{1,0:T(8,128)S(1)} %get-tuple-element.41.msg.refs_5_, f32[40,256]{1,0:T(8,128)S(1)} %collective-permute-done.other.refs_6_, ...), custom_call_target="tpu_custom_call" | custom-call | tf_op jit(solution)/shard_map/pallas_call | solution.py:24
  13.7 0.9 %collective-permute-done.4.refs_7_ = f32[40,128]{1,0:T(8,128)S(1)} collective-permute-done((f32[40,128]{1,0:T(8,128)S(1)}, f32[40,128]{1,0:T(8,128)S(1)}, u32[]{:S(2)}, u32[]{:S(2)}) %collective-permute-start.4) | collective-permute-done | bytes 20512 | tf_op jit(solution)/shard_map/ppermute | solution.py:579
  14.7 0.0 collective-permute-done.3.refs_1_.refs_0_
  14.7 0.6 %shard_map.135 = (f32[8,256]{1,0:T(8,128)S(1)}, f32[8,256]{1,0:T(8,128)S(1)}, f32[8,256]{1,0:T(8,128)S(1)}, bf16[8,128,256]{2,1,0:T(8,128)(2,1)S(1)}, f32[40,128]{1,0:T(8,128)S(1)}) custom-call(f32[144,128]{1,0:T(8,128)S(1)} %get-tuple-element.51.refs_0_, f32[144,128]{1,0:T(8,128)S(1)} %collective-permute-done.3.refs_1_.refs_0_, ...), custom_call_target="tpu_custom_call" | custom-call | tf_op jit(solution)/shard_map/pallas_call | solution.py:24
  15.2 0.5 %collective-permute-start.5 = (f32[40,128]{1,0:T(8,128)S(1)}, f32[40,128]{1,0:T(8,128)S(1)}, u32[]{:S(2)}, u32[]{:S(2)}) collective-permute-start(f32[40,128]{1,0:T(8,128)S(1)} %get-tuple-element.66), channel_id=1, source_target_pairs={{0,1},{1,0},{4,5},{5,4},{8,9},{9,8},{12,13},{13,12},{2,3},{3,2},{6... | collective-permute-start | bytes 61448 | tf_op jit(solution)/shard_map/ppermute | solution.py:579
  15.8 0.3 %shard_map.136 = (f32[8,128]{1,0:T(8,128)S(1)}, f32[8,128]{1,0:T(8,128)S(1)}, f32[8,128]{1,0:T(8,128)S(1)}) custom-call(f32[8,256]{1,0:T(8,128)S(1)} %get-tuple-element.60.values, f32[8,256]{1,0:T(8,128)S(1)} %get-tuple-element.61.winds, f32[8,256]{1,0:T(8,128)S(1)} %get-tuple-element.62.uppers, ...), custom_call_target="tpu_custom_call" | custom-call | tf_op jit(solution)/shard_map/pallas_call | solution.py:24
  16.1 0.5 %collective-permute-done.5.theirs.refs_1_ = f32[40,128]{1,0:T(8,128)S(1)} collective-permute-done((f32[40,128]{1,0:T(8,128)S(1)}, f32[40,128]{1,0:T(8,128)S(1)}, u32[]{:S(2)}, u32[]{:S(2)}) %collective-permute-start.5) | collective-permute-done | bytes 20512 | tf_op jit(solution)/shard_map/ppermute | solution.py:579
  16.6 2.6 %collective-permute-start.6 = (f32[32,128]{1,0:T(8,128)S(1)}, f32[32,128]{1,0:T(8,128)S(1)}, u32[]{:S(2)}, u32[]{:S(2)}) collective-permute-start(f32[32,128]{1,0:T(8,128)S(1)} %get-tuple-element.67), channel_id=1, source_target_pairs={{0,9},{1,13},{2,11},{3,15},{5,12},{4,8},{7,14},{6,10},{9,0},{8,4},... | collective-permute-start | bytes 49160 | tf_op jit(solution)/shard_map/ppermute | solution.py:602
  19.3 0.4 %collective-permute-start.7 = (f32[32,128]{1,0:T(8,128)S(1)}, f32[32,128]{1,0:T(8,128)S(1)}, u32[]{:S(2)}, u32[]{:S(2)}) collective-permute-start(f32[32,128]{1,0:T(8,128)S(1)} %get-tuple-element.68), channel_id=1, source_target_pairs={{0,5},{1,3},{2,7},{3,1},{5,0},{4,6},{7,2},{6,4},{9,12},{8,10},{11,... | collective-permute-start | bytes 49160 | tf_op jit(solution)/shard_map/ppermute | solution.py:602
  19.7 0.3 %shard_map.138 = (f32[64,128]{1,0:T(8,128)S(1)}, s32[16,256]{1,0:T(8,128)S(1)}, bf16[16,256,128]{2,1,0:T(8,128)(2,1)S(1)}) custom-call(s32[8,256]{1,0:T(8,128)S(1)} %get-tuple-element.48.refs_7_.refs_5_.marine, f32[8,256]{1,0:T(8,128)S(1)} %get-tuple-element.60.values, f32[144,128]{1,0:T(8,128)S(1)} %collective-permute-done.3.refs_1_.refs_0_, ...), custom_call_target="tpu_custom_call" | custom-call | tf_op jit(solution)/shard_map/pallas_call | solution.py:24
  20.0 0.7 %collective-permute-done.6.first = f32[32,128]{1,0:T(8,128)S(1)} collective-permute-done((f32[32,128]{1,0:T(8,128)S(1)}, f32[32,128]{1,0:T(8,128)S(1)}, u32[]{:S(2)}, u32[]{:S(2)}) %collective-permute-start.6) | collective-permute-done | bytes 16416 | tf_op jit(solution)/shard_map/ppermute | solution.py:602
  20.7 1.7 %collective-permute-done.7.second = f32[32,128]{1,0:T(8,128)S(1)} collective-permute-done((f32[32,128]{1,0:T(8,128)S(1)}, f32[32,128]{1,0:T(8,128)S(1)}, u32[]{:S(2)}, u32[]{:S(2)}) %collective-permute-start.7) | collective-permute-done | bytes 16416 | tf_op jit(solution)/shard_map/ppermute | solution.py:602
  22.4 0.1 collective-permute-start.8
  22.5 1.2 %collective-permute-done.8.other = f32[72,128]{1,0:T(8,128)S(1)} collective-permute-done((f32[72,128]{1,0:T(8,128)S(1)}, f32[72,128]{1,0:T(8,128)S(1)}, u32[]{:S(2)}, u32[]{:S(2)}) %collective-permute-start.8) | collective-permute-done | bytes 36896 | tf_op jit(solution)/shard_map/ppermute | solution.py:579
  23.7 0.7 %shard_map.141 = (f32[2,64,128]{2,1,0:T(8,128)}, f32[1,256]{1,0:T(1,128)}, f32[1,256]{1,0:T(1,128)}) custom-call(f32[64,128]{1,0:T(8,128)S(1)} %shard_map.140.slots, f32[2,64,128]{2,1,0:T(8,128)S(1)} %get-tuple-element.74.adjoint, f32[8,128]{1,0:T(8,128)S(1)} %get-tuple-element.47.refs_4_.share_rows, f32[72,128]{1,0:T(8,128)S(1)} %get-tuple-element.75.sums, ...), custom_call_target="tpu_custom_call" | custom-call | tf_op jit(solution)/shard_map/pallas_call | solution.py:24
  (3 shorter events, 0.0 us)
Async XLA Ops:
  1.6 1.4 %collective-permute-start = (f32[40,256]{1,0:T(8,128)S(1)}, f32[40,256]{1,0:T(8,128)S(1)}, u32[]{:S(2)}, u32[]{:S(2)}) collective-permute-start(f32[40,256]{1,0:T(8,128)S(1)} %get-tuple-element.41.msg.refs_5_), channel_id=1, source_target_pairs={{0,1},{1,0},{4,5},{5,4},{8,9},{9,8},{12,13},{13,12},{2,3},{3,2},{6... | collective-permute-start | bytes 122888 | tf_op jit(solution)/shard_map/ppermute | solution.py:579
  3.1 4.3 %collective-permute-start.1 = (f32[48,128]{1,0:T(8,128)S(1)}, f32[48,128]{1,0:T(8,128)S(1)}, u32[]{:S(2)}, u32[]{:S(2)}) collective-permute-start(f32[48,128]{1,0:T(8,128)S(1)} %get-tuple-element.44), channel_id=1, source_target_pairs={{0,5},{1,4},{4,1},{5,0},{8,13},{9,12},{12,9},{13,8},{2,7},{3,6},{6... | collective-permute-start | bytes 73736 | tf_op jit(solution)/shard_map/ppermute | solution.py:579
  5.8 1.6 %collective-permute-start.2 = (f32[16,128]{1,0:T(8,128)S(1)}, f32[16,128]{1,0:T(8,128)S(1)}, u32[]{:S(2)}, u32[]{:S(2)}) collective-permute-start(f32[16,128]{1,0:T(8,128)S(1)} %get-tuple-element.45), channel_id=1, source_target_pairs={{0,1},{1,0},{4,9},{5,8},{8,5},{9,4},{12,13},{13,12},{2,3},{3,2},{6... | collective-permute-start | bytes 24584 | tf_op jit(solution)/shard_map/ppermute | solution.py:588
  7.9 6.7 %collective-permute-start.3 = (f32[144,128]{1,0:T(8,128)S(1)}, f32[144,128]{1,0:T(8,128)S(1)}, u32[]{:S(2)}, u32[]{:S(2)}) collective-permute-start(f32[144,128]{1,0:T(8,128)S(1)} %get-tuple-element.51.refs_0_), channel_id=1, source_target_pairs={{0,2},{2,0},{1,3},{3,1},{4,6},{6,4},{5,7},{7,5},{8,10},{10,8},{9,1... | collective-permute-start | bytes 221192 | tf_op jit(solution)/shard_map/ppermute | solution.py:607
  9.7 4.9 %collective-permute-start.4 = (f32[40,128]{1,0:T(8,128)S(1)}, f32[40,128]{1,0:T(8,128)S(1)}, u32[]{:S(2)}, u32[]{:S(2)}) collective-permute-start(f32[40,128]{1,0:T(8,128)S(1)} %get-tuple-element.59), channel_id=1, source_target_pairs={{0,9},{1,8},{4,13},{5,12},{8,1},{9,0},{12,5},{13,4},{2,11},{3,10},... | collective-permute-start | bytes 61448 | tf_op jit(solution)/shard_map/ppermute | solution.py:579
  15.2 1.4 %collective-permute-start.5 = (f32[40,128]{1,0:T(8,128)S(1)}, f32[40,128]{1,0:T(8,128)S(1)}, u32[]{:S(2)}, u32[]{:S(2)}) collective-permute-start(f32[40,128]{1,0:T(8,128)S(1)} %get-tuple-element.66), channel_id=1, source_target_pairs={{0,1},{1,0},{4,5},{5,4},{8,9},{9,8},{12,13},{13,12},{2,3},{3,2},{6... | collective-permute-start | bytes 61448 | tf_op jit(solution)/shard_map/ppermute | solution.py:579
  16.6 4.1 %collective-permute-start.6 = (f32[32,128]{1,0:T(8,128)S(1)}, f32[32,128]{1,0:T(8,128)S(1)}, u32[]{:S(2)}, u32[]{:S(2)}) collective-permute-start(f32[32,128]{1,0:T(8,128)S(1)} %get-tuple-element.67), channel_id=1, source_target_pairs={{0,9},{1,13},{2,11},{3,15},{5,12},{4,8},{7,14},{6,10},{9,0},{8,4},... | collective-permute-start | bytes 49160 | tf_op jit(solution)/shard_map/ppermute | solution.py:602
  19.3 3.2 %collective-permute-start.7 = (f32[32,128]{1,0:T(8,128)S(1)}, f32[32,128]{1,0:T(8,128)S(1)}, u32[]{:S(2)}, u32[]{:S(2)}) collective-permute-start(f32[32,128]{1,0:T(8,128)S(1)} %get-tuple-element.68), channel_id=1, source_target_pairs={{0,5},{1,3},{2,7},{3,1},{5,0},{4,6},{7,2},{6,4},{9,12},{8,10},{11,... | collective-permute-start | bytes 49160 | tf_op jit(solution)/shard_map/ppermute | solution.py:602
  22.4 1.3 %collective-permute-start.8 = (f32[72,128]{1,0:T(8,128)S(1)}, f32[72,128]{1,0:T(8,128)S(1)}, u32[]{:S(2)}, u32[]{:S(2)}) collective-permute-start(f32[72,128]{1,0:T(8,128)S(1)} %get-tuple-element.75.sums), channel_id=1, source_target_pairs={{0,1},{1,0},{4,5},{5,4},{8,9},{9,8},{12,13},{13,12},{2,3},{3,2},{6... | collective-permute-start | bytes 110600 | tf_op jit(solution)/shard_map/ppermute | solution.py:579

commit v11 on v10

--- a/solution.py
+++ b/solution.py
@@ -54,7 +54,7 @@
     place = fold_place(cols) // (2 * HALO)
     slots, tiles = fold_slots(high, cols, fields)
     out = [jnp.zeros((8, cols), F32)] * tiles
-    for g, (k, at) in enumerate(slots):
+    for g, (k, at) in enumerate(slots[:-1]):
         for i in range(fields):
             slot = at * fields + i
             rows = ext[high * i + 8 * g : high * i + 8 * g + 8, :]
@@ -95,7 +95,7 @@
     for g, (k, at) in enumerate(fold_slots(high, cols, count)[0]):
         x = own[8 * g : 8 * g + 8]
         for z, i in enumerate(fields):
-            base = strip_base(z) + width
+            base = strip_base(z if len(fields) > 1 else 0) + width
             moved = turn_lanes(tiles[k], base - width * (at * count + i))
             x = jnp.where(lanes_from(x.shape, base, width), moved, x)
         out.append(x)
@@ -139,7 +139,7 @@
     for copy in copies:
         copy.start()
     sub = lax.axis_index("sub")
-    msg[...] = jnp.zeros_like(msg)
+    msg[4 * n : 4 * n + 16, :] = jnp.zeros((16, msg.shape[1]), F32)
     for z in range(levels + 1):
         ext[high * z + rows : high * (z + 1), :] = jnp.zeros((8, cols), F32)
     for copy in copies:
@@ -287,12 +287,13 @@
         left = jnp.where(tile > 0, jnp.where(even, far, near), 0.0)
         tiles.append(jnp.where(lax.rem(lane, 2 * HALO) < HALO, right, turn_lanes(left, 2 * HALO)))
     fold_out[...] = jnp.concatenate(tiles, axis=0)
-    mixed = []
-    for x in tiles:
-        shifted = [turn_lanes(x, -2 * HALO * z) for z in range(levels)]
-        mixed.append(sum(share_rows[z : z + 1, :] * y for z, y in enumerate(shifted)))
     wet = strips_beyond(tiles, strips[high : 2 * high, :], [levels], levels + 1)
-    heat = diffused(wet, [strips_beyond(mixed, strips[0:high, :], [0], levels + 1)])[0]
+    heat = strips[0:high, :]
+    for z in range(levels):
+        scaled = [share_rows[z : z + 1, :] * x for x in tiles]
+        beyond_z = strips_beyond(scaled, jnp.zeros_like(heat), [z], levels + 1)
+        heat += beyond_z
+    heat = diffused(wet, [heat])[0]
     heat = from_strips(heat[:rows], 0, block_heat[...])
     own_wet = ext[high * levels : high * levels + rows, :]
     lev_out[0:rows, :] = surface[...]
@@ -412,8 +413,8 @@
 
         @pl.when(lead)
         def _():
-            chip_out[0:8, :] = sums(2)
-            chip_out[8:16, :] = sums(1)
+            chip_out[0:8, :] = sums(1)
+            chip_out[8:16, :] = sums(2)
 
         @pl.when(jnp.logical_not(lead))
         def _():
@@ -458,8 +459,8 @@
 
     @pl.when(jnp.logical_not(lead))
     def _():
-        first[...] = sums(2)
-        second[...] = sums(1)
+        first[...] = sums(1)
+        second[...] = sums(2)
 
 
 def scatter(n, rows, cols, tile, cell_of, value_of, col_hot_of=None):
@@ -469,11 +470,9 @@
             at = 2 * step + band
             cell = cell_of(2 * (tile ^ step) + band)
             row, col = cell // cols, lax.rem(cell, cols)
-            row_mask = lax.broadcasted_iota(jnp.int32, (rows, cell.shape[1]), 0) == row
-            spread = jnp.concatenate(
-                [jnp.where(row_mask, x.astype(F32), 0.0).astype(BF16) for x in halves(value_of(at))],
-                axis=0,
-            )
+            row_hot = onehot(row, rows)
+            high, low = halves(value_of(at))
+            spread = jnp.concatenate([row_hot * high, row_hot * low], axis=0)
             if col_hot_of:
                 total += dot(spread, col_hot_of(at), 1, 0)
             else:
@@ -705,8 +704,8 @@
         first, second = call(
             merge_kernel, [(32, cols), (32, cols)], [values, *returns[1:], theirs]
         )
-        first = by_role(first, (3, 0), (2, 0))
-        second = by_role(second, (0, 1), (1, 0))
+        first = by_role(first, (3, 0), (1, 0))
+        second = by_role(second, (0, 1), (2, 0))
         scratch = [pltpu.VMEM((2 * n, cells), F32)]
         sums, second = call(
             functools.partial(post_kernel, n),

time: 24.6 us -> 24.5 us (level)
  waiting for transfers between devices: 5.93 us -> 5.68 us
  transfers between devices with their start and end apart: 9 -> 9, of which waited for: 6 -> 5; matrix products, arithmetic and copies ran while one was open for 0% -> 0% of each run, Pallas kernels for 10% -> 10%
where the time goes in v11:
time: 24.5 us; the launch traced here: 24.3 us
  starting transfers between devices  12.7 us (52%)
  waiting for transfers between devices  5.68 us (23%)
  Pallas kernels  5.18 us (21%)
  between operations  0.71 us (3%)
    ppermute x5, starting transfers between devices, traded(): return lax.ppermute(x, ('tile', 'sub'), pairs)  7.4 us
    pallas_call x12, Pallas kernels, call(): pl.pallas_call(kernel, out_shape=outs, in_specs=specs or [VMEM] * len(ope...  5.18 us
    ppermute x5, waiting for transfers between devices, traded(): return lax.ppermute(x, ('tile', 'sub'), pairs)  3.38 us
    ppermute x2, starting transfers between devices, by_role(): return lax.ppermute(x, ('tile', 'lev', 'sub'), pairs)  3.09 us
    ppermute x2, waiting for transfers between devices, by_role(): return lax.ppermute(x, ('tile', 'lev', 'sub'), pairs)  2.29 us
    ppermute x1, starting transfers between devices, lev_parts(): return [x, lax.ppermute(x, 'lev', [(0, 1), (1, 0)])]  1.88 us
  transfers between devices with their start and end apart: 9, of which 5 were waited for; matrix products, arithmetic and copies ran while one was open for 0% of the time, Pallas kernels for 10%

profile of v11, /device:TPU:0, one launch (start us, length us, event | category | flops | bytes accessed | tf_op | source)
XLA Modules:
  0.0 24.3 jit_solution(11914752371917802895)
XLA Ops:
  0.6 1.0 %shard_map.130 = (f32[40,256]{1,0:T(8,128)S(1)}, f32[216,128]{1,0:T(8,128)S(1)}) custom-call(f32[2,64,128]{2,1,0:T(8,128)} %refs_0_.2, s32[64,128]{1,0:T(8,128)} %refs_1_.2, f32[1,256]{1,0:T(1,128)} %bitcast.13, f32[1,256]{1,0:T(1,128)} %bitcast.14, f32[1,256]{1,0:T(1,128)} %bitcast.15, s32[8,256]{1,0:T(8,128)} %bitcast.9, f32[8,256]{1,0:T(8,128)} %bitcast.10), custom_call_target="tpu_custom_call" | custom-call | tf_op jit(solution)/shard_map/pallas_call | solution.py:24
  1.6 0.5 %collective-permute-start = (f32[40,256]{1,0:T(8,128)S(1)}, f32[40,256]{1,0:T(8,128)S(1)}, u32[]{:S(2)}, u32[]{:S(2)}) collective-permute-start(f32[40,256]{1,0:T(8,128)S(1)} %get-tuple-element.41.msg.refs_5_), channel_id=1, source_target_pairs={{0,1},{1,0},{4,5},{5,4},{8,9},{9,8},{12,13},{13,12},{2,3},{3,2},{6... | collective-permute-start | bytes 122888 | tf_op jit(solution)/shard_map/ppermute | solution.py:578
  2.1 0.9 %collective-permute-done.other.refs_6_ = f32[40,256]{1,0:T(8,128)S(1)} collective-permute-done((f32[40,256]{1,0:T(8,128)S(1)}, f32[40,256]{1,0:T(8,128)S(1)}, u32[]{:S(2)}, u32[]{:S(2)}) %collective-permute-start) | collective-permute-done | bytes 40992 | tf_op jit(solution)/shard_map/ppermute | solution.py:578
  3.0 0.1 shard_map.131
  3.1 2.7 %collective-permute-start.1 = (f32[48,128]{1,0:T(8,128)S(1)}, f32[48,128]{1,0:T(8,128)S(1)}, u32[]{:S(2)}, u32[]{:S(2)}) collective-permute-start(f32[48,128]{1,0:T(8,128)S(1)} %get-tuple-element.44), channel_id=1, source_target_pairs={{0,5},{1,4},{4,1},{5,0},{8,13},{9,12},{12,9},{13,8},{2,7},{3,6},{6... | collective-permute-start | bytes 73736 | tf_op jit(solution)/shard_map/ppermute | solution.py:578
  5.8 0.3 %collective-permute-start.2 = (f32[16,128]{1,0:T(8,128)S(1)}, f32[16,128]{1,0:T(8,128)S(1)}, u32[]{:S(2)}, u32[]{:S(2)}) collective-permute-start(f32[16,128]{1,0:T(8,128)S(1)} %get-tuple-element.45), channel_id=1, source_target_pairs={{0,1},{1,0},{4,9},{5,8},{8,5},{9,4},{12,13},{13,12},{2,3},{3,2},{6... | collective-permute-start | bytes 24584 | tf_op jit(solution)/shard_map/ppermute | solution.py:587
  6.1 1.2 %shard_map.132 = (f32[2,64,128]{2,1,0:T(8,128)S(1)}, f32[144,128]{1,0:T(8,128)S(1)}, f32[144,128]{1,0:T(8,128)S(1)}, f32[64,128]{1,0:T(8,128)S(1)}, f32[64,128]{...) custom-call(f32[216,128]{1,0:T(8,128)S(1)} %get-tuple-element.43.ext.refs_0_, ...), custom_call_target="tpu_custom_call" | custom-call | tf_op jit(solution)/shard_map/pallas_call | solution.py:24
  7.3 0.0 collective-permute-done.2.refs_2_
  7.4 0.0 collective-permute-done.1.refs_1_.near_in
  7.4 0.5 %shard_map.133 = (f32[16,128]{1,0:T(8,128)S(1)}, f32[144,128]{1,0:T(8,128)S(1)}, f32[40,128]{1,0:T(8,128)S(1)}) custom-call(f32[216,128]{1,0:T(8,128)S(1)} %get-tuple-element.43.ext.refs_0_, f32[48,128]{1,0:T(8,128)S(1)} %collective-permute-done.1.refs_1_.near_in, f32[16,128]{1,0:T(8,128)S(1)} %collective-permute-done.2.refs_2_, ...), custom_call_target="tpu_custom_call" | custom-call | tf_op jit(solution)/shard_map/pallas_call | solution.py:24
  7.9 1.9 %collective-permute-start.3 = (f32[144,128]{1,0:T(8,128)S(1)}, f32[144,128]{1,0:T(8,128)S(1)}, u32[]{:S(2)}, u32[]{:S(2)}) collective-permute-start(f32[144,128]{1,0:T(8,128)S(1)} %get-tuple-element.51.refs_0_), channel_id=1, source_target_pairs={{0,2},{2,0},{1,3},{3,1},{4,6},{6,4},{5,7},{7,5},{8,10},{10,8},{9,1... | collective-permute-start | bytes 221192 | tf_op jit(solution)/shard_map/ppermute | solution.py:606
  9.7 3.4 %collective-permute-start.4 = (f32[40,128]{1,0:T(8,128)S(1)}, f32[40,128]{1,0:T(8,128)S(1)}, u32[]{:S(2)}, u32[]{:S(2)}) collective-permute-start(f32[40,128]{1,0:T(8,128)S(1)} %get-tuple-element.59), channel_id=1, source_target_pairs={{0,9},{1,8},{4,13},{5,12},{8,1},{9,0},{12,5},{13,4},{2,11},{3,10},... | collective-permute-start | bytes 61448 | tf_op jit(solution)/shard_map/ppermute | solution.py:578
  13.2 0.5 %shard_map.134 = (f32[3,4,256]{2,1,0:T(4,128)S(1)}, bf16[4,256,128]{2,1,0:T(8,128)(2,1)S(1)}, f32[8,256]{1,0:T(8,128)S(1)}, f32[2,64,128]{2,1,0:T(8,128)S(1)}) custom-call(f32[40,256]{1,0:T(8,128)S(1)} %get-tuple-element.41.msg.refs_5_, f32[40,256]{1,0:T(8,128)S(1)} %collective-permute-done.other.refs_6_, ...), custom_call_target="tpu_custom_call" | custom-call | tf_op jit(solution)/shard_map/pallas_call | solution.py:24
  13.7 0.9 %collective-permute-done.4.refs_7_ = f32[40,128]{1,0:T(8,128)S(1)} collective-permute-done((f32[40,128]{1,0:T(8,128)S(1)}, f32[40,128]{1,0:T(8,128)S(1)}, u32[]{:S(2)}, u32[]{:S(2)}) %collective-permute-start.4) | collective-permute-done | bytes 20512 | tf_op jit(solution)/shard_map/ppermute | solution.py:578
  14.7 0.0 collective-permute-done.3.refs_1_.refs_0_
  14.7 0.6 %shard_map.135 = (f32[8,256]{1,0:T(8,128)S(1)}, f32[8,256]{1,0:T(8,128)S(1)}, f32[8,256]{1,0:T(8,128)S(1)}, bf16[8,128,256]{2,1,0:T(8,128)(2,1)S(1)}, f32[40,128]{1,0:T(8,128)S(1)}) custom-call(f32[144,128]{1,0:T(8,128)S(1)} %get-tuple-element.51.refs_0_, f32[144,128]{1,0:T(8,128)S(1)} %collective-permute-done.3.refs_1_.refs_0_, ...), custom_call_target="tpu_custom_call" | custom-call | tf_op jit(solution)/shard_map/pallas_call | solution.py:24
  15.2 0.5 %collective-permute-start.5 = (f32[40,128]{1,0:T(8,128)S(1)}, f32[40,128]{1,0:T(8,128)S(1)}, u32[]{:S(2)}, u32[]{:S(2)}) collective-permute-start(f32[40,128]{1,0:T(8,128)S(1)} %get-tuple-element.66), channel_id=1, source_target_pairs={{0,1},{1,0},{4,5},{5,4},{8,9},{9,8},{12,13},{13,12},{2,3},{3,2},{6... | collective-permute-start | bytes 61448 | tf_op jit(solution)/shard_map/ppermute | solution.py:578
  15.7 0.3 %shard_map.136 = (f32[8,128]{1,0:T(8,128)S(1)}, f32[8,128]{1,0:T(8,128)S(1)}, f32[8,128]{1,0:T(8,128)S(1)}) custom-call(f32[8,256]{1,0:T(8,128)S(1)} %get-tuple-element.60.values, f32[8,256]{1,0:T(8,128)S(1)} %get-tuple-element.61.winds, f32[8,256]{1,0:T(8,128)S(1)} %get-tuple-element.62.uppers, ...), custom_call_target="tpu_custom_call" | custom-call | tf_op jit(solution)/shard_map/pallas_call | solution.py:24
  16.0 0.5 %collective-permute-done.5.theirs.refs_1_ = f32[40,128]{1,0:T(8,128)S(1)} collective-permute-done((f32[40,128]{1,0:T(8,128)S(1)}, f32[40,128]{1,0:T(8,128)S(1)}, u32[]{:S(2)}, u32[]{:S(2)}) %collective-permute-start.5) | collective-permute-done | bytes 20512 | tf_op jit(solution)/shard_map/ppermute | solution.py:578
  16.6 1.6 %collective-permute-start.6 = (f32[32,128]{1,0:T(8,128)S(1)}, f32[32,128]{1,0:T(8,128)S(1)}, u32[]{:S(2)}, u32[]{:S(2)}) collective-permute-start(f32[32,128]{1,0:T(8,128)S(1)} %get-tuple-element.67), channel_id=1, source_target_pairs={{0,5},{1,13},{2,7},{3,15},{5,0},{4,8},{7,2},{6,10},{9,12},{8,4},{1... | collective-permute-start | bytes 49160 | tf_op jit(solution)/shard_map/ppermute | solution.py:601
  18.2 1.4 %collective-permute-start.7 = (f32[32,128]{1,0:T(8,128)S(1)}, f32[32,128]{1,0:T(8,128)S(1)}, u32[]{:S(2)}, u32[]{:S(2)}) collective-permute-start(f32[32,128]{1,0:T(8,128)S(1)} %get-tuple-element.68), channel_id=1, source_target_pairs={{0,9},{1,3},{2,11},{3,1},{5,12},{4,6},{7,14},{6,4},{9,0},{8,10},{1... | collective-permute-start | bytes 49160 | tf_op jit(solution)/shard_map/ppermute | solution.py:601
  19.7 0.3 %shard_map.138 = (f32[64,128]{1,0:T(8,128)S(1)}, s32[16,256]{1,0:T(8,128)S(1)}, bf16[16,256,128]{2,1,0:T(8,128)(2,1)S(1)}) custom-call(s32[8,256]{1,0:T(8,128)S(1)} %get-tuple-element.48.refs_7_.refs_5_.marine, f32[8,256]{1,0:T(8,128)S(1)} %get-tuple-element.60.values, f32[144,128]{1,0:T(8,128)S(1)} %collective-permute-done.3.refs_1_.refs_0_, ...), custom_call_target="tpu_custom_call" | custom-call | tf_op jit(solution)/shard_map/pallas_call | solution.py:24
  20.0 0.0 collective-permute-done.6.first
  20.0 2.3 %collective-permute-done.7.second = f32[32,128]{1,0:T(8,128)S(1)} collective-permute-done((f32[32,128]{1,0:T(8,128)S(1)}, f32[32,128]{1,0:T(8,128)S(1)}, u32[]{:S(2)}, u32[]{:S(2)}) %collective-permute-start.7) | collective-permute-done | bytes 16416 | tf_op jit(solution)/shard_map/ppermute | solution.py:601
  22.3 0.2 %collective-permute-start.8 = (f32[72,128]{1,0:T(8,128)S(1)}, f32[72,128]{1,0:T(8,128)S(1)}, u32[]{:S(2)}, u32[]{:S(2)}) collective-permute-start(f32[72,128]{1,0:T(8,128)S(1)} %get-tuple-element.75.sums), channel_id=1, source_target_pairs={{0,1},{1,0},{4,5},{5,4},{8,9},{9,8},{12,13},{13,12},{2,3},{3,2},{6... | collective-permute-start | bytes 110600 | tf_op jit(solution)/shard_map/ppermute | solution.py:578
  22.6 1.0 %collective-permute-done.8.other = f32[72,128]{1,0:T(8,128)S(1)} collective-permute-done((f32[72,128]{1,0:T(8,128)S(1)}, f32[72,128]{1,0:T(8,128)S(1)}, u32[]{:S(2)}, u32[]{:S(2)}) %collective-permute-start.8) | collective-permute-done | bytes 36896 | tf_op jit(solution)/shard_map/ppermute | solution.py:578
  23.6 0.7 %shard_map.141 = (f32[2,64,128]{2,1,0:T(8,128)}, f32[1,256]{1,0:T(1,128)}, f32[1,256]{1,0:T(1,128)}) custom-call(f32[64,128]{1,0:T(8,128)S(1)} %shard_map.140.slots, f32[2,64,128]{2,1,0:T(8,128)S(1)} %get-tuple-element.74.adjoint, f32[8,128]{1,0:T(8,128)S(1)} %get-tuple-element.47.refs_4_.share_rows, f32[72,128]{1,0:T(8,128)S(1)} %get-tuple-element.75.sums, ...), custom_call_target="tpu_custom_call" | custom-call | tf_op jit(solution)/shard_map/pallas_call | solution.py:24
  (3 shorter events, 0.0 us)
Async XLA Ops:
  1.6 1.4 %collective-permute-start = (f32[40,256]{1,0:T(8,128)S(1)}, f32[40,256]{1,0:T(8,128)S(1)}, u32[]{:S(2)}, u32[]{:S(2)}) collective-permute-start(f32[40,256]{1,0:T(8,128)S(1)} %get-tuple-element.41.msg.refs_5_), channel_id=1, source_target_pairs={{0,1},{1,0},{4,5},{5,4},{8,9},{9,8},{12,13},{13,12},{2,3},{3,2},{6... | collective-permute-start | bytes 122888 | tf_op jit(solution)/shard_map/ppermute | solution.py:578
  3.1 4.3 %collective-permute-start.1 = (f32[48,128]{1,0:T(8,128)S(1)}, f32[48,128]{1,0:T(8,128)S(1)}, u32[]{:S(2)}, u32[]{:S(2)}) collective-permute-start(f32[48,128]{1,0:T(8,128)S(1)} %get-tuple-element.44), channel_id=1, source_target_pairs={{0,5},{1,4},{4,1},{5,0},{8,13},{9,12},{12,9},{13,8},{2,7},{3,6},{6... | collective-permute-start | bytes 73736 | tf_op jit(solution)/shard_map/ppermute | solution.py:578
  5.8 1.6 %collective-permute-start.2 = (f32[16,128]{1,0:T(8,128)S(1)}, f32[16,128]{1,0:T(8,128)S(1)}, u32[]{:S(2)}, u32[]{:S(2)}) collective-permute-start(f32[16,128]{1,0:T(8,128)S(1)} %get-tuple-element.45), channel_id=1, source_target_pairs={{0,1},{1,0},{4,9},{5,8},{8,5},{9,4},{12,13},{13,12},{2,3},{3,2},{6... | collective-permute-start | bytes 24584 | tf_op jit(solution)/shard_map/ppermute | solution.py:587
  7.9 6.8 %collective-permute-start.3 = (f32[144,128]{1,0:T(8,128)S(1)}, f32[144,128]{1,0:T(8,128)S(1)}, u32[]{:S(2)}, u32[]{:S(2)}) collective-permute-start(f32[144,128]{1,0:T(8,128)S(1)} %get-tuple-element.51.refs_0_), channel_id=1, source_target_pairs={{0,2},{2,0},{1,3},{3,1},{4,6},{6,4},{5,7},{7,5},{8,10},{10,8},{9,1... | collective-permute-start | bytes 221192 | tf_op jit(solution)/shard_map/ppermute | solution.py:606
  9.7 4.9 %collective-permute-start.4 = (f32[40,128]{1,0:T(8,128)S(1)}, f32[40,128]{1,0:T(8,128)S(1)}, u32[]{:S(2)}, u32[]{:S(2)}) collective-permute-start(f32[40,128]{1,0:T(8,128)S(1)} %get-tuple-element.59), channel_id=1, source_target_pairs={{0,9},{1,8},{4,13},{5,12},{8,1},{9,0},{12,5},{13,4},{2,11},{3,10},... | collective-permute-start | bytes 61448 | tf_op jit(solution)/shard_map/ppermute | solution.py:578
  15.2 1.3 %collective-permute-start.5 = (f32[40,128]{1,0:T(8,128)S(1)}, f32[40,128]{1,0:T(8,128)S(1)}, u32[]{:S(2)}, u32[]{:S(2)}) collective-permute-start(f32[40,128]{1,0:T(8,128)S(1)} %get-tuple-element.66), channel_id=1, source_target_pairs={{0,1},{1,0},{4,5},{5,4},{8,9},{9,8},{12,13},{13,12},{2,3},{3,2},{6... | collective-permute-start | bytes 61448 | tf_op jit(solution)/shard_map/ppermute | solution.py:578
  16.6 3.4 %collective-permute-start.6 = (f32[32,128]{1,0:T(8,128)S(1)}, f32[32,128]{1,0:T(8,128)S(1)}, u32[]{:S(2)}, u32[]{:S(2)}) collective-permute-start(f32[32,128]{1,0:T(8,128)S(1)} %get-tuple-element.67), channel_id=1, source_target_pairs={{0,5},{1,13},{2,7},{3,15},{5,0},{4,8},{7,2},{6,10},{9,12},{8,4},{1... | collective-permute-start | bytes 49160 | tf_op jit(solution)/shard_map/ppermute | solution.py:601
  18.2 4.1 %collective-permute-start.7 = (f32[32,128]{1,0:T(8,128)S(1)}, f32[32,128]{1,0:T(8,128)S(1)}, u32[]{:S(2)}, u32[]{:S(2)}) collective-permute-start(f32[32,128]{1,0:T(8,128)S(1)} %get-tuple-element.68), channel_id=1, source_target_pairs={{0,9},{1,3},{2,11},{3,1},{5,12},{4,6},{7,14},{6,4},{9,0},{8,10},{1... | collective-permute-start | bytes 49160 | tf_op jit(solution)/shard_map/ppermute | solution.py:601
  22.3 1.3 %collective-permute-start.8 = (f32[72,128]{1,0:T(8,128)S(1)}, f32[72,128]{1,0:T(8,128)S(1)}, u32[]{:S(2)}, u32[]{:S(2)}) collective-permute-start(f32[72,128]{1,0:T(8,128)S(1)} %get-tuple-element.75.sums), channel_id=1, source_target_pairs={{0,1},{1,0},{4,5},{5,4},{8,9},{9,8},{12,13},{13,12},{2,3},{3,2},{6... | collective-permute-start | bytes 110600 | tf_op jit(solution)/shard_map/ppermute | solution.py:578

commit v12 on v11

--- a/solution.py
+++ b/solution.py
@@ -99,6 +99,19 @@
             moved = turn_lanes(tiles[k], base - width * (at * count + i))
             x = jnp.where(lanes_from(x.shape, base, width), moved, x)
         out.append(x)
+    return jnp.concatenate(out, axis=0)
+
+
+def strips_apart(right, left, own, i, count):
+    width = 2 * HALO
+    base = strip_base(0) + width
+    high, cols = own.shape
+    out = []
+    for g, (k, at) in enumerate(fold_slots(high, cols, count)[0]):
+        x = own[8 * g : 8 * g + 8]
+        by = base - width * (at * count + i)
+        x = jnp.where(lanes_from(x.shape, base, HALO), turn_lanes(right[k], by), x)
+        out.append(jnp.where(lanes_from(x.shape, base + HALO, HALO), turn_lanes(left[k], by + width), x))
     return jnp.concatenate(out, axis=0)
 
 
@@ -280,19 +293,20 @@
         write_pairs(out, 0, air)
     even = tile % 2 == 0
     lane = lax.broadcasted_iota(jnp.int32, (8, cols), 1)
-    tiles = []
+    tiles, rights, lefts = [], [], []
     for k in range(0, fold, 8):
         near, far = near_in[k : k + 8, :], edge_in[k : k + 8, :]
         right = jnp.where(tile < n - 1, jnp.where(even, near, far), 0.0)
         left = jnp.where(tile > 0, jnp.where(even, far, near), 0.0)
         tiles.append(jnp.where(lax.rem(lane, 2 * HALO) < HALO, right, turn_lanes(left, 2 * HALO)))
+        rights.append(right)
+        lefts.append(left)
     fold_out[...] = jnp.concatenate(tiles, axis=0)
-    wet = strips_beyond(tiles, strips[high : 2 * high, :], [levels], levels + 1)
+    wet = strips_apart(rights, lefts, strips[high : 2 * high, :], levels, levels + 1)
     heat = strips[0:high, :]
     for z in range(levels):
-        scaled = [share_rows[z : z + 1, :] * x for x in tiles]
-        beyond_z = strips_beyond(scaled, jnp.zeros_like(heat), [z], levels + 1)
-        heat += beyond_z
+        scaled = [[share_rows[z : z + 1, :] * x for x in side] for side in (rights, lefts)]
+        heat += strips_apart(*scaled, jnp.zeros_like(heat), z, levels + 1)
     heat = diffused(wet, [heat])[0]
     heat = from_strips(heat[:rows], 0, block_heat[...])
     own_wet = ext[high * levels : high * levels + rows, :]

time: 24.5 us -> 24.4 us (level)
  no operation moved by 1% of the time
where the time goes in v12:
time: 24.4 us; the launch traced here: 24.2 us
  starting transfers between devices  12.7 us (52%)
  waiting for transfers between devices  5.67 us (23%)
  Pallas kernels  5.14 us (21%)
  between operations  0.7 us (3%)
    ppermute x5, starting transfers between devices, traded(): return lax.ppermute(x, ('tile', 'sub'), pairs)  7.39 us
    pallas_call x12, Pallas kernels, call(): pl.pallas_call(kernel, out_shape=outs, in_specs=specs or [VMEM] * len(ope...  5.14 us
    ppermute x5, waiting for transfers between devices, traded(): return lax.ppermute(x, ('tile', 'sub'), pairs)  3.39 us
    ppermute x2, starting transfers between devices, by_role(): return lax.ppermute(x, ('tile', 'lev', 'sub'), pairs)  3.09 us
    ppermute x2, waiting for transfers between devices, by_role(): return lax.ppermute(x, ('tile', 'lev', 'sub'), pairs)  2.28 us
    ppermute x1, starting transfers between devices, lev_parts(): return [x, lax.ppermute(x, 'lev', [(0, 1), (1, 0)])]  1.84 us
  transfers between devices with their start and end apart: 9, of which 5 were waited for; matrix products, arithmetic and copies ran while one was open for 0% of the time, Pallas kernels for 10%

profile of v12, /device:TPU:0, one launch (start us, length us, event | category | flops | bytes accessed | tf_op | source)
XLA Modules:
  0.0 24.2 jit_solution(2192943963314194190)
XLA Ops:
  0.6 1.0 %shard_map.130 = (f32[40,256]{1,0:T(8,128)S(1)}, f32[216,128]{1,0:T(8,128)S(1)}) custom-call(f32[2,64,128]{2,1,0:T(8,128)} %refs_0_.2, s32[64,128]{1,0:T(8,128)} %refs_1_.2, f32[1,256]{1,0:T(1,128)} %bitcast.13, f32[1,256]{1,0:T(1,128)} %bitcast.14, f32[1,256]{1,0:T(1,128)} %bitcast.15, s32[8,256]{1,0:T(8,128)} %bitcast.9, f32[8,256]{1,0:T(8,128)} %bitcast.10), custom_call_target="tpu_custom_call" | custom-call | tf_op jit(solution)/shard_map/pallas_call | solution.py:24
  1.6 0.5 %collective-permute-start = (f32[40,256]{1,0:T(8,128)S(1)}, f32[40,256]{1,0:T(8,128)S(1)}, u32[]{:S(2)}, u32[]{:S(2)}) collective-permute-start(f32[40,256]{1,0:T(8,128)S(1)} %get-tuple-element.41.msg.refs_5_), channel_id=1, source_target_pairs={{0,1},{1,0},{4,5},{5,4},{8,9},{9,8},{12,13},{13,12},{2,3},{3,2},{6... | collective-permute-start | bytes 122888 | tf_op jit(solution)/shard_map/ppermute | solution.py:592
  2.1 0.9 %collective-permute-done.other.refs_6_ = f32[40,256]{1,0:T(8,128)S(1)} collective-permute-done((f32[40,256]{1,0:T(8,128)S(1)}, f32[40,256]{1,0:T(8,128)S(1)}, u32[]{:S(2)}, u32[]{:S(2)}) %collective-permute-start) | collective-permute-done | bytes 40992 | tf_op jit(solution)/shard_map/ppermute | solution.py:592
  3.0 0.1 shard_map.131
  3.1 2.7 %collective-permute-start.1 = (f32[48,128]{1,0:T(8,128)S(1)}, f32[48,128]{1,0:T(8,128)S(1)}, u32[]{:S(2)}, u32[]{:S(2)}) collective-permute-start(f32[48,128]{1,0:T(8,128)S(1)} %get-tuple-element.44), channel_id=1, source_target_pairs={{0,5},{1,4},{4,1},{5,0},{8,13},{9,12},{12,9},{13,8},{2,7},{3,6},{6... | collective-permute-start | bytes 73736 | tf_op jit(solution)/shard_map/ppermute | solution.py:592
  5.8 0.3 %collective-permute-start.2 = (f32[16,128]{1,0:T(8,128)S(1)}, f32[16,128]{1,0:T(8,128)S(1)}, u32[]{:S(2)}, u32[]{:S(2)}) collective-permute-start(f32[16,128]{1,0:T(8,128)S(1)} %get-tuple-element.45), channel_id=1, source_target_pairs={{0,1},{1,0},{4,9},{5,8},{8,5},{9,4},{12,13},{13,12},{2,3},{3,2},{6... | collective-permute-start | bytes 24584 | tf_op jit(solution)/shard_map/ppermute | solution.py:601
  6.1 1.2 %shard_map.132 = (f32[2,64,128]{2,1,0:T(8,128)S(1)}, f32[144,128]{1,0:T(8,128)S(1)}, f32[144,128]{1,0:T(8,128)S(1)}, f32[64,128]{1,0:T(8,128)S(1)}, f32[64,128]{...) custom-call(f32[216,128]{1,0:T(8,128)S(1)} %get-tuple-element.43.ext.refs_0_, ...), custom_call_target="tpu_custom_call" | custom-call | tf_op jit(solution)/shard_map/pallas_call | solution.py:24
  7.3 0.0 collective-permute-done.2.refs_2_
  7.4 0.0 collective-permute-done.1.refs_1_.near_in
  7.4 0.4 %shard_map.133 = (f32[16,128]{1,0:T(8,128)S(1)}, f32[144,128]{1,0:T(8,128)S(1)}, f32[40,128]{1,0:T(8,128)S(1)}) custom-call(f32[216,128]{1,0:T(8,128)S(1)} %get-tuple-element.43.ext.refs_0_, f32[48,128]{1,0:T(8,128)S(1)} %collective-permute-done.1.refs_1_.near_in, f32[16,128]{1,0:T(8,128)S(1)} %collective-permute-done.2.refs_2_, ...), custom_call_target="tpu_custom_call" | custom-call | tf_op jit(solution)/shard_map/pallas_call | solution.py:24
  7.8 1.8 %collective-permute-start.3 = (f32[144,128]{1,0:T(8,128)S(1)}, f32[144,128]{1,0:T(8,128)S(1)}, u32[]{:S(2)}, u32[]{:S(2)}) collective-permute-start(f32[144,128]{1,0:T(8,128)S(1)} %get-tuple-element.51.refs_0_), channel_id=1, source_target_pairs={{0,2},{2,0},{1,3},{3,1},{4,6},{6,4},{5,7},{7,5},{8,10},{10,8},{9,1... | collective-permute-start | bytes 221192 | tf_op jit(solution)/shard_map/ppermute | solution.py:620
  9.6 3.4 %collective-permute-start.4 = (f32[40,128]{1,0:T(8,128)S(1)}, f32[40,128]{1,0:T(8,128)S(1)}, u32[]{:S(2)}, u32[]{:S(2)}) collective-permute-start(f32[40,128]{1,0:T(8,128)S(1)} %get-tuple-element.59), channel_id=1, source_target_pairs={{0,9},{1,8},{4,13},{5,12},{8,1},{9,0},{12,5},{13,4},{2,11},{3,10},... | collective-permute-start | bytes 61448 | tf_op jit(solution)/shard_map/ppermute | solution.py:592
  13.1 0.5 %shard_map.134 = (f32[3,4,256]{2,1,0:T(4,128)S(1)}, bf16[4,256,128]{2,1,0:T(8,128)(2,1)S(1)}, f32[8,256]{1,0:T(8,128)S(1)}, f32[2,64,128]{2,1,0:T(8,128)S(1)}) custom-call(f32[40,256]{1,0:T(8,128)S(1)} %get-tuple-element.41.msg.refs_5_, f32[40,256]{1,0:T(8,128)S(1)} %collective-permute-done.other.refs_6_, ...), custom_call_target="tpu_custom_call" | custom-call | tf_op jit(solution)/shard_map/pallas_call | solution.py:24
  13.6 0.9 %collective-permute-done.4.refs_7_ = f32[40,128]{1,0:T(8,128)S(1)} collective-permute-done((f32[40,128]{1,0:T(8,128)S(1)}, f32[40,128]{1,0:T(8,128)S(1)}, u32[]{:S(2)}, u32[]{:S(2)}) %collective-permute-start.4) | collective-permute-done | bytes 20512 | tf_op jit(solution)/shard_map/ppermute | solution.py:592
  14.6 0.0 collective-permute-done.3.refs_1_.refs_0_
  14.6 0.6 %shard_map.135 = (f32[8,256]{1,0:T(8,128)S(1)}, f32[8,256]{1,0:T(8,128)S(1)}, f32[8,256]{1,0:T(8,128)S(1)}, bf16[8,128,256]{2,1,0:T(8,128)(2,1)S(1)}, f32[40,128]{1,0:T(8,128)S(1)}) custom-call(f32[144,128]{1,0:T(8,128)S(1)} %get-tuple-element.51.refs_0_, f32[144,128]{1,0:T(8,128)S(1)} %collective-permute-done.3.refs_1_.refs_0_, ...), custom_call_target="tpu_custom_call" | custom-call | tf_op jit(solution)/shard_map/pallas_call | solution.py:24
  15.1 0.5 %collective-permute-start.5 = (f32[40,128]{1,0:T(8,128)S(1)}, f32[40,128]{1,0:T(8,128)S(1)}, u32[]{:S(2)}, u32[]{:S(2)}) collective-permute-start(f32[40,128]{1,0:T(8,128)S(1)} %get-tuple-element.66), channel_id=1, source_target_pairs={{0,1},{1,0},{4,5},{5,4},{8,9},{9,8},{12,13},{13,12},{2,3},{3,2},{6... | collective-permute-start | bytes 61448 | tf_op jit(solution)/shard_map/ppermute | solution.py:592
  15.7 0.3 %shard_map.136 = (f32[8,128]{1,0:T(8,128)S(1)}, f32[8,128]{1,0:T(8,128)S(1)}, f32[8,128]{1,0:T(8,128)S(1)}) custom-call(f32[8,256]{1,0:T(8,128)S(1)} %get-tuple-element.60.values, f32[8,256]{1,0:T(8,128)S(1)} %get-tuple-element.61.winds, f32[8,256]{1,0:T(8,128)S(1)} %get-tuple-element.62.uppers, ...), custom_call_target="tpu_custom_call" | custom-call | tf_op jit(solution)/shard_map/pallas_call | solution.py:24
  15.9 0.5 %collective-permute-done.5.theirs.refs_1_ = f32[40,128]{1,0:T(8,128)S(1)} collective-permute-done((f32[40,128]{1,0:T(8,128)S(1)}, f32[40,128]{1,0:T(8,128)S(1)}, u32[]{:S(2)}, u32[]{:S(2)}) %collective-permute-start.5) | collective-permute-done | bytes 20512 | tf_op jit(solution)/shard_map/ppermute | solution.py:592
  16.5 1.6 %collective-permute-start.6 = (f32[32,128]{1,0:T(8,128)S(1)}, f32[32,128]{1,0:T(8,128)S(1)}, u32[]{:S(2)}, u32[]{:S(2)}) collective-permute-start(f32[32,128]{1,0:T(8,128)S(1)} %get-tuple-element.67), channel_id=1, source_target_pairs={{0,5},{1,13},{2,7},{3,15},{5,0},{4,8},{7,2},{6,10},{9,12},{8,4},{1... | collective-permute-start | bytes 49160 | tf_op jit(solution)/shard_map/ppermute | solution.py:615
  18.1 1.4 %collective-permute-start.7 = (f32[32,128]{1,0:T(8,128)S(1)}, f32[32,128]{1,0:T(8,128)S(1)}, u32[]{:S(2)}, u32[]{:S(2)}) collective-permute-start(f32[32,128]{1,0:T(8,128)S(1)} %get-tuple-element.68), channel_id=1, source_target_pairs={{0,9},{1,3},{2,11},{3,1},{5,12},{4,6},{7,14},{6,4},{9,0},{8,10},{1... | collective-permute-start | bytes 49160 | tf_op jit(solution)/shard_map/ppermute | solution.py:615
  19.6 0.3 %shard_map.138 = (f32[64,128]{1,0:T(8,128)S(1)}, s32[16,256]{1,0:T(8,128)S(1)}, bf16[16,256,128]{2,1,0:T(8,128)(2,1)S(1)}) custom-call(s32[8,256]{1,0:T(8,128)S(1)} %get-tuple-element.48.refs_7_.refs_5_.marine, f32[8,256]{1,0:T(8,128)S(1)} %get-tuple-element.60.values, f32[144,128]{1,0:T(8,128)S(1)} %collective-permute-done.3.refs_1_.refs_0_, ...), custom_call_target="tpu_custom_call" | custom-call | tf_op jit(solution)/shard_map/pallas_call | solution.py:24
  19.9 0.0 collective-permute-done.6.first
  19.9 2.3 %collective-permute-done.7.second = f32[32,128]{1,0:T(8,128)S(1)} collective-permute-done((f32[32,128]{1,0:T(8,128)S(1)}, f32[32,128]{1,0:T(8,128)S(1)}, u32[]{:S(2)}, u32[]{:S(2)}) %collective-permute-start.7) | collective-permute-done | bytes 16416 | tf_op jit(solution)/shard_map/ppermute | solution.py:615
  22.2 0.2 %collective-permute-start.8 = (f32[72,128]{1,0:T(8,128)S(1)}, f32[72,128]{1,0:T(8,128)S(1)}, u32[]{:S(2)}, u32[]{:S(2)}) collective-permute-start(f32[72,128]{1,0:T(8,128)S(1)} %get-tuple-element.75.sums), channel_id=1, source_target_pairs={{0,1},{1,0},{4,5},{5,4},{8,9},{9,8},{12,13},{13,12},{2,3},{3,2},{6... | collective-permute-start | bytes 110600 | tf_op jit(solution)/shard_map/ppermute | solution.py:592
  22.5 1.0 %collective-permute-done.8.other = f32[72,128]{1,0:T(8,128)S(1)} collective-permute-done((f32[72,128]{1,0:T(8,128)S(1)}, f32[72,128]{1,0:T(8,128)S(1)}, u32[]{:S(2)}, u32[]{:S(2)}) %collective-permute-start.8) | collective-permute-done | bytes 36896 | tf_op jit(solution)/shard_map/ppermute | solution.py:592
  23.5 0.7 %shard_map.141 = (f32[2,64,128]{2,1,0:T(8,128)}, f32[1,256]{1,0:T(1,128)}, f32[1,256]{1,0:T(1,128)}) custom-call(f32[64,128]{1,0:T(8,128)S(1)} %shard_map.140.slots, f32[2,64,128]{2,1,0:T(8,128)S(1)} %get-tuple-element.74.adjoint, f32[8,128]{1,0:T(8,128)S(1)} %get-tuple-element.47.refs_4_.share_rows, f32[72,128]{1,0:T(8,128)S(1)} %get-tuple-element.75.sums, ...), custom_call_target="tpu_custom_call" | custom-call | tf_op jit(solution)/shard_map/pallas_call | solution.py:24
  (3 shorter events, 0.0 us)
Async XLA Ops:
  1.6 1.4 %collective-permute-start = (f32[40,256]{1,0:T(8,128)S(1)}, f32[40,256]{1,0:T(8,128)S(1)}, u32[]{:S(2)}, u32[]{:S(2)}) collective-permute-start(f32[40,256]{1,0:T(8,128)S(1)} %get-tuple-element.41.msg.refs_5_), channel_id=1, source_target_pairs={{0,1},{1,0},{4,5},{5,4},{8,9},{9,8},{12,13},{13,12},{2,3},{3,2},{6... | collective-permute-start | bytes 122888 | tf_op jit(solution)/shard_map/ppermute | solution.py:592
  3.1 4.3 %collective-permute-start.1 = (f32[48,128]{1,0:T(8,128)S(1)}, f32[48,128]{1,0:T(8,128)S(1)}, u32[]{:S(2)}, u32[]{:S(2)}) collective-permute-start(f32[48,128]{1,0:T(8,128)S(1)} %get-tuple-element.44), channel_id=1, source_target_pairs={{0,5},{1,4},{4,1},{5,0},{8,13},{9,12},{12,9},{13,8},{2,7},{3,6},{6... | collective-permute-start | bytes 73736 | tf_op jit(solution)/shard_map/ppermute | solution.py:592
  5.8 1.6 %collective-permute-start.2 = (f32[16,128]{1,0:T(8,128)S(1)}, f32[16,128]{1,0:T(8,128)S(1)}, u32[]{:S(2)}, u32[]{:S(2)}) collective-permute-start(f32[16,128]{1,0:T(8,128)S(1)} %get-tuple-element.45), channel_id=1, source_target_pairs={{0,1},{1,0},{4,9},{5,8},{8,5},{9,4},{12,13},{13,12},{2,3},{3,2},{6... | collective-permute-start | bytes 24584 | tf_op jit(solution)/shard_map/ppermute | solution.py:601
  7.8 6.8 %collective-permute-start.3 = (f32[144,128]{1,0:T(8,128)S(1)}, f32[144,128]{1,0:T(8,128)S(1)}, u32[]{:S(2)}, u32[]{:S(2)}) collective-permute-start(f32[144,128]{1,0:T(8,128)S(1)} %get-tuple-element.51.refs_0_), channel_id=1, source_target_pairs={{0,2},{2,0},{1,3},{3,1},{4,6},{6,4},{5,7},{7,5},{8,10},{10,8},{9,1... | collective-permute-start | bytes 221192 | tf_op jit(solution)/shard_map/ppermute | solution.py:620
  9.6 4.9 %collective-permute-start.4 = (f32[40,128]{1,0:T(8,128)S(1)}, f32[40,128]{1,0:T(8,128)S(1)}, u32[]{:S(2)}, u32[]{:S(2)}) collective-permute-start(f32[40,128]{1,0:T(8,128)S(1)} %get-tuple-element.59), channel_id=1, source_target_pairs={{0,9},{1,8},{4,13},{5,12},{8,1},{9,0},{12,5},{13,4},{2,11},{3,10},... | collective-permute-start | bytes 61448 | tf_op jit(solution)/shard_map/ppermute | solution.py:592
  15.1 1.3 %collective-permute-start.5 = (f32[40,128]{1,0:T(8,128)S(1)}, f32[40,128]{1,0:T(8,128)S(1)}, u32[]{:S(2)}, u32[]{:S(2)}) collective-permute-start(f32[40,128]{1,0:T(8,128)S(1)} %get-tuple-element.66), channel_id=1, source_target_pairs={{0,1},{1,0},{4,5},{5,4},{8,9},{9,8},{12,13},{13,12},{2,3},{3,2},{6... | collective-permute-start | bytes 61448 | tf_op jit(solution)/shard_map/ppermute | solution.py:592
  16.5 3.4 %collective-permute-start.6 = (f32[32,128]{1,0:T(8,128)S(1)}, f32[32,128]{1,0:T(8,128)S(1)}, u32[]{:S(2)}, u32[]{:S(2)}) collective-permute-start(f32[32,128]{1,0:T(8,128)S(1)} %get-tuple-element.67), channel_id=1, source_target_pairs={{0,5},{1,13},{2,7},{3,15},{5,0},{4,8},{7,2},{6,10},{9,12},{8,4},{1... | collective-permute-start | bytes 49160 | tf_op jit(solution)/shard_map/ppermute | solution.py:615
  18.1 4.1 %collective-permute-start.7 = (f32[32,128]{1,0:T(8,128)S(1)}, f32[32,128]{1,0:T(8,128)S(1)}, u32[]{:S(2)}, u32[]{:S(2)}) collective-permute-start(f32[32,128]{1,0:T(8,128)S(1)} %get-tuple-element.68), channel_id=1, source_target_pairs={{0,9},{1,3},{2,11},{3,1},{5,12},{4,6},{7,14},{6,4},{9,0},{8,10},{1... | collective-permute-start | bytes 49160 | tf_op jit(solution)/shard_map/ppermute | solution.py:615
  22.2 1.3 %collective-permute-start.8 = (f32[72,128]{1,0:T(8,128)S(1)}, f32[72,128]{1,0:T(8,128)S(1)}, u32[]{:S(2)}, u32[]{:S(2)}) collective-permute-start(f32[72,128]{1,0:T(8,128)S(1)} %get-tuple-element.75.sums), channel_id=1, source_target_pairs={{0,1},{1,0},{4,5},{5,4},{8,9},{9,8},{12,13},{13,12},{2,3},{3,2},{6... | collective-permute-start | bytes 110600 | tf_op jit(solution)/shard_map/ppermute | solution.py:592

commit v13 on v12

--- a/solution.py
+++ b/solution.py
@@ -155,13 +155,9 @@
     msg[4 * n : 4 * n + 16, :] = jnp.zeros((16, msg.shape[1]), F32)
     for z in range(levels + 1):
         ext[high * z + rows : high * (z + 1), :] = jnp.zeros((8, cols), F32)
-    for copy in copies:
+    for copy in copies[: levels + 1]:
         copy.wait()
     ext[high * levels : high * levels + rows, :] = sea_in[...].astype(F32)
-    msg[0 : 2 * n, :] = index_in[...].astype(F32)
-    msg[2 * n : 4 * n, :] = weight_in[...]
-    for i, ref in enumerate((sky_in, breeze_in, energy_in)):
-        msg[4 * n + i : 4 * n + i + 1, :] = ref[...]
     base = 4 * n + 8
     for i in range(levels + 1):
         at, top, left = high * i, base + HALO * (i // 2), cols * (i % 2)
@@ -170,6 +166,12 @@
     edges = folded(ext, high, levels + 1)
     for k in range(2):
         msg[4 * n + 16 : 4 * n + 24, cols * k : cols * (k + 1)] = edges[8 * k : 8 * k + 8]
+    for copy in copies[levels + 1 :]:
+        copy.wait()
+    msg[0 : 2 * n, :] = index_in[...].astype(F32)
+    msg[2 * n : 4 * n, :] = weight_in[...]
+    for i, ref in enumerate((sky_in, breeze_in, energy_in)):
+        msg[4 * n + i : 4 * n + i + 1, :] = ref[...]
 
 
 def halo_rows(n, msg, i, cols):

time: 24.4 us -> 24.4 us (level)
  no operation moved by 1% of the time
where the time goes in v13:
time: 24.4 us; the launch traced here: 24.2 us
  starting transfers between devices  12.7 us (52%)
  waiting for transfers between devices  5.67 us (23%)
  Pallas kernels  5.13 us (21%)
  between operations  0.7 us (3%)
    ppermute x5, starting transfers between devices, traded(): return lax.ppermute(x, ('tile', 'sub'), pairs)  7.4 us
    pallas_call x12, Pallas kernels, call(): pl.pallas_call(kernel, out_shape=outs, in_specs=specs or [VMEM] * len(ope...  5.13 us
    ppermute x5, waiting for transfers between devices, traded(): return lax.ppermute(x, ('tile', 'sub'), pairs)  3.38 us
    ppermute x2, starting transfers between devices, by_role(): return lax.ppermute(x, ('tile', 'lev', 'sub'), pairs)  3.09 us
    ppermute x2, waiting for transfers between devices, by_role(): return lax.ppermute(x, ('tile', 'lev', 'sub'), pairs)  2.28 us
    ppermute x1, starting transfers between devices, lev_parts(): return [x, lax.ppermute(x, 'lev', [(0, 1), (1, 0)])]  1.84 us
  transfers between devices with their start and end apart: 9, of which 5 were waited for; matrix products, arithmetic and copies ran while one was open for 0% of the time, Pallas kernels for 10%

profile of v13, /device:TPU:0, one launch (start us, length us, event | category | flops | bytes accessed | tf_op | source)
XLA Modules:
  0.0 24.2 jit_solution(9982431245845203713)
XLA Ops:
  0.6 1.0 %shard_map.130 = (f32[40,256]{1,0:T(8,128)S(1)}, f32[216,128]{1,0:T(8,128)S(1)}) custom-call(f32[2,64,128]{2,1,0:T(8,128)} %refs_0_.2, s32[64,128]{1,0:T(8,128)} %refs_1_.2, f32[1,256]{1,0:T(1,128)} %bitcast.13, f32[1,256]{1,0:T(1,128)} %bitcast.14, f32[1,256]{1,0:T(1,128)} %bitcast.15, s32[8,256]{1,0:T(8,128)} %bitcast.9, f32[8,256]{1,0:T(8,128)} %bitcast.10), custom_call_target="tpu_custom_call" | custom-call | tf_op jit(solution)/shard_map/pallas_call | solution.py:24
  1.6 0.5 %collective-permute-start = (f32[40,256]{1,0:T(8,128)S(1)}, f32[40,256]{1,0:T(8,128)S(1)}, u32[]{:S(2)}, u32[]{:S(2)}) collective-permute-start(f32[40,256]{1,0:T(8,128)S(1)} %get-tuple-element.41.msg.refs_5_), channel_id=1, source_target_pairs={{0,1},{1,0},{4,5},{5,4},{8,9},{9,8},{12,13},{13,12},{2,3},{3,2},{6... | collective-permute-start | bytes 122888 | tf_op jit(solution)/shard_map/ppermute | solution.py:594
  2.1 0.9 %collective-permute-done.other.refs_6_ = f32[40,256]{1,0:T(8,128)S(1)} collective-permute-done((f32[40,256]{1,0:T(8,128)S(1)}, f32[40,256]{1,0:T(8,128)S(1)}, u32[]{:S(2)}, u32[]{:S(2)}) %collective-permute-start) | collective-permute-done | bytes 40992 | tf_op jit(solution)/shard_map/ppermute | solution.py:594
  3.0 0.1 shard_map.131
  3.1 2.7 %collective-permute-start.1 = (f32[48,128]{1,0:T(8,128)S(1)}, f32[48,128]{1,0:T(8,128)S(1)}, u32[]{:S(2)}, u32[]{:S(2)}) collective-permute-start(f32[48,128]{1,0:T(8,128)S(1)} %get-tuple-element.44), channel_id=1, source_target_pairs={{0,5},{1,4},{4,1},{5,0},{8,13},{9,12},{12,9},{13,8},{2,7},{3,6},{6... | collective-permute-start | bytes 73736 | tf_op jit(solution)/shard_map/ppermute | solution.py:594
  5.8 0.3 %collective-permute-start.2 = (f32[16,128]{1,0:T(8,128)S(1)}, f32[16,128]{1,0:T(8,128)S(1)}, u32[]{:S(2)}, u32[]{:S(2)}) collective-permute-start(f32[16,128]{1,0:T(8,128)S(1)} %get-tuple-element.45), channel_id=1, source_target_pairs={{0,1},{1,0},{4,9},{5,8},{8,5},{9,4},{12,13},{13,12},{2,3},{3,2},{6... | collective-permute-start | bytes 24584 | tf_op jit(solution)/shard_map/ppermute | solution.py:603
  6.1 1.2 %shard_map.132 = (f32[2,64,128]{2,1,0:T(8,128)S(1)}, f32[144,128]{1,0:T(8,128)S(1)}, f32[144,128]{1,0:T(8,128)S(1)}, f32[64,128]{1,0:T(8,128)S(1)}, f32[64,128]{...) custom-call(f32[216,128]{1,0:T(8,128)S(1)} %get-tuple-element.43.ext.refs_0_, ...), custom_call_target="tpu_custom_call" | custom-call | tf_op jit(solution)/shard_map/pallas_call | solution.py:24
  7.3 0.0 collective-permute-done.2.refs_2_
  7.4 0.0 collective-permute-done.1.refs_1_.near_in
  7.4 0.4 %shard_map.133 = (f32[16,128]{1,0:T(8,128)S(1)}, f32[144,128]{1,0:T(8,128)S(1)}, f32[40,128]{1,0:T(8,128)S(1)}) custom-call(f32[216,128]{1,0:T(8,128)S(1)} %get-tuple-element.43.ext.refs_0_, f32[48,128]{1,0:T(8,128)S(1)} %collective-permute-done.1.refs_1_.near_in, f32[16,128]{1,0:T(8,128)S(1)} %collective-permute-done.2.refs_2_, ...), custom_call_target="tpu_custom_call" | custom-call | tf_op jit(solution)/shard_map/pallas_call | solution.py:24
  7.8 1.8 %collective-permute-start.3 = (f32[144,128]{1,0:T(8,128)S(1)}, f32[144,128]{1,0:T(8,128)S(1)}, u32[]{:S(2)}, u32[]{:S(2)}) collective-permute-start(f32[144,128]{1,0:T(8,128)S(1)} %get-tuple-element.51.refs_0_), channel_id=1, source_target_pairs={{0,2},{2,0},{1,3},{3,1},{4,6},{6,4},{5,7},{7,5},{8,10},{10,8},{9,1... | collective-permute-start | bytes 221192 | tf_op jit(solution)/shard_map/ppermute | solution.py:622
  9.7 3.4 %collective-permute-start.4 = (f32[40,128]{1,0:T(8,128)S(1)}, f32[40,128]{1,0:T(8,128)S(1)}, u32[]{:S(2)}, u32[]{:S(2)}) collective-permute-start(f32[40,128]{1,0:T(8,128)S(1)} %get-tuple-element.59), channel_id=1, source_target_pairs={{0,9},{1,8},{4,13},{5,12},{8,1},{9,0},{12,5},{13,4},{2,11},{3,10},... | collective-permute-start | bytes 61448 | tf_op jit(solution)/shard_map/ppermute | solution.py:594
  13.1 0.5 %shard_map.134 = (f32[3,4,256]{2,1,0:T(4,128)S(1)}, bf16[4,256,128]{2,1,0:T(8,128)(2,1)S(1)}, f32[8,256]{1,0:T(8,128)S(1)}, f32[2,64,128]{2,1,0:T(8,128)S(1)}) custom-call(f32[40,256]{1,0:T(8,128)S(1)} %get-tuple-element.41.msg.refs_5_, f32[40,256]{1,0:T(8,128)S(1)} %collective-permute-done.other.refs_6_, ...), custom_call_target="tpu_custom_call" | custom-call | tf_op jit(solution)/shard_map/pallas_call | solution.py:24
  13.6 0.9 %collective-permute-done.4.refs_7_ = f32[40,128]{1,0:T(8,128)S(1)} collective-permute-done((f32[40,128]{1,0:T(8,128)S(1)}, f32[40,128]{1,0:T(8,128)S(1)}, u32[]{:S(2)}, u32[]{:S(2)}) %collective-permute-start.4) | collective-permute-done | bytes 20512 | tf_op jit(solution)/shard_map/ppermute | solution.py:594
  14.6 0.0 collective-permute-done.3.refs_1_.refs_0_
  14.6 0.6 %shard_map.135 = (f32[8,256]{1,0:T(8,128)S(1)}, f32[8,256]{1,0:T(8,128)S(1)}, f32[8,256]{1,0:T(8,128)S(1)}, bf16[8,128,256]{2,1,0:T(8,128)(2,1)S(1)}, f32[40,128]{1,0:T(8,128)S(1)}) custom-call(f32[144,128]{1,0:T(8,128)S(1)} %get-tuple-element.51.refs_0_, f32[144,128]{1,0:T(8,128)S(1)} %collective-permute-done.3.refs_1_.refs_0_, ...), custom_call_target="tpu_custom_call" | custom-call | tf_op jit(solution)/shard_map/pallas_call | solution.py:24
  15.2 0.5 %collective-permute-start.5 = (f32[40,128]{1,0:T(8,128)S(1)}, f32[40,128]{1,0:T(8,128)S(1)}, u32[]{:S(2)}, u32[]{:S(2)}) collective-permute-start(f32[40,128]{1,0:T(8,128)S(1)} %get-tuple-element.66), channel_id=1, source_target_pairs={{0,1},{1,0},{4,5},{5,4},{8,9},{9,8},{12,13},{13,12},{2,3},{3,2},{6... | collective-permute-start | bytes 61448 | tf_op jit(solution)/shard_map/ppermute | solution.py:594
  15.7 0.3 %shard_map.136 = (f32[8,128]{1,0:T(8,128)S(1)}, f32[8,128]{1,0:T(8,128)S(1)}, f32[8,128]{1,0:T(8,128)S(1)}) custom-call(f32[8,256]{1,0:T(8,128)S(1)} %get-tuple-element.60.values, f32[8,256]{1,0:T(8,128)S(1)} %get-tuple-element.61.winds, f32[8,256]{1,0:T(8,128)S(1)} %get-tuple-element.62.uppers, ...), custom_call_target="tpu_custom_call" | custom-call | tf_op jit(solution)/shard_map/pallas_call | solution.py:24
  16.0 0.5 %collective-permute-done.5.theirs.refs_1_ = f32[40,128]{1,0:T(8,128)S(1)} collective-permute-done((f32[40,128]{1,0:T(8,128)S(1)}, f32[40,128]{1,0:T(8,128)S(1)}, u32[]{:S(2)}, u32[]{:S(2)}) %collective-permute-start.5) | collective-permute-done | bytes 20512 | tf_op jit(solution)/shard_map/ppermute | solution.py:594
  16.5 1.6 %collective-permute-start.6 = (f32[32,128]{1,0:T(8,128)S(1)}, f32[32,128]{1,0:T(8,128)S(1)}, u32[]{:S(2)}, u32[]{:S(2)}) collective-permute-start(f32[32,128]{1,0:T(8,128)S(1)} %get-tuple-element.67), channel_id=1, source_target_pairs={{0,5},{1,13},{2,7},{3,15},{5,0},{4,8},{7,2},{6,10},{9,12},{8,4},{1... | collective-permute-start | bytes 49160 | tf_op jit(solution)/shard_map/ppermute | solution.py:617
  18.1 1.4 %collective-permute-start.7 = (f32[32,128]{1,0:T(8,128)S(1)}, f32[32,128]{1,0:T(8,128)S(1)}, u32[]{:S(2)}, u32[]{:S(2)}) collective-permute-start(f32[32,128]{1,0:T(8,128)S(1)} %get-tuple-element.68), channel_id=1, source_target_pairs={{0,9},{1,3},{2,11},{3,1},{5,12},{4,6},{7,14},{6,4},{9,0},{8,10},{1... | collective-permute-start | bytes 49160 | tf_op jit(solution)/shard_map/ppermute | solution.py:617
  19.6 0.3 %shard_map.138 = (f32[64,128]{1,0:T(8,128)S(1)}, s32[16,256]{1,0:T(8,128)S(1)}, bf16[16,256,128]{2,1,0:T(8,128)(2,1)S(1)}) custom-call(s32[8,256]{1,0:T(8,128)S(1)} %get-tuple-element.48.refs_7_.refs_5_.marine, f32[8,256]{1,0:T(8,128)S(1)} %get-tuple-element.60.values, f32[144,128]{1,0:T(8,128)S(1)} %collective-permute-done.3.refs_1_.refs_0_, ...), custom_call_target="tpu_custom_call" | custom-call | tf_op jit(solution)/shard_map/pallas_call | solution.py:24
  19.9 0.0 collective-permute-done.6.first
  19.9 2.3 %collective-permute-done.7.second = f32[32,128]{1,0:T(8,128)S(1)} collective-permute-done((f32[32,128]{1,0:T(8,128)S(1)}, f32[32,128]{1,0:T(8,128)S(1)}, u32[]{:S(2)}, u32[]{:S(2)}) %collective-permute-start.7) | collective-permute-done | bytes 16416 | tf_op jit(solution)/shard_map/ppermute | solution.py:617
  22.2 0.2 %collective-permute-start.8 = (f32[72,128]{1,0:T(8,128)S(1)}, f32[72,128]{1,0:T(8,128)S(1)}, u32[]{:S(2)}, u32[]{:S(2)}) collective-permute-start(f32[72,128]{1,0:T(8,128)S(1)} %get-tuple-element.75.sums), channel_id=1, source_target_pairs={{0,1},{1,0},{4,5},{5,4},{8,9},{9,8},{12,13},{13,12},{2,3},{3,2},{6... | collective-permute-start | bytes 110600 | tf_op jit(solution)/shard_map/ppermute | solution.py:594
  22.5 1.0 %collective-permute-done.8.other = f32[72,128]{1,0:T(8,128)S(1)} collective-permute-done((f32[72,128]{1,0:T(8,128)S(1)}, f32[72,128]{1,0:T(8,128)S(1)}, u32[]{:S(2)}, u32[]{:S(2)}) %collective-permute-start.8) | collective-permute-done | bytes 36896 | tf_op jit(solution)/shard_map/ppermute | solution.py:594
  23.5 0.7 %shard_map.141 = (f32[2,64,128]{2,1,0:T(8,128)}, f32[1,256]{1,0:T(1,128)}, f32[1,256]{1,0:T(1,128)}) custom-call(f32[64,128]{1,0:T(8,128)S(1)} %shard_map.140.slots, f32[2,64,128]{2,1,0:T(8,128)S(1)} %get-tuple-element.74.adjoint, f32[8,128]{1,0:T(8,128)S(1)} %get-tuple-element.47.refs_4_.share_rows, f32[72,128]{1,0:T(8,128)S(1)} %get-tuple-element.75.sums, ...), custom_call_target="tpu_custom_call" | custom-call | tf_op jit(solution)/shard_map/pallas_call | solution.py:24
  (3 shorter events, 0.0 us)
Async XLA Ops:
  1.6 1.4 %collective-permute-start = (f32[40,256]{1,0:T(8,128)S(1)}, f32[40,256]{1,0:T(8,128)S(1)}, u32[]{:S(2)}, u32[]{:S(2)}) collective-permute-start(f32[40,256]{1,0:T(8,128)S(1)} %get-tuple-element.41.msg.refs_5_), channel_id=1, source_target_pairs={{0,1},{1,0},{4,5},{5,4},{8,9},{9,8},{12,13},{13,12},{2,3},{3,2},{6... | collective-permute-start | bytes 122888 | tf_op jit(solution)/shard_map/ppermute | solution.py:594
  3.1 4.3 %collective-permute-start.1 = (f32[48,128]{1,0:T(8,128)S(1)}, f32[48,128]{1,0:T(8,128)S(1)}, u32[]{:S(2)}, u32[]{:S(2)}) collective-permute-start(f32[48,128]{1,0:T(8,128)S(1)} %get-tuple-element.44), channel_id=1, source_target_pairs={{0,5},{1,4},{4,1},{5,0},{8,13},{9,12},{12,9},{13,8},{2,7},{3,6},{6... | collective-permute-start | bytes 73736 | tf_op jit(solution)/shard_map/ppermute | solution.py:594
  5.8 1.6 %collective-permute-start.2 = (f32[16,128]{1,0:T(8,128)S(1)}, f32[16,128]{1,0:T(8,128)S(1)}, u32[]{:S(2)}, u32[]{:S(2)}) collective-permute-start(f32[16,128]{1,0:T(8,128)S(1)} %get-tuple-element.45), channel_id=1, source_target_pairs={{0,1},{1,0},{4,9},{5,8},{8,5},{9,4},{12,13},{13,12},{2,3},{3,2},{6... | collective-permute-start | bytes 24584 | tf_op jit(solution)/shard_map/ppermute | solution.py:603
  7.8 6.8 %collective-permute-start.3 = (f32[144,128]{1,0:T(8,128)S(1)}, f32[144,128]{1,0:T(8,128)S(1)}, u32[]{:S(2)}, u32[]{:S(2)}) collective-permute-start(f32[144,128]{1,0:T(8,128)S(1)} %get-tuple-element.51.refs_0_), channel_id=1, source_target_pairs={{0,2},{2,0},{1,3},{3,1},{4,6},{6,4},{5,7},{7,5},{8,10},{10,8},{9,1... | collective-permute-start | bytes 221192 | tf_op jit(solution)/shard_map/ppermute | solution.py:622
  9.7 4.9 %collective-permute-start.4 = (f32[40,128]{1,0:T(8,128)S(1)}, f32[40,128]{1,0:T(8,128)S(1)}, u32[]{:S(2)}, u32[]{:S(2)}) collective-permute-start(f32[40,128]{1,0:T(8,128)S(1)} %get-tuple-element.59), channel_id=1, source_target_pairs={{0,9},{1,8},{4,13},{5,12},{8,1},{9,0},{12,5},{13,4},{2,11},{3,10},... | collective-permute-start | bytes 61448 | tf_op jit(solution)/shard_map/ppermute | solution.py:594
  15.2 1.3 %collective-permute-start.5 = (f32[40,128]{1,0:T(8,128)S(1)}, f32[40,128]{1,0:T(8,128)S(1)}, u32[]{:S(2)}, u32[]{:S(2)}) collective-permute-start(f32[40,128]{1,0:T(8,128)S(1)} %get-tuple-element.66), channel_id=1, source_target_pairs={{0,1},{1,0},{4,5},{5,4},{8,9},{9,8},{12,13},{13,12},{2,3},{3,2},{6... | collective-permute-start | bytes 61448 | tf_op jit(solution)/shard_map/ppermute | solution.py:594
  16.5 3.4 %collective-permute-start.6 = (f32[32,128]{1,0:T(8,128)S(1)}, f32[32,128]{1,0:T(8,128)S(1)}, u32[]{:S(2)}, u32[]{:S(2)}) collective-permute-start(f32[32,128]{1,0:T(8,128)S(1)} %get-tuple-element.67), channel_id=1, source_target_pairs={{0,5},{1,13},{2,7},{3,15},{5,0},{4,8},{7,2},{6,10},{9,12},{8,4},{1... | collective-permute-start | bytes 49160 | tf_op jit(solution)/shard_map/ppermute | solution.py:617
  18.1 4.1 %collective-permute-start.7 = (f32[32,128]{1,0:T(8,128)S(1)}, f32[32,128]{1,0:T(8,128)S(1)}, u32[]{:S(2)}, u32[]{:S(2)}) collective-permute-start(f32[32,128]{1,0:T(8,128)S(1)} %get-tuple-element.68), channel_id=1, source_target_pairs={{0,9},{1,3},{2,11},{3,1},{5,12},{4,6},{7,14},{6,4},{9,0},{8,10},{1... | collective-permute-start | bytes 49160 | tf_op jit(solution)/shard_map/ppermute | solution.py:617
  22.2 1.3 %collective-permute-start.8 = (f32[72,128]{1,0:T(8,128)S(1)}, f32[72,128]{1,0:T(8,128)S(1)}, u32[]{:S(2)}, u32[]{:S(2)}) collective-permute-start(f32[72,128]{1,0:T(8,128)S(1)} %get-tuple-element.75.sums), channel_id=1, source_target_pairs={{0,1},{1,0},{4,5},{5,4},{8,9},{9,8},{12,13},{13,12},{2,3},{3,2},{6... | collective-permute-start | bytes 110600 | tf_op jit(solution)/shard_map/ppermute | solution.py:594
